TPU v7x, 32 devices: a whole 2x2x4 slice. The times are simulated.
32 devices in a mesh: region: 8 (over z, x), sub: 4 (over y, core).
Axes of the slice: x: 2, y: 2, z: 4, core: 2. Of those that a mesh axis runs over, the one named last changes fastest.
Arguments:
- kkt_inverse: bfloat16 [65536, 2048], P(('region', 'sub')), may hold values from -0.125 to 0.125
- cost_terms: bfloat16 [65536, 256], P(('region', 'sub')), may hold values from -6 to 6
- dual_start: float32 [49152, 256], P(('region', 'sub')), may hold values from -4 to 4
- consensus_start: float32 [8192, 256], P(('region', 'sub')), may hold values from -6 to 6
- block_target: int32 [32, 12], P(('region', 'sub')), may hold values from -1 to 15, as said below
Outputs:
- state: float32 [65536, 256], P(('region', 'sub'))
- duals: float32 [49152, 256], P(('region', 'sub'))
- consensus: float32 [8192, 256], P(('region', 'sub'))
- norms: float32 [2, 2], replicated
Inputs may be any that keep to these rules, and one draw needn't show every extreme that they name: `block_target`: A device has at most 2 live blocks bound for one region, and every device has exactly 2 for some region. At least 10 of a device's slots are live; some device has all 12 live.
All inputs are finite; a program needn't handle non-finite values.
Results may differ from a plain program's by a relative error of at most 0.0034.
Values sent between devices are 32-bit elements; how exact they have to be, the bound alone decides.
No kernel may reach another device: no remote copies, remote signals or barrier semaphores. Data moves between devices by JAX's collectives and lax.ppermute only.
A program may use at most 128 MiB of HBM per device.

v0:
```python
import jax
import jax.numpy as jnp
from jax import lax
from jax.sharding import PartitionSpec as P

BLOCK = 128
CAP = 2
ITERS = 2


penalty = 1.5


def shards(kkt_inverse, cost_terms, dual_start, consensus_start, block_target):
    highest = lax.Precision.HIGHEST
    scen = cost_terms.shape[1]
    target = block_target[0]
    blocks = target.shape[0]
    bound_rows = blocks * BLOCK
    owned = consensus_start.shape[0] // BLOCK
    peers = lax.axis_size("region")
    devices = peers * lax.axis_size("sub")
    live = target >= 0
    livef = live.astype(jnp.float32)
    base = jnp.dot(kkt_inverse, cost_terms, preferred_element_type=jnp.float32)
    coupling = kkt_inverse[:, :bound_rows]
    dual = dual_start.reshape(blocks, BLOCK * scen)
    cons = consensus_start.reshape(owned, BLOCK * scen)
    peer = jnp.where(live, target // owned, -1)
    same = (peer[:, None] == peer[None, :]) & live[:, None]
    earlier = jnp.arange(blocks)[:, None] < jnp.arange(blocks)[None, :]
    rank = jnp.sum((same & earlier).astype(jnp.int32), axis=0)
    slot = jnp.where(live, peer * CAP + rank, -1)
    match = slot[None, :] == jnp.arange(peers * CAP, dtype=jnp.int32)[:, None]
    send_hot = match.astype(jnp.float32)
    labels = jnp.max(jnp.where(match, (target % owned)[None, :], -1), axis=1)
    got_labels = lax.all_to_all(
        labels.reshape(peers, CAP), "region", split_axis=0, concat_axis=0, tiled=True
    ).reshape(peers * CAP)
    recv_hot = (got_labels[None, :] == jnp.arange(owned, dtype=jnp.int32)[:, None]).astype(
        jnp.float32
    )
    counts = jnp.sum(recv_hot, axis=1)

    def fetch(values):
        reply = jnp.dot(recv_hot.T, values, precision=highest).reshape(peers, CAP, -1)
        back = lax.all_to_all(reply, "region", split_axis=0, concat_axis=0, tiled=True).reshape(
            peers * CAP, -1
        )
        return jnp.dot(send_hot.T, back, precision=highest)

    floor_counts = jnp.maximum(counts, 1.0)
    fetched = fetch(cons)
    field = base
    rows = []
    for step in range(ITERS):
        drive = (
            (penalty * livef[:, None] * (fetched - dual))
            .reshape(bound_rows, scen)
            .astype(jnp.bfloat16)
        )
        field = base + jnp.dot(coupling, drive, preferred_element_type=jnp.float32)
        copies = field[:bound_rows].reshape(blocks, BLOCK * scen)
        outgoing = jnp.dot(send_hot, copies + dual, precision=highest).reshape(peers, CAP, -1)
        incoming = lax.all_to_all(
            outgoing, "region", split_axis=0, concat_axis=0, tiled=True
        ).reshape(peers * CAP, -1)
        sums = jnp.dot(recv_hot, incoming, precision=highest)
        renewed = sums / floor_counts[:, None]
        fetched = fetch(renewed)
        gap = copies - fetched
        primal = jnp.sum(livef[:, None] * gap * gap)
        change = renewed - cons
        moved = penalty * penalty * jnp.sum(counts[:, None] * change * change)
        dual = dual + livef[:, None] * gap
        cons = renewed
        rows.append(jnp.stack([primal, moved]))
    table = jnp.stack(rows)
    table = lax.psum(table, ("region", "sub"))
    norms = jnp.sqrt(table / (devices * scen * BLOCK))
    return (field, dual.reshape(bound_rows, scen), cons.reshape(owned * BLOCK, scen), norms)


def solution(mesh):
    in_specs = (
        P(("region", "sub"), None),
        P(("region", "sub"), None),
        P(("region", "sub"), None),
        P(("region", "sub"), None),
        P(("region", "sub"), None),
    )
    out_specs = (
        P(("region", "sub"), None),
        P(("region", "sub"), None),
        P(("region", "sub"), None),
        P(),
    )
    return jax.shard_map(shards, mesh=mesh, in_specs=in_specs, out_specs=out_specs, check_vma=False)
```

profile of v0, /device:TPU:0, one launch (start us, length us, event | category | flops | bytes accessed | tf_op | source)
XLA Modules:
  0.0 404.0 jit_solution(7077875290764358370)
XLA Ops:
  0.6 0.7 fusion.45
  4.3 7.3 %all-to-all-start = ((s32[8,1,2]{2,1,0:T(1,128)}), s32[8,1,2]{2,1,0:T(1,128)S(1)}, u32[]{:S(2)}, u32[]{:S(2)}) async-start(s32[8,1,2]{2,1,0:T(1,128)} %bitcast.5), calls=%async_computation | async-start | bytes 8192 | tf_op jit(solution)/shard_map/all_to_all | solution.py:37
  11.5 1.1 reshape.163
  12.7 5.3 %all-to-all-done = s32[8,1,2]{2,1,0:T(1,128)S(1)} async-done(((s32[8,1,2]{2,1,0:T(1,128)}), s32[8,1,2]{2,1,0:T(1,128)S(1)}, u32[]{:S(2)}, u32[]{:S(2)}) %all-to-all-start) | async-done | bytes 96 | tf_op jit(solution)/shard_map/all_to_all | solution.py:37
  18.0 1.0 fusion.31
  19.1 2.9 copy.25
  22.0 4.5 %all-to-all-start.1 = ((f32[8,2,32768]{2,1,0:T(2,128)}), f32[8,2,32768]{2,1,0:T(2,128)}, u32[]{:S(2)}, u32[]{:S(2)}) async-start(f32[8,2,32768]{2,1,0:T(2,128)} %copy.25), calls=%async_computation.1 | async-start | bytes 4194304 | tf_op jit(solution)/shard_map/all_to_all | solution.py:47
  26.5 1.6 reshape.151
  28.2 7.8 %fusion.47 = f32[2048,256]{1,0:T(8,128)} fusion(bf16[2048,2048]{1,0:T(8,128)(2,1)} %param.5, bf16[2048,256]{1,0:T(8,128)(2,1)S(1)} %copy-done), kind=kOutput, calls=%fused_computation.80 | convolution fusion | flops 2147483648 | bytes 11534336 | tf_op jit(solution)/shard_map/dot_general | solution.py:25
  36.0 37.4 %all-to-all-done.1 = f32[8,2,32768]{2,1,0:T(2,128)} async-done(((f32[8,2,32768]{2,1,0:T(2,128)}), f32[8,2,32768]{2,1,0:T(2,128)}, u32[]{:S(2)}, u32[]{:S(2)}) %all-to-all-start.1) | async-done | bytes 2097184 | tf_op jit(solution)/shard_map/all_to_all | solution.py:47
  73.4 3.7 reshape.150
  77.1 2.8 fusion.1
  80.6 4.8 %fusion.9 = f32[2048,256]{1,0:T(8,128)S(1)} fusion(bf16[1536,256]{1,0:T(8,128)(2,1)S(1)} %convert_element_type.29, bf16[2048,2048]{1,0:T(8,128)(2,1)} %param.5), kind=kOutput, calls=%fused_computation.15 | convolution fusion | flops 1610612736 | bytes 9175040 | tf_op jit(solution)/shard_map/dot_general | solution.py:62
  85.4 2.0 fusion.46
  87.4 1.6 reshape.164
  89.1 1.1 fusion.23
  90.2 3.0 copy.27
  93.1 3.8 all-to-all-start.2
  98.3 46.9 %all-to-all-done.2 = f32[8,2,32768]{2,1,0:T(2,128)S(1)} async-done(((f32[8,2,32768]{2,1,0:T(2,128)}), f32[8,2,32768]{2,1,0:T(2,128)S(1)}, u32[]{:S(2)}, u32[]{:S(2)}) %all-to-all-start.2) | async-done | bytes 2097184 | tf_op jit(solution)/shard_map/all_to_all | solution.py:65
  145.2 2.5 reshape.152
  147.7 2.4 convolution_divide_fusion.1
  150.1 1.1 fusion.37
  151.2 2.3 reshape.153
  153.5 4.4 %all-to-all-start.3 = ((f32[8,2,32768]{2,1,0:T(2,128)}), f32[8,2,32768]{2,1,0:T(2,128)}, u32[]{:S(2)}, u32[]{:S(2)}) async-start(f32[8,2,32768]{2,1,0:T(2,128)} %reshape.153), calls=%async_computation.3 | async-start | bytes 4194304 | tf_op jit(solution)/shard_map/all_to_all | solution.py:47
  157.9 1.6 reshape.155
  159.5 46.1 %all-to-all-done.3 = f32[8,2,32768]{2,1,0:T(2,128)} async-done(((f32[8,2,32768]{2,1,0:T(2,128)}), f32[8,2,32768]{2,1,0:T(2,128)}, u32[]{:S(2)}, u32[]{:S(2)}) %all-to-all-start.3) | async-done | bytes 2097184 | tf_op jit(solution)/shard_map/all_to_all | solution.py:47
  205.6 3.6 reshape.154
  209.2 5.7 %multiply_convert_fusion = (bf16[12,32768]{1,0:T(8,128)(2,1)S(1)}, f32[12,32768]{1,0:T(8,128)}, f32[12,32768]{1,0:T(8,128)}) fusion(f32[12]{0:T(128)S(1)} %broadcast_select_fusion, f32[12,32768]{1,0:T(8,128)} %copy-done.3, f32[12,32768]{1,0:T(8,128)S(1)} %reshape.155, f32[12]{0:T(128)S(1)} %get-tuple-element.13, f32[16,32768]{1,0:T(8,128)} %reshape.154, ...), kind=kOutput, calls=%fused_computation.21 | convolution fusion | flops 77856960 | bytes 9175184 | tf_op jit(solution)/shard_map/dot_general | solution.py:50
  215.6 5.2 %fusion.12 = f32[2048,256]{1,0:T(8,128)S(1)} fusion(f32[2048,256]{1,0:T(8,128)} %fusion.47, bf16[1536,256]{1,0:T(8,128)(2,1)S(1)} %convert_element_type.33, bf16[2048,2048]{1,0:T(8,128)(2,1)} %param.5), kind=kOutput, calls=%fused_computation.16 | convolution fusion | flops 1611137024 | bytes 11272192 | tf_op jit(solution)/shard_map/dot_general | solution.py:62
  220.8 1.3 copy-done.5
  222.1 1.2 slice.14
  223.4 1.6 reshape.156
  225.0 4.1 %fusion.17 = f32[16,32768]{1,0:T(8,128)} fusion(f32[12,32768]{1,0:T(8,128)S(1)} %reshape.156, f32[12,32768]{1,0:T(8,128)} %get-tuple-element.9, s32[12]{0:T(128)S(1)} %get-tuple-element.15), kind=kOutput, calls=%fused_computation.19 | convolution fusion | flops 75890880 | bytes 5242928 | tf_op jit(solution)/shard_map/dot_general | solution.py:64
  229.2 3.4 reshape.157
  232.6 4.7 %all-to-all-start.4 = ((f32[8,2,32768]{2,1,0:T(2,128)}), f32[8,2,32768]{2,1,0:T(2,128)}, u32[]{:S(2)}, u32[]{:S(2)}) async-start(f32[8,2,32768]{2,1,0:T(2,128)} %reshape.157), calls=%async_computation.4 | async-start | bytes 4194304 | tf_op jit(solution)/shard_map/all_to_all | solution.py:65
  237.5 47.5 %all-to-all-done.4 = f32[8,2,32768]{2,1,0:T(2,128)} async-done(((f32[8,2,32768]{2,1,0:T(2,128)}), f32[8,2,32768]{2,1,0:T(2,128)}, u32[]{:S(2)}, u32[]{:S(2)}) %all-to-all-start.4) | async-done | bytes 2097184 | tf_op jit(solution)/shard_map/all_to_all | solution.py:65
  285.0 3.6 reshape.158
  288.6 3.3 fusion.19
  292.0 2.4 fusion.36
  294.4 3.5 reshape.159
  297.9 4.4 %all-to-all-start.5 = ((f32[8,2,32768]{2,1,0:T(2,128)}), f32[8,2,32768]{2,1,0:T(2,128)}, u32[]{:S(2)}, u32[]{:S(2)}) async-start(f32[8,2,32768]{2,1,0:T(2,128)} %reshape.159), calls=%async_computation.5 | async-start | bytes 4194304 | tf_op jit(solution)/shard_map/all_to_all | solution.py:47
  303.6 46.4 %all-to-all-done.5 = f32[8,2,32768]{2,1,0:T(2,128)} async-done(((f32[8,2,32768]{2,1,0:T(2,128)}), f32[8,2,32768]{2,1,0:T(2,128)}, u32[]{:S(2)}, u32[]{:S(2)}) %all-to-all-start.5) | async-done | bytes 2097184 | tf_op jit(solution)/shard_map/all_to_all | solution.py:47
  349.9 3.7 reshape.160
  353.6 7.1 %fusion.15 = (f32[]{:T(128)}, f32[]{:T(128)}, f32[12,32768]{1,0:T(8,128)}) fusion(f32[12]{0:T(128)S(1)} %get-tuple-element.13, f32[12,32768]{1,0:T(8,128)} %copy-done.2, f32[12,32768]{1,0:T(8,128)} %get-tuple-element.17, f32[12,32768]{1,0:T(8,128)} %get-tuple-element.9, f32[12,32768]{1,0:T(8,128)S(1)} %reshape.156, f32[16,32768]{1,0:T(8,128)} %reshape.160, ...), kind=kOutput, calls=%fused_computation.17 | convolution fusion | flops 79036608 | bytes 9961576 | tf_op jit(solution)/shard_map/dot_general | solution.py:50
  360.7 1.4 maximum_bitcast_fusion
  362.1 0.9 reshape.162
  363.0 37.8 %psum.7 = f32[2,2]{1,0:T(2,128)S(1)} all-reduce(f32[2,2]{1,0:T(2,128)S(1)} %pad_maximum_fusion), channel_id=1, replica_groups=mesh['region'=8,'sub'=4] {'region','sub'}, use_global_device_ids=true, to_apply=%region_7.8 | all-reduce | flops 4 | bytes 32 | tf_op jit(solution)/shard_map/psum | solution.py:79
  401.4 2.6 reshape.161
  (40 shorter events, 6.5 us)
Async XLA Ops:
  0.6 27.6 %copy-start = (bf16[2048,256]{1,0:T(8,128)(2,1)S(1)}, bf16[2048,256]{1,0:T(8,128)(2,1)}, u32[]{:S(2)}) copy-start(bf16[2048,256]{1,0:T(8,128)(2,1)} %param.6) | copy-start | bytes 3145732
  4.3 13.6 %all-to-all-start = ((s32[8,1,2]{2,1,0:T(1,128)}), s32[8,1,2]{2,1,0:T(1,128)S(1)}, u32[]{:S(2)}, u32[]{:S(2)}) async-start(s32[8,1,2]{2,1,0:T(1,128)} %bitcast.5), calls=%async_computation | async-start | bytes 8192 | tf_op jit(solution)/shard_map/all_to_all | solution.py:37
  22.0 51.4 %all-to-all-start.1 = ((f32[8,2,32768]{2,1,0:T(2,128)}), f32[8,2,32768]{2,1,0:T(2,128)}, u32[]{:S(2)}, u32[]{:S(2)}) async-start(f32[8,2,32768]{2,1,0:T(2,128)} %copy.25), calls=%async_computation.1 | async-start | bytes 4194304 | tf_op jit(solution)/shard_map/all_to_all | solution.py:47
  26.5 1.7 copy-start.10
  28.2 48.9 %copy-start.3 = (f32[12,32768]{1,0:T(8,128)}, f32[12,32768]{1,0:T(8,128)S(1)}, u32[]{:S(2)}) copy-start(f32[12,32768]{1,0:T(8,128)S(1)} %reshape.151) | copy-start | bytes 4718596
  80.6 4.8 %copy-start.4 = (f32[1536,256]{1,0:T(8,128)S(1)}, f32[1536,256]{1,0:T(8,128)}, u32[]{:S(2)}) copy-start(f32[1536,256]{1,0:T(8,128)} %param.7) | copy-start | bytes 4718596
  80.6 4.8 %copy-start.6 = (f32[2048,256]{1,0:T(8,128)S(1)}, f32[2048,256]{1,0:T(8,128)}, u32[]{:S(2)}) copy-start(f32[2048,256]{1,0:T(8,128)} %fusion.47) | copy-start | bytes 6291460
  93.1 52.1 %all-to-all-start.2 = ((f32[8,2,32768]{2,1,0:T(2,128)}), f32[8,2,32768]{2,1,0:T(2,128)S(1)}, u32[]{:S(2)}, u32[]{:S(2)}) async-start(f32[8,2,32768]{2,1,0:T(2,128)} %copy.27), calls=%async_computation.2 | async-start | bytes 4194304 | tf_op jit(solution)/shard_map/all_to_all | solution.py:65
  150.1 3.4 copy-start.8
  153.5 52.1 %all-to-all-start.3 = ((f32[8,2,32768]{2,1,0:T(2,128)}), f32[8,2,32768]{2,1,0:T(2,128)}, u32[]{:S(2)}, u32[]{:S(2)}) async-start(f32[8,2,32768]{2,1,0:T(2,128)} %reshape.153), calls=%async_computation.3 | async-start | bytes 4194304 | tf_op jit(solution)/shard_map/all_to_all | solution.py:47
  159.5 49.7 %copy-start.2 = (f32[12,32768]{1,0:T(8,128)}, f32[12,32768]{1,0:T(8,128)S(1)}, u32[]{:S(2)}) copy-start(f32[12,32768]{1,0:T(8,128)S(1)} %reshape.155) | copy-start | bytes 4718596
  220.8 1.3 copy-start.5
  232.6 4.8 %copy-start.7 = (f32[256,256]{1,0:T(8,128)S(1)}, f32[256,256]{1,0:T(8,128)}, u32[]{:S(2)}) copy-start(f32[256,256]{1,0:T(8,128)} %param.8) | copy-start | bytes 786436
  232.6 52.4 %all-to-all-start.4 = ((f32[8,2,32768]{2,1,0:T(2,128)}), f32[8,2,32768]{2,1,0:T(2,128)}, u32[]{:S(2)}, u32[]{:S(2)}) async-start(f32[8,2,32768]{2,1,0:T(2,128)} %reshape.157), calls=%async_computation.4 | async-start | bytes 4194304 | tf_op jit(solution)/shard_map/all_to_all | solution.py:65
  237.5 51.1 %copy-start.9 = (f32[2,32768]{1,0:T(2,128)S(1)}, f32[2,32768]{1,0:T(2,128)}, u32[]{:S(2)}) copy-start(f32[2,32768]{1,0:T(2,128)} %copy-done.8) | copy-start | bytes 786436
  297.9 52.0 %all-to-all-start.5 = ((f32[8,2,32768]{2,1,0:T(2,128)}), f32[8,2,32768]{2,1,0:T(2,128)}, u32[]{:S(2)}, u32[]{:S(2)}) async-start(f32[8,2,32768]{2,1,0:T(2,128)} %reshape.159), calls=%async_computation.5 | async-start | bytes 4194304 | tf_op jit(solution)/shard_map/all_to_all | solution.py:47
  362.1 41.9 %copy-start.1 = (bf16[2048,256]{1,0:T(8,128)(2,1)S(1)}, bf16[2048,256]{1,0:T(8,128)(2,1)}, u32[]{:S(2)}) copy-start(bf16[2048,256]{1,0:T(8,128)(2,1)} %param.6) | copy-start | bytes 3145732
where the time goes:
time: 406 us; the launch traced here: 404 us
  waiting for transfers between devices  229 us (56%)
  local copies, waits for them, and re-layouts  48.9 us (12%)
  matrix products  48.9 us (12%)
  blocking collectives  37.8 us (9%)
  starting transfers between devices  29.1 us (7%)
  other arithmetic  7.66 us (2%)
    all_to_all x3, waiting for transfers between devices, fetch(): lax.all_to_all(reply, 'region', split_axis=0, concat_axis=0, tiled=True)  130 us
    all_to_all x2, waiting for transfers between devices, shards(): lax.all_to_all(outgoing, 'region', split_axis=0, concat_axis=0, tiled=True)  94.4 us
    psum x1, blocking collectives, shards(): table = lax.psum(table, ('region', 'sub'))  37.8 us
    dot_general x3, matrix products, fetch(): return jnp.dot(send_hot.T, back, precision=highest)  15.6 us
    all_to_all x3, starting transfers between devices, fetch(): lax.all_to_all(reply, 'region', split_axis=0, concat_axis=0, tiled=True)  13.3 us
    reshape x3, local copies, waits for them, and re-layouts, fetch(): lax.all_to_all(reply, 'region', split_axis=0, concat_axis=0, tiled=True)  11 us
    dot_general x2, matrix products, shards(): field = base + jnp.dot(coupling, drive, preferred_element_type=jnp.float32)  9.98 us
    all_to_all x2, starting transfers between devices, shards(): lax.all_to_all(outgoing, 'region', split_axis=0, concat_axis=0, tiled=True)  8.57 us
  transfers between devices with their start and end apart: 6, of which 6 were waited for; matrix products, arithmetic and copies ran while one was open for 3% of the time, Pallas kernels for 0%

commit v1 on v0

v1 whole, which is shorter than its diff:
```python
import jax
import jax.numpy as jnp
from jax import lax
from jax.experimental import pallas as pl
from jax.experimental.pallas import tpu as pltpu
from jax.sharding import PartitionSpec as P

BLOCK = 128
CAP = 2
ITERS = 2
HALVES = 2
TILE = 8


penalty = 1.5

VMEM = pl.BlockSpec(memory_space=pltpu.VMEM)
SMEM = pl.BlockSpec(memory_space=pltpu.SMEM)
ANY = pl.BlockSpec(memory_space=pl.ANY)


def grid_of(peers):
    columns = 1
    while (2 * columns) ** 2 <= peers:
        columns *= 2
    return peers // columns, columns


def ring_place(region, peers):
    rows, columns = grid_of(peers)
    row, column = region // columns, region % columns
    up = rows - 1 - row
    if columns == 1:
        return row
    right = up % 2 == 0
    if isinstance(region, int):
        if column == 0:
            return row
        return rows + up * (columns - 1) + (column - 1 if right else columns - 1 - column)
    along = jnp.where(right, column - 1, columns - 1 - column)
    return jnp.where(column == 0, row, rows + up * (columns - 1) + along)


def f32(*shape):
    return jax.ShapeDtypeStruct(shape, jnp.float32)


def call(body, name, ins, in_specs, outs, out_specs, scratch=(), aliases=None, flops=0, moved=1 << 20):
    return pl.pallas_call(
        body,
        name=name,
        out_shape=outs,
        in_specs=in_specs,
        out_specs=out_specs,
        scratch_shapes=scratch,
        input_output_aliases=aliases or {},
        cost_estimate=pl.CostEstimate(flops=flops, bytes_accessed=moved, transcendentals=0),
        compiler_params=pltpu.CompilerParams(vmem_limit_bytes=16 << 20),
    )(*ins)


def prepare(region, target, cons, peers):
    rows, scen = cons.shape
    blocks = target.shape[1]
    owned = rows // BLOCK
    width = scen // HALVES

    def body(region_ref, target_ref, cons_ref, table_ref, *half_refs):
        here = ring_place(region_ref[0], peers)
        for i in range(2 * CAP * peers):
            table_ref[i] = -1
        for j in range(blocks):
            t = target_ref[0, j]

            @pl.when(t >= 0)
            def _(t=t, j=j):
                owner = t // owned
                ahead = ring_place(owner, peers) - here
                ahead = jnp.where(ahead < 0, ahead + peers, ahead)
                first = CAP * ahead
                at = first + jnp.where(table_ref[first] >= 0, 1, 0)
                table_ref[at] = j
                table_ref[CAP * peers + at] = t - owner * owned

        for h, ref in enumerate(half_refs):
            ref[...] = cons_ref[:, h * width : (h + 1) * width]

    out = call(
        body,
        "prepare",
        (region, target, cons),
        [SMEM, SMEM, VMEM],
        [jax.ShapeDtypeStruct((2 * CAP * peers,), jnp.int32)] + [f32(rows, width)] * HALVES,
        [SMEM] + [VMEM] * HALVES,
    )
    return out[0], out[1:]


def base_product(kkt, cost):
    rows, scen = kkt.shape[0], cost.shape[1]
    step = 256

    def body(kkt_ref, cost_ref, out_ref):
        @pl.loop(0, rows // step)
        def _(i):
            at = pl.ds(pl.multiple_of(i * step, step), step)
            out_ref[at, :] = jnp.dot(kkt_ref[at, :], cost_ref[...], preferred_element_type=jnp.float32)

    return call(
        body, "base_product", (kkt, cost), [VMEM] * 2, f32(rows, scen), VMEM, flops=2 * rows * rows * scen, moved=12 << 20
    )


def slots_of(table_ref, peers):
    def each(do):
        for r in range(peers):
            for c in range(CAP):
                j = table_ref[CAP * r + c]

                @pl.when(j >= 0)
                def _(r=r, c=c, j=j):
                    b = table_ref[CAP * peers + CAP * r + c]
                    slot = pl.ds(pl.multiple_of(j * BLOCK, BLOCK), BLOCK)
                    block = pl.ds(pl.multiple_of(b * BLOCK, BLOCK), BLOCK)
                    do(r, slot, block)

    return each


def fold(x):
    return jnp.sum(x.reshape(-1, TILE, x.shape[-1]), axis=0)


def first_solve(h, table, pieces, dual, base, kkt, owned, counting):
    peers = len(pieces)
    bound, scen = dual.shape
    width = scen // HALVES
    cols = slice(h * width, (h + 1) * width)
    own = owned * BLOCK
    sent = own + (TILE if counting else 0)
    step = 512 if bound % 512 == 0 else BLOCK

    def body(*refs):
        table_ref, refs = refs[0], refs[1:]
        piece, (dual_ref, base_ref, kkt_ref, z_ref), refs = refs[:peers], refs[peers : peers + 4], refs[peers + 4 :]
        part, (drive_ref,) = refs[:peers], refs[peers:]
        each = slots_of(table_ref, peers)
        drive_ref[...] = jnp.zeros_like(drive_ref)

        def driven(r, slot, block):
            drive_ref[slot, :] = (penalty * (piece[r][block, :] - dual_ref[slot, cols])).astype(jnp.bfloat16)

        each(driven)

        @pl.loop(0, bound // step)
        def _(i):
            at = pl.ds(pl.multiple_of(i * step, step), step)
            got = jnp.dot(kkt_ref[at, :bound], drive_ref[...], preferred_element_type=jnp.float32)
            z_ref[at, :] = (base_ref[at, cols] + got) + dual_ref[at, cols]

        for r in range(peers):
            part[r][:own, :] = jnp.zeros((own, width), jnp.float32)
            if counting:
                row = lax.broadcasted_iota(jnp.int32, (TILE, width), 0)
                count = jnp.zeros((TILE, width), jnp.float32)
                for c in range(CAP):
                    b = table_ref[CAP * peers + CAP * r + c]
                    count = count + jnp.where(row == b, 1.0, 0.0)
                part[r][own:, :] = count

        def summed(r, slot, block):
            part[r][block, :] += z_ref[slot, :]

        each(summed)

    out = call(
        body,
        "first_solve",
        (table, *pieces, dual, base, kkt),
        [SMEM] + [VMEM] * (peers + 3),
        [f32(bound, width)] + [f32(sent, width)] * peers,
        [VMEM] * (1 + peers),
        [pltpu.VMEM((bound, width), jnp.bfloat16)],
        flops=2 * bound * bound * width,
        moved=8 << 20,
    )
    return out[0], out[1:]


def second_solve(h, table, pieces, z, dual, base, kkt, owned, state):
    peers = len(pieces)
    bound, scen = dual.shape
    rows = base.shape[0]
    width = scen // HALVES
    cols = slice(h * width, (h + 1) * width)
    own = owned * BLOCK
    step = 512 if rows % 512 == 0 else BLOCK
    given = 0 if state is None else 1

    def body(*refs):
        table_ref, refs = refs[0], refs[1:]
        piece, (z_ref, dual_ref, base_ref, kkt_ref), refs = refs[:peers], refs[peers : peers + 4], refs[peers + 4 + given :]
        state_ref, next_ref, norm_ref, refs = refs[0], refs[1], refs[2], refs[3:]
        part, (drive_ref, field_ref, sem) = refs[:peers], refs[peers:]
        each = slots_of(table_ref, peers)
        drive_ref[...] = jnp.zeros_like(drive_ref)
        norm_ref[...] = jnp.zeros_like(norm_ref)
        next_ref[...] = dual_ref[:, cols]

        def driven(r, slot, block):
            fetched = piece[r][block, :]
            renewed_dual = z_ref[slot, :] - fetched
            gap = renewed_dual - dual_ref[slot, cols]
            norm_ref[:TILE, :] += fold(gap * gap)
            next_ref[slot, :] = renewed_dual
            drive_ref[slot, :] = (penalty * (fetched - renewed_dual)).astype(jnp.bfloat16)

        each(driven)

        def store(i):
            at = pl.ds(pl.multiple_of(i * step, step), step)
            return pltpu.make_async_copy(field_ref.at[at, :], state_ref.at[at, cols], sem.at[i])

        for i in range(rows // step):
            at = pl.ds(i * step, step)
            got = jnp.dot(kkt_ref[at, :bound], drive_ref[...], preferred_element_type=jnp.float32)
            field_ref[at, :] = base_ref[at, cols] + got
            store(i).start()
        for r in range(peers):
            part[r][...] = jnp.zeros((own, width), jnp.float32)

        def summed(r, slot, block):
            copies = field_ref[slot, :]
            shift = copies - piece[r][block, :]
            norm_ref[TILE:, :] += fold(shift * shift)
            total = copies + next_ref[slot, :]
            next_ref[slot, :] = total
            part[r][block, :] += total

        each(summed)
        for i in range(rows // step):
            store(i).wait()

    before = () if state is None else (state,)
    out = call(
        body,
        "second_solve",
        (table, *pieces, z, dual, base, kkt, *before),
        [SMEM] + [VMEM] * (peers + 4) + [ANY] * given,
        [f32(rows, scen), f32(bound, width), f32(2 * TILE, width)] + [f32(own, width)] * peers,
        [ANY] + [VMEM] * (2 + peers),
        [
            pltpu.VMEM((bound, width), jnp.bfloat16),
            pltpu.VMEM((rows, width), jnp.float32),
            pltpu.SemaphoreType.DMA((rows // step,)),
        ],
        aliases={peers + 5: 0} if given else None,
        flops=2 * bound * rows * width,
        moved=10 << 20,
    )
    return out[0], out[1], out[2], out[3:]


def add_pairs(pairs):
    def body(*refs):
        for i in range(len(pairs)):
            refs[2 * len(pairs) + i][...] = refs[2 * i][...] + refs[2 * i + 1][...]

    out = call(
        body,
        "add_pairs",
        tuple(x for pair in pairs for x in pair),
        [VMEM] * (2 * len(pairs)),
        [f32(*pair[0].shape) for pair in pairs],
        [VMEM] * len(pairs),
    )
    return list(out)


def renew(parts, before, count, norms):
    own, width = before.shape
    owned = own // BLOCK
    counted = count is None

    def body(*refs):
        parts_ref, refs = refs[: len(parts)], refs[len(parts) :]
        before_ref, refs = refs[0], refs[1:]
        if not counted:
            count_ref, refs = refs[0], refs[1:]
        norm_refs, refs = refs[: len(norms)], refs[len(norms) :]
        new_ref, moved_ref = refs[0], refs[1]

        def total(at):
            value = parts_ref[0][at, :]
            for ref in parts_ref[1:]:
                value = value + ref[at, :]
            return value

        if counted:
            tile = total(slice(own, own + TILE))
            refs[2][...] = tile
        else:
            tile = count_ref[...]
        moved = jnp.zeros((TILE, width), jnp.float32)
        for b in range(owned):
            at = slice(b * BLOCK, (b + 1) * BLOCK)
            many = tile[b : b + 1, :]
            value = total(at) / jnp.maximum(many, 1.0)
            change = value - before_ref[at, :]
            moved = moved + many * fold(change * change)
            new_ref[at, :] = value
        moved_ref[...] = moved
        if norms:
            first = norm_refs[0][...] + norm_refs[1][...]
            sums = [
                first[:TILE, :],
                norm_refs[2][...] + norm_refs[3][...],
                first[TILE:, :],
                norm_refs[4][...] + moved,
            ]
            row = lax.broadcasted_iota(jnp.int32, (TILE, width), 0)
            block = jnp.zeros((TILE, width), jnp.float32)
            for i, x in enumerate(sums):
                block = jnp.where(row == i, jnp.sum(x, axis=0, keepdims=True), block)
            new_ref[own:, :] = block

    ins = (*parts, before) + (() if counted else (count,)) + tuple(norms)
    outs = [f32(own + (TILE if norms else 0), width), f32(TILE, width)] + ([f32(TILE, width)] if counted else [])
    return call(body, "renew", ins, [VMEM] * len(ins), outs, [VMEM] * len(outs))


def finish(h, table, pieces, z, scen, owned, outputs):
    peers = len(pieces)
    bound, width = z.shape
    cols = slice(h * width, (h + 1) * width)
    own = owned * BLOCK
    given = len(outputs)

    def body(*refs):
        table_ref, refs = refs[0], refs[1:]
        piece, z_ref, refs = refs[:peers], refs[peers], refs[peers + 1 + given :]
        dual_ref, cons_ref, new_ref, sem = refs
        kept = pltpu.make_async_copy(piece[0].at[:own, :], cons_ref.at[:, cols], sem.at[0])
        kept.start()
        each = slots_of(table_ref, peers)
        new_ref[...] = z_ref[...]

        def renewed(r, slot, block):
            new_ref[slot, :] = z_ref[slot, :] - piece[r][block, :]

        each(renewed)
        out = pltpu.make_async_copy(new_ref, dual_ref.at[:, cols], sem.at[1])
        out.start()
        out.wait()
        kept.wait()

    return call(
        body,
        "finish",
        (table, *pieces, z, *outputs),
        [SMEM] + [VMEM] * (peers + 1) + [ANY] * given,
        [f32(bound, scen), f32(own, scen)],
        [ANY] * 2,
        [pltpu.VMEM((bound, width), jnp.float32), pltpu.SemaphoreType.DMA((2,))],
        aliases={peers + 2: 0, peers + 3: 1} if given else None,
        moved=3 << 20,
    )


def sum_tails(pieces, own):
    width = pieces[0].shape[1]

    def body(*refs):
        total = refs[0][own:, :]
        for ref in refs[1:-1]:
            total = total + ref[own:, :]
        refs[-1][...] = total

    return call(body, "sum_tails", tuple(pieces), [VMEM] * len(pieces), f32(TILE, width), VMEM)


def norm_table(tiles, scale):
    def body(*refs):
        total = refs[0][...]
        for ref in refs[1:-1]:
            total = total + ref[...]
        total = jnp.sum(total, axis=1, keepdims=True)
        row = lax.broadcasted_iota(jnp.int32, (ITERS, 2), 0)
        col = lax.broadcasted_iota(jnp.int32, (ITERS, 2), 1)
        primal = jnp.where(row == 0, total[0:1, :], total[2:3, :] - total[3:4, :])
        moved = penalty * penalty * jnp.where(row == 0, total[1:2, :], total[3:4, :])
        refs[-1][...] = jnp.sqrt(jnp.maximum(jnp.where(col == 0, primal, moved), 0.0) / scale)

    return call(body, "norm_table", tuple(tiles), [VMEM] * len(tiles), f32(ITERS, 2), VMEM)


def shards(kkt, cost, dual, cons, target):
    scen = cost.shape[1]
    owned = cons.shape[0] // BLOCK
    peers = lax.axis_size("region")
    subs = lax.axis_size("sub")
    order = sorted(range(peers), key=lambda region: ring_place(region, peers))
    ahead = [(order[i], order[(i + 1) % peers]) for i in range(peers)]
    behind = [(b, a) for a, b in ahead]

    def forward(x):
        return lax.ppermute(x, "region", ahead)

    def backward(x):
        return lax.ppermute(x, "region", behind)

    def reach(h):
        long, short = peers // 2, (peers - 1) // 2
        return (long, short) if h % 2 == 0 else (short, long)

    def gather(h, piece):
        far, near = reach(h)
        pieces = [piece] * peers
        f = b = piece
        for k in range(1, max(far, near) + 1):
            if k <= far:
                f = pieces[(peers - k) % peers] = forward(f)
            if k <= near:
                b = pieces[k] = backward(b)
        return pieces

    def scatter(h, parts):
        far, near = reach(h)
        f, b = parts[far], parts[peers - near]
        for k in range(1, max(far, near) + 1):
            pairs = []
            if k <= far:
                f = forward(f)
            if k <= near:
                b = backward(b)
            if k < far:
                pairs.append((f, parts[far - k]))
            if k < near:
                pairs.append((b, parts[peers - near + k]))
            if pairs:
                added = add_pairs(pairs)
                if k < far:
                    f = added.pop(0)
                if k < near:
                    b = added.pop(0)
        return [parts[0], f, b]

    region = lax.axis_index("region").astype(jnp.int32).reshape(1)
    table, halves = prepare(region, target, cons, peers)
    base = base_product(kkt, cost)
    state, outputs = None, ()
    every = range(HALVES)
    pieces = [gather(h, halves[h]) for h in every]
    count = None
    z, renewed, moved1, moved2, gaps = {}, {}, {}, {}, {}
    for h in every:
        z[h], parts = first_solve(h, table, pieces[h], dual, base, kkt, owned, count is None)
        out = renew(scatter(h, parts), halves[h], count, ())
        renewed[h], moved1[h] = out[0], out[1]
        if count is None:
            count = out[2]
        pieces[h] = gather(h, renewed[h])
    for h in every:
        state, z[h], gaps[h], parts = second_solve(h, table, pieces[h], z[h], dual, base, kkt, owned, state)
        norms = (gaps[0], gaps[1], moved1[0], moved1[1], moved2[0]) if h == HALVES - 1 else ()
        out = renew(scatter(h, parts), renewed[h], count, norms)
        moved2[h] = out[1]
        pieces[h] = gather(h, out[0])
    tail = sum_tails(pieces[HALVES - 1], owned * BLOCK)
    turns = [lax.ppermute(tail, "sub", [(i, (i + k) % subs) for i in range(subs)]) for k in range(1, subs)]
    for h in every:
        outputs = finish(h, table, pieces[h], z[h], scen, owned, outputs)
    norms = norm_table([tail, *turns], float(peers * subs * scen * BLOCK))
    return (state, outputs[0], outputs[1], norms)


def solution(mesh):
    spec = P(("region", "sub"), None)
    return jax.shard_map(
        shards, mesh=mesh, in_specs=(spec,) * 5, out_specs=(spec, spec, spec, P()), check_vma=False
    )
```

time: 406 us -> 154 us (0.38)
  waiting for transfers between devices: 229 us -> 45 us
  starting transfers between devices: 29.1 us -> 79.1 us
  matrix products: 48.9 us -> 0 us
  local copies, waits for them, and re-layouts: 48.9 us -> 6.44 us
  blocking collectives: 37.8 us -> 0 us
  Pallas kernels: 0 us -> 23.1 us
  other arithmetic: 7.66 us -> 0 us
    all_to_all x6 -> x0, waiting for transfers between devices: 229 us -> none  [the longest x3 130 us: fetch(): lax.all_to_all(reply, 'region', split_axis=0, concat_axis=0, tiled=True)]
    ppermute x0 -> x73, starting transfers between devices: none -> 79.1 us  [the longest x35 42 us: backward(): return lax.ppermute(x, 'region', behind)]
    dot_general x13 -> x0, matrix products: 48.9 us -> none  [the longest x3 15.6 us: fetch(): return jnp.dot(send_hot.T, back, precision=highest)]
    ppermute x0 -> x73, waiting for transfers between devices: none -> 45 us  [the longest x35 23.8 us: forward(): return lax.ppermute(x, 'region', ahead)]
    psum x1 -> x0, blocking collectives: 37.8 us -> none  [shards(): table = lax.psum(table, ('region', 'sub'))]
    reshape x15 -> x0, local copies, waits for them, and re-layouts: 36 us -> none  [the longest x3 11 us: fetch(): lax.all_to_all(reply, 'region', split_axis=0, concat_axis=0, tiled=True)]
    all_to_all x6 -> x0, starting transfers between devices: 29.1 us -> none  [the longest x3 13.3 us: fetch(): lax.all_to_all(reply, 'region', split_axis=0, concat_axis=0, tiled=True)]
    pallas_call x0 -> x26, Pallas kernels: none -> 23.1 us  [call(): pl.pallas_call(body, name=name, out_shape=outs, in_specs=in_specs, out_sp...]
  transfers between devices with their start and end apart: 6 -> 73, of which waited for: 6 -> 39; matrix products, arithmetic and copies ran while one was open for 3% -> 0% of each run, Pallas kernels for 0% -> 13%
where the time goes in v1:
time: 154 us; the launch traced here: 155 us
  starting transfers between devices  79.1 us (51%)
  waiting for transfers between devices  45 us (29%)
  Pallas kernels  23.1 us (15%)
  local copies, waits for them, and re-layouts  6.44 us (4%)
    ppermute x35, starting transfers between devices, backward(): return lax.ppermute(x, 'region', behind)  42 us
    ppermute x35, starting transfers between devices, forward(): return lax.ppermute(x, 'region', ahead)  34.8 us
    ppermute x35, waiting for transfers between devices, forward(): return lax.ppermute(x, 'region', ahead)  23.8 us
    pallas_call x26, Pallas kernels, call(): pl.pallas_call(body, name=name, out_shape=outs, in_specs=in_specs, out_sp...  23.1 us
    ppermute x35, waiting for transfers between devices, backward(): return lax.ppermute(x, 'region', behind)  21.2 us
    unnamed x12, local copies, waits for them, and re-layouts  6.44 us
  transfers between devices with their start and end apart: 73, of which 39 were waited for; matrix products, arithmetic and copies ran while one was open for 0% of the time, Pallas kernels for 13%

profile of v1, /device:TPU:0, one launch (start us, length us, event | category | flops | bytes accessed | tf_op | source)
XLA Modules:
  0.0 154.6 jit_solution(4047770906456019652)
XLA Ops:
  2.2 1.4 prepare.1
  3.6 3.1 %collective-permute-start.17 = (f32[256,128]{1,0:T(8,128)S(1)}, f32[256,128]{1,0:T(8,128)S(1)}, u32[]{:S(2)}, u32[]{:S(2)}) collective-permute-start(f32[256,128]{1,0:T(8,128)S(1)} %get-tuple-element.89.refs_1_.refs_3_), channel_id=1, source_target_pairs={{0,8},{8,16},{16,24},{24,28},{28,20},{20,12},{12,4},{4,0},{1,9},{9... | collective-permute-start | bytes 393224 | tf_op jit(solution)/shard_map/ppermute | solution.py:407
  6.7 1.9 %collective-permute-start.14 = (f32[256,128]{1,0:T(8,128)S(1)}, f32[256,128]{1,0:T(8,128)S(1)}, u32[]{:S(2)}, u32[]{:S(2)}) collective-permute-start(f32[256,128]{1,0:T(8,128)S(1)} %get-tuple-element.89.refs_1_.refs_3_), channel_id=1, source_target_pairs={{8,0},{16,8},{24,16},{28,24},{20,28},{12,20},{4,12},{0,4},{9,1},{1... | collective-permute-start | bytes 393224 | tf_op jit(solution)/shard_map/ppermute | solution.py:410
  8.8 1.8 %collective-permute-done.17.refs_8_ = f32[256,128]{1,0:T(8,128)S(1)} collective-permute-done((f32[256,128]{1,0:T(8,128)S(1)}, f32[256,128]{1,0:T(8,128)S(1)}, u32[]{:S(2)}, u32[]{:S(2)}) %collective-permute-start.17) | collective-permute-done | bytes 131104 | tf_op jit(solution)/shard_map/ppermute | solution.py:407
  10.6 2.5 %collective-permute-start.18 = (f32[256,128]{1,0:T(8,128)S(1)}, f32[256,128]{1,0:T(8,128)S(1)}, u32[]{:S(2)}, u32[]{:S(2)}) collective-permute-start(f32[256,128]{1,0:T(8,128)S(1)} %collective-permute-done.17.refs_8_), channel_id=1, source_target_pairs={{0,8},{8,16},{16,24},{24,28},{28,20},{20,12},{12,4},{4,0},{1,9},{9... | collective-permute-start | bytes 393224 | tf_op jit(solution)/shard_map/ppermute | solution.py:407
  13.1 2.6 %collective-permute-done.14.refs_2_ = f32[256,128]{1,0:T(8,128)S(1)} collective-permute-done((f32[256,128]{1,0:T(8,128)S(1)}, f32[256,128]{1,0:T(8,128)S(1)}, u32[]{:S(2)}, u32[]{:S(2)}) %collective-permute-start.14) | collective-permute-done | bytes 131104 | tf_op jit(solution)/shard_map/ppermute | solution.py:410
  15.7 2.0 %collective-permute-start.5 = (f32[256,128]{1,0:T(8,128)S(1)}, f32[256,128]{1,0:T(8,128)S(1)}, u32[]{:S(2)}, u32[]{:S(2)}) collective-permute-start(f32[256,128]{1,0:T(8,128)S(1)} %collective-permute-done.4.refs_8_), channel_id=1, source_target_pairs={{0,8},{8,16},{16,24},{24,28},{28,20},{20,12},{12,4},{4,0},{1,9},{9... | collective-permute-start | bytes 393224 | tf_op jit(solution)/shard_map/ppermute | solution.py:407
  17.7 1.6 %collective-permute-start.19 = (f32[256,128]{1,0:T(8,128)S(1)}, f32[256,128]{1,0:T(8,128)S(1)}, u32[]{:S(2)}, u32[]{:S(2)}) collective-permute-start(f32[256,128]{1,0:T(8,128)S(1)} %collective-permute-done.18.refs_7_), channel_id=1, source_target_pairs={{0,8},{8,16},{16,24},{24,28},{28,20},{20,12},{12,4},{4,0},{1,9},{9... | collective-permute-start | bytes 393224 | tf_op jit(solution)/shard_map/ppermute | solution.py:407
  19.7 2.2 %collective-permute-done.15.refs_3_ = f32[256,128]{1,0:T(8,128)S(1)} collective-permute-done((f32[256,128]{1,0:T(8,128)S(1)}, f32[256,128]{1,0:T(8,128)S(1)}, u32[]{:S(2)}, u32[]{:S(2)}) %collective-permute-start.15) | collective-permute-done | bytes 131104 | tf_op jit(solution)/shard_map/ppermute | solution.py:410
  22.1 1.9 %collective-permute-start.6 = (f32[256,128]{1,0:T(8,128)S(1)}, f32[256,128]{1,0:T(8,128)S(1)}, u32[]{:S(2)}, u32[]{:S(2)}) collective-permute-start(f32[256,128]{1,0:T(8,128)S(1)} %collective-permute-done.5.refs_7_), channel_id=1, source_target_pairs={{0,8},{8,16},{16,24},{24,28},{28,20},{20,12},{12,4},{4,0},{1,9},{9... | collective-permute-start | bytes 393224 | tf_op jit(solution)/shard_map/ppermute | solution.py:407
  24.0 1.8 %collective-permute-start.20 = (f32[256,128]{1,0:T(8,128)S(1)}, f32[256,128]{1,0:T(8,128)S(1)}, u32[]{:S(2)}, u32[]{:S(2)}) collective-permute-start(f32[256,128]{1,0:T(8,128)S(1)} %collective-permute-done.19.refs_6_), channel_id=1, source_target_pairs={{0,8},{8,16},{16,24},{24,28},{28,20},{20,12},{12,4},{4,0},{1,9},{9... | collective-permute-start | bytes 393224 | tf_op jit(solution)/shard_map/ppermute | solution.py:407
  26.1 3.4 %copy-done = bf16[2048,2048]{1,0:T(8,128)(2,1)S(1)} copy-done((bf16[2048,2048]{1,0:T(8,128)(2,1)S(1)}, bf16[2048,2048]{1,0:T(8,128)(2,1)}, u32[]{:S(2)}) %copy-start) | copy-done | bytes 8388632
  30.7 3.5 %base_product.1.refs_10_.refs_11_ = f32[2048,256]{1,0:T(8,128)S(1)} custom-call(bf16[2048,2048]{1,0:T(8,128)(2,1)S(1)} %copy-done, bf16[2048,256]{1,0:T(8,128)(2,1)S(1)} %copy-done.3), custom_call_target="tpu_custom_call" | custom-call | flops 2147483648 | bytes 12582912 | tf_op jit(solution)/shard_map/base_product/pallas_call | solution.py:49
  34.5 2.8 %first_solve.3 = (f32[1536,128]{1,0:T(8,128)S(1)}, f32[264,128]{1,0:T(8,128)S(1)}, f32[264,128]{1,0:T(8,128)S(1)}, f32[264,128]{1,0:T(8,128)S(1)}, f32[264,128]{...) custom-call(s32[32]{0:T(128)S(1)} %get-tuple-element.75.refs_0_, ...), custom_call_target="tpu_custom_call" | custom-call | flops 603979776 | bytes 8388608 | tf_op jit(solution)/shard_map/first_solve/pallas_call | solution.py:49
  37.3 1.8 %collective-permute-start.21 = (f32[264,128]{1,0:T(8,128)S(1)}, f32[264,128]{1,0:T(8,128)S(1)}, u32[]{:S(2)}, u32[]{:S(2)}) collective-permute-start(f32[264,128]{1,0:T(8,128)S(1)} %get-tuple-element.91), channel_id=1, source_target_pairs={{0,8},{8,16},{16,24},{24,28},{28,20},{20,12},{12,4},{4,0},{1,9},{9... | collective-permute-start | bytes 405512 | tf_op jit(solution)/shard_map/ppermute | solution.py:407
  39.4 2.8 %first_solve.2 = (f32[1536,128]{1,0:T(8,128)S(1)}, f32[256,128]{1,0:T(8,128)S(1)}, f32[256,128]{1,0:T(8,128)S(1)}, f32[256,128]{1,0:T(8,128)S(1)}, f32[256,128]{...) custom-call(s32[32]{0:T(128)S(1)} %get-tuple-element.75.refs_0_, ...), custom_call_target="tpu_custom_call" | custom-call | flops 603979776 | bytes 8388608 | tf_op jit(solution)/shard_map/first_solve/pallas_call | solution.py:49
  42.2 1.8 %collective-permute-start.7 = (f32[256,128]{1,0:T(8,128)S(1)}, f32[256,128]{1,0:T(8,128)S(1)}, u32[]{:S(2)}, u32[]{:S(2)}) collective-permute-start(f32[256,128]{1,0:T(8,128)S(1)} %get-tuple-element.78), channel_id=1, source_target_pairs={{0,8},{8,16},{16,24},{24,28},{28,20},{20,12},{12,4},{4,0},{1,9},{9... | collective-permute-start | bytes 393224 | tf_op jit(solution)/shard_map/ppermute | solution.py:407
  45.5 1.6 %collective-permute-start.23 = (f32[264,128]{1,0:T(8,128)S(1)}, f32[264,128]{1,0:T(8,128)S(1)}, u32[]{:S(2)}, u32[]{:S(2)}) collective-permute-start(f32[264,128]{1,0:T(8,128)S(1)} %get-tuple-element.95), channel_id=1, source_target_pairs={{0,8},{8,16},{16,24},{24,28},{28,20},{20,12},{12,4},{4,0},{1,9},{9... | collective-permute-start | bytes 405512 | tf_op jit(solution)/shard_map/ppermute | solution.py:407
  51.3 2.1 %collective-permute-done.24.refs_2_ = f32[264,128]{1,0:T(8,128)S(1)} collective-permute-done((f32[264,128]{1,0:T(8,128)S(1)}, f32[264,128]{1,0:T(8,128)S(1)}, u32[]{:S(2)}, u32[]{:S(2)}) %collective-permute-start.24) | collective-permute-done | bytes 135200 | tf_op jit(solution)/shard_map/ppermute | solution.py:410
  53.4 1.8 %collective-permute-start.25 = (f32[264,128]{1,0:T(8,128)S(1)}, f32[264,128]{1,0:T(8,128)S(1)}, u32[]{:S(2)}, u32[]{:S(2)}) collective-permute-start(f32[264,128]{1,0:T(8,128)S(1)} %get-tuple-element.99), channel_id=1, source_target_pairs={{0,8},{8,16},{16,24},{24,28},{28,20},{20,12},{12,4},{4,0},{1,9},{9... | collective-permute-start | bytes 405512 | tf_op jit(solution)/shard_map/ppermute | solution.py:407
  56.7 1.5 collective-permute-start.12
  58.2 1.8 %collective-permute-start.27 = (f32[264,128]{1,0:T(8,128)S(1)}, f32[264,128]{1,0:T(8,128)S(1)}, u32[]{:S(2)}, u32[]{:S(2)}) collective-permute-start(f32[264,128]{1,0:T(8,128)S(1)} %get-tuple-element.101), channel_id=1, source_target_pairs={{8,0},{16,8},{24,16},{28,24},{20,28},{12,20},{4,12},{0,4},{9,1},{1... | collective-permute-start | bytes 405512 | tf_op jit(solution)/shard_map/ppermute | solution.py:410
  62.8 1.6 %collective-permute-start.13 = (f32[256,128]{1,0:T(8,128)S(1)}, f32[256,128]{1,0:T(8,128)S(1)}, u32[]{:S(2)}, u32[]{:S(2)}) collective-permute-start(f32[256,128]{1,0:T(8,128)S(1)} %add_pairs.14), channel_id=1, source_target_pairs={{8,0},{16,8},{24,16},{28,24},{20,28},{12,20},{4,12},{0,4},{9,1},{1... | collective-permute-start | bytes 393224 | tf_op jit(solution)/shard_map/ppermute | solution.py:410
  67.6 1.4 collective-permute-done.11.refs_1_
  69.3 1.5 collective-permute-start.28
  70.8 1.8 %collective-permute-start.35 = (f32[256,128]{1,0:T(8,128)S(1)}, f32[256,128]{1,0:T(8,128)S(1)}, u32[]{:S(2)}, u32[]{:S(2)}) collective-permute-start(f32[256,128]{1,0:T(8,128)S(1)} %get-tuple-element.105.refs_1_.refs_3_), channel_id=1, source_target_pairs={{8,0},{16,8},{24,16},{28,24},{20,28},{12,20},{4,12},{0,4},{9,1},{1... | collective-permute-start | bytes 393224 | tf_op jit(solution)/shard_map/ppermute | solution.py:410
  75.6 1.6 %collective-permute-start.29 = (f32[256,128]{1,0:T(8,128)S(1)}, f32[256,128]{1,0:T(8,128)S(1)}, u32[]{:S(2)}, u32[]{:S(2)}) collective-permute-start(f32[256,128]{1,0:T(8,128)S(1)} %collective-permute-done.28.refs_2_), channel_id=1, source_target_pairs={{8,0},{16,8},{24,16},{28,24},{20,28},{12,20},{4,12},{0,4},{9,1},{1... | collective-permute-start | bytes 393224 | tf_op jit(solution)/shard_map/ppermute | solution.py:410
  83.2 1.5 collective-permute-start.37
  85.4 1.8 %collective-permute-done.33.refs_7_ = f32[256,128]{1,0:T(8,128)S(1)} collective-permute-done((f32[256,128]{1,0:T(8,128)S(1)}, f32[256,128]{1,0:T(8,128)S(1)}, u32[]{:S(2)}, u32[]{:S(2)}) %collective-permute-start.33) | collective-permute-done | bytes 131104 | tf_op jit(solution)/shard_map/ppermute | solution.py:407
  89.4 2.4 %collective-permute-done.41.refs_5_ = f32[256,128]{1,0:T(8,128)S(1)} collective-permute-done((f32[256,128]{1,0:T(8,128)S(1)}, f32[256,128]{1,0:T(8,128)S(1)}, u32[]{:S(2)}, u32[]{:S(2)}) %collective-permute-start.41) | collective-permute-done | bytes 131104 | tf_op jit(solution)/shard_map/ppermute | solution.py:407
  91.7 3.6 %second_solve.2 = (f32[2048,256]{1,0:T(8,128)}, f32[1536,128]{1,0:T(8,128)S(1)}, f32[16,128]{1,0:T(8,128)S(1)}, f32[256,128]{1,0:T(8,128)S(1)}, f32[256,128]{1,0...) custom-call(s32[32]{0:T(128)S(1)} %get-tuple-element.75.refs_0_, ...), custom_call_target="tpu_custom_call" | custom-call | flops 805306368 | bytes 10485760 | tf_op jit(solution)/shard_map/second_solve/pallas_call | solution.py:49
  95.4 2.0 %collective-permute-start.50 = (f32[256,128]{1,0:T(8,128)S(1)}, f32[256,128]{1,0:T(8,128)S(1)}, u32[]{:S(2)}, u32[]{:S(2)}) collective-permute-start(f32[256,128]{1,0:T(8,128)S(1)} %get-tuple-element.128), channel_id=1, source_target_pairs={{8,0},{16,8},{24,16},{28,24},{20,28},{12,20},{4,12},{0,4},{9,1},{1... | collective-permute-start | bytes 393224 | tf_op jit(solution)/shard_map/ppermute | solution.py:410
  97.4 3.8 %second_solve.3 = (f32[2048,256]{1,0:T(8,128)}, f32[1536,128]{1,0:T(8,128)S(1)}, f32[16,128]{1,0:T(8,128)S(1)}, f32[256,128]{1,0:T(8,128)S(1)}, f32[256,128]{1,0...) custom-call(s32[32]{0:T(128)S(1)} %get-tuple-element.75.refs_0_, ...), custom_call_target="tpu_custom_call", output_to_operand_aliasing={{0}: (13, {})} | custom-call | flops 805306368 | bytes 10485760 | tf_op jit(solution)/shard_map/second_solve/pallas_call | solution.py:49
  101.3 2.0 %collective-permute-start.43 = (f32[256,128]{1,0:T(8,128)S(1)}, f32[256,128]{1,0:T(8,128)S(1)}, u32[]{:S(2)}, u32[]{:S(2)}) collective-permute-start(f32[256,128]{1,0:T(8,128)S(1)} %get-tuple-element.112), channel_id=1, source_target_pairs={{8,0},{16,8},{24,16},{28,24},{20,28},{12,20},{4,12},{0,4},{9,1},{1... | collective-permute-start | bytes 393224 | tf_op jit(solution)/shard_map/ppermute | solution.py:410
  103.5 1.9 %collective-permute-start.52 = (f32[256,128]{1,0:T(8,128)S(1)}, f32[256,128]{1,0:T(8,128)S(1)}, u32[]{:S(2)}, u32[]{:S(2)}) collective-permute-start(f32[256,128]{1,0:T(8,128)S(1)} %get-tuple-element.132), channel_id=1, source_target_pairs={{8,0},{16,8},{24,16},{28,24},{20,28},{12,20},{4,12},{0,4},{9,1},{1... | collective-permute-start | bytes 393224 | tf_op jit(solution)/shard_map/ppermute | solution.py:410
  107.7 1.5 collective-permute-start.45
  109.9 3.7 %collective-permute-done.44.refs_0_ = f32[256,128]{1,0:T(8,128)S(1)} collective-permute-done((f32[256,128]{1,0:T(8,128)S(1)}, f32[256,128]{1,0:T(8,128)S(1)}, u32[]{:S(2)}, u32[]{:S(2)}) %collective-permute-start.44) | collective-permute-done | bytes 131104 | tf_op jit(solution)/shard_map/ppermute | solution.py:407
  113.6 1.8 %collective-permute-start.47 = (f32[256,128]{1,0:T(8,128)S(1)}, f32[256,128]{1,0:T(8,128)S(1)}, u32[]{:S(2)}, u32[]{:S(2)}) collective-permute-start(f32[256,128]{1,0:T(8,128)S(1)} %get-tuple-element.119), channel_id=1, source_target_pairs={{8,0},{16,8},{24,16},{28,24},{20,28},{12,20},{4,12},{0,4},{9,1},{1... | collective-permute-start | bytes 393224 | tf_op jit(solution)/shard_map/ppermute | solution.py:410
  120.4 1.5 collective-permute-done.55.refs_2_
  121.8 4.2 %collective-permute-done.54.refs_1_ = f32[256,128]{1,0:T(8,128)S(1)} collective-permute-done((f32[256,128]{1,0:T(8,128)S(1)}, f32[256,128]{1,0:T(8,128)S(1)}, u32[]{:S(2)}, u32[]{:S(2)}) %collective-permute-start.54) | collective-permute-done | bytes 131104 | tf_op jit(solution)/shard_map/ppermute | solution.py:407
  130.2 1.6 %collective-permute-done.56.refs_2_.refs_1_ = f32[264,128]{1,0:T(8,128)S(1)} collective-permute-done((f32[264,128]{1,0:T(8,128)S(1)}, f32[264,128]{1,0:T(8,128)S(1)}, u32[]{:S(2)}, u32[]{:S(2)}) %collective-permute-start.56) | collective-permute-done | bytes 135200 | tf_op jit(solution)/shard_map/ppermute | solution.py:410
  132.8 2.2 %collective-permute-start.63 = (f32[256,128]{1,0:T(8,128)S(1)}, f32[256,128]{1,0:T(8,128)S(1)}, u32[]{:S(2)}, u32[]{:S(2)}) collective-permute-start(f32[256,128]{1,0:T(8,128)S(1)} %get-tuple-element.140.refs_1_), channel_id=1, source_target_pairs={{8,0},{16,8},{24,16},{28,24},{20,28},{12,20},{4,12},{0,4},{9,1},{1... | collective-permute-start | bytes 393224 | tf_op jit(solution)/shard_map/ppermute | solution.py:410
  138.2 1.8 %collective-permute-start.64 = (f32[256,128]{1,0:T(8,128)S(1)}, f32[256,128]{1,0:T(8,128)S(1)}, u32[]{:S(2)}, u32[]{:S(2)}) collective-permute-start(f32[256,128]{1,0:T(8,128)S(1)} %collective-permute-done.63.refs_2_), channel_id=1, source_target_pairs={{8,0},{16,8},{24,16},{28,24},{20,28},{12,20},{4,12},{0,4},{9,1},{1... | collective-permute-start | bytes 393224 | tf_op jit(solution)/shard_map/ppermute | solution.py:410
  141.8 1.7 %collective-permute-start.59 = (f32[264,128]{1,0:T(8,128)S(1)}, f32[264,128]{1,0:T(8,128)S(1)}, u32[]{:S(2)}, u32[]{:S(2)}) collective-permute-start(f32[264,128]{1,0:T(8,128)S(1)} %collective-permute-done.58.refs_4_.refs_3_), channel_id=1, source_target_pairs={{8,0},{16,8},{24,16},{28,24},{20,28},{12,20},{4,12},{0,4},{9,1},{1... | collective-permute-start | bytes 405512 | tf_op jit(solution)/shard_map/ppermute | solution.py:410
  143.5 2.0 %collective-permute-start.65 = (f32[256,128]{1,0:T(8,128)S(1)}, f32[256,128]{1,0:T(8,128)S(1)}, u32[]{:S(2)}, u32[]{:S(2)}) collective-permute-start(f32[256,128]{1,0:T(8,128)S(1)} %collective-permute-done.64.refs_3_), channel_id=1, source_target_pairs={{8,0},{16,8},{24,16},{28,24},{20,28},{12,20},{4,12},{0,4},{9,1},{1... | collective-permute-start | bytes 393224 | tf_op jit(solution)/shard_map/ppermute | solution.py:410
  147.7 1.4 collective-permute-start.72
  150.5 1.7 %finish.2 = (f32[1536,256]{1,0:T(8,128)}, f32[256,256]{1,0:T(8,128)}) custom-call(s32[32]{0:T(128)S(1)} %get-tuple-element.75.refs_0_, f32[256,128]{1,0:T(8,128)S(1)} %get-tuple-element.140.refs_1_, f32[256,128]{1,0:T(8,128)S(1)} %collective-permute-done.63.refs_2_, f32[256,128]{1,0:T(8,128)S(1)} %collective-permute-done.64.refs_3_, ...), custom_call_target="tpu_custom_call" | custom-call | bytes 3145728 | tf_op jit(solution)/shard_map/finish/pallas_call | solution.py:49
  152.1 1.7 %finish.3 = (f32[1536,256]{1,0:T(8,128)}, f32[256,256]{1,0:T(8,128)}) custom-call(s32[32]{0:T(128)S(1)} %get-tuple-element.75.refs_0_, f32[264,128]{1,0:T(8,128)S(1)} %get-tuple-element.138.refs_1_.refs_0_, f32[264,128]{1,0:T(8,128)S(1)} %collective-permute-done.56.refs_2_.refs_1_, ...), custom_call_target="tpu_custom_call", output_to_operand_aliasing={{0}: (10, {}), {1}: (11, {})} | custom-call | bytes 3145728 | tf_op jit(solution)/shard_map/finish/pallas_call | solution.py:49
  (136 shorter events, 52.2 us)
Async XLA Ops:
  3.6 7.0 %collective-permute-start.17 = (f32[256,128]{1,0:T(8,128)S(1)}, f32[256,128]{1,0:T(8,128)S(1)}, u32[]{:S(2)}, u32[]{:S(2)}) collective-permute-start(f32[256,128]{1,0:T(8,128)S(1)} %get-tuple-element.89.refs_1_.refs_3_), channel_id=1, source_target_pairs={{0,8},{8,16},{16,24},{24,28},{28,20},{20,12},{12,4},{4,0},{1,9},{9... | collective-permute-start | bytes 393224 | tf_op jit(solution)/shard_map/ppermute | solution.py:407
  6.7 6.4 %collective-permute-start = (f32[256,128]{1,0:T(8,128)S(1)}, f32[256,128]{1,0:T(8,128)S(1)}, u32[]{:S(2)}, u32[]{:S(2)}) collective-permute-start(f32[256,128]{1,0:T(8,128)S(1)} %get-tuple-element.76.refs_1_.refs_3_), channel_id=1, source_target_pairs={{8,0},{16,8},{24,16},{28,24},{20,28},{12,20},{4,12},{0,4},{9,1},{1... | collective-permute-start | bytes 393224 | tf_op jit(solution)/shard_map/ppermute | solution.py:410
  6.7 8.9 %collective-permute-start.14 = (f32[256,128]{1,0:T(8,128)S(1)}, f32[256,128]{1,0:T(8,128)S(1)}, u32[]{:S(2)}, u32[]{:S(2)}) collective-permute-start(f32[256,128]{1,0:T(8,128)S(1)} %get-tuple-element.89.refs_1_.refs_3_), channel_id=1, source_target_pairs={{8,0},{16,8},{24,16},{28,24},{20,28},{12,20},{4,12},{0,4},{9,1},{1... | collective-permute-start | bytes 393224 | tf_op jit(solution)/shard_map/ppermute | solution.py:410
  8.7 7.1 %collective-permute-start.4 = (f32[256,128]{1,0:T(8,128)S(1)}, f32[256,128]{1,0:T(8,128)S(1)}, u32[]{:S(2)}, u32[]{:S(2)}) collective-permute-start(f32[256,128]{1,0:T(8,128)S(1)} %get-tuple-element.76.refs_1_.refs_3_), channel_id=1, source_target_pairs={{0,8},{8,16},{16,24},{24,28},{28,20},{20,12},{12,4},{4,0},{1,9},{9... | collective-permute-start | bytes 393224 | tf_op jit(solution)/shard_map/ppermute | solution.py:407
  10.6 7.1 %collective-permute-start.18 = (f32[256,128]{1,0:T(8,128)S(1)}, f32[256,128]{1,0:T(8,128)S(1)}, u32[]{:S(2)}, u32[]{:S(2)}) collective-permute-start(f32[256,128]{1,0:T(8,128)S(1)} %collective-permute-done.17.refs_8_), channel_id=1, source_target_pairs={{0,8},{8,16},{16,24},{24,28},{28,20},{20,12},{12,4},{4,0},{1,9},{9... | collective-permute-start | bytes 393224 | tf_op jit(solution)/shard_map/ppermute | solution.py:407
  15.7 6.3 %collective-permute-start.15 = (f32[256,128]{1,0:T(8,128)S(1)}, f32[256,128]{1,0:T(8,128)S(1)}, u32[]{:S(2)}, u32[]{:S(2)}) collective-permute-start(f32[256,128]{1,0:T(8,128)S(1)} %collective-permute-done.14.refs_2_), channel_id=1, source_target_pairs={{8,0},{16,8},{24,16},{28,24},{20,28},{12,20},{4,12},{0,4},{9,1},{1... | collective-permute-start | bytes 393224 | tf_op jit(solution)/shard_map/ppermute | solution.py:410
  15.7 6.4 %collective-permute-start.5 = (f32[256,128]{1,0:T(8,128)S(1)}, f32[256,128]{1,0:T(8,128)S(1)}, u32[]{:S(2)}, u32[]{:S(2)}) collective-permute-start(f32[256,128]{1,0:T(8,128)S(1)} %collective-permute-done.4.refs_8_), channel_id=1, source_target_pairs={{0,8},{8,16},{16,24},{24,28},{28,20},{20,12},{12,4},{4,0},{1,9},{9... | collective-permute-start | bytes 393224 | tf_op jit(solution)/shard_map/ppermute | solution.py:407
  17.7 6.3 %collective-permute-start.19 = (f32[256,128]{1,0:T(8,128)S(1)}, f32[256,128]{1,0:T(8,128)S(1)}, u32[]{:S(2)}, u32[]{:S(2)}) collective-permute-start(f32[256,128]{1,0:T(8,128)S(1)} %collective-permute-done.18.refs_7_), channel_id=1, source_target_pairs={{0,8},{8,16},{16,24},{24,28},{28,20},{20,12},{12,4},{4,0},{1,9},{9... | collective-permute-start | bytes 393224 | tf_op jit(solution)/shard_map/ppermute | solution.py:407
  19.3 6.5 %collective-permute-start.2 = (f32[256,128]{1,0:T(8,128)S(1)}, f32[256,128]{1,0:T(8,128)S(1)}, u32[]{:S(2)}, u32[]{:S(2)}) collective-permute-start(f32[256,128]{1,0:T(8,128)S(1)} %collective-permute-done.1.refs_3_), channel_id=1, source_target_pairs={{8,0},{16,8},{24,16},{28,24},{20,28},{12,20},{4,12},{0,4},{9,1},{1... | collective-permute-start | bytes 393224 | tf_op jit(solution)/shard_map/ppermute | solution.py:410
  22.0 12.2 %collective-permute-start.16 = (f32[256,128]{1,0:T(8,128)S(1)}, f32[256,128]{1,0:T(8,128)S(1)}, u32[]{:S(2)}, u32[]{:S(2)}) collective-permute-start(f32[256,128]{1,0:T(8,128)S(1)} %collective-permute-done.15.refs_3_), channel_id=1, source_target_pairs={{8,0},{16,8},{24,16},{28,24},{20,28},{12,20},{4,12},{0,4},{9,1},{1... | collective-permute-start | bytes 393224 | tf_op jit(solution)/shard_map/ppermute | solution.py:410
  22.1 17.3 %collective-permute-start.6 = (f32[256,128]{1,0:T(8,128)S(1)}, f32[256,128]{1,0:T(8,128)S(1)}, u32[]{:S(2)}, u32[]{:S(2)}) collective-permute-start(f32[256,128]{1,0:T(8,128)S(1)} %collective-permute-done.5.refs_7_), channel_id=1, source_target_pairs={{0,8},{8,16},{16,24},{24,28},{28,20},{20,12},{12,4},{4,0},{1,9},{9... | collective-permute-start | bytes 393224 | tf_op jit(solution)/shard_map/ppermute | solution.py:407
  24.0 10.2 %collective-permute-start.20 = (f32[256,128]{1,0:T(8,128)S(1)}, f32[256,128]{1,0:T(8,128)S(1)}, u32[]{:S(2)}, u32[]{:S(2)}) collective-permute-start(f32[256,128]{1,0:T(8,128)S(1)} %collective-permute-done.19.refs_6_), channel_id=1, source_target_pairs={{0,8},{8,16},{16,24},{24,28},{28,20},{20,12},{12,4},{4,0},{1,9},{9... | collective-permute-start | bytes 393224 | tf_op jit(solution)/shard_map/ppermute | solution.py:407
  25.8 13.5 %collective-permute-start.3 = (f32[256,128]{1,0:T(8,128)S(1)}, f32[256,128]{1,0:T(8,128)S(1)}, u32[]{:S(2)}, u32[]{:S(2)}) collective-permute-start(f32[256,128]{1,0:T(8,128)S(1)} %collective-permute-done.2.refs_4_), channel_id=1, source_target_pairs={{8,0},{16,8},{24,16},{28,24},{20,28},{12,20},{4,12},{0,4},{9,1},{1... | collective-permute-start | bytes 393224 | tf_op jit(solution)/shard_map/ppermute | solution.py:410
  37.3 7.0 %collective-permute-start.21 = (f32[264,128]{1,0:T(8,128)S(1)}, f32[264,128]{1,0:T(8,128)S(1)}, u32[]{:S(2)}, u32[]{:S(2)}) collective-permute-start(f32[264,128]{1,0:T(8,128)S(1)} %get-tuple-element.91), channel_id=1, source_target_pairs={{0,8},{8,16},{16,24},{24,28},{28,20},{20,12},{12,4},{4,0},{1,9},{9... | collective-permute-start | bytes 405512 | tf_op jit(solution)/shard_map/ppermute | solution.py:407
  39.1 6.4 %collective-permute-start.22 = (f32[264,128]{1,0:T(8,128)S(1)}, f32[264,128]{1,0:T(8,128)S(1)}, u32[]{:S(2)}, u32[]{:S(2)}) collective-permute-start(f32[264,128]{1,0:T(8,128)S(1)} %get-tuple-element.93), channel_id=1, source_target_pairs={{8,0},{16,8},{24,16},{28,24},{20,28},{12,20},{4,12},{0,4},{9,1},{1... | collective-permute-start | bytes 405512 | tf_op jit(solution)/shard_map/ppermute | solution.py:410
  42.2 6.4 %collective-permute-start.7 = (f32[256,128]{1,0:T(8,128)S(1)}, f32[256,128]{1,0:T(8,128)S(1)}, u32[]{:S(2)}, u32[]{:S(2)}) collective-permute-start(f32[256,128]{1,0:T(8,128)S(1)} %get-tuple-element.78), channel_id=1, source_target_pairs={{0,8},{8,16},{16,24},{24,28},{28,20},{20,12},{12,4},{4,0},{1,9},{9... | collective-permute-start | bytes 393224 | tf_op jit(solution)/shard_map/ppermute | solution.py:407
  47.1 6.2 %collective-permute-start.24 = (f32[264,128]{1,0:T(8,128)S(1)}, f32[264,128]{1,0:T(8,128)S(1)}, u32[]{:S(2)}, u32[]{:S(2)}) collective-permute-start(f32[264,128]{1,0:T(8,128)S(1)} %get-tuple-element.97), channel_id=1, source_target_pairs={{8,0},{16,8},{24,16},{28,24},{20,28},{12,20},{4,12},{0,4},{9,1},{1... | collective-permute-start | bytes 405512 | tf_op jit(solution)/shard_map/ppermute | solution.py:410
  49.0 7.1 %collective-permute-start.10 = (f32[256,128]{1,0:T(8,128)S(1)}, f32[256,128]{1,0:T(8,128)S(1)}, u32[]{:S(2)}, u32[]{:S(2)}) collective-permute-start(f32[256,128]{1,0:T(8,128)S(1)} %get-tuple-element.84), channel_id=1, source_target_pairs={{8,0},{16,8},{24,16},{28,24},{20,28},{12,20},{4,12},{0,4},{9,1},{1... | collective-permute-start | bytes 393224 | tf_op jit(solution)/shard_map/ppermute | solution.py:410
  50.3 6.3 %collective-permute-start.9 = (f32[256,128]{1,0:T(8,128)S(1)}, f32[256,128]{1,0:T(8,128)S(1)}, u32[]{:S(2)}, u32[]{:S(2)}) collective-permute-start(f32[256,128]{1,0:T(8,128)S(1)} %get-tuple-element.82), channel_id=1, source_target_pairs={{0,8},{8,16},{16,24},{24,28},{28,20},{20,12},{12,4},{4,0},{1,9},{9... | collective-permute-start | bytes 393224 | tf_op jit(solution)/shard_map/ppermute | solution.py:407
  53.4 6.7 %collective-permute-start.25 = (f32[264,128]{1,0:T(8,128)S(1)}, f32[264,128]{1,0:T(8,128)S(1)}, u32[]{:S(2)}, u32[]{:S(2)}) collective-permute-start(f32[264,128]{1,0:T(8,128)S(1)} %get-tuple-element.99), channel_id=1, source_target_pairs={{0,8},{8,16},{16,24},{24,28},{28,20},{20,12},{12,4},{4,0},{1,9},{9... | collective-permute-start | bytes 405512 | tf_op jit(solution)/shard_map/ppermute | solution.py:407
  58.2 7.4 %collective-permute-start.27 = (f32[264,128]{1,0:T(8,128)S(1)}, f32[264,128]{1,0:T(8,128)S(1)}, u32[]{:S(2)}, u32[]{:S(2)}) collective-permute-start(f32[264,128]{1,0:T(8,128)S(1)} %get-tuple-element.101), channel_id=1, source_target_pairs={{8,0},{16,8},{24,16},{28,24},{20,28},{12,20},{4,12},{0,4},{9,1},{1... | collective-permute-start | bytes 405512 | tf_op jit(solution)/shard_map/ppermute | solution.py:410
  60.1 6.4 %collective-permute-start.26 = (f32[264,128]{1,0:T(8,128)S(1)}, f32[264,128]{1,0:T(8,128)S(1)}, u32[]{:S(2)}, u32[]{:S(2)}) collective-permute-start(f32[264,128]{1,0:T(8,128)S(1)} %add_pairs.17), channel_id=1, source_target_pairs={{0,8},{8,16},{16,24},{24,28},{28,20},{20,12},{12,4},{4,0},{1,9},{9... | collective-permute-start | bytes 405512 | tf_op jit(solution)/shard_map/ppermute | solution.py:407
  61.0 8.0 %collective-permute-start.11 = (f32[256,128]{1,0:T(8,128)S(1)}, f32[256,128]{1,0:T(8,128)S(1)}, u32[]{:S(2)}, u32[]{:S(2)}) collective-permute-start(f32[256,128]{1,0:T(8,128)S(1)} %get-tuple-element.86), channel_id=1, source_target_pairs={{0,8},{8,16},{16,24},{24,28},{28,20},{20,12},{12,4},{4,0},{1,9},{9... | collective-permute-start | bytes 393224 | tf_op jit(solution)/shard_map/ppermute | solution.py:407
  62.8 6.4 %collective-permute-start.13 = (f32[256,128]{1,0:T(8,128)S(1)}, f32[256,128]{1,0:T(8,128)S(1)}, u32[]{:S(2)}, u32[]{:S(2)}) collective-permute-start(f32[256,128]{1,0:T(8,128)S(1)} %add_pairs.14), channel_id=1, source_target_pairs={{8,0},{16,8},{24,16},{28,24},{20,28},{12,20},{4,12},{0,4},{9,1},{1... | collective-permute-start | bytes 393224 | tf_op jit(solution)/shard_map/ppermute | solution.py:410
  66.5 6.4 %collective-permute-start.38 = (f32[256,128]{1,0:T(8,128)S(1)}, f32[256,128]{1,0:T(8,128)S(1)}, u32[]{:S(2)}, u32[]{:S(2)}) collective-permute-start(f32[256,128]{1,0:T(8,128)S(1)} %get-tuple-element.105.refs_1_.refs_3_), channel_id=1, source_target_pairs={{0,8},{8,16},{16,24},{24,28},{28,20},{20,12},{12,4},{4,0},{1,9},{9... | collective-permute-start | bytes 393224 | tf_op jit(solution)/shard_map/ppermute | solution.py:407
  69.3 6.4 %collective-permute-start.28 = (f32[256,128]{1,0:T(8,128)S(1)}, f32[256,128]{1,0:T(8,128)S(1)}, u32[]{:S(2)}, u32[]{:S(2)}) collective-permute-start(f32[256,128]{1,0:T(8,128)S(1)} %get-tuple-element.103.refs_1_.refs_3_), channel_id=1, source_target_pairs={{8,0},{16,8},{24,16},{28,24},{20,28},{12,20},{4,12},{0,4},{9,1},{1... | collective-permute-start | bytes 393224 | tf_op jit(solution)/shard_map/ppermute | solution.py:410
  70.8 7.4 %collective-permute-start.35 = (f32[256,128]{1,0:T(8,128)S(1)}, f32[256,128]{1,0:T(8,128)S(1)}, u32[]{:S(2)}, u32[]{:S(2)}) collective-permute-start(f32[256,128]{1,0:T(8,128)S(1)} %get-tuple-element.105.refs_1_.refs_3_), channel_id=1, source_target_pairs={{8,0},{16,8},{24,16},{28,24},{20,28},{12,20},{4,12},{0,4},{9,1},{1... | collective-permute-start | bytes 393224 | tf_op jit(solution)/shard_map/ppermute | solution.py:410
  73.9 6.8 %collective-permute-start.32 = (f32[256,128]{1,0:T(8,128)S(1)}, f32[256,128]{1,0:T(8,128)S(1)}, u32[]{:S(2)}, u32[]{:S(2)}) collective-permute-start(f32[256,128]{1,0:T(8,128)S(1)} %get-tuple-element.103.refs_1_.refs_3_), channel_id=1, source_target_pairs={{0,8},{8,16},{16,24},{24,28},{28,20},{20,12},{12,4},{4,0},{1,9},{9... | collective-permute-start | bytes 393224 | tf_op jit(solution)/shard_map/ppermute | solution.py:407
  79.1 6.3 %collective-permute-start.40 = (f32[256,128]{1,0:T(8,128)S(1)}, f32[256,128]{1,0:T(8,128)S(1)}, u32[]{:S(2)}, u32[]{:S(2)}) collective-permute-start(f32[256,128]{1,0:T(8,128)S(1)} %collective-permute-done.39.refs_7_), channel_id=1, source_target_pairs={{0,8},{8,16},{16,24},{24,28},{28,20},{20,12},{12,4},{4,0},{1,9},{9... | collective-permute-start | bytes 393224 | tf_op jit(solution)/shard_map/ppermute | solution.py:407
  80.8 6.5 %collective-permute-start.33 = (f32[256,128]{1,0:T(8,128)S(1)}, f32[256,128]{1,0:T(8,128)S(1)}, u32[]{:S(2)}, u32[]{:S(2)}) collective-permute-start(f32[256,128]{1,0:T(8,128)S(1)} %collective-permute-done.32.refs_8_), channel_id=1, source_target_pairs={{0,8},{8,16},{16,24},{24,28},{28,20},{20,12},{12,4},{4,0},{1,9},{9... | collective-permute-start | bytes 393224 | tf_op jit(solution)/shard_map/ppermute | solution.py:407
  81.7 6.2 %collective-permute-start.30 = (f32[256,128]{1,0:T(8,128)S(1)}, f32[256,128]{1,0:T(8,128)S(1)}, u32[]{:S(2)}, u32[]{:S(2)}) collective-permute-start(f32[256,128]{1,0:T(8,128)S(1)} %collective-permute-done.29.refs_3_), channel_id=1, source_target_pairs={{8,0},{16,8},{24,16},{28,24},{20,28},{12,20},{4,12},{0,4},{9,1},{1... | collective-permute-start | bytes 393224 | tf_op jit(solution)/shard_map/ppermute | solution.py:410
  83.2 6.2 %collective-permute-start.37 = (f32[256,128]{1,0:T(8,128)S(1)}, f32[256,128]{1,0:T(8,128)S(1)}, u32[]{:S(2)}, u32[]{:S(2)}) collective-permute-start(f32[256,128]{1,0:T(8,128)S(1)} %collective-permute-done.36.refs_3_), channel_id=1, source_target_pairs={{8,0},{16,8},{24,16},{28,24},{20,28},{12,20},{4,12},{0,4},{9,1},{1... | collective-permute-start | bytes 393224 | tf_op jit(solution)/shard_map/ppermute | solution.py:410
  85.4 6.3 %collective-permute-start.41 = (f32[256,128]{1,0:T(8,128)S(1)}, f32[256,128]{1,0:T(8,128)S(1)}, u32[]{:S(2)}, u32[]{:S(2)}) collective-permute-start(f32[256,128]{1,0:T(8,128)S(1)} %collective-permute-done.40.refs_6_), channel_id=1, source_target_pairs={{0,8},{8,16},{16,24},{24,28},{28,20},{20,12},{12,4},{4,0},{1,9},{9... | collective-permute-start | bytes 393224 | tf_op jit(solution)/shard_map/ppermute | solution.py:407
  87.2 10.2 %collective-permute-start.34 = (f32[256,128]{1,0:T(8,128)S(1)}, f32[256,128]{1,0:T(8,128)S(1)}, u32[]{:S(2)}, u32[]{:S(2)}) collective-permute-start(f32[256,128]{1,0:T(8,128)S(1)} %collective-permute-done.33.refs_7_), channel_id=1, source_target_pairs={{0,8},{8,16},{16,24},{24,28},{28,20},{20,12},{12,4},{4,0},{1,9},{9... | collective-permute-start | bytes 393224 | tf_op jit(solution)/shard_map/ppermute | solution.py:407
  88.0 9.5 %collective-permute-start.31 = (f32[256,128]{1,0:T(8,128)S(1)}, f32[256,128]{1,0:T(8,128)S(1)}, u32[]{:S(2)}, u32[]{:S(2)}) collective-permute-start(f32[256,128]{1,0:T(8,128)S(1)} %collective-permute-done.30.refs_4_), channel_id=1, source_target_pairs={{8,0},{16,8},{24,16},{28,24},{20,28},{12,20},{4,12},{0,4},{9,1},{1... | collective-permute-start | bytes 393224 | tf_op jit(solution)/shard_map/ppermute | solution.py:410
  95.4 8.0 %collective-permute-start.49 = (f32[256,128]{1,0:T(8,128)S(1)}, f32[256,128]{1,0:T(8,128)S(1)}, u32[]{:S(2)}, u32[]{:S(2)}) collective-permute-start(f32[256,128]{1,0:T(8,128)S(1)} %get-tuple-element.126), channel_id=1, source_target_pairs={{0,8},{8,16},{16,24},{24,28},{28,20},{20,12},{12,4},{4,0},{1,9},{9... | collective-permute-start | bytes 393224 | tf_op jit(solution)/shard_map/ppermute | solution.py:407
  95.4 7.9 %collective-permute-start.50 = (f32[256,128]{1,0:T(8,128)S(1)}, f32[256,128]{1,0:T(8,128)S(1)}, u32[]{:S(2)}, u32[]{:S(2)}) collective-permute-start(f32[256,128]{1,0:T(8,128)S(1)} %get-tuple-element.128), channel_id=1, source_target_pairs={{8,0},{16,8},{24,16},{28,24},{20,28},{12,20},{4,12},{0,4},{9,1},{1... | collective-permute-start | bytes 393224 | tf_op jit(solution)/shard_map/ppermute | solution.py:410
  107.2 6.3 %collective-permute-start.44 = (f32[256,128]{1,0:T(8,128)S(1)}, f32[256,128]{1,0:T(8,128)S(1)}, u32[]{:S(2)}, u32[]{:S(2)}) collective-permute-start(f32[256,128]{1,0:T(8,128)S(1)} %get-tuple-element.114), channel_id=1, source_target_pairs={{0,8},{8,16},{16,24},{24,28},{28,20},{20,12},{12,4},{4,0},{1,9},{9... | collective-permute-start | bytes 393224 | tf_op jit(solution)/shard_map/ppermute | solution.py:407
  109.3 8.0 %collective-permute-start.53 = (f32[256,128]{1,0:T(8,128)S(1)}, f32[256,128]{1,0:T(8,128)S(1)}, u32[]{:S(2)}, u32[]{:S(2)}) collective-permute-start(f32[256,128]{1,0:T(8,128)S(1)} %get-tuple-element.134), channel_id=1, source_target_pairs={{0,8},{8,16},{16,24},{24,28},{28,20},{20,12},{12,4},{4,0},{1,9},{9... | collective-permute-start | bytes 393224 | tf_op jit(solution)/shard_map/ppermute | solution.py:407
  115.3 6.5 %collective-permute-start.55 = (f32[256,128]{1,0:T(8,128)S(1)}, f32[256,128]{1,0:T(8,128)S(1)}, u32[]{:S(2)}, u32[]{:S(2)}) collective-permute-start(f32[256,128]{1,0:T(8,128)S(1)} %get-tuple-element.136), channel_id=1, source_target_pairs={{8,0},{16,8},{24,16},{28,24},{20,28},{12,20},{4,12},{0,4},{9,1},{1... | collective-permute-start | bytes 393224 | tf_op jit(solution)/shard_map/ppermute | solution.py:410
  116.6 9.5 %collective-permute-start.46 = (f32[256,128]{1,0:T(8,128)S(1)}, f32[256,128]{1,0:T(8,128)S(1)}, u32[]{:S(2)}, u32[]{:S(2)}) collective-permute-start(f32[256,128]{1,0:T(8,128)S(1)} %get-tuple-element.118), channel_id=1, source_target_pairs={{0,8},{8,16},{16,24},{24,28},{28,20},{20,12},{12,4},{4,0},{1,9},{9... | collective-permute-start | bytes 393224 | tf_op jit(solution)/shard_map/ppermute | solution.py:407
  117.4 8.7 %collective-permute-start.54 = (f32[256,128]{1,0:T(8,128)S(1)}, f32[256,128]{1,0:T(8,128)S(1)}, u32[]{:S(2)}, u32[]{:S(2)}) collective-permute-start(f32[256,128]{1,0:T(8,128)S(1)} %add_pairs.23), channel_id=1, source_target_pairs={{0,8},{8,16},{16,24},{24,28},{28,20},{20,12},{12,4},{4,0},{1,9},{9... | collective-permute-start | bytes 393224 | tf_op jit(solution)/shard_map/ppermute | solution.py:407
  119.1 7.0 %collective-permute-start.48 = (f32[256,128]{1,0:T(8,128)S(1)}, f32[256,128]{1,0:T(8,128)S(1)}, u32[]{:S(2)}, u32[]{:S(2)}) collective-permute-start(f32[256,128]{1,0:T(8,128)S(1)} %add_pairs.20), channel_id=1, source_target_pairs={{8,0},{16,8},{24,16},{28,24},{20,28},{12,20},{4,12},{0,4},{9,1},{1... | collective-permute-start | bytes 393224 | tf_op jit(solution)/shard_map/ppermute | solution.py:410
  127.8 7.2 %collective-permute-start.66 = (f32[256,128]{1,0:T(8,128)S(1)}, f32[256,128]{1,0:T(8,128)S(1)}, u32[]{:S(2)}, u32[]{:S(2)}) collective-permute-start(f32[256,128]{1,0:T(8,128)S(1)} %get-tuple-element.140.refs_1_), channel_id=1, source_target_pairs={{0,8},{8,16},{16,24},{24,28},{28,20},{20,12},{12,4},{4,0},{1,9},{9... | collective-permute-start | bytes 393224 | tf_op jit(solution)/shard_map/ppermute | solution.py:407
  128.8 6.2 %collective-permute-start.60 = (f32[264,128]{1,0:T(8,128)S(1)}, f32[264,128]{1,0:T(8,128)S(1)}, u32[]{:S(2)}, u32[]{:S(2)}) collective-permute-start(f32[264,128]{1,0:T(8,128)S(1)} %get-tuple-element.138.refs_1_.refs_0_), channel_id=1, source_target_pairs={{0,8},{8,16},{16,24},{24,28},{28,20},{20,12},{12,4},{4,0},{1,9},{9... | collective-permute-start | bytes 405512 | tf_op jit(solution)/shard_map/ppermute | solution.py:407
  135.0 6.5 %collective-permute-start.61 = (f32[264,128]{1,0:T(8,128)S(1)}, f32[264,128]{1,0:T(8,128)S(1)}, u32[]{:S(2)}, u32[]{:S(2)}) collective-permute-start(f32[264,128]{1,0:T(8,128)S(1)} %collective-permute-done.60.refs_8_.refs_7_), channel_id=1, source_target_pairs={{0,8},{8,16},{16,24},{24,28},{28,20},{20,12},{12,4},{4,0},{1,9},{9... | collective-permute-start | bytes 405512 | tf_op jit(solution)/shard_map/ppermute | solution.py:407
  146.8 7.0 %collective-permute-start.70 = (f32[8,128]{1,0:T(8,128)S(1)}, f32[8,128]{1,0:T(8,128)S(1)}, u32[]{:S(2)}, u32[]{:S(2)}) collective-permute-start(f32[8,128]{1,0:T(8,128)S(1)} %sum_tails.1.refs_0_), channel_id=1, source_target_pairs={{0,1},{1,2},{2,3},{3,0},{4,5},{5,6},{6,7},{7,4},{8,9},{9,10},{10,1... | collective-permute-start | bytes 12296 | tf_op jit(solution)/shard_map/ppermute | solution.py:470
  146.9 7.0 %collective-permute-start.71 = (f32[8,128]{1,0:T(8,128)S(1)}, f32[8,128]{1,0:T(8,128)S(1)}, u32[]{:S(2)}, u32[]{:S(2)}) collective-permute-start(f32[8,128]{1,0:T(8,128)S(1)} %sum_tails.1.refs_0_), channel_id=1, source_target_pairs={{0,2},{1,3},{2,0},{3,1},{4,6},{5,7},{6,4},{7,5},{8,10},{9,11},{10,... | collective-permute-start | bytes 12296 | tf_op jit(solution)/shard_map/ppermute | solution.py:470
  (31 other events, 150.6 us)

commit v2 on v1

v2 whole, which is shorter than its diff:
```python
import math

import jax
import jax.numpy as jnp
from jax import lax
from jax.experimental import pallas as pl
from jax.experimental.pallas import tpu as pltpu
from jax.sharding import PartitionSpec as P

BLOCK = 128
CAP = 2
ITERS = 2
HALVES = 2
TILE = 8
LEAD = 1
BASE_AT = {2: 1, 3: 3}
CUTS = 8


penalty = 1.5

VMEM = pl.BlockSpec(memory_space=pltpu.VMEM)
SMEM = pl.BlockSpec(memory_space=pltpu.SMEM)
HBM = pl.BlockSpec(memory_space=pltpu.HBM)


def grid_of(peers):
    columns = 1
    while (2 * columns) ** 2 <= peers:
        columns *= 2
    return peers // columns, columns


def ring_place(region, peers):
    rows, columns = grid_of(peers)
    row, column = region // columns, region % columns
    up = rows - 1 - row
    if columns == 1:
        return row
    right = up % 2 == 0
    if isinstance(region, int):
        if column == 0:
            return row
        return rows + up * (columns - 1) + (column - 1 if right else columns - 1 - column)
    along = jnp.where(right, column - 1, columns - 1 - column)
    return jnp.where(column == 0, row, rows + up * (columns - 1) + along)


def f32(*shape):
    return jax.ShapeDtypeStruct(shape, jnp.float32)


def call(body, name, ins, in_specs, outs, out_specs, scratch=(), aliases=None, flops=0, moved=1 << 20, room=4, pins=()):
    ins = tuple(pltpu.with_memory_space_constraint(x, pltpu.HBM) if spec is HBM else x for x, spec in zip(ins, in_specs))
    many = isinstance(outs, (list, tuple))
    shapes, specs = (list(outs), list(out_specs)) if many else ([outs], [out_specs])
    for i, spec in enumerate(specs):
        if spec is HBM:
            shapes[i] = pltpu.HBM(shapes[i].shape, shapes[i].dtype)
        elif i in pins:
            shapes[i] = pltpu.VMEM(shapes[i].shape, shapes[i].dtype)
    return pl.pallas_call(
        body,
        name=name,
        out_shape=shapes if many else shapes[0],
        in_specs=in_specs,
        out_specs=out_specs,
        scratch_shapes=scratch,
        input_output_aliases=aliases or {},
        cost_estimate=pl.CostEstimate(flops=flops, bytes_accessed=moved, transcendentals=0),
        compiler_params=pltpu.CompilerParams(vmem_limit_bytes=room << 20),
    )(*ins)


def tie(values, others, near=()):
    values, others = list(values), list(others)

    def body(*refs):
        del refs

    out = call(
        body,
        "tie",
        (*values, *others, *near),
        [VMEM] * len(values) + [HBM] * len(others) + [VMEM] * len(near),
        [f32(*x.shape) for x in values],
        [VMEM] * len(values),
        aliases={i: i for i in range(len(values))},
        moved=0,
    )
    return list(out)


class Loads:
    def __init__(self, sem):
        self.sem, self.used, self.flying = sem, 0, {}

    def start(self, name, src, dst):
        copy = pltpu.make_async_copy(src, dst, self.sem.at[self.used])
        copy.start()
        self.used += 1
        self.flying[name] = copy

    def wait(self, name):
        self.flying.pop(name).wait()


def prepare(region, target, cons, kkt, cost, dual, peers):
    blocks = target.shape[1]
    owned = cons.shape[0] // BLOCK
    arrays = (cons, kkt, cost, dual)
    cuts = (1, CUTS, 1, 1)

    def body(region_ref, target_hbm, *refs):
        from_refs, table_ref, to_refs, target_ref, sem = refs[:4], refs[4], refs[5:9], refs[9], refs[10]
        loads = Loads(sem)
        loads.start("target", target_hbm, target_ref)
        for i, (src, dst) in enumerate(zip(from_refs, to_refs)):
            size = src.shape[0] // cuts[i]
            for c in range(cuts[i]):
                at = slice(c * size, (c + 1) * size)
                loads.start((i, c), src.at[at, :], dst.at[at, :])
        here = ring_place(region_ref[0], peers)
        for i in range(2 * CAP * peers):
            table_ref[i] = -1
        loads.wait("target")
        for j in range(blocks):
            t = target_ref[0, j]

            @pl.when(t >= 0)
            def _(t=t, j=j):
                owner = t // owned
                ahead = ring_place(owner, peers) - here
                ahead = jnp.where(ahead < 0, ahead + peers, ahead)
                first = CAP * ahead
                at = first + jnp.where(table_ref[first] >= 0, 1, 0)
                table_ref[at] = j
                table_ref[CAP * peers + at] = t - owner * owned

        for i in range(4):
            for c in range(cuts[i]):
                loads.wait((i, c))

    out = call(
        body,
        "prepare",
        (region, target, *arrays),
        [SMEM] + [HBM] * 5,
        [jax.ShapeDtypeStruct((2 * CAP * peers,), jnp.int32)] + [jax.ShapeDtypeStruct(x.shape, x.dtype) for x in arrays],
        [SMEM] + [VMEM] * 4,
        [pltpu.SMEM(target.shape, jnp.int32), pltpu.SemaphoreType.DMA((1 + sum(cuts),))],
        moved=12 << 20,
    )
    return out[0], out[1:]


def halve(pieces):
    rows, scen = pieces[0].shape
    width = scen // HALVES

    def body(*refs):
        for h in range(HALVES):
            refs[HALVES + h][...] = refs[h][:, h * width : (h + 1) * width]

    return call(body, "halve", tuple(pieces), [VMEM] * HALVES, [f32(rows, width)] * HALVES, [VMEM] * HALVES)


def columns(ref, h):
    width = ref.shape[1] // HALVES
    return ref.at[:, h * width : (h + 1) * width]


def base_rows(i, step, kkt, cost):
    rows, scen = kkt.shape[0], cost.shape[1]

    def body(kkt_ref, cost_ref, out_ref):
        out_ref[...] = jnp.dot(
            kkt_ref[i * step : (i + 1) * step, :], cost_ref[...], preferred_element_type=jnp.float32
        )

    return call(
        body,
        "base_rows",
        (kkt, cost),
        [VMEM, VMEM],
        f32(step, scen),
        VMEM,
        flops=2 * step * rows * scen,
        moved=3 << 20,
    )


def slots_of(table_ref, peers, blocks):
    out = []
    for r in range(peers):
        row = []
        for c in range(CAP):
            j = table_ref[CAP * r + c]
            b = table_ref[CAP * peers + CAP * r + c]
            read = jnp.maximum(j, 0)
            write = jnp.where(j < 0, blocks, j)
            row.append([pl.ds(pl.multiple_of(x * BLOCK, BLOCK), BLOCK) for x in (read, write, jnp.maximum(b, 0))] + [b])
        out.append(row)
    return out


def fold(x):
    return jnp.sum(x.reshape(-1, TILE, x.shape[-1]), axis=0)


def place(part_ref, totals, slots, owned):
    for o in range(owned):
        value = None
        for total, (_, _, _, b) in zip(totals, slots):
            mine = jnp.where(b == o, total, 0.0)
            value = mine if value is None else value + mine
        part_ref[o * BLOCK : (o + 1) * BLOCK, :] = value


def first_solve(h, table, pieces, dual, bases, kkt, owned, counting):
    peers = len(pieces)
    bound, scen = dual.shape
    width = scen // HALVES
    cols = slice(h * width, (h + 1) * width)
    own = owned * BLOCK
    sent = own + (TILE if counting else 0)
    step = bases[0].shape[0]
    chunks = bound // step

    def body(*refs):
        table_ref, refs = refs[0], refs[1:]
        piece, (dual_ref, kkt_ref), refs = refs[:peers], refs[peers : peers + 2], refs[peers + 2 :]
        piece = [ref if ref.shape[1] == width else columns(ref, h) for ref in piece]
        base_refs, z_ref, refs = refs[:chunks], refs[chunks], refs[chunks + 1 :]
        part, (drive_ref,) = refs[:peers], refs[peers:]
        slots = slots_of(table_ref, peers, bound // BLOCK)
        drive_ref[...] = jnp.zeros_like(drive_ref)
        for r in range(peers):
            for read, write, block, _ in slots[r]:
                drive_ref[write, :] = (penalty * (piece[r][block, :] - dual_ref[read, cols])).astype(jnp.bfloat16)
        for i in range(chunks):
            at = slice(i * step, (i + 1) * step)
            got = jnp.dot(kkt_ref[at, :bound], drive_ref[:bound, :], preferred_element_type=jnp.float32)
            z_ref[at, :] = (base_refs[i][:, cols] + got) + dual_ref[at, cols]
        for r in range(peers):
            place(part[r], [z_ref[read, :] for read, _, _, _ in slots[r]], slots[r], owned)
            if counting:
                row = lax.broadcasted_iota(jnp.int32, (TILE, width), 0)
                count = jnp.zeros((TILE, width), jnp.float32)
                for _, _, _, b in slots[r]:
                    count = count + jnp.where(row == b, 1.0, 0.0)
                part[r][own:, :] = count

    out = call(
        body,
        "first_solve",
        (table, *pieces, dual, kkt, *bases[:chunks]),
        [SMEM] + [VMEM] * (peers + 2 + chunks),
        [f32(bound, width)] + [f32(sent, width)] * peers,
        [VMEM] * (1 + peers),
        [pltpu.VMEM((bound + BLOCK, width), jnp.bfloat16)],
        flops=2 * bound * bound * width,
        moved=8 << 20,
    )
    return out[0], out[1:]


def second_solve(h, table, pieces, z, dual, bases, kkt, owned):
    peers = len(pieces)
    bound, scen = dual.shape
    step = bases[0].shape[0]
    chunks = bound // step
    width = scen // HALVES
    cols = slice(h * width, (h + 1) * width)
    own = owned * BLOCK

    def body(*refs):
        table_ref, refs = refs[0], refs[1:]
        piece, (z_ref, dual_ref, kkt_ref), refs = refs[:peers], refs[peers : peers + 3], refs[peers + 3 :]
        base_refs, refs = refs[:chunks], refs[chunks:]
        field_ref, drive_ref, next_ref, norm_ref, part = refs[0], refs[1], refs[2], refs[3], refs[4:]
        slots = slots_of(table_ref, peers, bound // BLOCK)
        drive_ref[...] = jnp.zeros_like(drive_ref)
        next_ref[:bound, :] = dual_ref[:, cols]
        gaps = jnp.zeros((TILE, width), jnp.float32)
        for r in range(peers):
            for read, write, block, b in slots[r]:
                fetched = piece[r][block, :]
                renewed_dual = z_ref[read, :] - fetched
                gap = renewed_dual - dual_ref[read, cols]
                gaps = gaps + jnp.where(b < 0, 0.0, fold(gap * gap))
                next_ref[write, :] = renewed_dual
                drive_ref[write, :] = (penalty * (fetched - renewed_dual)).astype(jnp.bfloat16)
        for i in range(chunks):
            at = slice(i * step, (i + 1) * step)
            got = jnp.dot(kkt_ref[at, :bound], drive_ref[:bound, :], preferred_element_type=jnp.float32)
            field_ref[at, :] = base_refs[i][:, cols] + got
        shifts = jnp.zeros((TILE, width), jnp.float32)
        for r in range(peers):
            totals = []
            for read, write, block, b in slots[r]:
                copies = field_ref[read, :]
                shift = copies - piece[r][block, :]
                shifts = shifts + jnp.where(b < 0, 0.0, fold(shift * shift))
                totals.append(copies + next_ref[read, :])
            for total, (_, write, _, _) in zip(totals, slots[r]):
                next_ref[write, :] = total
            place(part[r], totals, slots[r], owned)
        norm_ref[:TILE, :] = gaps
        norm_ref[TILE:, :] = shifts

    out = call(
        body,
        "second_solve",
        (table, *pieces, z, dual, kkt, *bases[:chunks]),
        [SMEM] + [VMEM] * (peers + 3 + chunks),
        [
            f32(bound, width),
            jax.ShapeDtypeStruct((bound + BLOCK, width), jnp.bfloat16),
            f32(bound + BLOCK, width),
            f32(2 * TILE, width),
        ]
        + [f32(own, width)] * peers,
        [VMEM] * (4 + peers),
        flops=2 * bound * bound * width,
        moved=8 << 20,
    )
    return out[0], out[1], out[2], out[3], out[4:]


def store_state(h, field, drive, bases, kkt, state):
    bound, width = field.shape
    rows = kkt.shape[0]
    step = bases[0].shape[0]
    cols = slice(h * width, (h + 1) * width)
    given = 0 if state is None else 1
    rest = bases[bound // step :]

    def body(field_ref, drive_ref, kkt_ref, *refs):
        base_refs, (state_hbm, rest_ref, sem) = refs[: len(rest)], refs[len(rest) + given :]
        loads = Loads(sem)
        loads.start("field", field_ref, state_hbm.at[:bound, cols])
        for i in range(len(rest)):
            at = slice(i * step, (i + 1) * step)
            there = slice(bound + i * step, bound + (i + 1) * step)
            got = jnp.dot(kkt_ref[there, :bound], drive_ref[:bound, :], preferred_element_type=jnp.float32)
            rest_ref[at, :] = base_refs[i][:, cols] + got
        loads.start("rest", rest_ref, state_hbm.at[bound:, cols])
        loads.wait("field")
        loads.wait("rest")

    before = () if state is None else (state,)
    return call(
        body,
        "store_state",
        (field, drive, kkt, *rest, *before),
        [VMEM] * (3 + len(rest)) + [HBM] * given,
        f32(rows, HALVES * width),
        HBM,
        [pltpu.VMEM((rows - bound, width), jnp.float32), pltpu.SemaphoreType.DMA((2,))],
        aliases={3 + len(rest): 0} if given else None,
        flops=2 * bound * (rows - bound) * width,
        moved=4 << 20,
    )


def add_pairs(pairs):
    def body(*refs):
        for i in range(len(pairs)):
            refs[2 * len(pairs) + i][...] = refs[2 * i][...] + refs[2 * i + 1][...]

    out = call(
        body,
        "add_pairs",
        tuple(x for pair in pairs for x in pair),
        [VMEM] * (2 * len(pairs)),
        [f32(*pair[0].shape) for pair in pairs],
        [VMEM] * len(pairs),
    )
    return list(out)


def renew(h, parts, before, count, norms):
    own, width = before.shape[0], parts[0].shape[1]
    owned = own // BLOCK
    counted = count is None

    def body(*refs):
        parts_ref, refs = refs[: len(parts)], refs[len(parts) :]
        before_ref, refs = refs[0] if before.shape[1] == width else columns(refs[0], h), refs[1:]
        if not counted:
            count_ref, refs = refs[0], refs[1:]
        norm_refs, refs = refs[: len(norms)], refs[len(norms) :]
        new_ref, moved_ref = refs[0], refs[1]

        def total(at):
            value = parts_ref[0][at, :]
            for ref in parts_ref[1:]:
                value = value + ref[at, :]
            return value

        if counted:
            tile = total(slice(own, own + TILE))
            refs[2][...] = tile
        else:
            tile = count_ref[...]
        moved = jnp.zeros((TILE, width), jnp.float32)
        for b in range(owned):
            at = slice(b * BLOCK, (b + 1) * BLOCK)
            many = tile[b : b + 1, :]
            value = total(at) / jnp.maximum(many, 1.0)
            change = value - before_ref[at, :]
            moved = moved + many * fold(change * change)
            new_ref[at, :] = value
        moved_ref[...] = moved
        if norms:
            gaps = norm_refs[0][...] + norm_refs[3][...]
            sums = [
                gaps[:TILE, :],
                norm_refs[1][...] + norm_refs[4][...],
                gaps[TILE:, :],
                norm_refs[2][...] + moved,
            ]
            row = lax.broadcasted_iota(jnp.int32, (TILE, width), 0)
            block = jnp.zeros((TILE, width), jnp.float32)
            for i, x in enumerate(sums):
                block = jnp.where(row == i, jnp.sum(x, axis=0, keepdims=True), block)
            new_ref[own:, :] = block

    ins = (*parts, before) + (() if counted else (count,)) + tuple(norms)
    outs = [f32(own + (TILE if norms else 0), width), f32(TILE, width)] + ([f32(TILE, width)] if counted else [])
    return call(body, "renew", ins, [VMEM] * len(ins), outs, [VMEM] * len(outs))


def finish(h, table, pieces, z, scen, owned, outputs):
    peers = len(pieces)
    bound, width = z.shape[0] - BLOCK, z.shape[1]
    cols = slice(h * width, (h + 1) * width)
    own = owned * BLOCK
    given = len(outputs)

    def body(*refs):
        table_ref, refs = refs[0], refs[1:]
        piece, z_ref, refs = refs[:peers], refs[peers], refs[peers + 1 + given :]
        dual_hbm, cons_hbm, dual_ref, sem = refs
        loads = Loads(sem)
        loads.start("cons", piece[0].at[:own, :], cons_hbm.at[:, cols])
        dual_ref[:bound, :] = z_ref[:bound, :]
        for r, slots in enumerate(slots_of(table_ref, peers, bound // BLOCK)):
            for read, write, block, _ in slots:
                dual_ref[write, :] = z_ref[read, :] - piece[r][block, :]
        loads.start("dual", dual_ref.at[:bound, :], dual_hbm.at[:, cols])
        loads.wait("dual")
        loads.wait("cons")

    return call(
        body,
        "finish",
        (table, *pieces, z, *outputs),
        [SMEM] + [VMEM] * (peers + 1) + [HBM] * given,
        [f32(bound, scen), f32(own, scen)],
        [HBM] * 2,
        [pltpu.VMEM((bound + BLOCK, width), jnp.float32), pltpu.SemaphoreType.DMA((2,))],
        aliases={peers + 2: 0, peers + 3: 1} if given else None,
        moved=3 << 20,
    )


def sum_tails(pieces, own, done):
    peers, width = len(pieces), pieces[0].shape[1]

    def body(*refs):
        total = refs[0][own:, :]
        for ref in refs[1:peers]:
            total = total + ref[own:, :]
        refs[-1][...] = total

    ins = (*pieces, *done)
    return call(body, "sum_tails", ins, [VMEM] * peers + [HBM] * len(done), f32(TILE, width), VMEM)


def norm_table(tiles, scale):
    def body(*refs):
        total = refs[0][...]
        for ref in refs[1:-1]:
            total = total + ref[...]
        total = jnp.sum(total, axis=1, keepdims=True)
        row = lax.broadcasted_iota(jnp.int32, (ITERS, 2), 0)
        col = lax.broadcasted_iota(jnp.int32, (ITERS, 2), 1)
        primal = jnp.where(row == 0, total[0:1, :], total[2:3, :] - total[3:4, :])
        moved = penalty * penalty * jnp.where(row == 0, total[1:2, :], total[3:4, :])
        refs[-1][...] = jnp.sqrt(jnp.maximum(jnp.where(col == 0, primal, moved), 0.0) / scale)

    return call(body, "norm_table", tuple(tiles), [VMEM] * len(tiles), f32(ITERS, 2), VMEM)


def shards(kkt, cost, dual, cons, target):
    scen = cost.shape[1]
    owned = cons.shape[0] // BLOCK
    peers = lax.axis_size("region")
    subs = lax.axis_size("sub")
    order = sorted(range(peers), key=lambda region: ring_place(region, peers))
    ahead = [(order[i], order[(i + 1) % peers]) for i in range(peers)]
    behind = [(b, a) for a, b in ahead]

    def forward(x):
        return lax.ppermute(x, "region", ahead)

    def backward(x):
        return lax.ppermute(x, "region", behind)

    def reach(h):
        long, short = peers // 2, (peers - 1) // 2
        return (long, short) if h % 2 == 0 else (short, long)

    def gather_all(piece, own, beside):
        across = peers // 2
        pieces = [own] * peers
        f = b = piece
        for k in range(1, across):
            if k > 1:
                f, b = pieces[peers - k + 1], pieces[k - 1] = beside(k, [f, b])
            f, b = pieces[peers - k], pieces[k] = forward(f), backward(b)
        f, b = halve(beside(across, [f, b]))
        return [[*pieces[:across], half, *pieces[across + 1 :]] for half in (forward(f), backward(b))]

    def gather(h, piece, beside=lambda k, x: x):
        far, near = reach(h)
        pieces = [piece] * peers
        f = b = piece
        for k in range(1, max(far, near) + 1):
            values = yield ([f] if k <= far else []) + ([b] if k <= near else [])
            values = beside(k, values)
            if k <= far:
                f = pieces[(peers - k) % peers] = forward(values.pop(0))
            if k <= near:
                b = pieces[k] = backward(values.pop(0))
        return pieces

    def scatter(h, parts):
        far, near = reach(h)
        f, b = parts[far], parts[peers - near]
        for k in range(1, max(far, near) + 1):
            going, coming = f, b
            values = yield ([f] if k <= far else []) + ([b] if k <= near else [])
            f = forward(values.pop(0)) if k <= far else going
            b = backward(values.pop(0)) if k <= near else coming
            pairs = []
            if k < far:
                pairs.append((f, parts[far - k]))
            if k < near:
                pairs.append((b, parts[peers - near + k]))
            if pairs:
                added = add_pairs(pairs)
                if k < far:
                    f = added.pop(0)
                if k < near:
                    b = added.pop(0)
        return [parts[0], f, b]

    region = lax.axis_index("region").astype(jnp.int32).reshape(1)
    table, (own, kkt, cost, dual) = prepare(region, target, cons, kkt, cost, dual, peers)
    step = math.gcd(dual.shape[0], kkt.shape[0])
    chunks = kkt.shape[0] // step
    bases = []

    def beside(k, values):
        some = [own] if k == 2 else []
        while len(bases) < min(chunks, BASE_AT.get(k, chunks if k > 3 else 0)):
            bases.append(base_rows(len(bases), step, kkt, cost))
            some.append(bases[-1])
        return tie(values, [], some) if some else values

    first = gather_all(cons, own, beside)
    known = {"state": None, "outputs": (), "count": None, "norms": []}

    def half(h):
        last = h == HALVES - 1
        pieces = first[h]
        z, parts = first_solve(h, table, pieces, dual, bases, kkt, owned, h == 0)
        arrived = yield from scatter(h, parts)
        out = renew(h, arrived, own, known["count"], ())
        averages, moved = out[0], out[1]
        if known["count"] is None:
            known["count"] = out[2]
        pieces = yield from gather(h, averages)
        field, drive, z, gaps, parts = second_solve(h, table, pieces, z, dual, bases, kkt, owned)
        known["state"] = store_state(h, field, drive, bases, kkt, known["state"])
        arrived = yield from scatter(h, parts)
        norms = known["norms"] + [gaps, moved]
        out = renew(h, arrived, averages, known["count"], norms if last else ())
        known["norms"] = norms + [out[1]]
        pieces = yield from gather(h, out[0])
        if last:
            known["tail"] = sum_tails(pieces, owned * BLOCK, [*known["outputs"], known["state"]])
        known["outputs"] = finish(h, table, pieces, z, scen, owned, known["outputs"])

    turns = [half(h) for h in range(HALVES)]
    waiting = [next(turn) for turn in turns]
    which = LEAD * [0]
    while any(w is not None for w in waiting):
        h = which.pop(0) if which else next_turn(waiting, h)
        values = list(waiting[h])
        try:
            waiting[h] = turns[h].send(values)
        except StopIteration:
            waiting[h] = None
    tail = known["tail"]
    turned = [lax.ppermute(tail, "sub", [(i, (i + k) % subs) for i in range(subs)]) for k in range(1, subs)]
    norms = norm_table([tail, *turned], float(peers * subs * scen * BLOCK))
    return (known["state"], *known["outputs"], norms)


def next_turn(waiting, h):
    for k in range(1, len(waiting) + 1):
        if waiting[(h + k) % len(waiting)] is not None:
            return (h + k) % len(waiting)


def solution(mesh):
    spec = P(("region", "sub"), None)
    return jax.shard_map(
        shards, mesh=mesh, in_specs=(spec,) * 5, out_specs=(spec, spec, spec, P()), check_vma=False
    )
```

time: 154 us -> 150 us (0.974)
  starting transfers between devices: 79.1 us -> 71.6 us
  waiting for transfers between devices: 45 us -> 51.8 us
  local copies, waits for them, and re-layouts: 6.44 us -> 0.04 us
  Pallas kernels: 23.1 us -> 25.6 us
    ppermute x35 -> x32, starting transfers between devices: 42 us -> 25.1 us  [backward(): return lax.ppermute(x, 'region', behind)]
    ppermute x35 -> x32, waiting for transfers between devices: 21.2 us -> 29.7 us  [backward(): return lax.ppermute(x, 'region', behind)]
    ppermute x35 -> x32, starting transfers between devices: 34.8 us -> 43.3 us  [forward(): return lax.ppermute(x, 'region', ahead)]
    unnamed x12 -> x2, local copies, waits for them, and re-layouts: 6.44 us -> 0.04 us
    pallas_call x26 -> x35, Pallas kernels: 23.1 us -> 25.6 us  [call(): pl.pallas_call(body, name=name, out_shape=shapes if many else shapes[0],...]
    ppermute x35 -> x32, waiting for transfers between devices: 23.8 us -> 22.1 us  [forward(): return lax.ppermute(x, 'region', ahead)]
  transfers between devices with their start and end apart: 73 -> 67, of which waited for: 39 -> 39; matrix products, arithmetic and copies ran while one was open for 0% -> 0% of each run, Pallas kernels for 13% -> 16%
where the time goes in v2:
time: 150 us
  starting transfers between devices  71.6 us (48%)
  waiting for transfers between devices  51.8 us (35%)
  Pallas kernels  25.6 us (17%)
    ppermute x32, starting transfers between devices, forward(): return lax.ppermute(x, 'region', ahead)  43.3 us
    ppermute x32, waiting for transfers between devices, backward(): return lax.ppermute(x, 'region', behind)  29.7 us
    pallas_call x35, Pallas kernels, call(): pl.pallas_call(body, name=name, out_shape=shapes if many else shapes[0],...  25.6 us
    ppermute x32, starting transfers between devices, backward(): return lax.ppermute(x, 'region', behind)  25.1 us
    ppermute x32, waiting for transfers between devices, forward(): return lax.ppermute(x, 'region', ahead)  22.1 us
    ppermute x3, starting transfers between devices, shards(): lax.ppermute(tail, 'sub', [(i, (i + k) % subs) for i in range(subs)])  3.16 us
  transfers between devices with their start and end apart: 67, of which 39 were waited for; matrix products, arithmetic and copies ran while one was open for 0% of the time, Pallas kernels for 16%

profile of v2, /device:TPU:0, one launch (start us, length us, event | category | flops | bytes accessed | tf_op | source)
XLA Modules:
  0.0 149.9 jit_solution(4599150253793396450)
XLA Ops:
  0.6 3.1 %collective-permute-start = (f32[256,256]{1,0:T(8,128)}, f32[256,256]{1,0:T(8,128)S(1)}, u32[]{:S(2)}, u32[]{:S(2)}) collective-permute-start(f32[256,256]{1,0:T(8,128)} %refs_0_.1), channel_id=1, source_target_pairs={{0,8},{8,16},{16,24},{24,28},{28,20},{20,12},{12,4},{4,0},{1,9},{9... | collective-permute-start | bytes 786440 | tf_op jit(solution)/shard_map/ppermute | solution.py:507
  3.7 5.0 %prepare.1 = (s32[32]{0:T(128)S(1)}, f32[256,256]{1,0:T(8,128)S(1)}, bf16[2048,2048]{1,0:T(8,128)(2,1)S(1)}, bf16[2048,256]{1,0:T(8,128)(2,1)S(1)}, f32[1536,256]{1,0:T(8,128)S(1)}) custom-call(s32[1]{0:T(128)} %bitcast.region_ref, s32[1,12]{1,0:T(1,128)} %target_hbm.1, f32[256,256]{1,0:T(8,128)} %refs_0_.1, bf16[2048,2048]{1,0:T(8,128)(2,1)} %refs_1_.1, ...), custom_call_target="tpu_custom_call" | custom-call | bytes 12582912 | tf_op jit(solution)/shard_map/prepare/pallas_call | solution.py:62
  10.1 1.5 %collective-permute-done.1.refs_1_ = f32[256,256]{1,0:T(8,128)S(1)} collective-permute-done((f32[256,256]{1,0:T(8,128)}, f32[256,256]{1,0:T(8,128)S(1)}, u32[]{:S(2)}, u32[]{:S(2)}) %collective-permute-start.1) | collective-permute-done | bytes 262176 | tf_op jit(solution)/shard_map/ppermute | solution.py:510
  11.7 1.6 %collective-permute-start.2 = (f32[256,256]{1,0:T(8,128)S(1)}, f32[256,256]{1,0:T(8,128)S(1)}, u32[]{:S(2)}, u32[]{:S(2)}) collective-permute-start(f32[256,256]{1,0:T(8,128)S(1)} %get-tuple-element.92.refs_8_), channel_id=1, source_target_pairs={{0,8},{8,16},{16,24},{24,28},{28,20},{20,12},{12,4},{4,0},{1,9},{9... | collective-permute-start | bytes 786440 | tf_op jit(solution)/shard_map/ppermute | solution.py:507
  15.2 3.4 %collective-permute-done.2.refs_0_ = f32[256,256]{1,0:T(8,128)S(1)} collective-permute-done((f32[256,256]{1,0:T(8,128)S(1)}, f32[256,256]{1,0:T(8,128)S(1)}, u32[]{:S(2)}, u32[]{:S(2)}) %collective-permute-start.2) | collective-permute-done | bytes 262176 | tf_op jit(solution)/shard_map/ppermute | solution.py:507
  19.8 1.6 %collective-permute-start.5 = (f32[256,256]{1,0:T(8,128)S(1)}, f32[256,256]{1,0:T(8,128)S(1)}, u32[]{:S(2)}, u32[]{:S(2)}) collective-permute-start(f32[256,256]{1,0:T(8,128)S(1)} %get-tuple-element.94.refs_7_), channel_id=1, source_target_pairs={{0,8},{8,16},{16,24},{24,28},{28,20},{20,12},{12,4},{4,0},{1,9},{9... | collective-permute-start | bytes 786440 | tf_op jit(solution)/shard_map/ppermute | solution.py:507
  22.6 3.6 %collective-permute-done.5.refs_6_ = f32[256,256]{1,0:T(8,128)S(1)} collective-permute-done((f32[256,256]{1,0:T(8,128)S(1)}, f32[256,256]{1,0:T(8,128)S(1)}, u32[]{:S(2)}, u32[]{:S(2)}) %collective-permute-start.5) | collective-permute-done | bytes 262176 | tf_op jit(solution)/shard_map/ppermute | solution.py:507
  26.2 1.6 %collective-permute-done.4.refs_4_ = f32[256,256]{1,0:T(8,128)S(1)} collective-permute-done((f32[256,256]{1,0:T(8,128)S(1)}, f32[256,256]{1,0:T(8,128)S(1)}, u32[]{:S(2)}, u32[]{:S(2)}) %collective-permute-start.4) | collective-permute-done | bytes 262176 | tf_op jit(solution)/shard_map/ppermute | solution.py:510
  27.9 2.3 %collective-permute-start.14 = (f32[256,128]{1,0:T(8,128)S(1)}, f32[256,128]{1,0:T(8,128)S(1)}, u32[]{:S(2)}, u32[]{:S(2)}) collective-permute-start(f32[256,128]{1,0:T(8,128)S(1)} %get-tuple-element.111), channel_id=1, source_target_pairs={{0,8},{8,16},{16,24},{24,28},{28,20},{20,12},{12,4},{4,0},{1,9},{9... | collective-permute-start | bytes 393224 | tf_op jit(solution)/shard_map/ppermute | solution.py:507
  30.1 2.8 %collective-permute-done.14.refs_5_ = f32[256,128]{1,0:T(8,128)S(1)} collective-permute-done((f32[256,128]{1,0:T(8,128)S(1)}, f32[256,128]{1,0:T(8,128)S(1)}, u32[]{:S(2)}, u32[]{:S(2)}) %collective-permute-start.14) | collective-permute-done | bytes 131104 | tf_op jit(solution)/shard_map/ppermute | solution.py:507
  32.9 2.3 %first_solve.3 = (f32[1536,128]{1,0:T(8,128)S(1)}, f32[264,128]{1,0:T(8,128)S(1)}, f32[264,128]{1,0:T(8,128)S(1)}, f32[264,128]{1,0:T(8,128)S(1)}, f32[264,128]{...) custom-call(s32[32]{0:T(128)S(1)} %get-tuple-element.87.refs_0_, ...), custom_call_target="tpu_custom_call" | custom-call | flops 603979776 | bytes 8388608 | tf_op jit(solution)/shard_map/first_solve/pallas_call | solution.py:62
  35.2 2.5 %collective-permute-start.15 = (f32[264,128]{1,0:T(8,128)S(1)}, f32[264,128]{1,0:T(8,128)S(1)}, u32[]{:S(2)}, u32[]{:S(2)}) collective-permute-start(f32[264,128]{1,0:T(8,128)S(1)} %get-tuple-element.113), channel_id=1, source_target_pairs={{0,8},{8,16},{16,24},{24,28},{28,20},{20,12},{12,4},{4,0},{1,9},{9... | collective-permute-start | bytes 405512 | tf_op jit(solution)/shard_map/ppermute | solution.py:507
  37.8 2.3 %first_solve.2 = (f32[1536,128]{1,0:T(8,128)S(1)}, f32[256,128]{1,0:T(8,128)S(1)}, f32[256,128]{1,0:T(8,128)S(1)}, f32[256,128]{1,0:T(8,128)S(1)}, f32[256,128]{...) custom-call(s32[32]{0:T(128)S(1)} %get-tuple-element.87.refs_0_, ...), custom_call_target="tpu_custom_call" | custom-call | flops 603979776 | bytes 8388608 | tf_op jit(solution)/shard_map/first_solve/pallas_call | solution.py:62
  40.1 2.1 %collective-permute-start.7 = (f32[256,128]{1,0:T(8,128)S(1)}, f32[256,128]{1,0:T(8,128)S(1)}, u32[]{:S(2)}, u32[]{:S(2)}) collective-permute-start(f32[256,128]{1,0:T(8,128)S(1)} %get-tuple-element.100), channel_id=1, source_target_pairs={{0,8},{8,16},{16,24},{24,28},{28,20},{20,12},{12,4},{4,0},{1,9},{9... | collective-permute-start | bytes 393224 | tf_op jit(solution)/shard_map/ppermute | solution.py:507
  47.3 2.0 %collective-permute-start.9 = (f32[256,128]{1,0:T(8,128)S(1)}, f32[256,128]{1,0:T(8,128)S(1)}, u32[]{:S(2)}, u32[]{:S(2)}) collective-permute-start(f32[256,128]{1,0:T(8,128)S(1)} %get-tuple-element.104), channel_id=1, source_target_pairs={{0,8},{8,16},{16,24},{24,28},{28,20},{20,12},{12,4},{4,0},{1,9},{9... | collective-permute-start | bytes 393224 | tf_op jit(solution)/shard_map/ppermute | solution.py:507
  49.3 1.5 collective-permute-done.18.refs_2_
  51.3 2.4 %collective-permute-done.10.refs_2_ = f32[256,128]{1,0:T(8,128)S(1)} collective-permute-done((f32[256,128]{1,0:T(8,128)S(1)}, f32[256,128]{1,0:T(8,128)S(1)}, u32[]{:S(2)}, u32[]{:S(2)}) %collective-permute-start.10) | collective-permute-done | bytes 131104 | tf_op jit(solution)/shard_map/ppermute | solution.py:510
  54.8 2.2 %collective-permute-done.19.refs_0_ = f32[264,128]{1,0:T(8,128)S(1)} collective-permute-done((f32[264,128]{1,0:T(8,128)S(1)}, f32[264,128]{1,0:T(8,128)S(1)}, u32[]{:S(2)}, u32[]{:S(2)}) %collective-permute-start.19) | collective-permute-done | bytes 135200 | tf_op jit(solution)/shard_map/ppermute | solution.py:507
  57.0 1.6 %collective-permute-start.20 = (f32[264,128]{1,0:T(8,128)S(1)}, f32[264,128]{1,0:T(8,128)S(1)}, u32[]{:S(2)}, u32[]{:S(2)}) collective-permute-start(f32[264,128]{1,0:T(8,128)S(1)} %add_pairs.17), channel_id=1, source_target_pairs={{0,8},{8,16},{16,24},{24,28},{28,20},{20,12},{12,4},{4,0},{1,9},{9... | collective-permute-start | bytes 405512 | tf_op jit(solution)/shard_map/ppermute | solution.py:507
  60.7 2.3 %collective-permute-done.21.refs_2_ = f32[264,128]{1,0:T(8,128)S(1)} collective-permute-done((f32[264,128]{1,0:T(8,128)S(1)}, f32[264,128]{1,0:T(8,128)S(1)}, u32[]{:S(2)}, u32[]{:S(2)}) %collective-permute-start.21) | collective-permute-done | bytes 135200 | tf_op jit(solution)/shard_map/ppermute | solution.py:510
  63.6 1.6 %collective-permute-start.32 = (f32[256,128]{1,0:T(8,128)S(1)}, f32[256,128]{1,0:T(8,128)S(1)}, u32[]{:S(2)}, u32[]{:S(2)}) collective-permute-start(f32[256,128]{1,0:T(8,128)S(1)} %get-tuple-element.129.refs_1_.refs_3_), channel_id=1, source_target_pairs={{0,8},{8,16},{16,24},{24,28},{28,20},{20,12},{12,4},{4,0},{1,9},{9... | collective-permute-start | bytes 393224 | tf_op jit(solution)/shard_map/ppermute | solution.py:507
  68.6 1.4 collective-permute-done.32.refs_8_
  70.0 1.5 %collective-permute-start.33 = (f32[256,128]{1,0:T(8,128)S(1)}, f32[256,128]{1,0:T(8,128)S(1)}, u32[]{:S(2)}, u32[]{:S(2)}) collective-permute-start(f32[256,128]{1,0:T(8,128)S(1)} %collective-permute-done.32.refs_8_), channel_id=1, source_target_pairs={{0,8},{8,16},{16,24},{24,28},{28,20},{20,12},{12,4},{4,0},{1,9},{9... | collective-permute-start | bytes 393224 | tf_op jit(solution)/shard_map/ppermute | solution.py:507
  75.4 1.5 %collective-permute-start.34 = (f32[256,128]{1,0:T(8,128)S(1)}, f32[256,128]{1,0:T(8,128)S(1)}, u32[]{:S(2)}, u32[]{:S(2)}) collective-permute-start(f32[256,128]{1,0:T(8,128)S(1)} %collective-permute-done.33.refs_7_), channel_id=1, source_target_pairs={{0,8},{8,16},{16,24},{24,28},{28,20},{20,12},{12,4},{4,0},{1,9},{9... | collective-permute-start | bytes 393224 | tf_op jit(solution)/shard_map/ppermute | solution.py:507
  76.9 1.4 collective-permute-start.27
  80.6 1.6 %collective-permute-start.35 = (f32[256,128]{1,0:T(8,128)S(1)}, f32[256,128]{1,0:T(8,128)S(1)}, u32[]{:S(2)}, u32[]{:S(2)}) collective-permute-start(f32[256,128]{1,0:T(8,128)S(1)} %collective-permute-done.34.refs_6_), channel_id=1, source_target_pairs={{0,8},{8,16},{16,24},{24,28},{28,20},{20,12},{12,4},{4,0},{1,9},{9... | collective-permute-start | bytes 393224 | tf_op jit(solution)/shard_map/ppermute | solution.py:507
  82.2 2.0 %collective-permute-start.28 = (f32[256,128]{1,0:T(8,128)S(1)}, f32[256,128]{1,0:T(8,128)S(1)}, u32[]{:S(2)}, u32[]{:S(2)}) collective-permute-start(f32[256,128]{1,0:T(8,128)S(1)} %collective-permute-done.27.refs_7_), channel_id=1, source_target_pairs={{0,8},{8,16},{16,24},{24,28},{28,20},{20,12},{12,4},{4,0},{1,9},{9... | collective-permute-start | bytes 393224 | tf_op jit(solution)/shard_map/ppermute | solution.py:507
  84.4 2.8 %collective-permute-done.31.refs_4_ = f32[256,128]{1,0:T(8,128)S(1)} collective-permute-done((f32[256,128]{1,0:T(8,128)S(1)}, f32[256,128]{1,0:T(8,128)S(1)}, u32[]{:S(2)}, u32[]{:S(2)}) %collective-permute-start.31) | collective-permute-done | bytes 131104 | tf_op jit(solution)/shard_map/ppermute | solution.py:510
  87.2 2.7 %second_solve.3 = (f32[1536,128]{1,0:T(8,128)S(1)}, bf16[1664,128]{1,0:T(8,128)(2,1)S(1)}, f32[1664,128]{1,0:T(8,128)S(1)}, f32[16,128]{1,0:T(8,128)S(1)}, f32[2...) custom-call(s32[32]{0:T(128)S(1)} %get-tuple-element.87.refs_0_, ...), custom_call_target="tpu_custom_call" | custom-call | flops 603979776 | bytes 8388608 | tf_op jit(solution)/shard_map/second_solve/pallas_call | solution.py:62
  92.0 2.7 %second_solve.2 = (f32[1536,128]{1,0:T(8,128)S(1)}, bf16[1664,128]{1,0:T(8,128)(2,1)S(1)}, f32[1664,128]{1,0:T(8,128)S(1)}, f32[16,128]{1,0:T(8,128)S(1)}, f32[2...) custom-call(s32[32]{0:T(128)S(1)} %get-tuple-element.87.refs_0_, ...), custom_call_target="tpu_custom_call" | custom-call | flops 603979776 | bytes 8388608 | tf_op jit(solution)/shard_map/second_solve/pallas_call | solution.py:62
  98.1 1.5 collective-permute-start.46
  103.7 1.8 %collective-permute-start.47 = (f32[256,128]{1,0:T(8,128)S(1)}, f32[256,128]{1,0:T(8,128)S(1)}, u32[]{:S(2)}, u32[]{:S(2)}) collective-permute-start(f32[256,128]{1,0:T(8,128)S(1)} %get-tuple-element.156), channel_id=1, source_target_pairs={{0,8},{8,16},{16,24},{24,28},{28,20},{20,12},{12,4},{4,0},{1,9},{9... | collective-permute-start | bytes 393224 | tf_op jit(solution)/shard_map/ppermute | solution.py:507
  105.5 1.6 %collective-permute-done.38.refs_0_ = f32[256,128]{1,0:T(8,128)S(1)} collective-permute-done((f32[256,128]{1,0:T(8,128)S(1)}, f32[256,128]{1,0:T(8,128)S(1)}, u32[]{:S(2)}, u32[]{:S(2)}) %collective-permute-start.38) | collective-permute-done | bytes 131104 | tf_op jit(solution)/shard_map/ppermute | solution.py:507
  111.6 1.5 %collective-permute-done.41.refs_0_ = f32[256,128]{1,0:T(8,128)S(1)} collective-permute-done((f32[256,128]{1,0:T(8,128)S(1)}, f32[256,128]{1,0:T(8,128)S(1)}, u32[]{:S(2)}, u32[]{:S(2)}) %collective-permute-start.41) | collective-permute-done | bytes 131104 | tf_op jit(solution)/shard_map/ppermute | solution.py:510
  114.3 1.6 %collective-permute-done.49.refs_2_ = f32[256,128]{1,0:T(8,128)S(1)} collective-permute-done((f32[256,128]{1,0:T(8,128)S(1)}, f32[256,128]{1,0:T(8,128)S(1)}, u32[]{:S(2)}, u32[]{:S(2)}) %collective-permute-start.49) | collective-permute-done | bytes 131104 | tf_op jit(solution)/shard_map/ppermute | solution.py:510
  115.9 1.8 %collective-permute-done.48.refs_1_ = f32[256,128]{1,0:T(8,128)S(1)} collective-permute-done((f32[256,128]{1,0:T(8,128)S(1)}, f32[256,128]{1,0:T(8,128)S(1)}, u32[]{:S(2)}, u32[]{:S(2)}) %collective-permute-start.48) | collective-permute-done | bytes 131104 | tf_op jit(solution)/shard_map/ppermute | solution.py:507
  119.7 1.6 %collective-permute-start.50 = (f32[264,128]{1,0:T(8,128)S(1)}, f32[264,128]{1,0:T(8,128)S(1)}, u32[]{:S(2)}, u32[]{:S(2)}) collective-permute-start(f32[264,128]{1,0:T(8,128)S(1)} %get-tuple-element.162.refs_1_.refs_0_), channel_id=1, source_target_pairs={{8,0},{16,8},{24,16},{28,24},{20,28},{12,20},{4,12},{0,4},{9,1},{1... | collective-permute-start | bytes 405512 | tf_op jit(solution)/shard_map/ppermute | solution.py:510
  121.9 2.8 %collective-permute-done.50.refs_2_.refs_1_ = f32[264,128]{1,0:T(8,128)S(1)} collective-permute-done((f32[264,128]{1,0:T(8,128)S(1)}, f32[264,128]{1,0:T(8,128)S(1)}, u32[]{:S(2)}, u32[]{:S(2)}) %collective-permute-start.50) | collective-permute-done | bytes 135200 | tf_op jit(solution)/shard_map/ppermute | solution.py:510
  124.7 1.6 %collective-permute-start.51 = (f32[264,128]{1,0:T(8,128)S(1)}, f32[264,128]{1,0:T(8,128)S(1)}, u32[]{:S(2)}, u32[]{:S(2)}) collective-permute-start(f32[264,128]{1,0:T(8,128)S(1)} %collective-permute-done.50.refs_2_.refs_1_), channel_id=1, source_target_pairs={{8,0},{16,8},{24,16},{28,24},{20,28},{12,20},{4,12},{0,4},{9,1},{1... | collective-permute-start | bytes 405512 | tf_op jit(solution)/shard_map/ppermute | solution.py:510
  126.8 1.5 %collective-permute-start.61 = (f32[256,128]{1,0:T(8,128)S(1)}, f32[256,128]{1,0:T(8,128)S(1)}, u32[]{:S(2)}, u32[]{:S(2)}) collective-permute-start(f32[256,128]{1,0:T(8,128)S(1)} %collective-permute-done.60.refs_8_), channel_id=1, source_target_pairs={{0,8},{8,16},{16,24},{24,28},{28,20},{20,12},{12,4},{4,0},{1,9},{9... | collective-permute-start | bytes 393224 | tf_op jit(solution)/shard_map/ppermute | solution.py:507
  129.7 1.6 %collective-permute-start.52 = (f32[264,128]{1,0:T(8,128)S(1)}, f32[264,128]{1,0:T(8,128)S(1)}, u32[]{:S(2)}, u32[]{:S(2)}) collective-permute-start(f32[264,128]{1,0:T(8,128)S(1)} %collective-permute-done.51.refs_3_.refs_2_), channel_id=1, source_target_pairs={{8,0},{16,8},{24,16},{28,24},{20,28},{12,20},{4,12},{0,4},{9,1},{1... | collective-permute-start | bytes 405512 | tf_op jit(solution)/shard_map/ppermute | solution.py:510
  131.3 1.4 collective-permute-start.58
  134.8 1.6 %collective-permute-start.53 = (f32[264,128]{1,0:T(8,128)S(1)}, f32[264,128]{1,0:T(8,128)S(1)}, u32[]{:S(2)}, u32[]{:S(2)}) collective-permute-start(f32[264,128]{1,0:T(8,128)S(1)} %collective-permute-done.52.refs_4_.refs_3_), channel_id=1, source_target_pairs={{8,0},{16,8},{24,16},{28,24},{20,28},{12,20},{4,12},{0,4},{9,1},{1... | collective-permute-start | bytes 405512 | tf_op jit(solution)/shard_map/ppermute | solution.py:510
  136.3 1.4 collective-permute-start.59
  141.3 1.4 collective-permute-done.63.refs_5_
  142.7 1.6 %finish.2 = (f32[1536,256]{1,0:T(8,128)}, f32[256,256]{1,0:T(8,128)}) custom-call(s32[32]{0:T(128)S(1)} %get-tuple-element.87.refs_0_, f32[256,128]{1,0:T(8,128)S(1)} %get-tuple-element.164.refs_1_, f32[256,128]{1,0:T(8,128)S(1)} %collective-permute-done.57.refs_2_, f32[256,128]{1,0:T(8,128)S(1)} %collective-permute-done.58.refs_3_, ...), custom_call_target="tpu_custom_call" | custom-call | bytes 3145728 | tf_op jit(solution)/shard_map/finish/pallas_call | solution.py:62
  144.5 1.7 %collective-permute-start.65 = (f32[8,128]{1,0:T(8,128)S(1)}, f32[8,128]{1,0:T(8,128)S(1)}, u32[]{:S(2)}, u32[]{:S(2)}) collective-permute-start(f32[8,128]{1,0:T(8,128)S(1)} %sum_tails.1.refs_0_), channel_id=1, source_target_pairs={{0,2},{1,3},{2,0},{3,1},{4,6},{5,7},{6,4},{7,5},{8,10},{9,11},{10,... | collective-permute-start | bytes 12296 | tf_op jit(solution)/shard_map/ppermute | solution.py:609
  147.6 1.6 %finish.3 = (f32[1536,256]{1,0:T(8,128)}, f32[256,256]{1,0:T(8,128)}) custom-call(s32[32]{0:T(128)S(1)} %get-tuple-element.87.refs_0_, f32[264,128]{1,0:T(8,128)S(1)} %get-tuple-element.162.refs_1_.refs_0_, f32[264,128]{1,0:T(8,128)S(1)} %collective-permute-done.50.refs_2_.refs_1_, ...), custom_call_target="tpu_custom_call", output_to_operand_aliasing={{0}: (10, {}), {1}: (11, {})} | custom-call | bytes 3145728 | tf_op jit(solution)/shard_map/finish/pallas_call | solution.py:62
  (123 shorter events, 52.5 us)
Async XLA Ops:
  0.6 9.5 %collective-permute-start = (f32[256,256]{1,0:T(8,128)}, f32[256,256]{1,0:T(8,128)S(1)}, u32[]{:S(2)}, u32[]{:S(2)}) collective-permute-start(f32[256,256]{1,0:T(8,128)} %refs_0_.1), channel_id=1, source_target_pairs={{0,8},{8,16},{16,24},{24,28},{28,20},{20,12},{12,4},{4,0},{1,9},{9... | collective-permute-start | bytes 786440 | tf_op jit(solution)/shard_map/ppermute | solution.py:507
  3.7 8.0 %collective-permute-start.1 = (f32[256,256]{1,0:T(8,128)}, f32[256,256]{1,0:T(8,128)S(1)}, u32[]{:S(2)}, u32[]{:S(2)}) collective-permute-start(f32[256,256]{1,0:T(8,128)} %refs_0_.1), channel_id=1, source_target_pairs={{8,0},{16,8},{24,16},{28,24},{20,28},{12,20},{4,12},{0,4},{9,1},{1... | collective-permute-start | bytes 786440 | tf_op jit(solution)/shard_map/ppermute | solution.py:510
  11.7 6.9 %collective-permute-start.2 = (f32[256,256]{1,0:T(8,128)S(1)}, f32[256,256]{1,0:T(8,128)S(1)}, u32[]{:S(2)}, u32[]{:S(2)}) collective-permute-start(f32[256,256]{1,0:T(8,128)S(1)} %get-tuple-element.92.refs_8_), channel_id=1, source_target_pairs={{0,8},{8,16},{16,24},{24,28},{28,20},{20,12},{12,4},{4,0},{1,9},{9... | collective-permute-start | bytes 786440 | tf_op jit(solution)/shard_map/ppermute | solution.py:507
  13.3 6.6 %collective-permute-start.3 = (f32[256,256]{1,0:T(8,128)S(1)}, f32[256,256]{1,0:T(8,128)S(1)}, u32[]{:S(2)}, u32[]{:S(2)}) collective-permute-start(f32[256,256]{1,0:T(8,128)S(1)} %get-tuple-element.91.refs_2_), channel_id=1, source_target_pairs={{8,0},{16,8},{24,16},{28,24},{20,28},{12,20},{4,12},{0,4},{9,1},{1... | collective-permute-start | bytes 786440 | tf_op jit(solution)/shard_map/ppermute | solution.py:510
  19.8 6.4 %collective-permute-start.5 = (f32[256,256]{1,0:T(8,128)S(1)}, f32[256,256]{1,0:T(8,128)S(1)}, u32[]{:S(2)}, u32[]{:S(2)}) collective-permute-start(f32[256,256]{1,0:T(8,128)S(1)} %get-tuple-element.94.refs_7_), channel_id=1, source_target_pairs={{0,8},{8,16},{16,24},{24,28},{28,20},{20,12},{12,4},{4,0},{1,9},{9... | collective-permute-start | bytes 786440 | tf_op jit(solution)/shard_map/ppermute | solution.py:507
  21.4 6.4 %collective-permute-start.4 = (f32[256,256]{1,0:T(8,128)S(1)}, f32[256,256]{1,0:T(8,128)S(1)}, u32[]{:S(2)}, u32[]{:S(2)}) collective-permute-start(f32[256,256]{1,0:T(8,128)S(1)} %get-tuple-element.93.refs_3_), channel_id=1, source_target_pairs={{8,0},{16,8},{24,16},{28,24},{20,28},{12,20},{4,12},{0,4},{9,1},{1... | collective-permute-start | bytes 786440 | tf_op jit(solution)/shard_map/ppermute | solution.py:510
  30.1 7.7 %collective-permute-start.6 = (f32[256,128]{1,0:T(8,128)S(1)}, f32[256,128]{1,0:T(8,128)S(1)}, u32[]{:S(2)}, u32[]{:S(2)}) collective-permute-start(f32[256,128]{1,0:T(8,128)S(1)} %get-tuple-element.97), channel_id=1, source_target_pairs={{8,0},{16,8},{24,16},{28,24},{20,28},{12,20},{4,12},{0,4},{9,1},{1... | collective-permute-start | bytes 393224 | tf_op jit(solution)/shard_map/ppermute | solution.py:510
  35.2 6.9 %collective-permute-start.15 = (f32[264,128]{1,0:T(8,128)S(1)}, f32[264,128]{1,0:T(8,128)S(1)}, u32[]{:S(2)}, u32[]{:S(2)}) collective-permute-start(f32[264,128]{1,0:T(8,128)S(1)} %get-tuple-element.113), channel_id=1, source_target_pairs={{0,8},{8,16},{16,24},{24,28},{28,20},{20,12},{12,4},{4,0},{1,9},{9... | collective-permute-start | bytes 405512 | tf_op jit(solution)/shard_map/ppermute | solution.py:507
  40.1 6.2 %collective-permute-start.7 = (f32[256,128]{1,0:T(8,128)S(1)}, f32[256,128]{1,0:T(8,128)S(1)}, u32[]{:S(2)}, u32[]{:S(2)}) collective-permute-start(f32[256,128]{1,0:T(8,128)S(1)} %get-tuple-element.100), channel_id=1, source_target_pairs={{0,8},{8,16},{16,24},{24,28},{28,20},{20,12},{12,4},{4,0},{1,9},{9... | collective-permute-start | bytes 393224 | tf_op jit(solution)/shard_map/ppermute | solution.py:507
  43.1 6.2 %collective-permute-start.17 = (f32[264,128]{1,0:T(8,128)S(1)}, f32[264,128]{1,0:T(8,128)S(1)}, u32[]{:S(2)}, u32[]{:S(2)}) collective-permute-start(f32[264,128]{1,0:T(8,128)S(1)} %get-tuple-element.117), channel_id=1, source_target_pairs={{0,8},{8,16},{16,24},{24,28},{28,20},{20,12},{12,4},{4,0},{1,9},{9... | collective-permute-start | bytes 405512 | tf_op jit(solution)/shard_map/ppermute | solution.py:507
  44.3 6.4 %collective-permute-start.18 = (f32[264,128]{1,0:T(8,128)S(1)}, f32[264,128]{1,0:T(8,128)S(1)}, u32[]{:S(2)}, u32[]{:S(2)}) collective-permute-start(f32[264,128]{1,0:T(8,128)S(1)} %get-tuple-element.119), channel_id=1, source_target_pairs={{8,0},{16,8},{24,16},{28,24},{20,28},{12,20},{4,12},{0,4},{9,1},{1... | collective-permute-start | bytes 405512 | tf_op jit(solution)/shard_map/ppermute | solution.py:510
  47.2 6.5 %collective-permute-start.10 = (f32[256,128]{1,0:T(8,128)S(1)}, f32[256,128]{1,0:T(8,128)S(1)}, u32[]{:S(2)}, u32[]{:S(2)}) collective-permute-start(f32[256,128]{1,0:T(8,128)S(1)} %get-tuple-element.106), channel_id=1, source_target_pairs={{8,0},{16,8},{24,16},{28,24},{20,28},{12,20},{4,12},{0,4},{9,1},{1... | collective-permute-start | bytes 393224 | tf_op jit(solution)/shard_map/ppermute | solution.py:510
  47.3 6.4 %collective-permute-start.9 = (f32[256,128]{1,0:T(8,128)S(1)}, f32[256,128]{1,0:T(8,128)S(1)}, u32[]{:S(2)}, u32[]{:S(2)}) collective-permute-start(f32[256,128]{1,0:T(8,128)S(1)} %get-tuple-element.104), channel_id=1, source_target_pairs={{0,8},{8,16},{16,24},{24,28},{28,20},{20,12},{12,4},{4,0},{1,9},{9... | collective-permute-start | bytes 393224 | tf_op jit(solution)/shard_map/ppermute | solution.py:507
  50.8 6.2 %collective-permute-start.19 = (f32[264,128]{1,0:T(8,128)S(1)}, f32[264,128]{1,0:T(8,128)S(1)}, u32[]{:S(2)}, u32[]{:S(2)}) collective-permute-start(f32[264,128]{1,0:T(8,128)S(1)} %get-tuple-element.121), channel_id=1, source_target_pairs={{0,8},{8,16},{16,24},{24,28},{28,20},{20,12},{12,4},{4,0},{1,9},{9... | collective-permute-start | bytes 405512 | tf_op jit(solution)/shard_map/ppermute | solution.py:507
  53.8 6.4 %collective-permute-start.12 = (f32[256,128]{1,0:T(8,128)S(1)}, f32[256,128]{1,0:T(8,128)S(1)}, u32[]{:S(2)}, u32[]{:S(2)}) collective-permute-start(f32[256,128]{1,0:T(8,128)S(1)} %get-tuple-element.109), channel_id=1, source_target_pairs={{8,0},{16,8},{24,16},{28,24},{20,28},{12,20},{4,12},{0,4},{9,1},{1... | collective-permute-start | bytes 393224 | tf_op jit(solution)/shard_map/ppermute | solution.py:510
  54.3 8.8 %collective-permute-start.21 = (f32[264,128]{1,0:T(8,128)S(1)}, f32[264,128]{1,0:T(8,128)S(1)}, u32[]{:S(2)}, u32[]{:S(2)}) collective-permute-start(f32[264,128]{1,0:T(8,128)S(1)} %get-tuple-element.123), channel_id=1, source_target_pairs={{8,0},{16,8},{24,16},{28,24},{20,28},{12,20},{4,12},{0,4},{9,1},{1... | collective-permute-start | bytes 405512 | tf_op jit(solution)/shard_map/ppermute | solution.py:510
  57.0 6.5 %collective-permute-start.20 = (f32[264,128]{1,0:T(8,128)S(1)}, f32[264,128]{1,0:T(8,128)S(1)}, u32[]{:S(2)}, u32[]{:S(2)}) collective-permute-start(f32[264,128]{1,0:T(8,128)S(1)} %add_pairs.17), channel_id=1, source_target_pairs={{0,8},{8,16},{16,24},{24,28},{28,20},{20,12},{12,4},{4,0},{1,9},{9... | collective-permute-start | bytes 405512 | tf_op jit(solution)/shard_map/ppermute | solution.py:507
  58.6 6.8 %collective-permute-start.11 = (f32[256,128]{1,0:T(8,128)S(1)}, f32[256,128]{1,0:T(8,128)S(1)}, u32[]{:S(2)}, u32[]{:S(2)}) collective-permute-start(f32[256,128]{1,0:T(8,128)S(1)} %get-tuple-element.108), channel_id=1, source_target_pairs={{0,8},{8,16},{16,24},{24,28},{28,20},{20,12},{12,4},{4,0},{1,9},{9... | collective-permute-start | bytes 393224 | tf_op jit(solution)/shard_map/ppermute | solution.py:507
  60.2 5.8 %collective-permute-start.13 = (f32[256,128]{1,0:T(8,128)S(1)}, f32[256,128]{1,0:T(8,128)S(1)}, u32[]{:S(2)}, u32[]{:S(2)}) collective-permute-start(f32[256,128]{1,0:T(8,128)S(1)} %add_pairs.14), channel_id=1, source_target_pairs={{8,0},{16,8},{24,16},{28,24},{20,28},{12,20},{4,12},{0,4},{9,1},{1... | collective-permute-start | bytes 393224 | tf_op jit(solution)/shard_map/ppermute | solution.py:510
  63.6 6.4 %collective-permute-start.32 = (f32[256,128]{1,0:T(8,128)S(1)}, f32[256,128]{1,0:T(8,128)S(1)}, u32[]{:S(2)}, u32[]{:S(2)}) collective-permute-start(f32[256,128]{1,0:T(8,128)S(1)} %get-tuple-element.129.refs_1_.refs_3_), channel_id=1, source_target_pairs={{0,8},{8,16},{16,24},{24,28},{28,20},{20,12},{12,4},{4,0},{1,9},{9... | collective-permute-start | bytes 393224 | tf_op jit(solution)/shard_map/ppermute | solution.py:507
  66.0 6.6 %collective-permute-start.22 = (f32[256,128]{1,0:T(8,128)S(1)}, f32[256,128]{1,0:T(8,128)S(1)}, u32[]{:S(2)}, u32[]{:S(2)}) collective-permute-start(f32[256,128]{1,0:T(8,128)S(1)} %get-tuple-element.125.refs_1_.refs_3_), channel_id=1, source_target_pairs={{8,0},{16,8},{24,16},{28,24},{20,28},{12,20},{4,12},{0,4},{9,1},{1... | collective-permute-start | bytes 393224 | tf_op jit(solution)/shard_map/ppermute | solution.py:510
  67.2 6.9 %collective-permute-start.29 = (f32[256,128]{1,0:T(8,128)S(1)}, f32[256,128]{1,0:T(8,128)S(1)}, u32[]{:S(2)}, u32[]{:S(2)}) collective-permute-start(f32[256,128]{1,0:T(8,128)S(1)} %get-tuple-element.129.refs_1_.refs_3_), channel_id=1, source_target_pairs={{8,0},{16,8},{24,16},{28,24},{20,28},{12,20},{4,12},{0,4},{9,1},{1... | collective-permute-start | bytes 393224 | tf_op jit(solution)/shard_map/ppermute | solution.py:510
  70.0 5.4 %collective-permute-start.33 = (f32[256,128]{1,0:T(8,128)S(1)}, f32[256,128]{1,0:T(8,128)S(1)}, u32[]{:S(2)}, u32[]{:S(2)}) collective-permute-start(f32[256,128]{1,0:T(8,128)S(1)} %collective-permute-done.32.refs_8_), channel_id=1, source_target_pairs={{0,8},{8,16},{16,24},{24,28},{28,20},{20,12},{12,4},{4,0},{1,9},{9... | collective-permute-start | bytes 393224 | tf_op jit(solution)/shard_map/ppermute | solution.py:507
  71.5 5.4 %collective-permute-start.26 = (f32[256,128]{1,0:T(8,128)S(1)}, f32[256,128]{1,0:T(8,128)S(1)}, u32[]{:S(2)}, u32[]{:S(2)}) collective-permute-start(f32[256,128]{1,0:T(8,128)S(1)} %get-tuple-element.125.refs_1_.refs_3_), channel_id=1, source_target_pairs={{0,8},{8,16},{16,24},{24,28},{28,20},{20,12},{12,4},{4,0},{1,9},{9... | collective-permute-start | bytes 393224 | tf_op jit(solution)/shard_map/ppermute | solution.py:507
  72.6 5.7 %collective-permute-start.23 = (f32[256,128]{1,0:T(8,128)S(1)}, f32[256,128]{1,0:T(8,128)S(1)}, u32[]{:S(2)}, u32[]{:S(2)}) collective-permute-start(f32[256,128]{1,0:T(8,128)S(1)} %collective-permute-done.22.refs_2_), channel_id=1, source_target_pairs={{8,0},{16,8},{24,16},{28,24},{20,28},{12,20},{4,12},{0,4},{9,1},{1... | collective-permute-start | bytes 393224 | tf_op jit(solution)/shard_map/ppermute | solution.py:510
  74.1 6.0 %collective-permute-start.30 = (f32[256,128]{1,0:T(8,128)S(1)}, f32[256,128]{1,0:T(8,128)S(1)}, u32[]{:S(2)}, u32[]{:S(2)}) collective-permute-start(f32[256,128]{1,0:T(8,128)S(1)} %collective-permute-done.29.refs_2_), channel_id=1, source_target_pairs={{8,0},{16,8},{24,16},{28,24},{20,28},{12,20},{4,12},{0,4},{9,1},{1... | collective-permute-start | bytes 393224 | tf_op jit(solution)/shard_map/ppermute | solution.py:510
  76.9 5.3 %collective-permute-start.27 = (f32[256,128]{1,0:T(8,128)S(1)}, f32[256,128]{1,0:T(8,128)S(1)}, u32[]{:S(2)}, u32[]{:S(2)}) collective-permute-start(f32[256,128]{1,0:T(8,128)S(1)} %collective-permute-done.26.refs_8_), channel_id=1, source_target_pairs={{0,8},{8,16},{16,24},{24,28},{28,20},{20,12},{12,4},{4,0},{1,9},{9... | collective-permute-start | bytes 393224 | tf_op jit(solution)/shard_map/ppermute | solution.py:507
  78.3 6.1 %collective-permute-start.24 = (f32[256,128]{1,0:T(8,128)S(1)}, f32[256,128]{1,0:T(8,128)S(1)}, u32[]{:S(2)}, u32[]{:S(2)}) collective-permute-start(f32[256,128]{1,0:T(8,128)S(1)} %collective-permute-done.23.refs_3_), channel_id=1, source_target_pairs={{8,0},{16,8},{24,16},{28,24},{20,28},{12,20},{4,12},{0,4},{9,1},{1... | collective-permute-start | bytes 393224 | tf_op jit(solution)/shard_map/ppermute | solution.py:510
  80.1 7.1 %collective-permute-start.31 = (f32[256,128]{1,0:T(8,128)S(1)}, f32[256,128]{1,0:T(8,128)S(1)}, u32[]{:S(2)}, u32[]{:S(2)}) collective-permute-start(f32[256,128]{1,0:T(8,128)S(1)} %collective-permute-done.30.refs_3_), channel_id=1, source_target_pairs={{8,0},{16,8},{24,16},{28,24},{20,28},{12,20},{4,12},{0,4},{9,1},{1... | collective-permute-start | bytes 393224 | tf_op jit(solution)/shard_map/ppermute | solution.py:510
  80.6 6.6 %collective-permute-start.35 = (f32[256,128]{1,0:T(8,128)S(1)}, f32[256,128]{1,0:T(8,128)S(1)}, u32[]{:S(2)}, u32[]{:S(2)}) collective-permute-start(f32[256,128]{1,0:T(8,128)S(1)} %collective-permute-done.34.refs_6_), channel_id=1, source_target_pairs={{0,8},{8,16},{16,24},{24,28},{28,20},{20,12},{12,4},{4,0},{1,9},{9... | collective-permute-start | bytes 393224 | tf_op jit(solution)/shard_map/ppermute | solution.py:507
  82.2 9.8 %collective-permute-start.28 = (f32[256,128]{1,0:T(8,128)S(1)}, f32[256,128]{1,0:T(8,128)S(1)}, u32[]{:S(2)}, u32[]{:S(2)}) collective-permute-start(f32[256,128]{1,0:T(8,128)S(1)} %collective-permute-done.27.refs_7_), channel_id=1, source_target_pairs={{0,8},{8,16},{16,24},{24,28},{28,20},{20,12},{12,4},{4,0},{1,9},{9... | collective-permute-start | bytes 393224 | tf_op jit(solution)/shard_map/ppermute | solution.py:507
  84.4 7.6 %collective-permute-start.25 = (f32[256,128]{1,0:T(8,128)S(1)}, f32[256,128]{1,0:T(8,128)S(1)}, u32[]{:S(2)}, u32[]{:S(2)}) collective-permute-start(f32[256,128]{1,0:T(8,128)S(1)} %collective-permute-done.24.refs_4_), channel_id=1, source_target_pairs={{8,0},{16,8},{24,16},{28,24},{20,28},{12,20},{4,12},{0,4},{9,1},{1... | collective-permute-start | bytes 393224 | tf_op jit(solution)/shard_map/ppermute | solution.py:510
  89.9 6.9 %collective-permute-start.43 = (f32[256,128]{1,0:T(8,128)S(1)}, f32[256,128]{1,0:T(8,128)S(1)}, u32[]{:S(2)}, u32[]{:S(2)}) collective-permute-start(f32[256,128]{1,0:T(8,128)S(1)} %get-tuple-element.148), channel_id=1, source_target_pairs={{0,8},{8,16},{16,24},{24,28},{28,20},{20,12},{12,4},{4,0},{1,9},{9... | collective-permute-start | bytes 393224 | tf_op jit(solution)/shard_map/ppermute | solution.py:507
  91.1 6.4 %collective-permute-start.44 = (f32[256,128]{1,0:T(8,128)S(1)}, f32[256,128]{1,0:T(8,128)S(1)}, u32[]{:S(2)}, u32[]{:S(2)}) collective-permute-start(f32[256,128]{1,0:T(8,128)S(1)} %get-tuple-element.150), channel_id=1, source_target_pairs={{8,0},{16,8},{24,16},{28,24},{20,28},{12,20},{4,12},{0,4},{9,1},{1... | collective-permute-start | bytes 393224 | tf_op jit(solution)/shard_map/ppermute | solution.py:510
  97.5 5.4 %collective-permute-start.45 = (f32[256,128]{1,0:T(8,128)S(1)}, f32[256,128]{1,0:T(8,128)S(1)}, u32[]{:S(2)}, u32[]{:S(2)}) collective-permute-start(f32[256,128]{1,0:T(8,128)S(1)} %get-tuple-element.152), channel_id=1, source_target_pairs={{0,8},{8,16},{16,24},{24,28},{28,20},{20,12},{12,4},{4,0},{1,9},{9... | collective-permute-start | bytes 393224 | tf_op jit(solution)/shard_map/ppermute | solution.py:507
  98.1 5.6 %collective-permute-start.46 = (f32[256,128]{1,0:T(8,128)S(1)}, f32[256,128]{1,0:T(8,128)S(1)}, u32[]{:S(2)}, u32[]{:S(2)}) collective-permute-start(f32[256,128]{1,0:T(8,128)S(1)} %get-tuple-element.154), channel_id=1, source_target_pairs={{8,0},{16,8},{24,16},{28,24},{20,28},{12,20},{4,12},{0,4},{9,1},{1... | collective-permute-start | bytes 393224 | tf_op jit(solution)/shard_map/ppermute | solution.py:510
  100.8 6.3 %collective-permute-start.38 = (f32[256,128]{1,0:T(8,128)S(1)}, f32[256,128]{1,0:T(8,128)S(1)}, u32[]{:S(2)}, u32[]{:S(2)}) collective-permute-start(f32[256,128]{1,0:T(8,128)S(1)} %get-tuple-element.138), channel_id=1, source_target_pairs={{0,8},{8,16},{16,24},{24,28},{28,20},{20,12},{12,4},{4,0},{1,9},{9... | collective-permute-start | bytes 393224 | tf_op jit(solution)/shard_map/ppermute | solution.py:507
  103.7 6.5 %collective-permute-start.47 = (f32[256,128]{1,0:T(8,128)S(1)}, f32[256,128]{1,0:T(8,128)S(1)}, u32[]{:S(2)}, u32[]{:S(2)}) collective-permute-start(f32[256,128]{1,0:T(8,128)S(1)} %get-tuple-element.156), channel_id=1, source_target_pairs={{0,8},{8,16},{16,24},{24,28},{28,20},{20,12},{12,4},{4,0},{1,9},{9... | collective-permute-start | bytes 393224 | tf_op jit(solution)/shard_map/ppermute | solution.py:507
  107.2 5.9 %collective-permute-start.41 = (f32[256,128]{1,0:T(8,128)S(1)}, f32[256,128]{1,0:T(8,128)S(1)}, u32[]{:S(2)}, u32[]{:S(2)}) collective-permute-start(f32[256,128]{1,0:T(8,128)S(1)} %get-tuple-element.143), channel_id=1, source_target_pairs={{8,0},{16,8},{24,16},{28,24},{20,28},{12,20},{4,12},{0,4},{9,1},{1... | collective-permute-start | bytes 393224 | tf_op jit(solution)/shard_map/ppermute | solution.py:510
  108.2 7.7 %collective-permute-start.49 = (f32[256,128]{1,0:T(8,128)S(1)}, f32[256,128]{1,0:T(8,128)S(1)}, u32[]{:S(2)}, u32[]{:S(2)}) collective-permute-start(f32[256,128]{1,0:T(8,128)S(1)} %get-tuple-element.158), channel_id=1, source_target_pairs={{8,0},{16,8},{24,16},{28,24},{20,28},{12,20},{4,12},{0,4},{9,1},{1... | collective-permute-start | bytes 393224 | tf_op jit(solution)/shard_map/ppermute | solution.py:510
  109.1 8.6 %collective-permute-start.40 = (f32[256,128]{1,0:T(8,128)S(1)}, f32[256,128]{1,0:T(8,128)S(1)}, u32[]{:S(2)}, u32[]{:S(2)}) collective-permute-start(f32[256,128]{1,0:T(8,128)S(1)} %get-tuple-element.142), channel_id=1, source_target_pairs={{0,8},{8,16},{16,24},{24,28},{28,20},{20,12},{12,4},{4,0},{1,9},{9... | collective-permute-start | bytes 393224 | tf_op jit(solution)/shard_map/ppermute | solution.py:507
  110.3 7.4 %collective-permute-start.48 = (f32[256,128]{1,0:T(8,128)S(1)}, f32[256,128]{1,0:T(8,128)S(1)}, u32[]{:S(2)}, u32[]{:S(2)}) collective-permute-start(f32[256,128]{1,0:T(8,128)S(1)} %add_pairs.23), channel_id=1, source_target_pairs={{0,8},{8,16},{16,24},{24,28},{28,20},{20,12},{12,4},{4,0},{1,9},{9... | collective-permute-start | bytes 393224 | tf_op jit(solution)/shard_map/ppermute | solution.py:507
  113.1 5.9 %collective-permute-start.42 = (f32[256,128]{1,0:T(8,128)S(1)}, f32[256,128]{1,0:T(8,128)S(1)}, u32[]{:S(2)}, u32[]{:S(2)}) collective-permute-start(f32[256,128]{1,0:T(8,128)S(1)} %add_pairs.20), channel_id=1, source_target_pairs={{8,0},{16,8},{24,16},{28,24},{20,28},{12,20},{4,12},{0,4},{9,1},{1... | collective-permute-start | bytes 393224 | tf_op jit(solution)/shard_map/ppermute | solution.py:510
  121.3 5.5 %collective-permute-start.60 = (f32[256,128]{1,0:T(8,128)S(1)}, f32[256,128]{1,0:T(8,128)S(1)}, u32[]{:S(2)}, u32[]{:S(2)}) collective-permute-start(f32[256,128]{1,0:T(8,128)S(1)} %get-tuple-element.164.refs_1_), channel_id=1, source_target_pairs={{0,8},{8,16},{16,24},{24,28},{28,20},{20,12},{12,4},{4,0},{1,9},{9... | collective-permute-start | bytes 393224 | tf_op jit(solution)/shard_map/ppermute | solution.py:507
  121.7 6.6 %collective-permute-start.54 = (f32[264,128]{1,0:T(8,128)S(1)}, f32[264,128]{1,0:T(8,128)S(1)}, u32[]{:S(2)}, u32[]{:S(2)}) collective-permute-start(f32[264,128]{1,0:T(8,128)S(1)} %get-tuple-element.162.refs_1_.refs_0_), channel_id=1, source_target_pairs={{0,8},{8,16},{16,24},{24,28},{28,20},{20,12},{12,4},{4,0},{1,9},{9... | collective-permute-start | bytes 405512 | tf_op jit(solution)/shard_map/ppermute | solution.py:507
  126.8 5.9 %collective-permute-start.61 = (f32[256,128]{1,0:T(8,128)S(1)}, f32[256,128]{1,0:T(8,128)S(1)}, u32[]{:S(2)}, u32[]{:S(2)}) collective-permute-start(f32[256,128]{1,0:T(8,128)S(1)} %collective-permute-done.60.refs_8_), channel_id=1, source_target_pairs={{0,8},{8,16},{16,24},{24,28},{28,20},{20,12},{12,4},{4,0},{1,9},{9... | collective-permute-start | bytes 393224 | tf_op jit(solution)/shard_map/ppermute | solution.py:507
  133.4 11.0 %collective-permute-start.56 = (f32[264,128]{1,0:T(8,128)S(1)}, f32[264,128]{1,0:T(8,128)S(1)}, u32[]{:S(2)}, u32[]{:S(2)}) collective-permute-start(f32[264,128]{1,0:T(8,128)S(1)} %collective-permute-done.55.refs_7_.refs_6_), channel_id=1, source_target_pairs={{0,8},{8,16},{16,24},{24,28},{28,20},{20,12},{12,4},{4,0},{1,9},{9... | collective-permute-start | bytes 405512 | tf_op jit(solution)/shard_map/ppermute | solution.py:507
  134.8 9.6 %collective-permute-start.53 = (f32[264,128]{1,0:T(8,128)S(1)}, f32[264,128]{1,0:T(8,128)S(1)}, u32[]{:S(2)}, u32[]{:S(2)}) collective-permute-start(f32[264,128]{1,0:T(8,128)S(1)} %collective-permute-done.52.refs_4_.refs_3_), channel_id=1, source_target_pairs={{8,0},{16,8},{24,16},{28,24},{20,28},{12,20},{4,12},{0,4},{9,1},{1... | collective-permute-start | bytes 405512 | tf_op jit(solution)/shard_map/ppermute | solution.py:510
  (19 other events, 93.3 us)

commit v3 on v2

--- a/solution.py
+++ b/solution.py
@@ -13,7 +13,8 @@
 HALVES = 2
 TILE = 8
 LEAD = 1
-BASE_AT = {2: 1, 3: 3}
+LOAD_TURN = 2
+BASE_AT = {4: 2, 6: 4}
 CUTS = 8
 
 
@@ -105,14 +106,32 @@
         self.flying.pop(name).wait()
 
 
-def prepare(region, target, cons, kkt, cost, dual, peers):
+def split(cons):
+    rows, scen = cons.shape
+    width = scen // HALVES
+
+    def body(cons_ref, *refs):
+        copies = [
+            pltpu.make_async_copy(cons_ref.at[:, h * width : (h + 1) * width], refs[h], refs[-1].at[h])
+            for h in range(HALVES)
+        ]
+        for copy in copies:
+            copy.start()
+        for copy in copies:
+            copy.wait()
+
+    return call(
+        body, "split", (cons,), [HBM], [f32(rows, width)] * HALVES, [VMEM] * HALVES, [pltpu.SemaphoreType.DMA((HALVES,))]
+    )
+
+
+def prepare(region, target, owned, kkt, cost, dual, peers):
     blocks = target.shape[1]
-    owned = cons.shape[0] // BLOCK
-    arrays = (cons, kkt, cost, dual)
-    cuts = (1, CUTS, 1, 1)
+    arrays = (kkt, cost, dual)
+    cuts = (CUTS, 1, 1)
 
     def body(region_ref, target_hbm, *refs):
-        from_refs, table_ref, to_refs, target_ref, sem = refs[:4], refs[4], refs[5:9], refs[9], refs[10]
+        from_refs, table_ref, to_refs, target_ref, sem = refs[:3], refs[3], refs[4:7], refs[7], refs[8]
         loads = Loads(sem)
         loads.start("target", target_hbm, target_ref)
         for i, (src, dst) in enumerate(zip(from_refs, to_refs)):
@@ -137,7 +156,7 @@
                 table_ref[at] = j
                 table_ref[CAP * peers + at] = t - owner * owned
 
-        for i in range(4):
+        for i in range(3):
             for c in range(cuts[i]):
                 loads.wait((i, c))
 
@@ -145,9 +164,9 @@
         body,
         "prepare",
         (region, target, *arrays),
-        [SMEM] + [HBM] * 5,
+        [SMEM] + [HBM] * 4,
         [jax.ShapeDtypeStruct((2 * CAP * peers,), jnp.int32)] + [jax.ShapeDtypeStruct(x.shape, x.dtype) for x in arrays],
-        [SMEM] + [VMEM] * 4,
+        [SMEM] + [VMEM] * 3,
         [pltpu.SMEM(target.shape, jnp.int32), pltpu.SemaphoreType.DMA((1 + sum(cuts),))],
         moved=12 << 20,
     )
@@ -513,17 +532,6 @@
         long, short = peers // 2, (peers - 1) // 2
         return (long, short) if h % 2 == 0 else (short, long)
 
-    def gather_all(piece, own, beside):
-        across = peers // 2
-        pieces = [own] * peers
-        f = b = piece
-        for k in range(1, across):
-            if k > 1:
-                f, b = pieces[peers - k + 1], pieces[k - 1] = beside(k, [f, b])
-            f, b = pieces[peers - k], pieces[k] = forward(f), backward(b)
-        f, b = halve(beside(across, [f, b]))
-        return [[*pieces[:across], half, *pieces[across + 1 :]] for half in (forward(f), backward(b))]
-
     def gather(h, piece, beside=lambda k, x: x):
         far, near = reach(h)
         pieces = [piece] * peers
@@ -551,7 +559,7 @@
             if k < near:
                 pairs.append((b, parts[peers - near + k]))
             if pairs:
-                added = add_pairs(pairs)
+                added = [add_pairs([pair])[0] for pair in pairs]
                 if k < far:
                     f = added.pop(0)
                 if k < near:
@@ -559,27 +567,28 @@
         return [parts[0], f, b]
 
     region = lax.axis_index("region").astype(jnp.int32).reshape(1)
-    table, (own, kkt, cost, dual) = prepare(region, target, cons, kkt, cost, dual, peers)
+    halves = split(cons)
+    table, (kkt, cost, dual) = prepare(region, target, owned, kkt, cost, dual, peers)
     step = math.gcd(dual.shape[0], kkt.shape[0])
     chunks = kkt.shape[0] // step
     bases = []
 
-    def beside(k, values):
-        some = [own] if k == 2 else []
-        while len(bases) < min(chunks, BASE_AT.get(k, chunks if k > 3 else 0)):
+    def beside(h, k, values):
+        turn = HALVES * (k - 1) + h
+        some = [dual] if turn == LOAD_TURN else []
+        while len(bases) < min(chunks, BASE_AT.get(turn, 0)):
             bases.append(base_rows(len(bases), step, kkt, cost))
             some.append(bases[-1])
         return tie(values, [], some) if some else values
 
-    first = gather_all(cons, own, beside)
     known = {"state": None, "outputs": (), "count": None, "norms": []}
 
     def half(h):
         last = h == HALVES - 1
-        pieces = first[h]
+        pieces = yield from gather(h, halves[h], lambda k, values: beside(h, k, values))
         z, parts = first_solve(h, table, pieces, dual, bases, kkt, owned, h == 0)
         arrived = yield from scatter(h, parts)
-        out = renew(h, arrived, own, known["count"], ())
+        out = renew(h, arrived, halves[h], known["count"], ())
         averages, moved = out[0], out[1]
         if known["count"] is None:
             known["count"] = out[2]

time: 150 us -> 146 us (0.973)
  waiting for transfers between devices: 51.8 us -> 37.2 us
  starting transfers between devices: 71.6 us -> 80.6 us
    ppermute x32 -> x35, starting transfers between devices: 25.1 us -> 35.3 us  [backward(): return lax.ppermute(x, 'region', behind)]
    ppermute x32 -> x35, waiting for transfers between devices: 29.7 us -> 21.6 us  [backward(): return lax.ppermute(x, 'region', behind)]
    ppermute x32 -> x35, waiting for transfers between devices: 22.1 us -> 15.7 us  [forward(): return lax.ppermute(x, 'region', ahead)]
    ppermute x32 -> x35, starting transfers between devices: 43.3 us -> 42.2 us  [forward(): return lax.ppermute(x, 'region', ahead)]
    pallas_call x35 -> x43, Pallas kernels: 25.6 us -> 26.5 us  [call(): pl.pallas_call(body, name=name, out_shape=shapes if many else shapes[0],...]
  transfers between devices with their start and end apart: 67 -> 73, of which waited for: 39 -> 35; matrix products, arithmetic and copies ran while one was open for 0% -> 0% of each run, Pallas kernels for 16% -> 17%
where the time goes in v3:
time: 146 us; the launch traced here: 145 us
  starting transfers between devices  80.6 us (55%)
  waiting for transfers between devices  37.2 us (25%)
  Pallas kernels  26.5 us (18%)
    ppermute x35, starting transfers between devices, forward(): return lax.ppermute(x, 'region', ahead)  42.2 us
    ppermute x35, starting transfers between devices, backward(): return lax.ppermute(x, 'region', behind)  35.3 us
    pallas_call x43, Pallas kernels, call(): pl.pallas_call(body, name=name, out_shape=shapes if many else shapes[0],...  26.5 us
    ppermute x35, waiting for transfers between devices, backward(): return lax.ppermute(x, 'region', behind)  21.6 us
    ppermute x35, waiting for transfers between devices, forward(): return lax.ppermute(x, 'region', ahead)  15.7 us
    ppermute x3, starting transfers between devices, shards(): lax.ppermute(tail, 'sub', [(i, (i + k) % subs) for i in range(subs)])  3.03 us
  transfers between devices with their start and end apart: 73, of which 35 were waited for; matrix products, arithmetic and copies ran while one was open for 0% of the time, Pallas kernels for 17%

profile of v3, /device:TPU:0, one launch (start us, length us, event | category | flops | bytes accessed | tf_op | source)
XLA Modules:
  0.0 145.3 jit_solution(2782343796116639098)
XLA Ops:
  1.6 3.1 %collective-permute-start.15 = (f32[256,128]{1,0:T(8,128)S(1)}, f32[256,128]{1,0:T(8,128)S(1)}, u32[]{:S(2)}, u32[]{:S(2)}) collective-permute-start(f32[256,128]{1,0:T(8,128)S(1)} %get-tuple-element.81.refs_1_.refs_3_), channel_id=1, source_target_pairs={{0,8},{8,16},{16,24},{24,28},{28,20},{20,12},{12,4},{4,0},{1,9},{9... | collective-permute-start | bytes 393224 | tf_op jit(solution)/shard_map/ppermute | solution.py:526
  4.7 1.9 %collective-permute-start = (f32[256,128]{1,0:T(8,128)S(1)}, f32[256,128]{1,0:T(8,128)S(1)}, u32[]{:S(2)}, u32[]{:S(2)}) collective-permute-start(f32[256,128]{1,0:T(8,128)S(1)} %get-tuple-element.69.refs_1_.refs_3_), channel_id=1, source_target_pairs={{8,0},{16,8},{24,16},{28,24},{20,28},{12,20},{4,12},{0,4},{9,1},{1... | collective-permute-start | bytes 393224 | tf_op jit(solution)/shard_map/ppermute | solution.py:529
  6.6 4.9 %prepare.1 = (s32[32]{0:T(128)S(1)}, bf16[2048,2048]{1,0:T(8,128)(2,1)S(1)}, bf16[2048,256]{1,0:T(8,128)(2,1)S(1)}, f32[1536,256]{1,0:T(8,128)S(1)}) custom-call(s32[1]{0:T(128)} %bitcast.region_ref, s32[1,12]{1,0:T(1,128)} %target_hbm.1, bf16[2048,2048]{1,0:T(8,128)(2,1)} %refs_0_.1, bf16[2048,256]{1,0:T(8,128)(2,1)} %refs_1_.1, f32[1536,256]{1,0:T(8,128)} %refs_2_.1), custom_call_target="tpu_custom_call" | custom-call | bytes 12582912 | tf_op jit(solution)/shard_map/prepare/pallas_call | solution.py:63
  17.7 1.7 %collective-permute-start.19 = (f32[256,128]{1,0:T(8,128)S(1)}, f32[256,128]{1,0:T(8,128)S(1)}, u32[]{:S(2)}, u32[]{:S(2)}) collective-permute-start(f32[256,128]{1,0:T(8,128)S(1)} %get-tuple-element.85), channel_id=1, source_target_pairs={{0,8},{8,16},{16,24},{24,28},{28,20},{20,12},{12,4},{4,0},{1,9},{9... | collective-permute-start | bytes 393224 | tf_op jit(solution)/shard_map/ppermute | solution.py:526
  23.5 1.6 %collective-permute-start.18 = (f32[256,128]{1,0:T(8,128)S(1)}, f32[256,128]{1,0:T(8,128)S(1)}, u32[]{:S(2)}, u32[]{:S(2)}) collective-permute-start(f32[256,128]{1,0:T(8,128)S(1)} %get-tuple-element.84), channel_id=1, source_target_pairs={{8,0},{16,8},{24,16},{28,24},{20,28},{12,20},{4,12},{0,4},{9,1},{1... | collective-permute-start | bytes 393224 | tf_op jit(solution)/shard_map/ppermute | solution.py:529
  25.9 1.5 %collective-permute-start.6 = (f32[256,128]{1,0:T(8,128)S(1)}, f32[256,128]{1,0:T(8,128)S(1)}, u32[]{:S(2)}, u32[]{:S(2)}) collective-permute-start(f32[256,128]{1,0:T(8,128)S(1)} %collective-permute-done.5.refs_7_), channel_id=1, source_target_pairs={{0,8},{8,16},{16,24},{24,28},{28,20},{20,12},{12,4},{4,0},{1,9},{9... | collective-permute-start | bytes 393224 | tf_op jit(solution)/shard_map/ppermute | solution.py:526
  28.8 1.4 collective-permute-done.20.refs_5_
  30.2 2.3 %first_solve.3 = (f32[1536,128]{1,0:T(8,128)S(1)}, f32[264,128]{1,0:T(8,128)S(1)}, f32[264,128]{1,0:T(8,128)S(1)}, f32[264,128]{1,0:T(8,128)S(1)}, f32[264,128]{...) custom-call(s32[32]{0:T(128)S(1)} %get-tuple-element.68.refs_0_, ...), custom_call_target="tpu_custom_call" | custom-call | flops 603979776 | bytes 8388608 | tf_op jit(solution)/shard_map/first_solve/pallas_call | solution.py:63
  33.0 2.3 %first_solve.2 = (f32[1536,128]{1,0:T(8,128)S(1)}, f32[256,128]{1,0:T(8,128)S(1)}, f32[256,128]{1,0:T(8,128)S(1)}, f32[256,128]{1,0:T(8,128)S(1)}, f32[256,128]{...) custom-call(s32[32]{0:T(128)S(1)} %get-tuple-element.68.refs_0_, ...), custom_call_target="tpu_custom_call" | custom-call | flops 603979776 | bytes 8388608 | tf_op jit(solution)/shard_map/first_solve/pallas_call | solution.py:63
  35.3 1.6 %collective-permute-start.10 = (f32[256,128]{1,0:T(8,128)S(1)}, f32[256,128]{1,0:T(8,128)S(1)}, u32[]{:S(2)}, u32[]{:S(2)}) collective-permute-start(f32[256,128]{1,0:T(8,128)S(1)} %get-tuple-element.77), channel_id=1, source_target_pairs={{8,0},{16,8},{24,16},{28,24},{20,28},{12,20},{4,12},{0,4},{9,1},{1... | collective-permute-start | bytes 393224 | tf_op jit(solution)/shard_map/ppermute | solution.py:529
  36.9 1.6 %collective-permute-start.25 = (f32[264,128]{1,0:T(8,128)S(1)}, f32[264,128]{1,0:T(8,128)S(1)}, u32[]{:S(2)}, u32[]{:S(2)}) collective-permute-start(f32[264,128]{1,0:T(8,128)S(1)} %get-tuple-element.91), channel_id=1, source_target_pairs={{8,0},{16,8},{24,16},{28,24},{20,28},{12,20},{4,12},{0,4},{9,1},{1... | collective-permute-start | bytes 405512 | tf_op jit(solution)/shard_map/ppermute | solution.py:529
  40.1 1.6 %collective-permute-done.10.refs_0_ = f32[256,128]{1,0:T(8,128)S(1)} collective-permute-done((f32[256,128]{1,0:T(8,128)S(1)}, f32[256,128]{1,0:T(8,128)S(1)}, u32[]{:S(2)}, u32[]{:S(2)}) %collective-permute-start.10) | collective-permute-done | bytes 131104 | tf_op jit(solution)/shard_map/ppermute | solution.py:529
  41.7 1.7 %collective-permute-start.11 = (f32[256,128]{1,0:T(8,128)S(1)}, f32[256,128]{1,0:T(8,128)S(1)}, u32[]{:S(2)}, u32[]{:S(2)}) collective-permute-start(f32[256,128]{1,0:T(8,128)S(1)} %add_pairs.22), channel_id=1, source_target_pairs={{8,0},{16,8},{24,16},{28,24},{20,28},{12,20},{4,12},{0,4},{9,1},{1... | collective-permute-start | bytes 393224 | tf_op jit(solution)/shard_map/ppermute | solution.py:529
  45.3 1.4 collective-permute-start.23
  48.1 2.0 %collective-permute-start.12 = (f32[256,128]{1,0:T(8,128)S(1)}, f32[256,128]{1,0:T(8,128)S(1)}, u32[]{:S(2)}, u32[]{:S(2)}) collective-permute-start(f32[256,128]{1,0:T(8,128)S(1)} %add_pairs.23), channel_id=1, source_target_pairs={{8,0},{16,8},{24,16},{28,24},{20,28},{12,20},{4,12},{0,4},{9,1},{1... | collective-permute-start | bytes 393224 | tf_op jit(solution)/shard_map/ppermute | solution.py:529
  50.1 1.6 %collective-permute-start.27 = (f32[264,128]{1,0:T(8,128)S(1)}, f32[264,128]{1,0:T(8,128)S(1)}, u32[]{:S(2)}, u32[]{:S(2)}) collective-permute-start(f32[264,128]{1,0:T(8,128)S(1)} %add_pairs.29), channel_id=1, source_target_pairs={{8,0},{16,8},{24,16},{28,24},{20,28},{12,20},{4,12},{0,4},{9,1},{1... | collective-permute-start | bytes 405512 | tf_op jit(solution)/shard_map/ppermute | solution.py:529
  51.8 1.5 %collective-permute-start.24 = (f32[264,128]{1,0:T(8,128)S(1)}, f32[264,128]{1,0:T(8,128)S(1)}, u32[]{:S(2)}, u32[]{:S(2)}) collective-permute-start(f32[264,128]{1,0:T(8,128)S(1)} %add_pairs.27), channel_id=1, source_target_pairs={{0,8},{8,16},{16,24},{24,28},{28,20},{20,12},{12,4},{4,0},{1,9},{9... | collective-permute-start | bytes 405512 | tf_op jit(solution)/shard_map/ppermute | solution.py:526
  54.5 1.3 collective-permute-start.9
  56.9 1.5 %collective-permute-start.38 = (f32[256,128]{1,0:T(8,128)S(1)}, f32[256,128]{1,0:T(8,128)S(1)}, u32[]{:S(2)}, u32[]{:S(2)}) collective-permute-start(f32[256,128]{1,0:T(8,128)S(1)} %get-tuple-element.99.refs_1_.refs_3_), channel_id=1, source_target_pairs={{0,8},{8,16},{16,24},{24,28},{28,20},{20,12},{12,4},{4,0},{1,9},{9... | collective-permute-start | bytes 393224 | tf_op jit(solution)/shard_map/ppermute | solution.py:526
  58.4 2.5 %collective-permute-done.9.refs_1_ = f32[256,128]{1,0:T(8,128)S(1)} collective-permute-done((f32[256,128]{1,0:T(8,128)S(1)}, f32[256,128]{1,0:T(8,128)S(1)}, u32[]{:S(2)}, u32[]{:S(2)}) %collective-permute-start.9) | collective-permute-done | bytes 131104 | tf_op jit(solution)/shard_map/ppermute | solution.py:526
  60.9 1.4 collective-permute-done.13.refs_2_
  62.5 1.8 %collective-permute-start.35 = (f32[256,128]{1,0:T(8,128)S(1)}, f32[256,128]{1,0:T(8,128)S(1)}, u32[]{:S(2)}, u32[]{:S(2)}) collective-permute-start(f32[256,128]{1,0:T(8,128)S(1)} %get-tuple-element.99.refs_1_.refs_3_), channel_id=1, source_target_pairs={{8,0},{16,8},{24,16},{28,24},{20,28},{12,20},{4,12},{0,4},{9,1},{1... | collective-permute-start | bytes 393224 | tf_op jit(solution)/shard_map/ppermute | solution.py:529
  65.0 1.4 collective-permute-start.32
  66.4 2.3 %collective-permute-done.28.refs_2_ = f32[256,128]{1,0:T(8,128)S(1)} collective-permute-done((f32[256,128]{1,0:T(8,128)S(1)}, f32[256,128]{1,0:T(8,128)S(1)}, u32[]{:S(2)}, u32[]{:S(2)}) %collective-permute-start.28) | collective-permute-done | bytes 131104 | tf_op jit(solution)/shard_map/ppermute | solution.py:529
  68.7 2.8 %collective-permute-done.35.refs_2_ = f32[256,128]{1,0:T(8,128)S(1)} collective-permute-done((f32[256,128]{1,0:T(8,128)S(1)}, f32[256,128]{1,0:T(8,128)S(1)}, u32[]{:S(2)}, u32[]{:S(2)}) %collective-permute-start.35) | collective-permute-done | bytes 131104 | tf_op jit(solution)/shard_map/ppermute | solution.py:529
  71.5 2.0 %collective-permute-start.40 = (f32[256,128]{1,0:T(8,128)S(1)}, f32[256,128]{1,0:T(8,128)S(1)}, u32[]{:S(2)}, u32[]{:S(2)}) collective-permute-start(f32[256,128]{1,0:T(8,128)S(1)} %collective-permute-done.39.refs_7_), channel_id=1, source_target_pairs={{0,8},{8,16},{16,24},{24,28},{28,20},{20,12},{12,4},{4,0},{1,9},{9... | collective-permute-start | bytes 393224 | tf_op jit(solution)/shard_map/ppermute | solution.py:526
  77.1 2.5 %collective-permute-start.41 = (f32[256,128]{1,0:T(8,128)S(1)}, f32[256,128]{1,0:T(8,128)S(1)}, u32[]{:S(2)}, u32[]{:S(2)}) collective-permute-start(f32[256,128]{1,0:T(8,128)S(1)} %collective-permute-done.40.refs_6_), channel_id=1, source_target_pairs={{0,8},{8,16},{16,24},{24,28},{28,20},{20,12},{12,4},{4,0},{1,9},{9... | collective-permute-start | bytes 393224 | tf_op jit(solution)/shard_map/ppermute | solution.py:526
  79.6 1.4 collective-permute-start.34
  83.5 2.7 %second_solve.3 = (f32[1536,128]{1,0:T(8,128)S(1)}, bf16[1664,128]{1,0:T(8,128)(2,1)S(1)}, f32[1664,128]{1,0:T(8,128)S(1)}, f32[16,128]{1,0:T(8,128)S(1)}, f32[2...) custom-call(s32[32]{0:T(128)S(1)} %get-tuple-element.68.refs_0_, ...), custom_call_target="tpu_custom_call" | custom-call | flops 603979776 | bytes 8388608 | tf_op jit(solution)/shard_map/second_solve/pallas_call | solution.py:63
  86.1 2.5 %collective-permute-start.49 = (f32[256,128]{1,0:T(8,128)S(1)}, f32[256,128]{1,0:T(8,128)S(1)}, u32[]{:S(2)}, u32[]{:S(2)}) collective-permute-start(f32[256,128]{1,0:T(8,128)S(1)} %get-tuple-element.114), channel_id=1, source_target_pairs={{0,8},{8,16},{16,24},{24,28},{28,20},{20,12},{12,4},{4,0},{1,9},{9... | collective-permute-start | bytes 393224 | tf_op jit(solution)/shard_map/ppermute | solution.py:526
  88.7 2.7 %second_solve.2 = (f32[1536,128]{1,0:T(8,128)S(1)}, bf16[1664,128]{1,0:T(8,128)(2,1)S(1)}, f32[1664,128]{1,0:T(8,128)S(1)}, f32[16,128]{1,0:T(8,128)S(1)}, f32[2...) custom-call(s32[32]{0:T(128)S(1)} %get-tuple-element.68.refs_0_, ...), custom_call_target="tpu_custom_call" | custom-call | flops 603979776 | bytes 8388608 | tf_op jit(solution)/shard_map/second_solve/pallas_call | solution.py:63
  91.6 1.9 %collective-permute-start.42 = (f32[256,128]{1,0:T(8,128)S(1)}, f32[256,128]{1,0:T(8,128)S(1)}, u32[]{:S(2)}, u32[]{:S(2)}) collective-permute-start(f32[256,128]{1,0:T(8,128)S(1)} %get-tuple-element.104), channel_id=1, source_target_pairs={{0,8},{8,16},{16,24},{24,28},{28,20},{20,12},{12,4},{4,0},{1,9},{9... | collective-permute-start | bytes 393224 | tf_op jit(solution)/shard_map/ppermute | solution.py:526
  93.5 2.0 %collective-permute-start.50 = (f32[256,128]{1,0:T(8,128)S(1)}, f32[256,128]{1,0:T(8,128)S(1)}, u32[]{:S(2)}, u32[]{:S(2)}) collective-permute-start(f32[256,128]{1,0:T(8,128)S(1)} %add_pairs.35), channel_id=1, source_target_pairs={{0,8},{8,16},{16,24},{24,28},{28,20},{20,12},{12,4},{4,0},{1,9},{9... | collective-permute-start | bytes 393224 | tf_op jit(solution)/shard_map/ppermute | solution.py:526
  95.6 1.4 collective-permute-done.45.refs_0_
  100.6 1.4 collective-permute-start.51
  110.4 3.0 %collective-permute-done.52.refs_1_ = f32[256,128]{1,0:T(8,128)S(1)} collective-permute-done((f32[256,128]{1,0:T(8,128)S(1)}, f32[256,128]{1,0:T(8,128)S(1)}, u32[]{:S(2)}, u32[]{:S(2)}) %collective-permute-start.52) | collective-permute-done | bytes 131104 | tf_op jit(solution)/shard_map/ppermute | solution.py:526
  117.0 1.5 %collective-permute-start.60 = (f32[264,128]{1,0:T(8,128)S(1)}, f32[264,128]{1,0:T(8,128)S(1)}, u32[]{:S(2)}, u32[]{:S(2)}) collective-permute-start(f32[264,128]{1,0:T(8,128)S(1)} %get-tuple-element.124.refs_1_.refs_0_), channel_id=1, source_target_pairs={{0,8},{8,16},{16,24},{24,28},{28,20},{20,12},{12,4},{4,0},{1,9},{9... | collective-permute-start | bytes 405512 | tf_op jit(solution)/shard_map/ppermute | solution.py:526
  118.5 1.5 %collective-permute-done.56.refs_2_.refs_1_ = f32[264,128]{1,0:T(8,128)S(1)} collective-permute-done((f32[264,128]{1,0:T(8,128)S(1)}, f32[264,128]{1,0:T(8,128)S(1)}, u32[]{:S(2)}, u32[]{:S(2)}) %collective-permute-start.56) | collective-permute-done | bytes 135200 | tf_op jit(solution)/shard_map/ppermute | solution.py:529
  120.0 1.9 %collective-permute-start.57 = (f32[264,128]{1,0:T(8,128)S(1)}, f32[264,128]{1,0:T(8,128)S(1)}, u32[]{:S(2)}, u32[]{:S(2)}) collective-permute-start(f32[264,128]{1,0:T(8,128)S(1)} %collective-permute-done.56.refs_2_.refs_1_), channel_id=1, source_target_pairs={{8,0},{16,8},{24,16},{28,24},{20,28},{12,20},{4,12},{0,4},{9,1},{1... | collective-permute-start | bytes 405512 | tf_op jit(solution)/shard_map/ppermute | solution.py:529
  125.0 1.9 %collective-permute-start.58 = (f32[264,128]{1,0:T(8,128)S(1)}, f32[264,128]{1,0:T(8,128)S(1)}, u32[]{:S(2)}, u32[]{:S(2)}) collective-permute-start(f32[264,128]{1,0:T(8,128)S(1)} %collective-permute-done.57.refs_3_.refs_2_), channel_id=1, source_target_pairs={{8,0},{16,8},{24,16},{28,24},{20,28},{12,20},{4,12},{0,4},{9,1},{1... | collective-permute-start | bytes 405512 | tf_op jit(solution)/shard_map/ppermute | solution.py:529
  126.9 1.4 collective-permute-start.64
  130.3 1.6 %collective-permute-start.59 = (f32[264,128]{1,0:T(8,128)S(1)}, f32[264,128]{1,0:T(8,128)S(1)}, u32[]{:S(2)}, u32[]{:S(2)}) collective-permute-start(f32[264,128]{1,0:T(8,128)S(1)} %collective-permute-done.58.refs_4_.refs_3_), channel_id=1, source_target_pairs={{8,0},{16,8},{24,16},{28,24},{20,28},{12,20},{4,12},{0,4},{9,1},{1... | collective-permute-start | bytes 405512 | tf_op jit(solution)/shard_map/ppermute | solution.py:529
  131.9 1.4 collective-permute-start.65
  136.9 1.4 collective-permute-done.69.refs_5_
  138.3 1.6 %finish.2 = (f32[1536,256]{1,0:T(8,128)}, f32[256,256]{1,0:T(8,128)}) custom-call(s32[32]{0:T(128)S(1)} %get-tuple-element.68.refs_0_, f32[256,128]{1,0:T(8,128)S(1)} %get-tuple-element.126.refs_1_, f32[256,128]{1,0:T(8,128)S(1)} %collective-permute-done.63.refs_2_, f32[256,128]{1,0:T(8,128)S(1)} %collective-permute-done.64.refs_3_, ...), custom_call_target="tpu_custom_call" | custom-call | bytes 3145728 | tf_op jit(solution)/shard_map/finish/pallas_call | solution.py:63
  140.0 1.6 %collective-permute-start.71 = (f32[8,128]{1,0:T(8,128)S(1)}, f32[8,128]{1,0:T(8,128)S(1)}, u32[]{:S(2)}, u32[]{:S(2)}) collective-permute-start(f32[8,128]{1,0:T(8,128)S(1)} %sum_tails.1.refs_0_), channel_id=1, source_target_pairs={{0,2},{1,3},{2,0},{3,1},{4,6},{5,7},{6,4},{7,5},{8,10},{9,11},{10,... | collective-permute-start | bytes 12296 | tf_op jit(solution)/shard_map/ppermute | solution.py:618
  141.6 1.4 collective-permute-start.72
  143.0 1.6 %finish.3 = (f32[1536,256]{1,0:T(8,128)}, f32[256,256]{1,0:T(8,128)}) custom-call(s32[32]{0:T(128)S(1)} %get-tuple-element.68.refs_0_, f32[264,128]{1,0:T(8,128)S(1)} %get-tuple-element.124.refs_1_.refs_0_, f32[264,128]{1,0:T(8,128)S(1)} %collective-permute-done.56.refs_2_.refs_1_, ...), custom_call_target="tpu_custom_call", output_to_operand_aliasing={{0}: (10, {}), {1}: (11, {})} | custom-call | bytes 3145728 | tf_op jit(solution)/shard_map/finish/pallas_call | solution.py:63
  (146 shorter events, 53.4 us)
Async XLA Ops:
  1.6 9.9 %collective-permute-start.15 = (f32[256,128]{1,0:T(8,128)S(1)}, f32[256,128]{1,0:T(8,128)S(1)}, u32[]{:S(2)}, u32[]{:S(2)}) collective-permute-start(f32[256,128]{1,0:T(8,128)S(1)} %get-tuple-element.81.refs_1_.refs_3_), channel_id=1, source_target_pairs={{0,8},{8,16},{16,24},{24,28},{28,20},{20,12},{12,4},{4,0},{1,9},{9... | collective-permute-start | bytes 393224 | tf_op jit(solution)/shard_map/ppermute | solution.py:526
  4.7 6.9 %collective-permute-start.14 = (f32[256,128]{1,0:T(8,128)S(1)}, f32[256,128]{1,0:T(8,128)S(1)}, u32[]{:S(2)}, u32[]{:S(2)}) collective-permute-start(f32[256,128]{1,0:T(8,128)S(1)} %get-tuple-element.81.refs_1_.refs_3_), channel_id=1, source_target_pairs={{8,0},{16,8},{24,16},{28,24},{20,28},{12,20},{4,12},{0,4},{9,1},{1... | collective-permute-start | bytes 393224 | tf_op jit(solution)/shard_map/ppermute | solution.py:529
  4.7 10.0 %collective-permute-start = (f32[256,128]{1,0:T(8,128)S(1)}, f32[256,128]{1,0:T(8,128)S(1)}, u32[]{:S(2)}, u32[]{:S(2)}) collective-permute-start(f32[256,128]{1,0:T(8,128)S(1)} %get-tuple-element.69.refs_1_.refs_3_), channel_id=1, source_target_pairs={{8,0},{16,8},{24,16},{28,24},{20,28},{12,20},{4,12},{0,4},{9,1},{1... | collective-permute-start | bytes 393224 | tf_op jit(solution)/shard_map/ppermute | solution.py:529
  11.6 5.9 %collective-permute-start.17 = (f32[256,128]{1,0:T(8,128)S(1)}, f32[256,128]{1,0:T(8,128)S(1)}, u32[]{:S(2)}, u32[]{:S(2)}) collective-permute-start(f32[256,128]{1,0:T(8,128)S(1)} %get-tuple-element.83), channel_id=1, source_target_pairs={{0,8},{8,16},{16,24},{24,28},{28,20},{20,12},{12,4},{4,0},{1,9},{9... | collective-permute-start | bytes 393224 | tf_op jit(solution)/shard_map/ppermute | solution.py:526
  13.7 6.3 %collective-permute-start.4 = (f32[256,128]{1,0:T(8,128)S(1)}, f32[256,128]{1,0:T(8,128)S(1)}, u32[]{:S(2)}, u32[]{:S(2)}) collective-permute-start(f32[256,128]{1,0:T(8,128)S(1)} %get-tuple-element.69.refs_1_.refs_3_), channel_id=1, source_target_pairs={{0,8},{8,16},{16,24},{24,28},{28,20},{20,12},{12,4},{4,0},{1,9},{9... | collective-permute-start | bytes 393224 | tf_op jit(solution)/shard_map/ppermute | solution.py:526
  14.7 6.3 %collective-permute-start.1 = (f32[256,128]{1,0:T(8,128)S(1)}, f32[256,128]{1,0:T(8,128)S(1)}, u32[]{:S(2)}, u32[]{:S(2)}) collective-permute-start(f32[256,128]{1,0:T(8,128)S(1)} %collective-permute-done.refs_2_), channel_id=1, source_target_pairs={{8,0},{16,8},{24,16},{28,24},{20,28},{12,20},{4,12},{0,4},{9,1},{1... | collective-permute-start | bytes 393224 | tf_op jit(solution)/shard_map/ppermute | solution.py:529
  17.7 7.4 %collective-permute-start.19 = (f32[256,128]{1,0:T(8,128)S(1)}, f32[256,128]{1,0:T(8,128)S(1)}, u32[]{:S(2)}, u32[]{:S(2)}) collective-permute-start(f32[256,128]{1,0:T(8,128)S(1)} %get-tuple-element.85), channel_id=1, source_target_pairs={{0,8},{8,16},{16,24},{24,28},{28,20},{20,12},{12,4},{4,0},{1,9},{9... | collective-permute-start | bytes 393224 | tf_op jit(solution)/shard_map/ppermute | solution.py:526
  20.0 5.9 %collective-permute-start.5 = (f32[256,128]{1,0:T(8,128)S(1)}, f32[256,128]{1,0:T(8,128)S(1)}, u32[]{:S(2)}, u32[]{:S(2)}) collective-permute-start(f32[256,128]{1,0:T(8,128)S(1)} %collective-permute-done.4.refs_8_), channel_id=1, source_target_pairs={{0,8},{8,16},{16,24},{24,28},{28,20},{20,12},{12,4},{4,0},{1,9},{9... | collective-permute-start | bytes 393224 | tf_op jit(solution)/shard_map/ppermute | solution.py:526
  21.0 6.3 %collective-permute-start.2 = (f32[256,128]{1,0:T(8,128)S(1)}, f32[256,128]{1,0:T(8,128)S(1)}, u32[]{:S(2)}, u32[]{:S(2)}) collective-permute-start(f32[256,128]{1,0:T(8,128)S(1)} %collective-permute-done.1.refs_3_), channel_id=1, source_target_pairs={{8,0},{16,8},{24,16},{28,24},{20,28},{12,20},{4,12},{0,4},{9,1},{1... | collective-permute-start | bytes 393224 | tf_op jit(solution)/shard_map/ppermute | solution.py:529
  25.9 7.1 %collective-permute-start.6 = (f32[256,128]{1,0:T(8,128)S(1)}, f32[256,128]{1,0:T(8,128)S(1)}, u32[]{:S(2)}, u32[]{:S(2)}) collective-permute-start(f32[256,128]{1,0:T(8,128)S(1)} %collective-permute-done.5.refs_7_), channel_id=1, source_target_pairs={{0,8},{8,16},{16,24},{24,28},{28,20},{20,12},{12,4},{4,0},{1,9},{9... | collective-permute-start | bytes 393224 | tf_op jit(solution)/shard_map/ppermute | solution.py:526
  32.5 6.2 %collective-permute-start.21 = (f32[264,128]{1,0:T(8,128)S(1)}, f32[264,128]{1,0:T(8,128)S(1)}, u32[]{:S(2)}, u32[]{:S(2)}) collective-permute-start(f32[264,128]{1,0:T(8,128)S(1)} %get-tuple-element.87), channel_id=1, source_target_pairs={{0,8},{8,16},{16,24},{24,28},{28,20},{20,12},{12,4},{4,0},{1,9},{9... | collective-permute-start | bytes 405512 | tf_op jit(solution)/shard_map/ppermute | solution.py:526
  35.3 6.3 %collective-permute-start.10 = (f32[256,128]{1,0:T(8,128)S(1)}, f32[256,128]{1,0:T(8,128)S(1)}, u32[]{:S(2)}, u32[]{:S(2)}) collective-permute-start(f32[256,128]{1,0:T(8,128)S(1)} %get-tuple-element.77), channel_id=1, source_target_pairs={{8,0},{16,8},{24,16},{28,24},{20,28},{12,20},{4,12},{0,4},{9,1},{1... | collective-permute-start | bytes 393224 | tf_op jit(solution)/shard_map/ppermute | solution.py:529
  36.9 7.6 %collective-permute-start.25 = (f32[264,128]{1,0:T(8,128)S(1)}, f32[264,128]{1,0:T(8,128)S(1)}, u32[]{:S(2)}, u32[]{:S(2)}) collective-permute-start(f32[264,128]{1,0:T(8,128)S(1)} %get-tuple-element.91), channel_id=1, source_target_pairs={{8,0},{16,8},{24,16},{28,24},{20,28},{12,20},{4,12},{0,4},{9,1},{1... | collective-permute-start | bytes 405512 | tf_op jit(solution)/shard_map/ppermute | solution.py:529
  38.7 6.6 %collective-permute-start.22 = (f32[264,128]{1,0:T(8,128)S(1)}, f32[264,128]{1,0:T(8,128)S(1)}, u32[]{:S(2)}, u32[]{:S(2)}) collective-permute-start(f32[264,128]{1,0:T(8,128)S(1)} %add_pairs.25), channel_id=1, source_target_pairs={{0,8},{8,16},{16,24},{24,28},{28,20},{20,12},{12,4},{4,0},{1,9},{9... | collective-permute-start | bytes 405512 | tf_op jit(solution)/shard_map/ppermute | solution.py:526
  39.0 8.9 %collective-permute-start.7 = (f32[256,128]{1,0:T(8,128)S(1)}, f32[256,128]{1,0:T(8,128)S(1)}, u32[]{:S(2)}, u32[]{:S(2)}) collective-permute-start(f32[256,128]{1,0:T(8,128)S(1)} %get-tuple-element.74), channel_id=1, source_target_pairs={{0,8},{8,16},{16,24},{24,28},{28,20},{20,12},{12,4},{4,0},{1,9},{9... | collective-permute-start | bytes 393224 | tf_op jit(solution)/shard_map/ppermute | solution.py:526
  41.7 6.4 %collective-permute-start.11 = (f32[256,128]{1,0:T(8,128)S(1)}, f32[256,128]{1,0:T(8,128)S(1)}, u32[]{:S(2)}, u32[]{:S(2)}) collective-permute-start(f32[256,128]{1,0:T(8,128)S(1)} %add_pairs.22), channel_id=1, source_target_pairs={{8,0},{16,8},{24,16},{28,24},{20,28},{12,20},{4,12},{0,4},{9,1},{1... | collective-permute-start | bytes 393224 | tf_op jit(solution)/shard_map/ppermute | solution.py:529
  45.3 6.4 %collective-permute-start.23 = (f32[264,128]{1,0:T(8,128)S(1)}, f32[264,128]{1,0:T(8,128)S(1)}, u32[]{:S(2)}, u32[]{:S(2)}) collective-permute-start(f32[264,128]{1,0:T(8,128)S(1)} %add_pairs.26), channel_id=1, source_target_pairs={{0,8},{8,16},{16,24},{24,28},{28,20},{20,12},{12,4},{4,0},{1,9},{9... | collective-permute-start | bytes 405512 | tf_op jit(solution)/shard_map/ppermute | solution.py:526
  48.0 6.5 %collective-permute-start.8 = (f32[256,128]{1,0:T(8,128)S(1)}, f32[256,128]{1,0:T(8,128)S(1)}, u32[]{:S(2)}, u32[]{:S(2)}) collective-permute-start(f32[256,128]{1,0:T(8,128)S(1)} %add_pairs.20), channel_id=1, source_target_pairs={{0,8},{8,16},{16,24},{24,28},{28,20},{20,12},{12,4},{4,0},{1,9},{9... | collective-permute-start | bytes 393224 | tf_op jit(solution)/shard_map/ppermute | solution.py:526
  48.1 7.7 %collective-permute-start.12 = (f32[256,128]{1,0:T(8,128)S(1)}, f32[256,128]{1,0:T(8,128)S(1)}, u32[]{:S(2)}, u32[]{:S(2)}) collective-permute-start(f32[256,128]{1,0:T(8,128)S(1)} %add_pairs.23), channel_id=1, source_target_pairs={{8,0},{16,8},{24,16},{28,24},{20,28},{12,20},{4,12},{0,4},{9,1},{1... | collective-permute-start | bytes 393224 | tf_op jit(solution)/shard_map/ppermute | solution.py:529
  50.1 6.5 %collective-permute-start.27 = (f32[264,128]{1,0:T(8,128)S(1)}, f32[264,128]{1,0:T(8,128)S(1)}, u32[]{:S(2)}, u32[]{:S(2)}) collective-permute-start(f32[264,128]{1,0:T(8,128)S(1)} %add_pairs.29), channel_id=1, source_target_pairs={{8,0},{16,8},{24,16},{28,24},{20,28},{12,20},{4,12},{0,4},{9,1},{1... | collective-permute-start | bytes 405512 | tf_op jit(solution)/shard_map/ppermute | solution.py:529
  54.5 6.4 %collective-permute-start.9 = (f32[256,128]{1,0:T(8,128)S(1)}, f32[256,128]{1,0:T(8,128)S(1)}, u32[]{:S(2)}, u32[]{:S(2)}) collective-permute-start(f32[256,128]{1,0:T(8,128)S(1)} %add_pairs.21), channel_id=1, source_target_pairs={{0,8},{8,16},{16,24},{24,28},{28,20},{20,12},{12,4},{4,0},{1,9},{9... | collective-permute-start | bytes 393224 | tf_op jit(solution)/shard_map/ppermute | solution.py:526
  55.8 6.4 %collective-permute-start.13 = (f32[256,128]{1,0:T(8,128)S(1)}, f32[256,128]{1,0:T(8,128)S(1)}, u32[]{:S(2)}, u32[]{:S(2)}) collective-permute-start(f32[256,128]{1,0:T(8,128)S(1)} %add_pairs.24), channel_id=1, source_target_pairs={{8,0},{16,8},{24,16},{28,24},{20,28},{12,20},{4,12},{0,4},{9,1},{1... | collective-permute-start | bytes 393224 | tf_op jit(solution)/shard_map/ppermute | solution.py:529
  56.9 7.4 %collective-permute-start.38 = (f32[256,128]{1,0:T(8,128)S(1)}, f32[256,128]{1,0:T(8,128)S(1)}, u32[]{:S(2)}, u32[]{:S(2)}) collective-permute-start(f32[256,128]{1,0:T(8,128)S(1)} %get-tuple-element.99.refs_1_.refs_3_), channel_id=1, source_target_pairs={{0,8},{8,16},{16,24},{24,28},{28,20},{20,12},{12,4},{4,0},{1,9},{9... | collective-permute-start | bytes 393224 | tf_op jit(solution)/shard_map/ppermute | solution.py:526
  62.3 6.4 %collective-permute-start.28 = (f32[256,128]{1,0:T(8,128)S(1)}, f32[256,128]{1,0:T(8,128)S(1)}, u32[]{:S(2)}, u32[]{:S(2)}) collective-permute-start(f32[256,128]{1,0:T(8,128)S(1)} %get-tuple-element.95.refs_1_.refs_3_), channel_id=1, source_target_pairs={{8,0},{16,8},{24,16},{28,24},{20,28},{12,20},{4,12},{0,4},{9,1},{1... | collective-permute-start | bytes 393224 | tf_op jit(solution)/shard_map/ppermute | solution.py:529
  62.5 9.0 %collective-permute-start.35 = (f32[256,128]{1,0:T(8,128)S(1)}, f32[256,128]{1,0:T(8,128)S(1)}, u32[]{:S(2)}, u32[]{:S(2)}) collective-permute-start(f32[256,128]{1,0:T(8,128)S(1)} %get-tuple-element.99.refs_1_.refs_3_), channel_id=1, source_target_pairs={{8,0},{16,8},{24,16},{28,24},{20,28},{12,20},{4,12},{0,4},{9,1},{1... | collective-permute-start | bytes 393224 | tf_op jit(solution)/shard_map/ppermute | solution.py:529
  64.3 7.3 %collective-permute-start.39 = (f32[256,128]{1,0:T(8,128)S(1)}, f32[256,128]{1,0:T(8,128)S(1)}, u32[]{:S(2)}, u32[]{:S(2)}) collective-permute-start(f32[256,128]{1,0:T(8,128)S(1)} %collective-permute-done.38.refs_8_), channel_id=1, source_target_pairs={{0,8},{8,16},{16,24},{24,28},{28,20},{20,12},{12,4},{4,0},{1,9},{9... | collective-permute-start | bytes 393224 | tf_op jit(solution)/shard_map/ppermute | solution.py:526
  65.0 8.5 %collective-permute-start.32 = (f32[256,128]{1,0:T(8,128)S(1)}, f32[256,128]{1,0:T(8,128)S(1)}, u32[]{:S(2)}, u32[]{:S(2)}) collective-permute-start(f32[256,128]{1,0:T(8,128)S(1)} %get-tuple-element.95.refs_1_.refs_3_), channel_id=1, source_target_pairs={{0,8},{8,16},{16,24},{24,28},{28,20},{20,12},{12,4},{4,0},{1,9},{9... | collective-permute-start | bytes 393224 | tf_op jit(solution)/shard_map/ppermute | solution.py:526
  68.7 6.0 %collective-permute-start.29 = (f32[256,128]{1,0:T(8,128)S(1)}, f32[256,128]{1,0:T(8,128)S(1)}, u32[]{:S(2)}, u32[]{:S(2)}) collective-permute-start(f32[256,128]{1,0:T(8,128)S(1)} %collective-permute-done.28.refs_2_), channel_id=1, source_target_pairs={{8,0},{16,8},{24,16},{28,24},{20,28},{12,20},{4,12},{0,4},{9,1},{1... | collective-permute-start | bytes 393224 | tf_op jit(solution)/shard_map/ppermute | solution.py:529
  73.6 6.0 %collective-permute-start.33 = (f32[256,128]{1,0:T(8,128)S(1)}, f32[256,128]{1,0:T(8,128)S(1)}, u32[]{:S(2)}, u32[]{:S(2)}) collective-permute-start(f32[256,128]{1,0:T(8,128)S(1)} %collective-permute-done.32.refs_8_), channel_id=1, source_target_pairs={{0,8},{8,16},{16,24},{24,28},{28,20},{20,12},{12,4},{4,0},{1,9},{9... | collective-permute-start | bytes 393224 | tf_op jit(solution)/shard_map/ppermute | solution.py:526
  74.7 6.3 %collective-permute-start.30 = (f32[256,128]{1,0:T(8,128)S(1)}, f32[256,128]{1,0:T(8,128)S(1)}, u32[]{:S(2)}, u32[]{:S(2)}) collective-permute-start(f32[256,128]{1,0:T(8,128)S(1)} %collective-permute-done.29.refs_3_), channel_id=1, source_target_pairs={{8,0},{16,8},{24,16},{28,24},{20,28},{12,20},{4,12},{0,4},{9,1},{1... | collective-permute-start | bytes 393224 | tf_op jit(solution)/shard_map/ppermute | solution.py:529
  76.5 6.4 %collective-permute-start.37 = (f32[256,128]{1,0:T(8,128)S(1)}, f32[256,128]{1,0:T(8,128)S(1)}, u32[]{:S(2)}, u32[]{:S(2)}) collective-permute-start(f32[256,128]{1,0:T(8,128)S(1)} %collective-permute-done.36.refs_3_), channel_id=1, source_target_pairs={{8,0},{16,8},{24,16},{28,24},{20,28},{12,20},{4,12},{0,4},{9,1},{1... | collective-permute-start | bytes 393224 | tf_op jit(solution)/shard_map/ppermute | solution.py:529
  77.1 6.4 %collective-permute-start.41 = (f32[256,128]{1,0:T(8,128)S(1)}, f32[256,128]{1,0:T(8,128)S(1)}, u32[]{:S(2)}, u32[]{:S(2)}) collective-permute-start(f32[256,128]{1,0:T(8,128)S(1)} %collective-permute-done.40.refs_6_), channel_id=1, source_target_pairs={{0,8},{8,16},{16,24},{24,28},{28,20},{20,12},{12,4},{4,0},{1,9},{9... | collective-permute-start | bytes 393224 | tf_op jit(solution)/shard_map/ppermute | solution.py:526
  79.6 9.1 %collective-permute-start.34 = (f32[256,128]{1,0:T(8,128)S(1)}, f32[256,128]{1,0:T(8,128)S(1)}, u32[]{:S(2)}, u32[]{:S(2)}) collective-permute-start(f32[256,128]{1,0:T(8,128)S(1)} %collective-permute-done.33.refs_7_), channel_id=1, source_target_pairs={{0,8},{8,16},{16,24},{24,28},{28,20},{20,12},{12,4},{4,0},{1,9},{9... | collective-permute-start | bytes 393224 | tf_op jit(solution)/shard_map/ppermute | solution.py:526
  81.0 7.7 %collective-permute-start.31 = (f32[256,128]{1,0:T(8,128)S(1)}, f32[256,128]{1,0:T(8,128)S(1)}, u32[]{:S(2)}, u32[]{:S(2)}) collective-permute-start(f32[256,128]{1,0:T(8,128)S(1)} %collective-permute-done.30.refs_4_), channel_id=1, source_target_pairs={{8,0},{16,8},{24,16},{28,24},{20,28},{12,20},{4,12},{0,4},{9,1},{1... | collective-permute-start | bytes 393224 | tf_op jit(solution)/shard_map/ppermute | solution.py:529
  86.1 7.4 %collective-permute-start.49 = (f32[256,128]{1,0:T(8,128)S(1)}, f32[256,128]{1,0:T(8,128)S(1)}, u32[]{:S(2)}, u32[]{:S(2)}) collective-permute-start(f32[256,128]{1,0:T(8,128)S(1)} %get-tuple-element.114), channel_id=1, source_target_pairs={{0,8},{8,16},{16,24},{24,28},{28,20},{20,12},{12,4},{4,0},{1,9},{9... | collective-permute-start | bytes 393224 | tf_op jit(solution)/shard_map/ppermute | solution.py:526
  91.4 6.9 %collective-permute-start.53 = (f32[256,128]{1,0:T(8,128)S(1)}, f32[256,128]{1,0:T(8,128)S(1)}, u32[]{:S(2)}, u32[]{:S(2)}) collective-permute-start(f32[256,128]{1,0:T(8,128)S(1)} %get-tuple-element.118), channel_id=1, source_target_pairs={{8,0},{16,8},{24,16},{28,24},{20,28},{12,20},{4,12},{0,4},{9,1},{1... | collective-permute-start | bytes 393224 | tf_op jit(solution)/shard_map/ppermute | solution.py:529
  91.6 7.7 %collective-permute-start.42 = (f32[256,128]{1,0:T(8,128)S(1)}, f32[256,128]{1,0:T(8,128)S(1)}, u32[]{:S(2)}, u32[]{:S(2)}) collective-permute-start(f32[256,128]{1,0:T(8,128)S(1)} %get-tuple-element.104), channel_id=1, source_target_pairs={{0,8},{8,16},{16,24},{24,28},{28,20},{20,12},{12,4},{4,0},{1,9},{9... | collective-permute-start | bytes 393224 | tf_op jit(solution)/shard_map/ppermute | solution.py:526
  93.5 7.0 %collective-permute-start.50 = (f32[256,128]{1,0:T(8,128)S(1)}, f32[256,128]{1,0:T(8,128)S(1)}, u32[]{:S(2)}, u32[]{:S(2)}) collective-permute-start(f32[256,128]{1,0:T(8,128)S(1)} %add_pairs.35), channel_id=1, source_target_pairs={{0,8},{8,16},{16,24},{24,28},{28,20},{20,12},{12,4},{4,0},{1,9},{9... | collective-permute-start | bytes 393224 | tf_op jit(solution)/shard_map/ppermute | solution.py:526
  99.3 6.5 %collective-permute-start.43 = (f32[256,128]{1,0:T(8,128)S(1)}, f32[256,128]{1,0:T(8,128)S(1)}, u32[]{:S(2)}, u32[]{:S(2)}) collective-permute-start(f32[256,128]{1,0:T(8,128)S(1)} %add_pairs.30), channel_id=1, source_target_pairs={{0,8},{8,16},{16,24},{24,28},{28,20},{20,12},{12,4},{4,0},{1,9},{9... | collective-permute-start | bytes 393224 | tf_op jit(solution)/shard_map/ppermute | solution.py:526
  100.6 6.8 %collective-permute-start.51 = (f32[256,128]{1,0:T(8,128)S(1)}, f32[256,128]{1,0:T(8,128)S(1)}, u32[]{:S(2)}, u32[]{:S(2)}) collective-permute-start(f32[256,128]{1,0:T(8,128)S(1)} %add_pairs.36), channel_id=1, source_target_pairs={{0,8},{8,16},{16,24},{24,28},{28,20},{20,12},{12,4},{4,0},{1,9},{9... | collective-permute-start | bytes 393224 | tf_op jit(solution)/shard_map/ppermute | solution.py:526
  103.8 6.7 %collective-permute-start.55 = (f32[256,128]{1,0:T(8,128)S(1)}, f32[256,128]{1,0:T(8,128)S(1)}, u32[]{:S(2)}, u32[]{:S(2)}) collective-permute-start(f32[256,128]{1,0:T(8,128)S(1)} %add_pairs.39), channel_id=1, source_target_pairs={{8,0},{16,8},{24,16},{28,24},{20,28},{12,20},{4,12},{0,4},{9,1},{1... | collective-permute-start | bytes 393224 | tf_op jit(solution)/shard_map/ppermute | solution.py:529
  105.8 7.7 %collective-permute-start.44 = (f32[256,128]{1,0:T(8,128)S(1)}, f32[256,128]{1,0:T(8,128)S(1)}, u32[]{:S(2)}, u32[]{:S(2)}) collective-permute-start(f32[256,128]{1,0:T(8,128)S(1)} %add_pairs.31), channel_id=1, source_target_pairs={{0,8},{8,16},{16,24},{24,28},{28,20},{20,12},{12,4},{4,0},{1,9},{9... | collective-permute-start | bytes 393224 | tf_op jit(solution)/shard_map/ppermute | solution.py:526
  107.3 6.1 %collective-permute-start.52 = (f32[256,128]{1,0:T(8,128)S(1)}, f32[256,128]{1,0:T(8,128)S(1)}, u32[]{:S(2)}, u32[]{:S(2)}) collective-permute-start(f32[256,128]{1,0:T(8,128)S(1)} %add_pairs.37), channel_id=1, source_target_pairs={{0,8},{8,16},{16,24},{24,28},{28,20},{20,12},{12,4},{4,0},{1,9},{9... | collective-permute-start | bytes 393224 | tf_op jit(solution)/shard_map/ppermute | solution.py:526
  108.2 6.1 %collective-permute-start.48 = (f32[256,128]{1,0:T(8,128)S(1)}, f32[256,128]{1,0:T(8,128)S(1)}, u32[]{:S(2)}, u32[]{:S(2)}) collective-permute-start(f32[256,128]{1,0:T(8,128)S(1)} %add_pairs.34), channel_id=1, source_target_pairs={{8,0},{16,8},{24,16},{28,24},{20,28},{12,20},{4,12},{0,4},{9,1},{1... | collective-permute-start | bytes 393224 | tf_op jit(solution)/shard_map/ppermute | solution.py:529
  116.3 6.6 %collective-permute-start.66 = (f32[256,128]{1,0:T(8,128)S(1)}, f32[256,128]{1,0:T(8,128)S(1)}, u32[]{:S(2)}, u32[]{:S(2)}) collective-permute-start(f32[256,128]{1,0:T(8,128)S(1)} %get-tuple-element.126.refs_1_), channel_id=1, source_target_pairs={{0,8},{8,16},{16,24},{24,28},{28,20},{20,12},{12,4},{4,0},{1,9},{9... | collective-permute-start | bytes 393224 | tf_op jit(solution)/shard_map/ppermute | solution.py:526
  117.0 6.9 %collective-permute-start.60 = (f32[264,128]{1,0:T(8,128)S(1)}, f32[264,128]{1,0:T(8,128)S(1)}, u32[]{:S(2)}, u32[]{:S(2)}) collective-permute-start(f32[264,128]{1,0:T(8,128)S(1)} %get-tuple-element.124.refs_1_.refs_0_), channel_id=1, source_target_pairs={{0,8},{8,16},{16,24},{24,28},{28,20},{20,12},{12,4},{4,0},{1,9},{9... | collective-permute-start | bytes 405512 | tf_op jit(solution)/shard_map/ppermute | solution.py:526
  129.4 10.5 %collective-permute-start.62 = (f32[264,128]{1,0:T(8,128)S(1)}, f32[264,128]{1,0:T(8,128)S(1)}, u32[]{:S(2)}, u32[]{:S(2)}) collective-permute-start(f32[264,128]{1,0:T(8,128)S(1)} %collective-permute-done.61.refs_7_.refs_6_), channel_id=1, source_target_pairs={{0,8},{8,16},{16,24},{24,28},{28,20},{20,12},{12,4},{4,0},{1,9},{9... | collective-permute-start | bytes 405512 | tf_op jit(solution)/shard_map/ppermute | solution.py:526
  130.3 9.6 %collective-permute-start.59 = (f32[264,128]{1,0:T(8,128)S(1)}, f32[264,128]{1,0:T(8,128)S(1)}, u32[]{:S(2)}, u32[]{:S(2)}) collective-permute-start(f32[264,128]{1,0:T(8,128)S(1)} %collective-permute-done.58.refs_4_.refs_3_), channel_id=1, source_target_pairs={{8,0},{16,8},{24,16},{28,24},{20,28},{12,20},{4,12},{0,4},{9,1},{1... | collective-permute-start | bytes 405512 | tf_op jit(solution)/shard_map/ppermute | solution.py:529
  (25 other events, 127.7 us)

commit v4 on v3

--- a/solution.py
+++ b/solution.py
@@ -347,38 +347,40 @@
     return out[0], out[1], out[2], out[3], out[4:]
 
 
-def store_state(h, field, drive, bases, kkt, state):
-    bound, width = field.shape
+def store_state(fields, drives, bases, kkt):
+    bound, width = fields[0].shape
     rows = kkt.shape[0]
     step = bases[0].shape[0]
-    cols = slice(h * width, (h + 1) * width)
-    given = 0 if state is None else 1
     rest = bases[bound // step :]
 
-    def body(field_ref, drive_ref, kkt_ref, *refs):
-        base_refs, (state_hbm, rest_ref, sem) = refs[: len(rest)], refs[len(rest) + given :]
+    def body(*refs):
+        field_refs, drive_refs, kkt_ref, refs = refs[:HALVES], refs[HALVES : 2 * HALVES], refs[2 * HALVES], refs[2 * HALVES + 1 :]
+        base_refs, (state_hbm, rest_ref, sem) = refs[: len(rest)], refs[len(rest) :]
         loads = Loads(sem)
-        loads.start("field", field_ref, state_hbm.at[:bound, cols])
-        for i in range(len(rest)):
-            at = slice(i * step, (i + 1) * step)
-            there = slice(bound + i * step, bound + (i + 1) * step)
-            got = jnp.dot(kkt_ref[there, :bound], drive_ref[:bound, :], preferred_element_type=jnp.float32)
-            rest_ref[at, :] = base_refs[i][:, cols] + got
-        loads.start("rest", rest_ref, state_hbm.at[bound:, cols])
-        loads.wait("field")
+        for h in range(HALVES):
+            cols = slice(h * width, (h + 1) * width)
+            loads.start(h, field_refs[h], state_hbm.at[:bound, cols])
+        for h in range(HALVES):
+            cols = slice(h * width, (h + 1) * width)
+            for i in range(len(rest)):
+                at = slice(i * step, (i + 1) * step)
+                there = slice(bound + i * step, bound + (i + 1) * step)
+                got = jnp.dot(kkt_ref[there, :bound], drive_refs[h][:bound, :], preferred_element_type=jnp.float32)
+                rest_ref[at, cols] = base_refs[i][:, cols] + got
+        loads.start("rest", rest_ref, state_hbm.at[bound:, :])
+        for h in range(HALVES):
+            loads.wait(h)
         loads.wait("rest")
 
-    before = () if state is None else (state,)
     return call(
         body,
         "store_state",
-        (field, drive, kkt, *rest, *before),
-        [VMEM] * (3 + len(rest)) + [HBM] * given,
+        (*fields, *drives, kkt, *rest),
+        [VMEM] * (2 * HALVES + 1 + len(rest)),
         f32(rows, HALVES * width),
         HBM,
-        [pltpu.VMEM((rows - bound, width), jnp.float32), pltpu.SemaphoreType.DMA((2,))],
-        aliases={3 + len(rest): 0} if given else None,
-        flops=2 * bound * (rows - bound) * width,
+        [pltpu.VMEM((rows - bound, HALVES * width), jnp.float32), pltpu.SemaphoreType.DMA((HALVES + 1,))],
+        flops=2 * bound * (rows - bound) * HALVES * width,
         moved=4 << 20,
     )
 
@@ -451,37 +453,39 @@
     return call(body, "renew", ins, [VMEM] * len(ins), outs, [VMEM] * len(outs))
 
 
-def finish(h, table, pieces, z, scen, owned, outputs):
-    peers = len(pieces)
-    bound, width = z.shape[0] - BLOCK, z.shape[1]
-    cols = slice(h * width, (h + 1) * width)
+def finish(table, pieces, zs, owned):
+    peers = len(pieces[0])
+    bound, width = zs[0].shape[0] - BLOCK, zs[0].shape[1]
     own = owned * BLOCK
-    given = len(outputs)
 
     def body(*refs):
         table_ref, refs = refs[0], refs[1:]
-        piece, z_ref, refs = refs[:peers], refs[peers], refs[peers + 1 + given :]
-        dual_hbm, cons_hbm, dual_ref, sem = refs
+        halves, refs = [refs[h * peers : (h + 1) * peers] for h in range(HALVES)], refs[HALVES * peers :]
+        z_refs, (dual_hbm, cons_hbm, dual_ref, sem) = refs[:HALVES], refs[HALVES:]
         loads = Loads(sem)
-        loads.start("cons", piece[0].at[:own, :], cons_hbm.at[:, cols])
-        dual_ref[:bound, :] = z_ref[:bound, :]
-        for r, slots in enumerate(slots_of(table_ref, peers, bound // BLOCK)):
-            for read, write, block, _ in slots:
-                dual_ref[write, :] = z_ref[read, :] - piece[r][block, :]
-        loads.start("dual", dual_ref.at[:bound, :], dual_hbm.at[:, cols])
-        loads.wait("dual")
-        loads.wait("cons")
-
+        slots = slots_of(table_ref, peers, bound // BLOCK)
+        for h in range(HALVES):
+            cols = slice(h * width, (h + 1) * width)
+            loads.start(("cons", h), halves[h][0].at[:own, :], cons_hbm.at[:, cols])
+            dual_ref[:bound, cols] = z_refs[h][:bound, :]
+            for r in range(peers):
+                for read, write, block, _ in slots[r]:
+                    dual_ref[write, cols] = z_refs[h][read, :] - halves[h][r][block, :]
+        loads.start("dual", dual_ref.at[:bound, :], dual_hbm)
+        for name in list(loads.flying):
+            loads.wait(name)
+
+    scen = HALVES * width
     return call(
         body,
         "finish",
-        (table, *pieces, z, *outputs),
-        [SMEM] + [VMEM] * (peers + 1) + [HBM] * given,
+        (table, *[piece for half in pieces for piece in half], *zs),
+        [SMEM] + [VMEM] * (HALVES * (peers + 1)),
         [f32(bound, scen), f32(own, scen)],
         [HBM] * 2,
-        [pltpu.VMEM((bound + BLOCK, width), jnp.float32), pltpu.SemaphoreType.DMA((2,))],
-        aliases={peers + 2: 0, peers + 3: 1} if given else None,
+        [pltpu.VMEM((bound + BLOCK, scen), jnp.float32), pltpu.SemaphoreType.DMA((1 + HALVES,))],
         moved=3 << 20,
+        room=14,
     )
 
 
@@ -581,7 +585,7 @@
             some.append(bases[-1])
         return tie(values, [], some) if some else values
 
-    known = {"state": None, "outputs": (), "count": None, "norms": []}
+    known = {"count": None, "norms": [], "solved": [], "last": []}
 
     def half(h):
         last = h == HALVES - 1
@@ -594,15 +598,13 @@
             known["count"] = out[2]
         pieces = yield from gather(h, averages)
         field, drive, z, gaps, parts = second_solve(h, table, pieces, z, dual, bases, kkt, owned)
-        known["state"] = store_state(h, field, drive, bases, kkt, known["state"])
+        known["solved"].append((field, drive))
         arrived = yield from scatter(h, parts)
         norms = known["norms"] + [gaps, moved]
         out = renew(h, arrived, averages, known["count"], norms if last else ())
         known["norms"] = norms + [out[1]]
         pieces = yield from gather(h, out[0])
-        if last:
-            known["tail"] = sum_tails(pieces, owned * BLOCK, [*known["outputs"], known["state"]])
-        known["outputs"] = finish(h, table, pieces, z, scen, owned, known["outputs"])
+        known["last"].append((pieces, z))
 
     turns = [half(h) for h in range(HALVES)]
     waiting = [next(turn) for turn in turns]
@@ -614,10 +616,13 @@
             waiting[h] = turns[h].send(values)
         except StopIteration:
             waiting[h] = None
-    tail = known["tail"]
+    fields, drives = zip(*known["solved"])
+    state = store_state(fields, drives, bases, kkt)
+    pieces, zs = zip(*known["last"])
+    tail = sum_tails(pieces[-1], owned * BLOCK, [state])
     turned = [lax.ppermute(tail, "sub", [(i, (i + k) % subs) for i in range(subs)]) for k in range(1, subs)]
     norms = norm_table([tail, *turned], float(peers * subs * scen * BLOCK))
-    return (known["state"], *known["outputs"], norms)
+    return (state, *finish(table, pieces, zs, owned), norms)
 
 
 def next_turn(waiting, h):

time: 146 us -> 142 us (0.973)
  waiting for transfers between devices: 37.2 us -> 35 us
  Pallas kernels: 26.5 us -> 24.6 us
    ppermute x35, starting transfers between devices: 42.2 us -> 46.8 us  [forward(): return lax.ppermute(x, 'region', ahead)]
    ppermute x35, waiting for transfers between devices: 15.7 us -> 11.2 us  [forward(): return lax.ppermute(x, 'region', ahead)]
    ppermute x35, starting transfers between devices: 35.3 us -> 31.5 us  [backward(): return lax.ppermute(x, 'region', behind)]
    ppermute x35, waiting for transfers between devices: 21.6 us -> 23.7 us  [backward(): return lax.ppermute(x, 'region', behind)]
    pallas_call x43 -> x41, Pallas kernels: 26.5 us -> 24.6 us  [call(): pl.pallas_call(body, name=name, out_shape=shapes if many else shapes[0],...]
  transfers between devices with their start and end apart: 73 -> 73, of which waited for: 35 -> 32; matrix products, arithmetic and copies ran while one was open for 0% -> 0% of each run, Pallas kernels for 17% -> 16%
where the time goes in v4:
time: 142 us
  starting transfers between devices  81.4 us (57%)
  waiting for transfers between devices  35 us (25%)
  Pallas kernels  24.6 us (17%)
    ppermute x35, starting transfers between devices, forward(): return lax.ppermute(x, 'region', ahead)  46.8 us
    ppermute x35, starting transfers between devices, backward(): return lax.ppermute(x, 'region', behind)  31.5 us
    pallas_call x41, Pallas kernels, call(): pl.pallas_call(body, name=name, out_shape=shapes if many else shapes[0],...  24.6 us
    ppermute x35, waiting for transfers between devices, backward(): return lax.ppermute(x, 'region', behind)  23.7 us
    ppermute x35, waiting for transfers between devices, forward(): return lax.ppermute(x, 'region', ahead)  11.2 us
    ppermute x3, starting transfers between devices, shards(): lax.ppermute(tail, 'sub', [(i, (i + k) % subs) for i in range(subs)])  3.03 us
  transfers between devices with their start and end apart: 73, of which 32 were waited for; matrix products, arithmetic and copies ran while one was open for 0% of the time, Pallas kernels for 16%

profile of v4, /device:TPU:0, one launch (start us, length us, event | category | flops | bytes accessed | tf_op | source)
XLA Modules:
  0.0 142.0 jit_solution(15045622273828545398)
XLA Ops:
  1.6 3.1 %collective-permute-start.1 = (f32[256,128]{1,0:T(8,128)S(1)}, f32[256,128]{1,0:T(8,128)S(1)}, u32[]{:S(2)}, u32[]{:S(2)}) collective-permute-start(f32[256,128]{1,0:T(8,128)S(1)} %get-tuple-element.67.refs_1_.refs_3_), channel_id=1, source_target_pairs={{0,8},{8,16},{16,24},{24,28},{28,20},{20,12},{12,4},{4,0},{1,9},{9... | collective-permute-start | bytes 393224 | tf_op jit(solution)/shard_map/ppermute | solution.py:530
  4.7 1.9 %collective-permute-start.21 = (f32[256,128]{1,0:T(8,128)S(1)}, f32[256,128]{1,0:T(8,128)S(1)}, u32[]{:S(2)}, u32[]{:S(2)}) collective-permute-start(f32[256,128]{1,0:T(8,128)S(1)} %get-tuple-element.86.refs_1_.refs_3_), channel_id=1, source_target_pairs={{8,0},{16,8},{24,16},{28,24},{20,28},{12,20},{4,12},{0,4},{9,1},{1... | collective-permute-start | bytes 393224 | tf_op jit(solution)/shard_map/ppermute | solution.py:533
  6.6 4.9 %prepare.1 = (s32[32]{0:T(128)S(1)}, bf16[2048,2048]{1,0:T(8,128)(2,1)S(1)}, bf16[2048,256]{1,0:T(8,128)(2,1)S(1)}, f32[1536,256]{1,0:T(8,128)S(1)}) custom-call(s32[1]{0:T(128)} %bitcast.region_ref, s32[1,12]{1,0:T(1,128)} %target_hbm.1, bf16[2048,2048]{1,0:T(8,128)(2,1)} %refs_0_.1, bf16[2048,256]{1,0:T(8,128)(2,1)} %refs_1_.1, f32[1536,256]{1,0:T(8,128)} %refs_2_.1), custom_call_target="tpu_custom_call" | custom-call | bytes 12582912 | tf_op jit(solution)/shard_map/prepare/pallas_call | solution.py:63
  17.7 1.7 %collective-permute-start.5 = (f32[256,128]{1,0:T(8,128)S(1)}, f32[256,128]{1,0:T(8,128)S(1)}, u32[]{:S(2)}, u32[]{:S(2)}) collective-permute-start(f32[256,128]{1,0:T(8,128)S(1)} %get-tuple-element.74), channel_id=1, source_target_pairs={{0,8},{8,16},{16,24},{24,28},{28,20},{20,12},{12,4},{4,0},{1,9},{9... | collective-permute-start | bytes 393224 | tf_op jit(solution)/shard_map/ppermute | solution.py:530
  23.5 1.6 %collective-permute-start.4 = (f32[256,128]{1,0:T(8,128)S(1)}, f32[256,128]{1,0:T(8,128)S(1)}, u32[]{:S(2)}, u32[]{:S(2)}) collective-permute-start(f32[256,128]{1,0:T(8,128)S(1)} %get-tuple-element.73), channel_id=1, source_target_pairs={{8,0},{16,8},{24,16},{28,24},{20,28},{12,20},{4,12},{0,4},{9,1},{1... | collective-permute-start | bytes 393224 | tf_op jit(solution)/shard_map/ppermute | solution.py:533
  25.9 1.5 %collective-permute-start.27 = (f32[256,128]{1,0:T(8,128)S(1)}, f32[256,128]{1,0:T(8,128)S(1)}, u32[]{:S(2)}, u32[]{:S(2)}) collective-permute-start(f32[256,128]{1,0:T(8,128)S(1)} %collective-permute-done.26.refs_7_), channel_id=1, source_target_pairs={{0,8},{8,16},{16,24},{24,28},{28,20},{20,12},{12,4},{4,0},{1,9},{9... | collective-permute-start | bytes 393224 | tf_op jit(solution)/shard_map/ppermute | solution.py:530
  28.8 1.4 collective-permute-done.6.refs_5_
  30.2 2.3 %first_solve.2 = (f32[1536,128]{1,0:T(8,128)S(1)}, f32[264,128]{1,0:T(8,128)S(1)}, f32[264,128]{1,0:T(8,128)S(1)}, f32[264,128]{1,0:T(8,128)S(1)}, f32[264,128]{...) custom-call(s32[32]{0:T(128)S(1)} %get-tuple-element.66.refs_0_, ...), custom_call_target="tpu_custom_call" | custom-call | flops 603979776 | bytes 8388608 | tf_op jit(solution)/shard_map/first_solve/pallas_call | solution.py:63
  33.0 2.3 %first_solve.3 = (f32[1536,128]{1,0:T(8,128)S(1)}, f32[256,128]{1,0:T(8,128)S(1)}, f32[256,128]{1,0:T(8,128)S(1)}, f32[256,128]{1,0:T(8,128)S(1)}, f32[256,128]{...) custom-call(s32[32]{0:T(128)S(1)} %get-tuple-element.66.refs_0_, ...), custom_call_target="tpu_custom_call" | custom-call | flops 603979776 | bytes 8388608 | tf_op jit(solution)/shard_map/first_solve/pallas_call | solution.py:63
  35.3 1.6 %collective-permute-start.31 = (f32[256,128]{1,0:T(8,128)S(1)}, f32[256,128]{1,0:T(8,128)S(1)}, u32[]{:S(2)}, u32[]{:S(2)}) collective-permute-start(f32[256,128]{1,0:T(8,128)S(1)} %get-tuple-element.91), channel_id=1, source_target_pairs={{8,0},{16,8},{24,16},{28,24},{20,28},{12,20},{4,12},{0,4},{9,1},{1... | collective-permute-start | bytes 393224 | tf_op jit(solution)/shard_map/ppermute | solution.py:533
  36.9 1.6 %collective-permute-start.11 = (f32[264,128]{1,0:T(8,128)S(1)}, f32[264,128]{1,0:T(8,128)S(1)}, u32[]{:S(2)}, u32[]{:S(2)}) collective-permute-start(f32[264,128]{1,0:T(8,128)S(1)} %get-tuple-element.80), channel_id=1, source_target_pairs={{8,0},{16,8},{24,16},{28,24},{20,28},{12,20},{4,12},{0,4},{9,1},{1... | collective-permute-start | bytes 405512 | tf_op jit(solution)/shard_map/ppermute | solution.py:533
  40.1 1.6 %collective-permute-done.31.refs_0_ = f32[256,128]{1,0:T(8,128)S(1)} collective-permute-done((f32[256,128]{1,0:T(8,128)S(1)}, f32[256,128]{1,0:T(8,128)S(1)}, u32[]{:S(2)}, u32[]{:S(2)}) %collective-permute-start.31) | collective-permute-done | bytes 131104 | tf_op jit(solution)/shard_map/ppermute | solution.py:533
  41.7 1.7 %collective-permute-start.32 = (f32[256,128]{1,0:T(8,128)S(1)}, f32[256,128]{1,0:T(8,128)S(1)}, u32[]{:S(2)}, u32[]{:S(2)}) collective-permute-start(f32[256,128]{1,0:T(8,128)S(1)} %add_pairs.27), channel_id=1, source_target_pairs={{8,0},{16,8},{24,16},{28,24},{20,28},{12,20},{4,12},{0,4},{9,1},{1... | collective-permute-start | bytes 393224 | tf_op jit(solution)/shard_map/ppermute | solution.py:533
  45.3 1.4 collective-permute-start.9
  48.1 2.0 %collective-permute-start.33 = (f32[256,128]{1,0:T(8,128)S(1)}, f32[256,128]{1,0:T(8,128)S(1)}, u32[]{:S(2)}, u32[]{:S(2)}) collective-permute-start(f32[256,128]{1,0:T(8,128)S(1)} %add_pairs.28), channel_id=1, source_target_pairs={{8,0},{16,8},{24,16},{28,24},{20,28},{12,20},{4,12},{0,4},{9,1},{1... | collective-permute-start | bytes 393224 | tf_op jit(solution)/shard_map/ppermute | solution.py:533
  50.1 1.6 %collective-permute-start.13 = (f32[264,128]{1,0:T(8,128)S(1)}, f32[264,128]{1,0:T(8,128)S(1)}, u32[]{:S(2)}, u32[]{:S(2)}) collective-permute-start(f32[264,128]{1,0:T(8,128)S(1)} %add_pairs.24), channel_id=1, source_target_pairs={{8,0},{16,8},{24,16},{28,24},{20,28},{12,20},{4,12},{0,4},{9,1},{1... | collective-permute-start | bytes 405512 | tf_op jit(solution)/shard_map/ppermute | solution.py:533
  51.8 1.4 %collective-permute-start.10 = (f32[264,128]{1,0:T(8,128)S(1)}, f32[264,128]{1,0:T(8,128)S(1)}, u32[]{:S(2)}, u32[]{:S(2)}) collective-permute-start(f32[264,128]{1,0:T(8,128)S(1)} %add_pairs.22), channel_id=1, source_target_pairs={{0,8},{8,16},{16,24},{24,28},{28,20},{20,12},{12,4},{4,0},{1,9},{9... | collective-permute-start | bytes 405512 | tf_op jit(solution)/shard_map/ppermute | solution.py:530
  54.5 1.3 collective-permute-start.30
  56.9 1.4 %collective-permute-start.17 = (f32[256,128]{1,0:T(8,128)S(1)}, f32[256,128]{1,0:T(8,128)S(1)}, u32[]{:S(2)}, u32[]{:S(2)}) collective-permute-start(f32[256,128]{1,0:T(8,128)S(1)} %get-tuple-element.83.refs_1_.refs_3_), channel_id=1, source_target_pairs={{0,8},{8,16},{16,24},{24,28},{28,20},{20,12},{12,4},{4,0},{1,9},{9... | collective-permute-start | bytes 393224 | tf_op jit(solution)/shard_map/ppermute | solution.py:530
  58.4 2.5 %collective-permute-done.30.refs_1_ = f32[256,128]{1,0:T(8,128)S(1)} collective-permute-done((f32[256,128]{1,0:T(8,128)S(1)}, f32[256,128]{1,0:T(8,128)S(1)}, u32[]{:S(2)}, u32[]{:S(2)}) %collective-permute-start.30) | collective-permute-done | bytes 131104 | tf_op jit(solution)/shard_map/ppermute | solution.py:530
  60.9 1.4 collective-permute-done.34.refs_2_
  62.5 1.8 %collective-permute-start.14 = (f32[256,128]{1,0:T(8,128)S(1)}, f32[256,128]{1,0:T(8,128)S(1)}, u32[]{:S(2)}, u32[]{:S(2)}) collective-permute-start(f32[256,128]{1,0:T(8,128)S(1)} %get-tuple-element.83.refs_1_.refs_3_), channel_id=1, source_target_pairs={{8,0},{16,8},{24,16},{28,24},{20,28},{12,20},{4,12},{0,4},{9,1},{1... | collective-permute-start | bytes 393224 | tf_op jit(solution)/shard_map/ppermute | solution.py:533
  65.0 1.4 collective-permute-start.39
  66.4 2.3 %collective-permute-done.35.refs_2_ = f32[256,128]{1,0:T(8,128)S(1)} collective-permute-done((f32[256,128]{1,0:T(8,128)S(1)}, f32[256,128]{1,0:T(8,128)S(1)}, u32[]{:S(2)}, u32[]{:S(2)}) %collective-permute-start.35) | collective-permute-done | bytes 131104 | tf_op jit(solution)/shard_map/ppermute | solution.py:533
  68.7 2.8 %collective-permute-done.14.refs_2_ = f32[256,128]{1,0:T(8,128)S(1)} collective-permute-done((f32[256,128]{1,0:T(8,128)S(1)}, f32[256,128]{1,0:T(8,128)S(1)}, u32[]{:S(2)}, u32[]{:S(2)}) %collective-permute-start.14) | collective-permute-done | bytes 131104 | tf_op jit(solution)/shard_map/ppermute | solution.py:533
  71.5 2.0 %collective-permute-start.19 = (f32[256,128]{1,0:T(8,128)S(1)}, f32[256,128]{1,0:T(8,128)S(1)}, u32[]{:S(2)}, u32[]{:S(2)}) collective-permute-start(f32[256,128]{1,0:T(8,128)S(1)} %collective-permute-done.18.refs_7_), channel_id=1, source_target_pairs={{0,8},{8,16},{16,24},{24,28},{28,20},{20,12},{12,4},{4,0},{1,9},{9... | collective-permute-start | bytes 393224 | tf_op jit(solution)/shard_map/ppermute | solution.py:530
  77.2 2.5 %collective-permute-start.20 = (f32[256,128]{1,0:T(8,128)S(1)}, f32[256,128]{1,0:T(8,128)S(1)}, u32[]{:S(2)}, u32[]{:S(2)}) collective-permute-start(f32[256,128]{1,0:T(8,128)S(1)} %collective-permute-done.19.refs_6_), channel_id=1, source_target_pairs={{0,8},{8,16},{16,24},{24,28},{28,20},{20,12},{12,4},{4,0},{1,9},{9... | collective-permute-start | bytes 393224 | tf_op jit(solution)/shard_map/ppermute | solution.py:530
  79.7 1.4 collective-permute-start.41
  83.5 2.7 %second_solve.2 = (f32[1536,128]{1,0:T(8,128)S(1)}, bf16[1664,128]{1,0:T(8,128)(2,1)S(1)}, f32[1664,128]{1,0:T(8,128)S(1)}, f32[16,128]{1,0:T(8,128)S(1)}, f32[2...) custom-call(s32[32]{0:T(128)S(1)} %get-tuple-element.66.refs_0_, ...), custom_call_target="tpu_custom_call" | custom-call | flops 603979776 | bytes 8388608 | tf_op jit(solution)/shard_map/second_solve/pallas_call | solution.py:63
  86.2 2.1 %collective-permute-start.42 = (f32[256,128]{1,0:T(8,128)S(1)}, f32[256,128]{1,0:T(8,128)S(1)}, u32[]{:S(2)}, u32[]{:S(2)}) collective-permute-start(f32[256,128]{1,0:T(8,128)S(1)} %get-tuple-element.102), channel_id=1, source_target_pairs={{0,8},{8,16},{16,24},{24,28},{28,20},{20,12},{12,4},{4,0},{1,9},{9... | collective-permute-start | bytes 393224 | tf_op jit(solution)/shard_map/ppermute | solution.py:530
  88.3 2.7 %second_solve.3 = (f32[1536,128]{1,0:T(8,128)S(1)}, bf16[1664,128]{1,0:T(8,128)(2,1)S(1)}, f32[1664,128]{1,0:T(8,128)S(1)}, f32[16,128]{1,0:T(8,128)S(1)}, f32[2...) custom-call(s32[32]{0:T(128)S(1)} %get-tuple-element.66.refs_0_, ...), custom_call_target="tpu_custom_call" | custom-call | flops 603979776 | bytes 8388608 | tf_op jit(solution)/shard_map/second_solve/pallas_call | solution.py:63
  91.0 2.0 %collective-permute-start.56 = (f32[256,128]{1,0:T(8,128)S(1)}, f32[256,128]{1,0:T(8,128)S(1)}, u32[]{:S(2)}, u32[]{:S(2)}) collective-permute-start(f32[256,128]{1,0:T(8,128)S(1)} %get-tuple-element.111), channel_id=1, source_target_pairs={{0,8},{8,16},{16,24},{24,28},{28,20},{20,12},{12,4},{4,0},{1,9},{9... | collective-permute-start | bytes 393224 | tf_op jit(solution)/shard_map/ppermute | solution.py:530
  93.1 2.0 %collective-permute-start.43 = (f32[256,128]{1,0:T(8,128)S(1)}, f32[256,128]{1,0:T(8,128)S(1)}, u32[]{:S(2)}, u32[]{:S(2)}) collective-permute-start(f32[256,128]{1,0:T(8,128)S(1)} %add_pairs.30), channel_id=1, source_target_pairs={{0,8},{8,16},{16,24},{24,28},{28,20},{20,12},{12,4},{4,0},{1,9},{9... | collective-permute-start | bytes 393224 | tf_op jit(solution)/shard_map/ppermute | solution.py:530
  95.1 1.8 %collective-permute-done.59.refs_0_ = f32[256,128]{1,0:T(8,128)S(1)} collective-permute-done((f32[256,128]{1,0:T(8,128)S(1)}, f32[256,128]{1,0:T(8,128)S(1)}, u32[]{:S(2)}, u32[]{:S(2)}) %collective-permute-start.59) | collective-permute-done | bytes 131104 | tf_op jit(solution)/shard_map/ppermute | solution.py:533
  97.3 1.8 %collective-permute-start.57 = (f32[256,128]{1,0:T(8,128)S(1)}, f32[256,128]{1,0:T(8,128)S(1)}, u32[]{:S(2)}, u32[]{:S(2)}) collective-permute-start(f32[256,128]{1,0:T(8,128)S(1)} %add_pairs.35), channel_id=1, source_target_pairs={{0,8},{8,16},{16,24},{24,28},{28,20},{20,12},{12,4},{4,0},{1,9},{9... | collective-permute-start | bytes 393224 | tf_op jit(solution)/shard_map/ppermute | solution.py:530
  99.5 1.8 %collective-permute-start.44 = (f32[256,128]{1,0:T(8,128)S(1)}, f32[256,128]{1,0:T(8,128)S(1)}, u32[]{:S(2)}, u32[]{:S(2)}) collective-permute-start(f32[256,128]{1,0:T(8,128)S(1)} %add_pairs.31), channel_id=1, source_target_pairs={{0,8},{8,16},{16,24},{24,28},{28,20},{20,12},{12,4},{4,0},{1,9},{9... | collective-permute-start | bytes 393224 | tf_op jit(solution)/shard_map/ppermute | solution.py:530
  101.3 1.5 %collective-permute-done.60.refs_0_ = f32[256,128]{1,0:T(8,128)S(1)} collective-permute-done((f32[256,128]{1,0:T(8,128)S(1)}, f32[256,128]{1,0:T(8,128)S(1)}, u32[]{:S(2)}, u32[]{:S(2)}) %collective-permute-start.60) | collective-permute-done | bytes 131104 | tf_op jit(solution)/shard_map/ppermute | solution.py:533
  103.8 1.8 %collective-permute-start.58 = (f32[256,128]{1,0:T(8,128)S(1)}, f32[256,128]{1,0:T(8,128)S(1)}, u32[]{:S(2)}, u32[]{:S(2)}) collective-permute-start(f32[256,128]{1,0:T(8,128)S(1)} %add_pairs.36), channel_id=1, source_target_pairs={{0,8},{8,16},{16,24},{24,28},{28,20},{20,12},{12,4},{4,0},{1,9},{9... | collective-permute-start | bytes 393224 | tf_op jit(solution)/shard_map/ppermute | solution.py:530
  106.3 1.4 collective-permute-start.45
  107.7 1.4 collective-permute-done.61.refs_0_
  110.1 1.6 %collective-permute-done.48.refs_2_ = f32[256,128]{1,0:T(8,128)S(1)} collective-permute-done((f32[256,128]{1,0:T(8,128)S(1)}, f32[256,128]{1,0:T(8,128)S(1)}, u32[]{:S(2)}, u32[]{:S(2)}) %collective-permute-start.48) | collective-permute-done | bytes 131104 | tf_op jit(solution)/shard_map/ppermute | solution.py:533
  112.7 2.2 %collective-permute-done.62.refs_2_ = f32[256,128]{1,0:T(8,128)S(1)} collective-permute-done((f32[256,128]{1,0:T(8,128)S(1)}, f32[256,128]{1,0:T(8,128)S(1)}, u32[]{:S(2)}, u32[]{:S(2)}) %collective-permute-start.62) | collective-permute-done | bytes 131104 | tf_op jit(solution)/shard_map/ppermute | solution.py:533
  117.6 1.9 %collective-permute-start.67 = (f32[264,128]{1,0:T(8,128)S(1)}, f32[264,128]{1,0:T(8,128)S(1)}, u32[]{:S(2)}, u32[]{:S(2)}) collective-permute-start(f32[264,128]{1,0:T(8,128)S(1)} %get-tuple-element.123.refs_9_.refs_0_), channel_id=1, source_target_pairs={{0,8},{8,16},{16,24},{24,28},{28,20},{20,12},{12,4},{4,0},{1,9},{9... | collective-permute-start | bytes 405512 | tf_op jit(solution)/shard_map/ppermute | solution.py:530
  121.7 1.6 %collective-permute-start.49 = (f32[256,128]{1,0:T(8,128)S(1)}, f32[256,128]{1,0:T(8,128)S(1)}, u32[]{:S(2)}, u32[]{:S(2)}) collective-permute-start(f32[256,128]{1,0:T(8,128)S(1)} %get-tuple-element.109.refs_1_), channel_id=1, source_target_pairs={{8,0},{16,8},{24,16},{28,24},{20,28},{12,20},{4,12},{0,4},{9,1},{1... | collective-permute-start | bytes 393224 | tf_op jit(solution)/shard_map/ppermute | solution.py:533
  134.2 1.8 %store_state.1.refs_8_ = f32[2048,256]{1,0:T(8,128)} custom-call(f32[1536,128]{1,0:T(8,128)S(1)} %get-tuple-element.85.refs_0_, f32[1536,128]{1,0:T(8,128)S(1)} %get-tuple-element.98.refs_1_, bf16[1664,128]{1,0:T(8,128)(2,1)S(1)} %get-tuple-element.99.refs_2_, bf16[1664,128]{1,0:T(8,128)(2,1)S(1)} %get-tuple-element.100.refs_3_, ...), custom_call_target="tpu_custom_call" | custom-call | flops 402653184 | bytes 4194304 | tf_op jit(solution)/shard_map/store_state/pallas_call | solution.py:63
  136.1 1.6 %collective-permute-start.71 = (f32[8,128]{1,0:T(8,128)S(1)}, f32[8,128]{1,0:T(8,128)S(1)}, u32[]{:S(2)}, u32[]{:S(2)}) collective-permute-start(f32[8,128]{1,0:T(8,128)S(1)} %sum_tails.1.refs_0_), channel_id=1, source_target_pairs={{0,2},{1,3},{2,0},{3,1},{4,6},{5,7},{6,4},{7,5},{8,10},{9,11},{10,... | collective-permute-start | bytes 12296 | tf_op jit(solution)/shard_map/ppermute | solution.py:623
  137.7 1.4 collective-permute-start.72
  139.1 2.2 %finish.1 = (f32[1536,256]{1,0:T(8,128)}, f32[256,256]{1,0:T(8,128)}) custom-call(s32[32]{0:T(128)S(1)} %get-tuple-element.66.refs_0_, f32[256,128]{1,0:T(8,128)S(1)} %get-tuple-element.109.refs_1_, f32[256,128]{1,0:T(8,128)S(1)} %collective-permute-done.49.refs_2_, f32[256,128]{1,0:T(8,128)S(1)} %collective-permute-done.50.refs_3_, ...), custom_call_target="tpu_custom_call" | custom-call | bytes 3145728 | tf_op jit(solution)/shard_map/finish/pallas_call | solution.py:63
  (144 shorter events, 49.2 us)
Async XLA Ops:
  1.6 9.9 %collective-permute-start.1 = (f32[256,128]{1,0:T(8,128)S(1)}, f32[256,128]{1,0:T(8,128)S(1)}, u32[]{:S(2)}, u32[]{:S(2)}) collective-permute-start(f32[256,128]{1,0:T(8,128)S(1)} %get-tuple-element.67.refs_1_.refs_3_), channel_id=1, source_target_pairs={{0,8},{8,16},{16,24},{24,28},{28,20},{20,12},{12,4},{4,0},{1,9},{9... | collective-permute-start | bytes 393224 | tf_op jit(solution)/shard_map/ppermute | solution.py:530
  4.7 6.9 %collective-permute-start = (f32[256,128]{1,0:T(8,128)S(1)}, f32[256,128]{1,0:T(8,128)S(1)}, u32[]{:S(2)}, u32[]{:S(2)}) collective-permute-start(f32[256,128]{1,0:T(8,128)S(1)} %get-tuple-element.67.refs_1_.refs_3_), channel_id=1, source_target_pairs={{8,0},{16,8},{24,16},{28,24},{20,28},{12,20},{4,12},{0,4},{9,1},{1... | collective-permute-start | bytes 393224 | tf_op jit(solution)/shard_map/ppermute | solution.py:533
  4.7 10.0 %collective-permute-start.21 = (f32[256,128]{1,0:T(8,128)S(1)}, f32[256,128]{1,0:T(8,128)S(1)}, u32[]{:S(2)}, u32[]{:S(2)}) collective-permute-start(f32[256,128]{1,0:T(8,128)S(1)} %get-tuple-element.86.refs_1_.refs_3_), channel_id=1, source_target_pairs={{8,0},{16,8},{24,16},{28,24},{20,28},{12,20},{4,12},{0,4},{9,1},{1... | collective-permute-start | bytes 393224 | tf_op jit(solution)/shard_map/ppermute | solution.py:533
  13.7 6.3 %collective-permute-start.25 = (f32[256,128]{1,0:T(8,128)S(1)}, f32[256,128]{1,0:T(8,128)S(1)}, u32[]{:S(2)}, u32[]{:S(2)}) collective-permute-start(f32[256,128]{1,0:T(8,128)S(1)} %get-tuple-element.86.refs_1_.refs_3_), channel_id=1, source_target_pairs={{0,8},{8,16},{16,24},{24,28},{28,20},{20,12},{12,4},{4,0},{1,9},{9... | collective-permute-start | bytes 393224 | tf_op jit(solution)/shard_map/ppermute | solution.py:530
  14.7 6.3 %collective-permute-start.22 = (f32[256,128]{1,0:T(8,128)S(1)}, f32[256,128]{1,0:T(8,128)S(1)}, u32[]{:S(2)}, u32[]{:S(2)}) collective-permute-start(f32[256,128]{1,0:T(8,128)S(1)} %collective-permute-done.21.refs_2_), channel_id=1, source_target_pairs={{8,0},{16,8},{24,16},{28,24},{20,28},{12,20},{4,12},{0,4},{9,1},{1... | collective-permute-start | bytes 393224 | tf_op jit(solution)/shard_map/ppermute | solution.py:533
  17.7 7.4 %collective-permute-start.5 = (f32[256,128]{1,0:T(8,128)S(1)}, f32[256,128]{1,0:T(8,128)S(1)}, u32[]{:S(2)}, u32[]{:S(2)}) collective-permute-start(f32[256,128]{1,0:T(8,128)S(1)} %get-tuple-element.74), channel_id=1, source_target_pairs={{0,8},{8,16},{16,24},{24,28},{28,20},{20,12},{12,4},{4,0},{1,9},{9... | collective-permute-start | bytes 393224 | tf_op jit(solution)/shard_map/ppermute | solution.py:530
  21.0 6.3 %collective-permute-start.23 = (f32[256,128]{1,0:T(8,128)S(1)}, f32[256,128]{1,0:T(8,128)S(1)}, u32[]{:S(2)}, u32[]{:S(2)}) collective-permute-start(f32[256,128]{1,0:T(8,128)S(1)} %collective-permute-done.22.refs_3_), channel_id=1, source_target_pairs={{8,0},{16,8},{24,16},{28,24},{20,28},{12,20},{4,12},{0,4},{9,1},{1... | collective-permute-start | bytes 393224 | tf_op jit(solution)/shard_map/ppermute | solution.py:533
  25.9 7.1 %collective-permute-start.27 = (f32[256,128]{1,0:T(8,128)S(1)}, f32[256,128]{1,0:T(8,128)S(1)}, u32[]{:S(2)}, u32[]{:S(2)}) collective-permute-start(f32[256,128]{1,0:T(8,128)S(1)} %collective-permute-done.26.refs_7_), channel_id=1, source_target_pairs={{0,8},{8,16},{16,24},{24,28},{28,20},{20,12},{12,4},{4,0},{1,9},{9... | collective-permute-start | bytes 393224 | tf_op jit(solution)/shard_map/ppermute | solution.py:530
  32.5 6.2 %collective-permute-start.7 = (f32[264,128]{1,0:T(8,128)S(1)}, f32[264,128]{1,0:T(8,128)S(1)}, u32[]{:S(2)}, u32[]{:S(2)}) collective-permute-start(f32[264,128]{1,0:T(8,128)S(1)} %get-tuple-element.76), channel_id=1, source_target_pairs={{0,8},{8,16},{16,24},{24,28},{28,20},{20,12},{12,4},{4,0},{1,9},{9... | collective-permute-start | bytes 405512 | tf_op jit(solution)/shard_map/ppermute | solution.py:530
  35.3 6.3 %collective-permute-start.31 = (f32[256,128]{1,0:T(8,128)S(1)}, f32[256,128]{1,0:T(8,128)S(1)}, u32[]{:S(2)}, u32[]{:S(2)}) collective-permute-start(f32[256,128]{1,0:T(8,128)S(1)} %get-tuple-element.91), channel_id=1, source_target_pairs={{8,0},{16,8},{24,16},{28,24},{20,28},{12,20},{4,12},{0,4},{9,1},{1... | collective-permute-start | bytes 393224 | tf_op jit(solution)/shard_map/ppermute | solution.py:533
  36.9 7.6 %collective-permute-start.11 = (f32[264,128]{1,0:T(8,128)S(1)}, f32[264,128]{1,0:T(8,128)S(1)}, u32[]{:S(2)}, u32[]{:S(2)}) collective-permute-start(f32[264,128]{1,0:T(8,128)S(1)} %get-tuple-element.80), channel_id=1, source_target_pairs={{8,0},{16,8},{24,16},{28,24},{20,28},{12,20},{4,12},{0,4},{9,1},{1... | collective-permute-start | bytes 405512 | tf_op jit(solution)/shard_map/ppermute | solution.py:533
  38.7 6.6 %collective-permute-start.8 = (f32[264,128]{1,0:T(8,128)S(1)}, f32[264,128]{1,0:T(8,128)S(1)}, u32[]{:S(2)}, u32[]{:S(2)}) collective-permute-start(f32[264,128]{1,0:T(8,128)S(1)} %add_pairs.20), channel_id=1, source_target_pairs={{0,8},{8,16},{16,24},{24,28},{28,20},{20,12},{12,4},{4,0},{1,9},{9... | collective-permute-start | bytes 405512 | tf_op jit(solution)/shard_map/ppermute | solution.py:530
  39.0 8.9 %collective-permute-start.28 = (f32[256,128]{1,0:T(8,128)S(1)}, f32[256,128]{1,0:T(8,128)S(1)}, u32[]{:S(2)}, u32[]{:S(2)}) collective-permute-start(f32[256,128]{1,0:T(8,128)S(1)} %get-tuple-element.88), channel_id=1, source_target_pairs={{0,8},{8,16},{16,24},{24,28},{28,20},{20,12},{12,4},{4,0},{1,9},{9... | collective-permute-start | bytes 393224 | tf_op jit(solution)/shard_map/ppermute | solution.py:530
  41.7 6.4 %collective-permute-start.32 = (f32[256,128]{1,0:T(8,128)S(1)}, f32[256,128]{1,0:T(8,128)S(1)}, u32[]{:S(2)}, u32[]{:S(2)}) collective-permute-start(f32[256,128]{1,0:T(8,128)S(1)} %add_pairs.27), channel_id=1, source_target_pairs={{8,0},{16,8},{24,16},{28,24},{20,28},{12,20},{4,12},{0,4},{9,1},{1... | collective-permute-start | bytes 393224 | tf_op jit(solution)/shard_map/ppermute | solution.py:533
  45.3 6.5 %collective-permute-start.9 = (f32[264,128]{1,0:T(8,128)S(1)}, f32[264,128]{1,0:T(8,128)S(1)}, u32[]{:S(2)}, u32[]{:S(2)}) collective-permute-start(f32[264,128]{1,0:T(8,128)S(1)} %add_pairs.21), channel_id=1, source_target_pairs={{0,8},{8,16},{16,24},{24,28},{28,20},{20,12},{12,4},{4,0},{1,9},{9... | collective-permute-start | bytes 405512 | tf_op jit(solution)/shard_map/ppermute | solution.py:530
  48.0 6.5 %collective-permute-start.29 = (f32[256,128]{1,0:T(8,128)S(1)}, f32[256,128]{1,0:T(8,128)S(1)}, u32[]{:S(2)}, u32[]{:S(2)}) collective-permute-start(f32[256,128]{1,0:T(8,128)S(1)} %add_pairs.25), channel_id=1, source_target_pairs={{0,8},{8,16},{16,24},{24,28},{28,20},{20,12},{12,4},{4,0},{1,9},{9... | collective-permute-start | bytes 393224 | tf_op jit(solution)/shard_map/ppermute | solution.py:530
  48.1 7.7 %collective-permute-start.33 = (f32[256,128]{1,0:T(8,128)S(1)}, f32[256,128]{1,0:T(8,128)S(1)}, u32[]{:S(2)}, u32[]{:S(2)}) collective-permute-start(f32[256,128]{1,0:T(8,128)S(1)} %add_pairs.28), channel_id=1, source_target_pairs={{8,0},{16,8},{24,16},{28,24},{20,28},{12,20},{4,12},{0,4},{9,1},{1... | collective-permute-start | bytes 393224 | tf_op jit(solution)/shard_map/ppermute | solution.py:533
  50.1 6.5 %collective-permute-start.13 = (f32[264,128]{1,0:T(8,128)S(1)}, f32[264,128]{1,0:T(8,128)S(1)}, u32[]{:S(2)}, u32[]{:S(2)}) collective-permute-start(f32[264,128]{1,0:T(8,128)S(1)} %add_pairs.24), channel_id=1, source_target_pairs={{8,0},{16,8},{24,16},{28,24},{20,28},{12,20},{4,12},{0,4},{9,1},{1... | collective-permute-start | bytes 405512 | tf_op jit(solution)/shard_map/ppermute | solution.py:533
  54.5 6.4 %collective-permute-start.30 = (f32[256,128]{1,0:T(8,128)S(1)}, f32[256,128]{1,0:T(8,128)S(1)}, u32[]{:S(2)}, u32[]{:S(2)}) collective-permute-start(f32[256,128]{1,0:T(8,128)S(1)} %add_pairs.26), channel_id=1, source_target_pairs={{0,8},{8,16},{16,24},{24,28},{28,20},{20,12},{12,4},{4,0},{1,9},{9... | collective-permute-start | bytes 393224 | tf_op jit(solution)/shard_map/ppermute | solution.py:530
  55.8 6.4 %collective-permute-start.34 = (f32[256,128]{1,0:T(8,128)S(1)}, f32[256,128]{1,0:T(8,128)S(1)}, u32[]{:S(2)}, u32[]{:S(2)}) collective-permute-start(f32[256,128]{1,0:T(8,128)S(1)} %add_pairs.29), channel_id=1, source_target_pairs={{8,0},{16,8},{24,16},{28,24},{20,28},{12,20},{4,12},{0,4},{9,1},{1... | collective-permute-start | bytes 393224 | tf_op jit(solution)/shard_map/ppermute | solution.py:533
  56.9 7.4 %collective-permute-start.17 = (f32[256,128]{1,0:T(8,128)S(1)}, f32[256,128]{1,0:T(8,128)S(1)}, u32[]{:S(2)}, u32[]{:S(2)}) collective-permute-start(f32[256,128]{1,0:T(8,128)S(1)} %get-tuple-element.83.refs_1_.refs_3_), channel_id=1, source_target_pairs={{0,8},{8,16},{16,24},{24,28},{28,20},{20,12},{12,4},{4,0},{1,9},{9... | collective-permute-start | bytes 393224 | tf_op jit(solution)/shard_map/ppermute | solution.py:530
  62.3 6.4 %collective-permute-start.35 = (f32[256,128]{1,0:T(8,128)S(1)}, f32[256,128]{1,0:T(8,128)S(1)}, u32[]{:S(2)}, u32[]{:S(2)}) collective-permute-start(f32[256,128]{1,0:T(8,128)S(1)} %get-tuple-element.96.refs_1_.refs_3_), channel_id=1, source_target_pairs={{8,0},{16,8},{24,16},{28,24},{20,28},{12,20},{4,12},{0,4},{9,1},{1... | collective-permute-start | bytes 393224 | tf_op jit(solution)/shard_map/ppermute | solution.py:533
  62.5 9.0 %collective-permute-start.14 = (f32[256,128]{1,0:T(8,128)S(1)}, f32[256,128]{1,0:T(8,128)S(1)}, u32[]{:S(2)}, u32[]{:S(2)}) collective-permute-start(f32[256,128]{1,0:T(8,128)S(1)} %get-tuple-element.83.refs_1_.refs_3_), channel_id=1, source_target_pairs={{8,0},{16,8},{24,16},{28,24},{20,28},{12,20},{4,12},{0,4},{9,1},{1... | collective-permute-start | bytes 393224 | tf_op jit(solution)/shard_map/ppermute | solution.py:533
  64.3 7.2 %collective-permute-start.18 = (f32[256,128]{1,0:T(8,128)S(1)}, f32[256,128]{1,0:T(8,128)S(1)}, u32[]{:S(2)}, u32[]{:S(2)}) collective-permute-start(f32[256,128]{1,0:T(8,128)S(1)} %collective-permute-done.17.refs_8_), channel_id=1, source_target_pairs={{0,8},{8,16},{16,24},{24,28},{28,20},{20,12},{12,4},{4,0},{1,9},{9... | collective-permute-start | bytes 393224 | tf_op jit(solution)/shard_map/ppermute | solution.py:530
  65.0 8.5 %collective-permute-start.39 = (f32[256,128]{1,0:T(8,128)S(1)}, f32[256,128]{1,0:T(8,128)S(1)}, u32[]{:S(2)}, u32[]{:S(2)}) collective-permute-start(f32[256,128]{1,0:T(8,128)S(1)} %get-tuple-element.96.refs_1_.refs_3_), channel_id=1, source_target_pairs={{0,8},{8,16},{16,24},{24,28},{28,20},{20,12},{12,4},{4,0},{1,9},{9... | collective-permute-start | bytes 393224 | tf_op jit(solution)/shard_map/ppermute | solution.py:530
  68.7 6.0 %collective-permute-start.36 = (f32[256,128]{1,0:T(8,128)S(1)}, f32[256,128]{1,0:T(8,128)S(1)}, u32[]{:S(2)}, u32[]{:S(2)}) collective-permute-start(f32[256,128]{1,0:T(8,128)S(1)} %collective-permute-done.35.refs_2_), channel_id=1, source_target_pairs={{8,0},{16,8},{24,16},{28,24},{20,28},{12,20},{4,12},{0,4},{9,1},{1... | collective-permute-start | bytes 393224 | tf_op jit(solution)/shard_map/ppermute | solution.py:533
  73.6 6.1 %collective-permute-start.40 = (f32[256,128]{1,0:T(8,128)S(1)}, f32[256,128]{1,0:T(8,128)S(1)}, u32[]{:S(2)}, u32[]{:S(2)}) collective-permute-start(f32[256,128]{1,0:T(8,128)S(1)} %collective-permute-done.39.refs_8_), channel_id=1, source_target_pairs={{0,8},{8,16},{16,24},{24,28},{28,20},{20,12},{12,4},{4,0},{1,9},{9... | collective-permute-start | bytes 393224 | tf_op jit(solution)/shard_map/ppermute | solution.py:530
  74.7 6.4 %collective-permute-start.37 = (f32[256,128]{1,0:T(8,128)S(1)}, f32[256,128]{1,0:T(8,128)S(1)}, u32[]{:S(2)}, u32[]{:S(2)}) collective-permute-start(f32[256,128]{1,0:T(8,128)S(1)} %collective-permute-done.36.refs_3_), channel_id=1, source_target_pairs={{8,0},{16,8},{24,16},{28,24},{20,28},{12,20},{4,12},{0,4},{9,1},{1... | collective-permute-start | bytes 393224 | tf_op jit(solution)/shard_map/ppermute | solution.py:533
  76.5 6.3 %collective-permute-start.16 = (f32[256,128]{1,0:T(8,128)S(1)}, f32[256,128]{1,0:T(8,128)S(1)}, u32[]{:S(2)}, u32[]{:S(2)}) collective-permute-start(f32[256,128]{1,0:T(8,128)S(1)} %collective-permute-done.15.refs_3_), channel_id=1, source_target_pairs={{8,0},{16,8},{24,16},{28,24},{20,28},{12,20},{4,12},{0,4},{9,1},{1... | collective-permute-start | bytes 393224 | tf_op jit(solution)/shard_map/ppermute | solution.py:533
  77.2 6.3 %collective-permute-start.20 = (f32[256,128]{1,0:T(8,128)S(1)}, f32[256,128]{1,0:T(8,128)S(1)}, u32[]{:S(2)}, u32[]{:S(2)}) collective-permute-start(f32[256,128]{1,0:T(8,128)S(1)} %collective-permute-done.19.refs_6_), channel_id=1, source_target_pairs={{0,8},{8,16},{16,24},{24,28},{28,20},{20,12},{12,4},{4,0},{1,9},{9... | collective-permute-start | bytes 393224 | tf_op jit(solution)/shard_map/ppermute | solution.py:530
  79.7 8.6 %collective-permute-start.41 = (f32[256,128]{1,0:T(8,128)S(1)}, f32[256,128]{1,0:T(8,128)S(1)}, u32[]{:S(2)}, u32[]{:S(2)}) collective-permute-start(f32[256,128]{1,0:T(8,128)S(1)} %collective-permute-done.40.refs_7_), channel_id=1, source_target_pairs={{0,8},{8,16},{16,24},{24,28},{28,20},{20,12},{12,4},{4,0},{1,9},{9... | collective-permute-start | bytes 393224 | tf_op jit(solution)/shard_map/ppermute | solution.py:530
  81.1 7.2 %collective-permute-start.38 = (f32[256,128]{1,0:T(8,128)S(1)}, f32[256,128]{1,0:T(8,128)S(1)}, u32[]{:S(2)}, u32[]{:S(2)}) collective-permute-start(f32[256,128]{1,0:T(8,128)S(1)} %collective-permute-done.37.refs_4_), channel_id=1, source_target_pairs={{8,0},{16,8},{24,16},{28,24},{20,28},{12,20},{4,12},{0,4},{9,1},{1... | collective-permute-start | bytes 393224 | tf_op jit(solution)/shard_map/ppermute | solution.py:533
  86.2 6.9 %collective-permute-start.42 = (f32[256,128]{1,0:T(8,128)S(1)}, f32[256,128]{1,0:T(8,128)S(1)}, u32[]{:S(2)}, u32[]{:S(2)}) collective-permute-start(f32[256,128]{1,0:T(8,128)S(1)} %get-tuple-element.102), channel_id=1, source_target_pairs={{0,8},{8,16},{16,24},{24,28},{28,20},{20,12},{12,4},{4,0},{1,9},{9... | collective-permute-start | bytes 393224 | tf_op jit(solution)/shard_map/ppermute | solution.py:530
  91.0 6.0 %collective-permute-start.59 = (f32[256,128]{1,0:T(8,128)S(1)}, f32[256,128]{1,0:T(8,128)S(1)}, u32[]{:S(2)}, u32[]{:S(2)}) collective-permute-start(f32[256,128]{1,0:T(8,128)S(1)} %get-tuple-element.114), channel_id=1, source_target_pairs={{8,0},{16,8},{24,16},{28,24},{20,28},{12,20},{4,12},{0,4},{9,1},{1... | collective-permute-start | bytes 393224 | tf_op jit(solution)/shard_map/ppermute | solution.py:533
  91.0 6.3 %collective-permute-start.56 = (f32[256,128]{1,0:T(8,128)S(1)}, f32[256,128]{1,0:T(8,128)S(1)}, u32[]{:S(2)}, u32[]{:S(2)}) collective-permute-start(f32[256,128]{1,0:T(8,128)S(1)} %get-tuple-element.111), channel_id=1, source_target_pairs={{0,8},{8,16},{16,24},{24,28},{28,20},{20,12},{12,4},{4,0},{1,9},{9... | collective-permute-start | bytes 393224 | tf_op jit(solution)/shard_map/ppermute | solution.py:530
  93.0 6.1 %collective-permute-start.46 = (f32[256,128]{1,0:T(8,128)S(1)}, f32[256,128]{1,0:T(8,128)S(1)}, u32[]{:S(2)}, u32[]{:S(2)}) collective-permute-start(f32[256,128]{1,0:T(8,128)S(1)} %get-tuple-element.106), channel_id=1, source_target_pairs={{8,0},{16,8},{24,16},{28,24},{20,28},{12,20},{4,12},{0,4},{9,1},{1... | collective-permute-start | bytes 393224 | tf_op jit(solution)/shard_map/ppermute | solution.py:533
  93.1 6.4 %collective-permute-start.43 = (f32[256,128]{1,0:T(8,128)S(1)}, f32[256,128]{1,0:T(8,128)S(1)}, u32[]{:S(2)}, u32[]{:S(2)}) collective-permute-start(f32[256,128]{1,0:T(8,128)S(1)} %add_pairs.30), channel_id=1, source_target_pairs={{0,8},{8,16},{16,24},{24,28},{28,20},{20,12},{12,4},{4,0},{1,9},{9... | collective-permute-start | bytes 393224 | tf_op jit(solution)/shard_map/ppermute | solution.py:530
  97.3 6.4 %collective-permute-start.57 = (f32[256,128]{1,0:T(8,128)S(1)}, f32[256,128]{1,0:T(8,128)S(1)}, u32[]{:S(2)}, u32[]{:S(2)}) collective-permute-start(f32[256,128]{1,0:T(8,128)S(1)} %add_pairs.35), channel_id=1, source_target_pairs={{0,8},{8,16},{16,24},{24,28},{28,20},{20,12},{12,4},{4,0},{1,9},{9... | collective-permute-start | bytes 393224 | tf_op jit(solution)/shard_map/ppermute | solution.py:530
  99.1 6.4 %collective-permute-start.47 = (f32[256,128]{1,0:T(8,128)S(1)}, f32[256,128]{1,0:T(8,128)S(1)}, u32[]{:S(2)}, u32[]{:S(2)}) collective-permute-start(f32[256,128]{1,0:T(8,128)S(1)} %add_pairs.33), channel_id=1, source_target_pairs={{8,0},{16,8},{24,16},{28,24},{20,28},{12,20},{4,12},{0,4},{9,1},{1... | collective-permute-start | bytes 393224 | tf_op jit(solution)/shard_map/ppermute | solution.py:533
  99.5 6.8 %collective-permute-start.44 = (f32[256,128]{1,0:T(8,128)S(1)}, f32[256,128]{1,0:T(8,128)S(1)}, u32[]{:S(2)}, u32[]{:S(2)}) collective-permute-start(f32[256,128]{1,0:T(8,128)S(1)} %add_pairs.31), channel_id=1, source_target_pairs={{0,8},{8,16},{16,24},{24,28},{28,20},{20,12},{12,4},{4,0},{1,9},{9... | collective-permute-start | bytes 393224 | tf_op jit(solution)/shard_map/ppermute | solution.py:530
  102.8 6.4 %collective-permute-start.61 = (f32[256,128]{1,0:T(8,128)S(1)}, f32[256,128]{1,0:T(8,128)S(1)}, u32[]{:S(2)}, u32[]{:S(2)}) collective-permute-start(f32[256,128]{1,0:T(8,128)S(1)} %add_pairs.38), channel_id=1, source_target_pairs={{8,0},{16,8},{24,16},{28,24},{20,28},{12,20},{4,12},{0,4},{9,1},{1... | collective-permute-start | bytes 393224 | tf_op jit(solution)/shard_map/ppermute | solution.py:533
  103.8 9.0 %collective-permute-start.58 = (f32[256,128]{1,0:T(8,128)S(1)}, f32[256,128]{1,0:T(8,128)S(1)}, u32[]{:S(2)}, u32[]{:S(2)}) collective-permute-start(f32[256,128]{1,0:T(8,128)S(1)} %add_pairs.36), channel_id=1, source_target_pairs={{0,8},{8,16},{16,24},{24,28},{28,20},{20,12},{12,4},{4,0},{1,9},{9... | collective-permute-start | bytes 393224 | tf_op jit(solution)/shard_map/ppermute | solution.py:530
  105.6 6.1 %collective-permute-start.48 = (f32[256,128]{1,0:T(8,128)S(1)}, f32[256,128]{1,0:T(8,128)S(1)}, u32[]{:S(2)}, u32[]{:S(2)}) collective-permute-start(f32[256,128]{1,0:T(8,128)S(1)} %add_pairs.34), channel_id=1, source_target_pairs={{8,0},{16,8},{24,16},{28,24},{20,28},{12,20},{4,12},{0,4},{9,1},{1... | collective-permute-start | bytes 393224 | tf_op jit(solution)/shard_map/ppermute | solution.py:533
  106.3 6.4 %collective-permute-start.45 = (f32[256,128]{1,0:T(8,128)S(1)}, f32[256,128]{1,0:T(8,128)S(1)}, u32[]{:S(2)}, u32[]{:S(2)}) collective-permute-start(f32[256,128]{1,0:T(8,128)S(1)} %add_pairs.32), channel_id=1, source_target_pairs={{0,8},{8,16},{16,24},{24,28},{28,20},{20,12},{12,4},{4,0},{1,9},{9... | collective-permute-start | bytes 393224 | tf_op jit(solution)/shard_map/ppermute | solution.py:530
  116.6 6.7 %collective-permute-start.52 = (f32[256,128]{1,0:T(8,128)S(1)}, f32[256,128]{1,0:T(8,128)S(1)}, u32[]{:S(2)}, u32[]{:S(2)}) collective-permute-start(f32[256,128]{1,0:T(8,128)S(1)} %get-tuple-element.109.refs_1_), channel_id=1, source_target_pairs={{0,8},{8,16},{16,24},{24,28},{28,20},{20,12},{12,4},{4,0},{1,9},{9... | collective-permute-start | bytes 393224 | tf_op jit(solution)/shard_map/ppermute | solution.py:530
  117.6 6.1 %collective-permute-start.67 = (f32[264,128]{1,0:T(8,128)S(1)}, f32[264,128]{1,0:T(8,128)S(1)}, u32[]{:S(2)}, u32[]{:S(2)}) collective-permute-start(f32[264,128]{1,0:T(8,128)S(1)} %get-tuple-element.123.refs_9_.refs_0_), channel_id=1, source_target_pairs={{0,8},{8,16},{16,24},{24,28},{28,20},{20,12},{12,4},{4,0},{1,9},{9... | collective-permute-start | bytes 405512 | tf_op jit(solution)/shard_map/ppermute | solution.py:530
  129.7 6.3 %collective-permute-start.69 = (f32[264,128]{1,0:T(8,128)S(1)}, f32[264,128]{1,0:T(8,128)S(1)}, u32[]{:S(2)}, u32[]{:S(2)}) collective-permute-start(f32[264,128]{1,0:T(8,128)S(1)} %collective-permute-done.68.refs_15_.refs_6_), channel_id=1, source_target_pairs={{0,8},{8,16},{16,24},{24,28},{28,20},{20,12},{12,4},{4,0},{1,9},{9... | collective-permute-start | bytes 405512 | tf_op jit(solution)/shard_map/ppermute | solution.py:530
  132.1 6.9 %collective-permute-start.51 = (f32[256,128]{1,0:T(8,128)S(1)}, f32[256,128]{1,0:T(8,128)S(1)}, u32[]{:S(2)}, u32[]{:S(2)}) collective-permute-start(f32[256,128]{1,0:T(8,128)S(1)} %collective-permute-done.50.refs_3_), channel_id=1, source_target_pairs={{8,0},{16,8},{24,16},{28,24},{20,28},{12,20},{4,12},{0,4},{9,1},{1... | collective-permute-start | bytes 393224 | tf_op jit(solution)/shard_map/ppermute | solution.py:533
  (25 other events, 132.1 us)

commit v5 on v4

--- a/solution.py
+++ b/solution.py
@@ -106,32 +106,27 @@
         self.flying.pop(name).wait()
 
 
-def split(cons):
-    rows, scen = cons.shape
+def halve(arrays):
+    rows, scen = arrays[0].shape
     width = scen // HALVES
 
-    def body(cons_ref, *refs):
-        copies = [
-            pltpu.make_async_copy(cons_ref.at[:, h * width : (h + 1) * width], refs[h], refs[-1].at[h])
-            for h in range(HALVES)
-        ]
-        for copy in copies:
-            copy.start()
-        for copy in copies:
-            copy.wait()
-
-    return call(
-        body, "split", (cons,), [HBM], [f32(rows, width)] * HALVES, [VMEM] * HALVES, [pltpu.SemaphoreType.DMA((HALVES,))]
-    )
-
-
-def prepare(region, target, owned, kkt, cost, dual, peers):
+    def body(*refs):
+        for i in range(len(arrays)):
+            for h in range(HALVES):
+                refs[len(arrays) + HALVES * i + h][...] = refs[i][:, h * width : (h + 1) * width]
+
+    many = HALVES * len(arrays)
+    out = call(body, "halve", tuple(arrays), [VMEM] * len(arrays), [f32(rows, width)] * many, [VMEM] * many)
+    return [out[HALVES * i : HALVES * (i + 1)] for i in range(len(arrays))]
+
+
+def prepare(region, target, owned, kkt, cost, dual, cons, peers):
     blocks = target.shape[1]
-    arrays = (kkt, cost, dual)
-    cuts = (CUTS, 1, 1)
+    arrays = (kkt, cost, dual, cons)
+    cuts = (CUTS, 1, 1, 1)
 
     def body(region_ref, target_hbm, *refs):
-        from_refs, table_ref, to_refs, target_ref, sem = refs[:3], refs[3], refs[4:7], refs[7], refs[8]
+        from_refs, table_ref, to_refs, target_ref, sem = refs[:4], refs[4], refs[5:9], refs[9], refs[10]
         loads = Loads(sem)
         loads.start("target", target_hbm, target_ref)
         for i, (src, dst) in enumerate(zip(from_refs, to_refs)):
@@ -156,7 +151,7 @@
                 table_ref[at] = j
                 table_ref[CAP * peers + at] = t - owner * owned
 
-        for i in range(3):
+        for i in range(4):
             for c in range(cuts[i]):
                 loads.wait((i, c))
 
@@ -164,24 +159,13 @@
         body,
         "prepare",
         (region, target, *arrays),
-        [SMEM] + [HBM] * 4,
+        [SMEM] + [HBM] * 5,
         [jax.ShapeDtypeStruct((2 * CAP * peers,), jnp.int32)] + [jax.ShapeDtypeStruct(x.shape, x.dtype) for x in arrays],
-        [SMEM] + [VMEM] * 3,
+        [SMEM] + [VMEM] * 4,
         [pltpu.SMEM(target.shape, jnp.int32), pltpu.SemaphoreType.DMA((1 + sum(cuts),))],
         moved=12 << 20,
     )
     return out[0], out[1:]
-
-
-def halve(pieces):
-    rows, scen = pieces[0].shape
-    width = scen // HALVES
-
-    def body(*refs):
-        for h in range(HALVES):
-            refs[HALVES + h][...] = refs[h][:, h * width : (h + 1) * width]
-
-    return call(body, "halve", tuple(pieces), [VMEM] * HALVES, [f32(rows, width)] * HALVES, [VMEM] * HALVES)
 
 
 def columns(ref, h):
@@ -257,10 +241,12 @@
         for r in range(peers):
             for read, write, block, _ in slots[r]:
                 drive_ref[write, :] = (penalty * (piece[r][block, :] - dual_ref[read, cols])).astype(jnp.bfloat16)
-        for i in range(chunks):
-            at = slice(i * step, (i + 1) * step)
+        for i in range(chunks * 2):
+            half = step // 2
+            at = slice(i * half, (i + 1) * half)
+            here = slice(i % 2 * half, (i % 2 + 1) * half)
             got = jnp.dot(kkt_ref[at, :bound], drive_ref[:bound, :], preferred_element_type=jnp.float32)
-            z_ref[at, :] = (base_refs[i][:, cols] + got) + dual_ref[at, cols]
+            z_ref[at, :] = (base_refs[i // 2][here, cols] + got) + dual_ref[at, cols]
         for r in range(peers):
             place(part[r], [z_ref[read, :] for read, _, _, _ in slots[r]], slots[r], owned)
             if counting:
@@ -310,10 +296,12 @@
                 gaps = gaps + jnp.where(b < 0, 0.0, fold(gap * gap))
                 next_ref[write, :] = renewed_dual
                 drive_ref[write, :] = (penalty * (fetched - renewed_dual)).astype(jnp.bfloat16)
-        for i in range(chunks):
-            at = slice(i * step, (i + 1) * step)
+        for i in range(chunks * 2):
+            half = step // 2
+            at = slice(i * half, (i + 1) * half)
+            here = slice(i % 2 * half, (i % 2 + 1) * half)
             got = jnp.dot(kkt_ref[at, :bound], drive_ref[:bound, :], preferred_element_type=jnp.float32)
-            field_ref[at, :] = base_refs[i][:, cols] + got
+            field_ref[at, :] = base_refs[i // 2][here, cols] + got
         shifts = jnp.zeros((TILE, width), jnp.float32)
         for r in range(peers):
             totals = []
@@ -534,13 +522,15 @@
 
     def reach(h):
         long, short = peers // 2, (peers - 1) // 2
-        return (long, short) if h % 2 == 0 else (short, long)
-
-    def gather(h, piece, beside=lambda k, x: x):
+        return (long, short)
+
+    def gather(h, piece, beside=lambda k, x: x, came=None):
         far, near = reach(h)
         pieces = [piece] * peers
         f = b = piece
-        for k in range(1, max(far, near) + 1):
+        if came:
+            f, b = pieces[peers - 1], pieces[1] = came
+        for k in range(2 if came else 1, max(far, near) + 1):
             values = yield ([f] if k <= far else []) + ([b] if k <= near else [])
             values = beside(k, values)
             if k <= far:
@@ -571,8 +561,8 @@
         return [parts[0], f, b]
 
     region = lax.axis_index("region").astype(jnp.int32).reshape(1)
-    halves = split(cons)
-    table, (kkt, cost, dual) = prepare(region, target, owned, kkt, cost, dual, peers)
+    firsts = halve([forward(cons), backward(cons)])
+    table, (kkt, cost, dual, own) = prepare(region, target, owned, kkt, cost, dual, cons, peers)
     step = math.gcd(dual.shape[0], kkt.shape[0])
     chunks = kkt.shape[0] // step
     bases = []
@@ -589,10 +579,10 @@
 
     def half(h):
         last = h == HALVES - 1
-        pieces = yield from gather(h, halves[h], lambda k, values: beside(h, k, values))
+        pieces = yield from gather(h, own, lambda k, values: beside(h, k, values), [halves[h] for halves in firsts])
         z, parts = first_solve(h, table, pieces, dual, bases, kkt, owned, h == 0)
         arrived = yield from scatter(h, parts)
-        out = renew(h, arrived, halves[h], known["count"], ())
+        out = renew(h, arrived, own, known["count"], ())
         averages, moved = out[0], out[1]
         if known["count"] is None:
             known["count"] = out[2]
@@ -620,7 +610,7 @@
     state = store_state(fields, drives, bases, kkt)
     pieces, zs = zip(*known["last"])
     tail = sum_tails(pieces[-1], owned * BLOCK, [state])
-    turned = [lax.ppermute(tail, "sub", [(i, (i + k) % subs) for i in range(subs)]) for k in range(1, subs)]
+    turned = [lax.ppermute(tail, "sub", [(i, i ^ k) for i in range(subs)]) for k in range(1, subs)]
     norms = norm_table([tail, *turned], float(peers * subs * scen * BLOCK))
     return (state, *finish(table, pieces, zs, owned), norms)
 

time: 142 us -> 140 us (0.986)
    ppermute x35 -> x39, waiting for transfers between devices: 11.2 us -> 31.5 us  [forward(): return lax.ppermute(x, 'region', ahead)]
    ppermute x35 -> x29, waiting for transfers between devices: 23.7 us -> 3.82 us  [backward(): return lax.ppermute(x, 'region', behind)]
    ppermute x35 -> x29, starting transfers between devices: 31.5 us -> 17.9 us  [backward(): return lax.ppermute(x, 'region', behind)]
    ppermute x35 -> x39, starting transfers between devices: 46.8 us -> 60.2 us  [forward(): return lax.ppermute(x, 'region', ahead)]
  transfers between devices with their start and end apart: 73 -> 71, of which waited for: 32 -> 35; matrix products, arithmetic and copies ran while one was open for 0% -> 0% of each run, Pallas kernels for 16% -> 16%
where the time goes in v5:
time: 140 us
  starting transfers between devices  80 us (57%)
  waiting for transfers between devices  35.8 us (26%)
  Pallas kernels  23.5 us (17%)
    ppermute x39, starting transfers between devices, forward(): return lax.ppermute(x, 'region', ahead)  60.2 us
    ppermute x39, waiting for transfers between devices, forward(): return lax.ppermute(x, 'region', ahead)  31.5 us
    pallas_call x41, Pallas kernels, call(): pl.pallas_call(body, name=name, out_shape=shapes if many else shapes[0],...  23.5 us
    ppermute x29, starting transfers between devices, backward(): return lax.ppermute(x, 'region', behind)  17.9 us
    ppermute x29, waiting for transfers between devices, backward(): return lax.ppermute(x, 'region', behind)  3.82 us
  transfers between devices with their start and end apart: 71, of which 35 were waited for; matrix products, arithmetic and copies ran while one was open for 0% of the time, Pallas kernels for 16%

profile of v5, /device:TPU:0, one launch (start us, length us, event | category | flops | bytes accessed | tf_op | source)
XLA Modules:
  0.0 140.2 jit_solution(1590292884273081768)
XLA Ops:
  0.6 3.1 %collective-permute-start = (f32[256,256]{1,0:T(8,128)}, f32[256,256]{1,0:T(8,128)S(1)}, u32[]{:S(2)}, u32[]{:S(2)}) collective-permute-start(f32[256,256]{1,0:T(8,128)} %refs_3_.1), channel_id=1, source_target_pairs={{0,8},{8,16},{16,24},{24,28},{28,20},{20,12},{12,4},{4,0},{1,9},{9... | collective-permute-start | bytes 786440 | tf_op jit(solution)/shard_map/ppermute | solution.py:518
  3.7 4.9 %prepare.1 = (s32[32]{0:T(128)S(1)}, bf16[2048,2048]{1,0:T(8,128)(2,1)S(1)}, bf16[2048,256]{1,0:T(8,128)(2,1)S(1)}, f32[1536,256]{1,0:T(8,128)S(1)}, f32[256,256]{1,0:T(8,128)S(1)}) custom-call(s32[1]{0:T(128)} %bitcast.region_ref, s32[1,12]{1,0:T(1,128)} %target_hbm.1, bf16[2048,2048]{1,0:T(8,128)(2,1)} %refs_0_.1, bf16[2048,256]{1,0:T(8,128)(2,1)} %refs_1_.1, ...), custom_call_target="tpu_custom_call" | custom-call | bytes 12582912 | tf_op jit(solution)/shard_map/prepare/pallas_call | solution.py:63
  8.6 1.5 %collective-permute-done.refs_0_ = f32[256,256]{1,0:T(8,128)S(1)} collective-permute-done((f32[256,256]{1,0:T(8,128)}, f32[256,256]{1,0:T(8,128)S(1)}, u32[]{:S(2)}, u32[]{:S(2)}) %collective-permute-start) | collective-permute-done | bytes 262176 | tf_op jit(solution)/shard_map/ppermute | solution.py:518
  10.1 1.5 %collective-permute-done.1.refs_1_ = f32[256,256]{1,0:T(8,128)S(1)} collective-permute-done((f32[256,256]{1,0:T(8,128)}, f32[256,256]{1,0:T(8,128)S(1)}, u32[]{:S(2)}, u32[]{:S(2)}) %collective-permute-start.1) | collective-permute-done | bytes 262176 | tf_op jit(solution)/shard_map/ppermute | solution.py:521
  11.8 1.6 %collective-permute-start.3 = (f32[256,128]{1,0:T(8,128)S(1)}, f32[256,128]{1,0:T(8,128)S(1)}, u32[]{:S(2)}, u32[]{:S(2)}) collective-permute-start(f32[256,128]{1,0:T(8,128)S(1)} %get-tuple-element.75), channel_id=1, source_target_pairs={{0,8},{8,16},{16,24},{24,28},{28,20},{20,12},{12,4},{4,0},{1,9},{9... | collective-permute-start | bytes 393224 | tf_op jit(solution)/shard_map/ppermute | solution.py:518
  13.8 1.6 %collective-permute-start.23 = (f32[256,128]{1,0:T(8,128)S(1)}, f32[256,128]{1,0:T(8,128)S(1)}, u32[]{:S(2)}, u32[]{:S(2)}) collective-permute-start(f32[256,128]{1,0:T(8,128)S(1)} %get-tuple-element.92.refs_8_), channel_id=1, source_target_pairs={{0,8},{8,16},{16,24},{24,28},{28,20},{20,12},{12,4},{4,0},{1,9},{9... | collective-permute-start | bytes 393224 | tf_op jit(solution)/shard_map/ppermute | solution.py:518
  18.4 1.6 %collective-permute-start.5 = (f32[256,128]{1,0:T(8,128)S(1)}, f32[256,128]{1,0:T(8,128)S(1)}, u32[]{:S(2)}, u32[]{:S(2)}) collective-permute-start(f32[256,128]{1,0:T(8,128)S(1)} %get-tuple-element.79), channel_id=1, source_target_pairs={{0,8},{8,16},{16,24},{24,28},{28,20},{20,12},{12,4},{4,0},{1,9},{9... | collective-permute-start | bytes 393224 | tf_op jit(solution)/shard_map/ppermute | solution.py:518
  20.5 1.6 %collective-permute-start.24 = (f32[256,128]{1,0:T(8,128)S(1)}, f32[256,128]{1,0:T(8,128)S(1)}, u32[]{:S(2)}, u32[]{:S(2)}) collective-permute-start(f32[256,128]{1,0:T(8,128)S(1)} %collective-permute-done.23.refs_7_), channel_id=1, source_target_pairs={{0,8},{8,16},{16,24},{24,28},{28,20},{20,12},{12,4},{4,0},{1,9},{9... | collective-permute-start | bytes 393224 | tf_op jit(solution)/shard_map/ppermute | solution.py:518
  24.0 1.6 %collective-permute-start.6 = (f32[256,128]{1,0:T(8,128)S(1)}, f32[256,128]{1,0:T(8,128)S(1)}, u32[]{:S(2)}, u32[]{:S(2)}) collective-permute-start(f32[256,128]{1,0:T(8,128)S(1)} %tie.5), channel_id=1, source_target_pairs={{0,8},{8,16},{16,24},{24,28},{28,20},{20,12},{12,4},{4,0},{1,9},{9... | collective-permute-start | bytes 393224 | tf_op jit(solution)/shard_map/ppermute | solution.py:518
  26.8 1.6 %collective-permute-start.25 = (f32[256,128]{1,0:T(8,128)S(1)}, f32[256,128]{1,0:T(8,128)S(1)}, u32[]{:S(2)}, u32[]{:S(2)}) collective-permute-start(f32[256,128]{1,0:T(8,128)S(1)} %collective-permute-done.24.refs_6_), channel_id=1, source_target_pairs={{0,8},{8,16},{16,24},{24,28},{28,20},{20,12},{12,4},{4,0},{1,9},{9... | collective-permute-start | bytes 393224 | tf_op jit(solution)/shard_map/ppermute | solution.py:518
  29.0 2.3 %first_solve.2 = (f32[1536,128]{1,0:T(8,128)S(1)}, f32[264,128]{1,0:T(8,128)S(1)}, f32[264,128]{1,0:T(8,128)S(1)}, f32[264,128]{1,0:T(8,128)S(1)}, f32[264,128]{...) custom-call(s32[32]{0:T(128)S(1)} %get-tuple-element.69.refs_0_, ...), custom_call_target="tpu_custom_call" | custom-call | flops 603979776 | bytes 8388608 | tf_op jit(solution)/shard_map/first_solve/pallas_call | solution.py:63
  31.3 1.6 %collective-permute-start.7 = (f32[264,128]{1,0:T(8,128)S(1)}, f32[264,128]{1,0:T(8,128)S(1)}, u32[]{:S(2)}, u32[]{:S(2)}) collective-permute-start(f32[264,128]{1,0:T(8,128)S(1)} %get-tuple-element.81), channel_id=1, source_target_pairs={{0,8},{8,16},{16,24},{24,28},{28,20},{20,12},{12,4},{4,0},{1,9},{9... | collective-permute-start | bytes 405512 | tf_op jit(solution)/shard_map/ppermute | solution.py:518
  33.0 2.3 %first_solve.3 = (f32[1536,128]{1,0:T(8,128)S(1)}, f32[256,128]{1,0:T(8,128)S(1)}, f32[256,128]{1,0:T(8,128)S(1)}, f32[256,128]{1,0:T(8,128)S(1)}, f32[256,128]{...) custom-call(s32[32]{0:T(128)S(1)} %get-tuple-element.69.refs_0_, ...), custom_call_target="tpu_custom_call" | custom-call | flops 603979776 | bytes 8388608 | tf_op jit(solution)/shard_map/first_solve/pallas_call | solution.py:63
  35.3 1.6 %collective-permute-start.26 = (f32[256,128]{1,0:T(8,128)S(1)}, f32[256,128]{1,0:T(8,128)S(1)}, u32[]{:S(2)}, u32[]{:S(2)}) collective-permute-start(f32[256,128]{1,0:T(8,128)S(1)} %get-tuple-element.94), channel_id=1, source_target_pairs={{0,8},{8,16},{16,24},{24,28},{28,20},{20,12},{12,4},{4,0},{1,9},{9... | collective-permute-start | bytes 393224 | tf_op jit(solution)/shard_map/ppermute | solution.py:518
  37.8 1.6 %collective-permute-start.8 = (f32[264,128]{1,0:T(8,128)S(1)}, f32[264,128]{1,0:T(8,128)S(1)}, u32[]{:S(2)}, u32[]{:S(2)}) collective-permute-start(f32[264,128]{1,0:T(8,128)S(1)} %add_pairs.20), channel_id=1, source_target_pairs={{0,8},{8,16},{16,24},{24,28},{28,20},{20,12},{12,4},{4,0},{1,9},{9... | collective-permute-start | bytes 405512 | tf_op jit(solution)/shard_map/ppermute | solution.py:518
  39.9 1.6 %collective-permute-done.26.refs_0_ = f32[256,128]{1,0:T(8,128)S(1)} collective-permute-done((f32[256,128]{1,0:T(8,128)S(1)}, f32[256,128]{1,0:T(8,128)S(1)}, u32[]{:S(2)}, u32[]{:S(2)}) %collective-permute-start.26) | collective-permute-done | bytes 131104 | tf_op jit(solution)/shard_map/ppermute | solution.py:518
  41.5 1.7 %collective-permute-start.27 = (f32[256,128]{1,0:T(8,128)S(1)}, f32[256,128]{1,0:T(8,128)S(1)}, u32[]{:S(2)}, u32[]{:S(2)}) collective-permute-start(f32[256,128]{1,0:T(8,128)S(1)} %add_pairs.25), channel_id=1, source_target_pairs={{0,8},{8,16},{16,24},{24,28},{28,20},{20,12},{12,4},{4,0},{1,9},{9... | collective-permute-start | bytes 393224 | tf_op jit(solution)/shard_map/ppermute | solution.py:518
  44.4 1.7 %collective-permute-start.9 = (f32[264,128]{1,0:T(8,128)S(1)}, f32[264,128]{1,0:T(8,128)S(1)}, u32[]{:S(2)}, u32[]{:S(2)}) collective-permute-start(f32[264,128]{1,0:T(8,128)S(1)} %add_pairs.21), channel_id=1, source_target_pairs={{0,8},{8,16},{16,24},{24,28},{28,20},{20,12},{12,4},{4,0},{1,9},{9... | collective-permute-start | bytes 405512 | tf_op jit(solution)/shard_map/ppermute | solution.py:518
  47.7 1.5 %collective-permute-start.28 = (f32[256,128]{1,0:T(8,128)S(1)}, f32[256,128]{1,0:T(8,128)S(1)}, u32[]{:S(2)}, u32[]{:S(2)}) collective-permute-start(f32[256,128]{1,0:T(8,128)S(1)} %add_pairs.26), channel_id=1, source_target_pairs={{0,8},{8,16},{16,24},{24,28},{28,20},{20,12},{12,4},{4,0},{1,9},{9... | collective-permute-start | bytes 393224 | tf_op jit(solution)/shard_map/ppermute | solution.py:518
  50.8 1.7 %collective-permute-start.10 = (f32[264,128]{1,0:T(8,128)S(1)}, f32[264,128]{1,0:T(8,128)S(1)}, u32[]{:S(2)}, u32[]{:S(2)}) collective-permute-start(f32[264,128]{1,0:T(8,128)S(1)} %add_pairs.22), channel_id=1, source_target_pairs={{0,8},{8,16},{16,24},{24,28},{28,20},{20,12},{12,4},{4,0},{1,9},{9... | collective-permute-start | bytes 405512 | tf_op jit(solution)/shard_map/ppermute | solution.py:518
  53.6 1.7 %collective-permute-start.29 = (f32[256,128]{1,0:T(8,128)S(1)}, f32[256,128]{1,0:T(8,128)S(1)}, u32[]{:S(2)}, u32[]{:S(2)}) collective-permute-start(f32[256,128]{1,0:T(8,128)S(1)} %add_pairs.27), channel_id=1, source_target_pairs={{0,8},{8,16},{16,24},{24,28},{28,20},{20,12},{12,4},{4,0},{1,9},{9... | collective-permute-start | bytes 393224 | tf_op jit(solution)/shard_map/ppermute | solution.py:518
  55.3 1.8 %collective-permute-done.10.refs_1_ = f32[264,128]{1,0:T(8,128)S(1)} collective-permute-done((f32[264,128]{1,0:T(8,128)S(1)}, f32[264,128]{1,0:T(8,128)S(1)}, u32[]{:S(2)}, u32[]{:S(2)}) %collective-permute-start.10) | collective-permute-done | bytes 135200 | tf_op jit(solution)/shard_map/ppermute | solution.py:518
  57.1 1.5 %collective-permute-start.17 = (f32[256,128]{1,0:T(8,128)S(1)}, f32[256,128]{1,0:T(8,128)S(1)}, u32[]{:S(2)}, u32[]{:S(2)}) collective-permute-start(f32[256,128]{1,0:T(8,128)S(1)} %get-tuple-element.88.refs_1_.refs_3_), channel_id=1, source_target_pairs={{0,8},{8,16},{16,24},{24,28},{28,20},{20,12},{12,4},{4,0},{1,9},{9... | collective-permute-start | bytes 393224 | tf_op jit(solution)/shard_map/ppermute | solution.py:518
  60.1 1.7 %collective-permute-start.36 = (f32[256,128]{1,0:T(8,128)S(1)}, f32[256,128]{1,0:T(8,128)S(1)}, u32[]{:S(2)}, u32[]{:S(2)}) collective-permute-start(f32[256,128]{1,0:T(8,128)S(1)} %get-tuple-element.102.refs_1_.refs_3_), channel_id=1, source_target_pairs={{0,8},{8,16},{16,24},{24,28},{28,20},{20,12},{12,4},{4,0},{1,9},{9... | collective-permute-start | bytes 393224 | tf_op jit(solution)/shard_map/ppermute | solution.py:518
  66.4 1.5 %collective-permute-start.37 = (f32[256,128]{1,0:T(8,128)S(1)}, f32[256,128]{1,0:T(8,128)S(1)}, u32[]{:S(2)}, u32[]{:S(2)}) collective-permute-start(f32[256,128]{1,0:T(8,128)S(1)} %collective-permute-done.36.refs_8_), channel_id=1, source_target_pairs={{0,8},{8,16},{16,24},{24,28},{28,20},{20,12},{12,4},{4,0},{1,9},{9... | collective-permute-start | bytes 393224 | tf_op jit(solution)/shard_map/ppermute | solution.py:518
  69.5 1.6 %collective-permute-start.19 = (f32[256,128]{1,0:T(8,128)S(1)}, f32[256,128]{1,0:T(8,128)S(1)}, u32[]{:S(2)}, u32[]{:S(2)}) collective-permute-start(f32[256,128]{1,0:T(8,128)S(1)} %collective-permute-done.18.refs_7_), channel_id=1, source_target_pairs={{0,8},{8,16},{16,24},{24,28},{28,20},{20,12},{12,4},{4,0},{1,9},{9... | collective-permute-start | bytes 393224 | tf_op jit(solution)/shard_map/ppermute | solution.py:518
  76.9 1.9 %collective-permute-done.38.refs_6_ = f32[256,128]{1,0:T(8,128)S(1)} collective-permute-done((f32[256,128]{1,0:T(8,128)S(1)}, f32[256,128]{1,0:T(8,128)S(1)}, u32[]{:S(2)}, u32[]{:S(2)}) %collective-permute-start.38) | collective-permute-done | bytes 131104 | tf_op jit(solution)/shard_map/ppermute | solution.py:518
  80.7 2.7 %second_solve.2 = (f32[1536,128]{1,0:T(8,128)S(1)}, bf16[1664,128]{1,0:T(8,128)(2,1)S(1)}, f32[1664,128]{1,0:T(8,128)S(1)}, f32[16,128]{1,0:T(8,128)S(1)}, f32[2...) custom-call(s32[32]{0:T(128)S(1)} %get-tuple-element.69.refs_0_, ...), custom_call_target="tpu_custom_call" | custom-call | flops 603979776 | bytes 8388608 | tf_op jit(solution)/shard_map/second_solve/pallas_call | solution.py:63
  83.4 2.0 %collective-permute-start.40 = (f32[256,128]{1,0:T(8,128)S(1)}, f32[256,128]{1,0:T(8,128)S(1)}, u32[]{:S(2)}, u32[]{:S(2)}) collective-permute-start(f32[256,128]{1,0:T(8,128)S(1)} %get-tuple-element.108), channel_id=1, source_target_pairs={{0,8},{8,16},{16,24},{24,28},{28,20},{20,12},{12,4},{4,0},{1,9},{9... | collective-permute-start | bytes 393224 | tf_op jit(solution)/shard_map/ppermute | solution.py:518
  85.4 2.7 %second_solve.3 = (f32[1536,128]{1,0:T(8,128)S(1)}, bf16[1664,128]{1,0:T(8,128)(2,1)S(1)}, f32[1664,128]{1,0:T(8,128)S(1)}, f32[16,128]{1,0:T(8,128)S(1)}, f32[2...) custom-call(s32[32]{0:T(128)S(1)} %get-tuple-element.69.refs_0_, ...), custom_call_target="tpu_custom_call" | custom-call | flops 603979776 | bytes 8388608 | tf_op jit(solution)/shard_map/second_solve/pallas_call | solution.py:63
  88.7 1.5 %collective-permute-start.58 = (f32[256,128]{1,0:T(8,128)S(1)}, f32[256,128]{1,0:T(8,128)S(1)}, u32[]{:S(2)}, u32[]{:S(2)}) collective-permute-start(f32[256,128]{1,0:T(8,128)S(1)} %get-tuple-element.121), channel_id=1, source_target_pairs={{8,0},{16,8},{24,16},{28,24},{20,28},{12,20},{4,12},{0,4},{9,1},{1... | collective-permute-start | bytes 393224 | tf_op jit(solution)/shard_map/ppermute | solution.py:521
  90.2 2.0 %collective-permute-start.41 = (f32[256,128]{1,0:T(8,128)S(1)}, f32[256,128]{1,0:T(8,128)S(1)}, u32[]{:S(2)}, u32[]{:S(2)}) collective-permute-start(f32[256,128]{1,0:T(8,128)S(1)} %add_pairs.30), channel_id=1, source_target_pairs={{0,8},{8,16},{16,24},{24,28},{28,20},{20,12},{12,4},{4,0},{1,9},{9... | collective-permute-start | bytes 393224 | tf_op jit(solution)/shard_map/ppermute | solution.py:518
  92.3 1.7 %collective-permute-done.54.refs_0_ = f32[256,128]{1,0:T(8,128)S(1)} collective-permute-done((f32[256,128]{1,0:T(8,128)S(1)}, f32[256,128]{1,0:T(8,128)S(1)}, u32[]{:S(2)}, u32[]{:S(2)}) %collective-permute-start.54) | collective-permute-done | bytes 131104 | tf_op jit(solution)/shard_map/ppermute | solution.py:518
  94.6 1.6 %collective-permute-start.59 = (f32[256,128]{1,0:T(8,128)S(1)}, f32[256,128]{1,0:T(8,128)S(1)}, u32[]{:S(2)}, u32[]{:S(2)}) collective-permute-start(f32[256,128]{1,0:T(8,128)S(1)} %add_pairs.38), channel_id=1, source_target_pairs={{8,0},{16,8},{24,16},{28,24},{20,28},{12,20},{4,12},{0,4},{9,1},{1... | collective-permute-start | bytes 393224 | tf_op jit(solution)/shard_map/ppermute | solution.py:521
  96.8 1.7 %collective-permute-start.42 = (f32[256,128]{1,0:T(8,128)S(1)}, f32[256,128]{1,0:T(8,128)S(1)}, u32[]{:S(2)}, u32[]{:S(2)}) collective-permute-start(f32[256,128]{1,0:T(8,128)S(1)} %add_pairs.31), channel_id=1, source_target_pairs={{0,8},{8,16},{16,24},{24,28},{28,20},{20,12},{12,4},{4,0},{1,9},{9... | collective-permute-start | bytes 393224 | tf_op jit(solution)/shard_map/ppermute | solution.py:518
  103.2 1.7 %collective-permute-start.43 = (f32[256,128]{1,0:T(8,128)S(1)}, f32[256,128]{1,0:T(8,128)S(1)}, u32[]{:S(2)}, u32[]{:S(2)}) collective-permute-start(f32[256,128]{1,0:T(8,128)S(1)} %add_pairs.32), channel_id=1, source_target_pairs={{0,8},{8,16},{16,24},{24,28},{28,20},{20,12},{12,4},{4,0},{1,9},{9... | collective-permute-start | bytes 393224 | tf_op jit(solution)/shard_map/ppermute | solution.py:518
  106.0 1.7 %collective-permute-start.57 = (f32[256,128]{1,0:T(8,128)S(1)}, f32[256,128]{1,0:T(8,128)S(1)}, u32[]{:S(2)}, u32[]{:S(2)}) collective-permute-start(f32[256,128]{1,0:T(8,128)S(1)} %add_pairs.37), channel_id=1, source_target_pairs={{0,8},{8,16},{16,24},{24,28},{28,20},{20,12},{12,4},{4,0},{1,9},{9... | collective-permute-start | bytes 393224 | tf_op jit(solution)/shard_map/ppermute | solution.py:518
  109.0 3.4 %collective-permute-done.57.refs_1_ = f32[256,128]{1,0:T(8,128)S(1)} collective-permute-done((f32[256,128]{1,0:T(8,128)S(1)}, f32[256,128]{1,0:T(8,128)S(1)}, u32[]{:S(2)}, u32[]{:S(2)}) %collective-permute-start.57) | collective-permute-done | bytes 131104 | tf_op jit(solution)/shard_map/ppermute | solution.py:518
  113.1 1.6 %collective-permute-start.64 = (f32[264,128]{1,0:T(8,128)S(1)}, f32[264,128]{1,0:T(8,128)S(1)}, u32[]{:S(2)}, u32[]{:S(2)}) collective-permute-start(f32[264,128]{1,0:T(8,128)S(1)} %get-tuple-element.129.refs_9_.refs_0_), channel_id=1, source_target_pairs={{0,8},{8,16},{16,24},{24,28},{28,20},{20,12},{12,4},{4,0},{1,9},{9... | collective-permute-start | bytes 405512 | tf_op jit(solution)/shard_map/ppermute | solution.py:518
  116.7 2.8 %collective-permute-done.64.refs_16_.refs_7_ = f32[264,128]{1,0:T(8,128)S(1)} collective-permute-done((f32[264,128]{1,0:T(8,128)S(1)}, f32[264,128]{1,0:T(8,128)S(1)}, u32[]{:S(2)}, u32[]{:S(2)}) %collective-permute-start.64) | collective-permute-done | bytes 135200 | tf_op jit(solution)/shard_map/ppermute | solution.py:518
  119.5 1.5 %collective-permute-start.65 = (f32[264,128]{1,0:T(8,128)S(1)}, f32[264,128]{1,0:T(8,128)S(1)}, u32[]{:S(2)}, u32[]{:S(2)}) collective-permute-start(f32[264,128]{1,0:T(8,128)S(1)} %collective-permute-done.64.refs_16_.refs_7_), channel_id=1, source_target_pairs={{0,8},{8,16},{16,24},{24,28},{28,20},{20,12},{12,4},{4,0},{1,9},{9... | collective-permute-start | bytes 405512 | tf_op jit(solution)/shard_map/ppermute | solution.py:518
  121.5 1.5 %collective-permute-start.51 = (f32[256,128]{1,0:T(8,128)S(1)}, f32[256,128]{1,0:T(8,128)S(1)}, u32[]{:S(2)}, u32[]{:S(2)}) collective-permute-start(f32[256,128]{1,0:T(8,128)S(1)} %collective-permute-done.50.refs_8_), channel_id=1, source_target_pairs={{0,8},{8,16},{16,24},{24,28},{28,20},{20,12},{12,4},{4,0},{1,9},{9... | collective-permute-start | bytes 393224 | tf_op jit(solution)/shard_map/ppermute | solution.py:518
  124.5 1.5 %collective-permute-start.66 = (f32[264,128]{1,0:T(8,128)S(1)}, f32[264,128]{1,0:T(8,128)S(1)}, u32[]{:S(2)}, u32[]{:S(2)}) collective-permute-start(f32[264,128]{1,0:T(8,128)S(1)} %collective-permute-done.65.refs_15_.refs_6_), channel_id=1, source_target_pairs={{0,8},{8,16},{16,24},{24,28},{28,20},{20,12},{12,4},{4,0},{1,9},{9... | collective-permute-start | bytes 405512 | tf_op jit(solution)/shard_map/ppermute | solution.py:518
  126.5 1.5 %collective-permute-start.52 = (f32[256,128]{1,0:T(8,128)S(1)}, f32[256,128]{1,0:T(8,128)S(1)}, u32[]{:S(2)}, u32[]{:S(2)}) collective-permute-start(f32[256,128]{1,0:T(8,128)S(1)} %collective-permute-done.51.refs_7_), channel_id=1, source_target_pairs={{0,8},{8,16},{16,24},{24,28},{28,20},{20,12},{12,4},{4,0},{1,9},{9... | collective-permute-start | bytes 393224 | tf_op jit(solution)/shard_map/ppermute | solution.py:518
  129.5 1.5 %collective-permute-start.67 = (f32[264,128]{1,0:T(8,128)S(1)}, f32[264,128]{1,0:T(8,128)S(1)}, u32[]{:S(2)}, u32[]{:S(2)}) collective-permute-start(f32[264,128]{1,0:T(8,128)S(1)} %collective-permute-done.66.refs_14_.refs_5_), channel_id=1, source_target_pairs={{0,8},{8,16},{16,24},{24,28},{28,20},{20,12},{12,4},{4,0},{1,9},{9... | collective-permute-start | bytes 405512 | tf_op jit(solution)/shard_map/ppermute | solution.py:518
  131.5 1.5 %collective-permute-start.53 = (f32[256,128]{1,0:T(8,128)S(1)}, f32[256,128]{1,0:T(8,128)S(1)}, u32[]{:S(2)}, u32[]{:S(2)}) collective-permute-start(f32[256,128]{1,0:T(8,128)S(1)} %collective-permute-done.52.refs_6_), channel_id=1, source_target_pairs={{0,8},{8,16},{16,24},{24,28},{28,20},{20,12},{12,4},{4,0},{1,9},{9... | collective-permute-start | bytes 393224 | tf_op jit(solution)/shard_map/ppermute | solution.py:518
  133.1 1.8 %store_state.1.refs_8_ = f32[2048,256]{1,0:T(8,128)} custom-call(f32[1536,128]{1,0:T(8,128)S(1)} %get-tuple-element.90.refs_0_, f32[1536,128]{1,0:T(8,128)S(1)} %get-tuple-element.104.refs_1_, bf16[1664,128]{1,0:T(8,128)(2,1)S(1)} %get-tuple-element.105.refs_2_, bf16[1664,128]{1,0:T(8,128)(2,1)S(1)} %get-tuple-element.106.refs_3_, ...), custom_call_target="tpu_custom_call" | custom-call | flops 402653184 | bytes 4194304 | tf_op jit(solution)/shard_map/store_state/pallas_call | solution.py:63
  136.9 2.2 %finish.1 = (f32[1536,256]{1,0:T(8,128)}, f32[256,256]{1,0:T(8,128)}) custom-call(s32[32]{0:T(128)S(1)} %get-tuple-element.69.refs_0_, f32[256,128]{1,0:T(8,128)S(1)} %get-tuple-element.115.refs_1_, f32[256,128]{1,0:T(8,128)S(1)} %collective-permute-done.47.refs_2_, f32[256,128]{1,0:T(8,128)S(1)} %collective-permute-done.48.refs_3_, ...), custom_call_target="tpu_custom_call" | custom-call | bytes 3145728 | tf_op jit(solution)/shard_map/finish/pallas_call | solution.py:63
  (140 shorter events, 49.1 us)
Async XLA Ops:
  0.6 9.5 %collective-permute-start = (f32[256,256]{1,0:T(8,128)}, f32[256,256]{1,0:T(8,128)S(1)}, u32[]{:S(2)}, u32[]{:S(2)}) collective-permute-start(f32[256,256]{1,0:T(8,128)} %refs_3_.1), channel_id=1, source_target_pairs={{0,8},{8,16},{16,24},{24,28},{28,20},{20,12},{12,4},{4,0},{1,9},{9... | collective-permute-start | bytes 786440 | tf_op jit(solution)/shard_map/ppermute | solution.py:518
  3.7 8.0 %collective-permute-start.1 = (f32[256,256]{1,0:T(8,128)}, f32[256,256]{1,0:T(8,128)S(1)}, u32[]{:S(2)}, u32[]{:S(2)}) collective-permute-start(f32[256,256]{1,0:T(8,128)} %refs_3_.1), channel_id=1, source_target_pairs={{8,0},{16,8},{24,16},{28,24},{20,28},{12,20},{4,12},{0,4},{9,1},{1... | collective-permute-start | bytes 786440 | tf_op jit(solution)/shard_map/ppermute | solution.py:521
  13.8 6.6 %collective-permute-start.23 = (f32[256,128]{1,0:T(8,128)S(1)}, f32[256,128]{1,0:T(8,128)S(1)}, u32[]{:S(2)}, u32[]{:S(2)}) collective-permute-start(f32[256,128]{1,0:T(8,128)S(1)} %get-tuple-element.92.refs_8_), channel_id=1, source_target_pairs={{0,8},{8,16},{16,24},{24,28},{28,20},{20,12},{12,4},{4,0},{1,9},{9... | collective-permute-start | bytes 393224 | tf_op jit(solution)/shard_map/ppermute | solution.py:518
  20.0 6.3 %collective-permute-start.21 = (f32[256,128]{1,0:T(8,128)S(1)}, f32[256,128]{1,0:T(8,128)S(1)}, u32[]{:S(2)}, u32[]{:S(2)}) collective-permute-start(f32[256,128]{1,0:T(8,128)S(1)} %get-tuple-element.91.refs_2_), channel_id=1, source_target_pairs={{8,0},{16,8},{24,16},{28,24},{20,28},{12,20},{4,12},{0,4},{9,1},{1... | collective-permute-start | bytes 393224 | tf_op jit(solution)/shard_map/ppermute | solution.py:521
  20.5 6.4 %collective-permute-start.24 = (f32[256,128]{1,0:T(8,128)S(1)}, f32[256,128]{1,0:T(8,128)S(1)}, u32[]{:S(2)}, u32[]{:S(2)}) collective-permute-start(f32[256,128]{1,0:T(8,128)S(1)} %collective-permute-done.23.refs_7_), channel_id=1, source_target_pairs={{0,8},{8,16},{16,24},{24,28},{28,20},{20,12},{12,4},{4,0},{1,9},{9... | collective-permute-start | bytes 393224 | tf_op jit(solution)/shard_map/ppermute | solution.py:518
  26.4 6.6 %collective-permute-start.22 = (f32[256,128]{1,0:T(8,128)S(1)}, f32[256,128]{1,0:T(8,128)S(1)}, u32[]{:S(2)}, u32[]{:S(2)}) collective-permute-start(f32[256,128]{1,0:T(8,128)S(1)} %collective-permute-done.21.refs_3_), channel_id=1, source_target_pairs={{8,0},{16,8},{24,16},{28,24},{20,28},{12,20},{4,12},{0,4},{9,1},{1... | collective-permute-start | bytes 393224 | tf_op jit(solution)/shard_map/ppermute | solution.py:521
  26.8 6.1 %collective-permute-start.25 = (f32[256,128]{1,0:T(8,128)S(1)}, f32[256,128]{1,0:T(8,128)S(1)}, u32[]{:S(2)}, u32[]{:S(2)}) collective-permute-start(f32[256,128]{1,0:T(8,128)S(1)} %collective-permute-done.24.refs_6_), channel_id=1, source_target_pairs={{0,8},{8,16},{16,24},{24,28},{28,20},{20,12},{12,4},{4,0},{1,9},{9... | collective-permute-start | bytes 393224 | tf_op jit(solution)/shard_map/ppermute | solution.py:518
  31.3 6.5 %collective-permute-start.7 = (f32[264,128]{1,0:T(8,128)S(1)}, f32[264,128]{1,0:T(8,128)S(1)}, u32[]{:S(2)}, u32[]{:S(2)}) collective-permute-start(f32[264,128]{1,0:T(8,128)S(1)} %get-tuple-element.81), channel_id=1, source_target_pairs={{0,8},{8,16},{16,24},{24,28},{28,20},{20,12},{12,4},{4,0},{1,9},{9... | collective-permute-start | bytes 405512 | tf_op jit(solution)/shard_map/ppermute | solution.py:518
  35.3 6.2 %collective-permute-start.26 = (f32[256,128]{1,0:T(8,128)S(1)}, f32[256,128]{1,0:T(8,128)S(1)}, u32[]{:S(2)}, u32[]{:S(2)}) collective-permute-start(f32[256,128]{1,0:T(8,128)S(1)} %get-tuple-element.94), channel_id=1, source_target_pairs={{0,8},{8,16},{16,24},{24,28},{28,20},{20,12},{12,4},{4,0},{1,9},{9... | collective-permute-start | bytes 393224 | tf_op jit(solution)/shard_map/ppermute | solution.py:518
  36.9 6.5 %collective-permute-start.11 = (f32[264,128]{1,0:T(8,128)S(1)}, f32[264,128]{1,0:T(8,128)S(1)}, u32[]{:S(2)}, u32[]{:S(2)}) collective-permute-start(f32[264,128]{1,0:T(8,128)S(1)} %get-tuple-element.85), channel_id=1, source_target_pairs={{8,0},{16,8},{24,16},{28,24},{20,28},{12,20},{4,12},{0,4},{9,1},{1... | collective-permute-start | bytes 405512 | tf_op jit(solution)/shard_map/ppermute | solution.py:521
  37.8 6.5 %collective-permute-start.8 = (f32[264,128]{1,0:T(8,128)S(1)}, f32[264,128]{1,0:T(8,128)S(1)}, u32[]{:S(2)}, u32[]{:S(2)}) collective-permute-start(f32[264,128]{1,0:T(8,128)S(1)} %add_pairs.20), channel_id=1, source_target_pairs={{0,8},{8,16},{16,24},{24,28},{28,20},{20,12},{12,4},{4,0},{1,9},{9... | collective-permute-start | bytes 405512 | tf_op jit(solution)/shard_map/ppermute | solution.py:518
  39.4 6.7 %collective-permute-start.30 = (f32[256,128]{1,0:T(8,128)S(1)}, f32[256,128]{1,0:T(8,128)S(1)}, u32[]{:S(2)}, u32[]{:S(2)}) collective-permute-start(f32[256,128]{1,0:T(8,128)S(1)} %get-tuple-element.98), channel_id=1, source_target_pairs={{8,0},{16,8},{24,16},{28,24},{20,28},{12,20},{4,12},{0,4},{9,1},{1... | collective-permute-start | bytes 393224 | tf_op jit(solution)/shard_map/ppermute | solution.py:521
  41.5 6.2 %collective-permute-start.27 = (f32[256,128]{1,0:T(8,128)S(1)}, f32[256,128]{1,0:T(8,128)S(1)}, u32[]{:S(2)}, u32[]{:S(2)}) collective-permute-start(f32[256,128]{1,0:T(8,128)S(1)} %add_pairs.25), channel_id=1, source_target_pairs={{0,8},{8,16},{16,24},{24,28},{28,20},{20,12},{12,4},{4,0},{1,9},{9... | collective-permute-start | bytes 393224 | tf_op jit(solution)/shard_map/ppermute | solution.py:518
  43.4 5.7 %collective-permute-start.12 = (f32[264,128]{1,0:T(8,128)S(1)}, f32[264,128]{1,0:T(8,128)S(1)}, u32[]{:S(2)}, u32[]{:S(2)}) collective-permute-start(f32[264,128]{1,0:T(8,128)S(1)} %add_pairs.23), channel_id=1, source_target_pairs={{8,0},{16,8},{24,16},{28,24},{20,28},{12,20},{4,12},{0,4},{9,1},{1... | collective-permute-start | bytes 405512 | tf_op jit(solution)/shard_map/ppermute | solution.py:521
  44.4 6.5 %collective-permute-start.9 = (f32[264,128]{1,0:T(8,128)S(1)}, f32[264,128]{1,0:T(8,128)S(1)}, u32[]{:S(2)}, u32[]{:S(2)}) collective-permute-start(f32[264,128]{1,0:T(8,128)S(1)} %add_pairs.21), channel_id=1, source_target_pairs={{0,8},{8,16},{16,24},{24,28},{28,20},{20,12},{12,4},{4,0},{1,9},{9... | collective-permute-start | bytes 405512 | tf_op jit(solution)/shard_map/ppermute | solution.py:518
  46.2 6.4 %collective-permute-start.31 = (f32[256,128]{1,0:T(8,128)S(1)}, f32[256,128]{1,0:T(8,128)S(1)}, u32[]{:S(2)}, u32[]{:S(2)}) collective-permute-start(f32[256,128]{1,0:T(8,128)S(1)} %add_pairs.28), channel_id=1, source_target_pairs={{8,0},{16,8},{24,16},{28,24},{20,28},{12,20},{4,12},{0,4},{9,1},{1... | collective-permute-start | bytes 393224 | tf_op jit(solution)/shard_map/ppermute | solution.py:521
  47.7 5.9 %collective-permute-start.28 = (f32[256,128]{1,0:T(8,128)S(1)}, f32[256,128]{1,0:T(8,128)S(1)}, u32[]{:S(2)}, u32[]{:S(2)}) collective-permute-start(f32[256,128]{1,0:T(8,128)S(1)} %add_pairs.26), channel_id=1, source_target_pairs={{0,8},{8,16},{16,24},{24,28},{28,20},{20,12},{12,4},{4,0},{1,9},{9... | collective-permute-start | bytes 393224 | tf_op jit(solution)/shard_map/ppermute | solution.py:518
  49.1 6.1 %collective-permute-start.13 = (f32[264,128]{1,0:T(8,128)S(1)}, f32[264,128]{1,0:T(8,128)S(1)}, u32[]{:S(2)}, u32[]{:S(2)}) collective-permute-start(f32[264,128]{1,0:T(8,128)S(1)} %add_pairs.24), channel_id=1, source_target_pairs={{8,0},{16,8},{24,16},{28,24},{20,28},{12,20},{4,12},{0,4},{9,1},{1... | collective-permute-start | bytes 405512 | tf_op jit(solution)/shard_map/ppermute | solution.py:521
  50.8 6.3 %collective-permute-start.10 = (f32[264,128]{1,0:T(8,128)S(1)}, f32[264,128]{1,0:T(8,128)S(1)}, u32[]{:S(2)}, u32[]{:S(2)}) collective-permute-start(f32[264,128]{1,0:T(8,128)S(1)} %add_pairs.22), channel_id=1, source_target_pairs={{0,8},{8,16},{16,24},{24,28},{28,20},{20,12},{12,4},{4,0},{1,9},{9... | collective-permute-start | bytes 405512 | tf_op jit(solution)/shard_map/ppermute | solution.py:518
  52.6 6.2 %collective-permute-start.32 = (f32[256,128]{1,0:T(8,128)S(1)}, f32[256,128]{1,0:T(8,128)S(1)}, u32[]{:S(2)}, u32[]{:S(2)}) collective-permute-start(f32[256,128]{1,0:T(8,128)S(1)} %add_pairs.29), channel_id=1, source_target_pairs={{8,0},{16,8},{24,16},{28,24},{20,28},{12,20},{4,12},{0,4},{9,1},{1... | collective-permute-start | bytes 393224 | tf_op jit(solution)/shard_map/ppermute | solution.py:521
  53.6 6.5 %collective-permute-start.29 = (f32[256,128]{1,0:T(8,128)S(1)}, f32[256,128]{1,0:T(8,128)S(1)}, u32[]{:S(2)}, u32[]{:S(2)}) collective-permute-start(f32[256,128]{1,0:T(8,128)S(1)} %add_pairs.27), channel_id=1, source_target_pairs={{0,8},{8,16},{16,24},{24,28},{28,20},{20,12},{12,4},{4,0},{1,9},{9... | collective-permute-start | bytes 393224 | tf_op jit(solution)/shard_map/ppermute | solution.py:518
  57.1 6.4 %collective-permute-start.17 = (f32[256,128]{1,0:T(8,128)S(1)}, f32[256,128]{1,0:T(8,128)S(1)}, u32[]{:S(2)}, u32[]{:S(2)}) collective-permute-start(f32[256,128]{1,0:T(8,128)S(1)} %get-tuple-element.88.refs_1_.refs_3_), channel_id=1, source_target_pairs={{0,8},{8,16},{16,24},{24,28},{28,20},{20,12},{12,4},{4,0},{1,9},{9... | collective-permute-start | bytes 393224 | tf_op jit(solution)/shard_map/ppermute | solution.py:518
  60.1 6.3 %collective-permute-start.36 = (f32[256,128]{1,0:T(8,128)S(1)}, f32[256,128]{1,0:T(8,128)S(1)}, u32[]{:S(2)}, u32[]{:S(2)}) collective-permute-start(f32[256,128]{1,0:T(8,128)S(1)} %get-tuple-element.102.refs_1_.refs_3_), channel_id=1, source_target_pairs={{0,8},{8,16},{16,24},{24,28},{28,20},{20,12},{12,4},{4,0},{1,9},{9... | collective-permute-start | bytes 393224 | tf_op jit(solution)/shard_map/ppermute | solution.py:518
  61.8 6.1 %collective-permute-start.14 = (f32[256,128]{1,0:T(8,128)S(1)}, f32[256,128]{1,0:T(8,128)S(1)}, u32[]{:S(2)}, u32[]{:S(2)}) collective-permute-start(f32[256,128]{1,0:T(8,128)S(1)} %get-tuple-element.88.refs_1_.refs_3_), channel_id=1, source_target_pairs={{8,0},{16,8},{24,16},{28,24},{20,28},{12,20},{4,12},{0,4},{9,1},{1... | collective-permute-start | bytes 393224 | tf_op jit(solution)/shard_map/ppermute | solution.py:521
  63.6 5.9 %collective-permute-start.18 = (f32[256,128]{1,0:T(8,128)S(1)}, f32[256,128]{1,0:T(8,128)S(1)}, u32[]{:S(2)}, u32[]{:S(2)}) collective-permute-start(f32[256,128]{1,0:T(8,128)S(1)} %collective-permute-done.17.refs_8_), channel_id=1, source_target_pairs={{0,8},{8,16},{16,24},{24,28},{28,20},{20,12},{12,4},{4,0},{1,9},{9... | collective-permute-start | bytes 393224 | tf_op jit(solution)/shard_map/ppermute | solution.py:518
  64.7 6.3 %collective-permute-start.33 = (f32[256,128]{1,0:T(8,128)S(1)}, f32[256,128]{1,0:T(8,128)S(1)}, u32[]{:S(2)}, u32[]{:S(2)}) collective-permute-start(f32[256,128]{1,0:T(8,128)S(1)} %get-tuple-element.102.refs_1_.refs_3_), channel_id=1, source_target_pairs={{8,0},{16,8},{24,16},{28,24},{20,28},{12,20},{4,12},{0,4},{9,1},{1... | collective-permute-start | bytes 393224 | tf_op jit(solution)/shard_map/ppermute | solution.py:521
  66.4 6.4 %collective-permute-start.37 = (f32[256,128]{1,0:T(8,128)S(1)}, f32[256,128]{1,0:T(8,128)S(1)}, u32[]{:S(2)}, u32[]{:S(2)}) collective-permute-start(f32[256,128]{1,0:T(8,128)S(1)} %collective-permute-done.36.refs_8_), channel_id=1, source_target_pairs={{0,8},{8,16},{16,24},{24,28},{28,20},{20,12},{12,4},{4,0},{1,9},{9... | collective-permute-start | bytes 393224 | tf_op jit(solution)/shard_map/ppermute | solution.py:518
  67.9 6.2 %collective-permute-start.15 = (f32[256,128]{1,0:T(8,128)S(1)}, f32[256,128]{1,0:T(8,128)S(1)}, u32[]{:S(2)}, u32[]{:S(2)}) collective-permute-start(f32[256,128]{1,0:T(8,128)S(1)} %collective-permute-done.14.refs_2_), channel_id=1, source_target_pairs={{8,0},{16,8},{24,16},{28,24},{20,28},{12,20},{4,12},{0,4},{9,1},{1... | collective-permute-start | bytes 393224 | tf_op jit(solution)/shard_map/ppermute | solution.py:521
  72.8 5.9 %collective-permute-start.38 = (f32[256,128]{1,0:T(8,128)S(1)}, f32[256,128]{1,0:T(8,128)S(1)}, u32[]{:S(2)}, u32[]{:S(2)}) collective-permute-start(f32[256,128]{1,0:T(8,128)S(1)} %collective-permute-done.37.refs_7_), channel_id=1, source_target_pairs={{0,8},{8,16},{16,24},{24,28},{28,20},{20,12},{12,4},{4,0},{1,9},{9... | collective-permute-start | bytes 393224 | tf_op jit(solution)/shard_map/ppermute | solution.py:518
  74.1 5.9 %collective-permute-start.16 = (f32[256,128]{1,0:T(8,128)S(1)}, f32[256,128]{1,0:T(8,128)S(1)}, u32[]{:S(2)}, u32[]{:S(2)}) collective-permute-start(f32[256,128]{1,0:T(8,128)S(1)} %collective-permute-done.15.refs_3_), channel_id=1, source_target_pairs={{8,0},{16,8},{24,16},{28,24},{20,28},{12,20},{4,12},{0,4},{9,1},{1... | collective-permute-start | bytes 393224 | tf_op jit(solution)/shard_map/ppermute | solution.py:521
  74.9 5.8 %collective-permute-start.20 = (f32[256,128]{1,0:T(8,128)S(1)}, f32[256,128]{1,0:T(8,128)S(1)}, u32[]{:S(2)}, u32[]{:S(2)}) collective-permute-start(f32[256,128]{1,0:T(8,128)S(1)} %collective-permute-done.19.refs_6_), channel_id=1, source_target_pairs={{0,8},{8,16},{16,24},{24,28},{28,20},{20,12},{12,4},{4,0},{1,9},{9... | collective-permute-start | bytes 393224 | tf_op jit(solution)/shard_map/ppermute | solution.py:518
  76.2 9.2 %collective-permute-start.35 = (f32[256,128]{1,0:T(8,128)S(1)}, f32[256,128]{1,0:T(8,128)S(1)}, u32[]{:S(2)}, u32[]{:S(2)}) collective-permute-start(f32[256,128]{1,0:T(8,128)S(1)} %collective-permute-done.34.refs_3_), channel_id=1, source_target_pairs={{8,0},{16,8},{24,16},{28,24},{20,28},{12,20},{4,12},{0,4},{9,1},{1... | collective-permute-start | bytes 393224 | tf_op jit(solution)/shard_map/ppermute | solution.py:521
  78.8 6.6 %collective-permute-start.39 = (f32[256,128]{1,0:T(8,128)S(1)}, f32[256,128]{1,0:T(8,128)S(1)}, u32[]{:S(2)}, u32[]{:S(2)}) collective-permute-start(f32[256,128]{1,0:T(8,128)S(1)} %collective-permute-done.38.refs_6_), channel_id=1, source_target_pairs={{0,8},{8,16},{16,24},{24,28},{28,20},{20,12},{12,4},{4,0},{1,9},{9... | collective-permute-start | bytes 393224 | tf_op jit(solution)/shard_map/ppermute | solution.py:518
  83.4 6.8 %collective-permute-start.40 = (f32[256,128]{1,0:T(8,128)S(1)}, f32[256,128]{1,0:T(8,128)S(1)}, u32[]{:S(2)}, u32[]{:S(2)}) collective-permute-start(f32[256,128]{1,0:T(8,128)S(1)} %get-tuple-element.108), channel_id=1, source_target_pairs={{0,8},{8,16},{16,24},{24,28},{28,20},{20,12},{12,4},{4,0},{1,9},{9... | collective-permute-start | bytes 393224 | tf_op jit(solution)/shard_map/ppermute | solution.py:518
  88.1 5.9 %collective-permute-start.54 = (f32[256,128]{1,0:T(8,128)S(1)}, f32[256,128]{1,0:T(8,128)S(1)}, u32[]{:S(2)}, u32[]{:S(2)}) collective-permute-start(f32[256,128]{1,0:T(8,128)S(1)} %get-tuple-element.117), channel_id=1, source_target_pairs={{0,8},{8,16},{16,24},{24,28},{28,20},{20,12},{12,4},{4,0},{1,9},{9... | collective-permute-start | bytes 393224 | tf_op jit(solution)/shard_map/ppermute | solution.py:518
  88.7 5.9 %collective-permute-start.58 = (f32[256,128]{1,0:T(8,128)S(1)}, f32[256,128]{1,0:T(8,128)S(1)}, u32[]{:S(2)}, u32[]{:S(2)}) collective-permute-start(f32[256,128]{1,0:T(8,128)S(1)} %get-tuple-element.121), channel_id=1, source_target_pairs={{8,0},{16,8},{24,16},{28,24},{20,28},{12,20},{4,12},{0,4},{9,1},{1... | collective-permute-start | bytes 393224 | tf_op jit(solution)/shard_map/ppermute | solution.py:521
  90.2 6.0 %collective-permute-start.44 = (f32[256,128]{1,0:T(8,128)S(1)}, f32[256,128]{1,0:T(8,128)S(1)}, u32[]{:S(2)}, u32[]{:S(2)}) collective-permute-start(f32[256,128]{1,0:T(8,128)S(1)} %get-tuple-element.112), channel_id=1, source_target_pairs={{8,0},{16,8},{24,16},{28,24},{20,28},{12,20},{4,12},{0,4},{9,1},{1... | collective-permute-start | bytes 393224 | tf_op jit(solution)/shard_map/ppermute | solution.py:521
  90.2 6.5 %collective-permute-start.41 = (f32[256,128]{1,0:T(8,128)S(1)}, f32[256,128]{1,0:T(8,128)S(1)}, u32[]{:S(2)}, u32[]{:S(2)}) collective-permute-start(f32[256,128]{1,0:T(8,128)S(1)} %add_pairs.30), channel_id=1, source_target_pairs={{0,8},{8,16},{16,24},{24,28},{28,20},{20,12},{12,4},{4,0},{1,9},{9... | collective-permute-start | bytes 393224 | tf_op jit(solution)/shard_map/ppermute | solution.py:518
  96.8 6.4 %collective-permute-start.42 = (f32[256,128]{1,0:T(8,128)S(1)}, f32[256,128]{1,0:T(8,128)S(1)}, u32[]{:S(2)}, u32[]{:S(2)}) collective-permute-start(f32[256,128]{1,0:T(8,128)S(1)} %add_pairs.31), channel_id=1, source_target_pairs={{0,8},{8,16},{16,24},{24,28},{28,20},{20,12},{12,4},{4,0},{1,9},{9... | collective-permute-start | bytes 393224 | tf_op jit(solution)/shard_map/ppermute | solution.py:518
  99.0 7.0 %collective-permute-start.56 = (f32[256,128]{1,0:T(8,128)S(1)}, f32[256,128]{1,0:T(8,128)S(1)}, u32[]{:S(2)}, u32[]{:S(2)}) collective-permute-start(f32[256,128]{1,0:T(8,128)S(1)} %add_pairs.36), channel_id=1, source_target_pairs={{0,8},{8,16},{16,24},{24,28},{28,20},{20,12},{12,4},{4,0},{1,9},{9... | collective-permute-start | bytes 393224 | tf_op jit(solution)/shard_map/ppermute | solution.py:518
  100.1 8.9 %collective-permute-start.60 = (f32[256,128]{1,0:T(8,128)S(1)}, f32[256,128]{1,0:T(8,128)S(1)}, u32[]{:S(2)}, u32[]{:S(2)}) collective-permute-start(f32[256,128]{1,0:T(8,128)S(1)} %add_pairs.39), channel_id=1, source_target_pairs={{8,0},{16,8},{24,16},{28,24},{20,28},{12,20},{4,12},{0,4},{9,1},{1... | collective-permute-start | bytes 393224 | tf_op jit(solution)/shard_map/ppermute | solution.py:521
  101.2 6.5 %collective-permute-start.46 = (f32[256,128]{1,0:T(8,128)S(1)}, f32[256,128]{1,0:T(8,128)S(1)}, u32[]{:S(2)}, u32[]{:S(2)}) collective-permute-start(f32[256,128]{1,0:T(8,128)S(1)} %add_pairs.34), channel_id=1, source_target_pairs={{8,0},{16,8},{24,16},{28,24},{20,28},{12,20},{4,12},{0,4},{9,1},{1... | collective-permute-start | bytes 393224 | tf_op jit(solution)/shard_map/ppermute | solution.py:521
  106.0 6.4 %collective-permute-start.57 = (f32[256,128]{1,0:T(8,128)S(1)}, f32[256,128]{1,0:T(8,128)S(1)}, u32[]{:S(2)}, u32[]{:S(2)}) collective-permute-start(f32[256,128]{1,0:T(8,128)S(1)} %add_pairs.37), channel_id=1, source_target_pairs={{0,8},{8,16},{16,24},{24,28},{28,20},{20,12},{12,4},{4,0},{1,9},{9... | collective-permute-start | bytes 393224 | tf_op jit(solution)/shard_map/ppermute | solution.py:518
  113.1 6.4 %collective-permute-start.64 = (f32[264,128]{1,0:T(8,128)S(1)}, f32[264,128]{1,0:T(8,128)S(1)}, u32[]{:S(2)}, u32[]{:S(2)}) collective-permute-start(f32[264,128]{1,0:T(8,128)S(1)} %get-tuple-element.129.refs_9_.refs_0_), channel_id=1, source_target_pairs={{0,8},{8,16},{16,24},{24,28},{28,20},{20,12},{12,4},{4,0},{1,9},{9... | collective-permute-start | bytes 405512 | tf_op jit(solution)/shard_map/ppermute | solution.py:518
  114.7 6.8 %collective-permute-start.50 = (f32[256,128]{1,0:T(8,128)S(1)}, f32[256,128]{1,0:T(8,128)S(1)}, u32[]{:S(2)}, u32[]{:S(2)}) collective-permute-start(f32[256,128]{1,0:T(8,128)S(1)} %get-tuple-element.115.refs_1_), channel_id=1, source_target_pairs={{0,8},{8,16},{16,24},{24,28},{28,20},{20,12},{12,4},{4,0},{1,9},{9... | collective-permute-start | bytes 393224 | tf_op jit(solution)/shard_map/ppermute | solution.py:518
  115.5 7.6 %collective-permute-start.61 = (f32[264,128]{1,0:T(8,128)S(1)}, f32[264,128]{1,0:T(8,128)S(1)}, u32[]{:S(2)}, u32[]{:S(2)}) collective-permute-start(f32[264,128]{1,0:T(8,128)S(1)} %get-tuple-element.129.refs_9_.refs_0_), channel_id=1, source_target_pairs={{8,0},{16,8},{24,16},{28,24},{20,28},{12,20},{4,12},{0,4},{9,1},{1... | collective-permute-start | bytes 405512 | tf_op jit(solution)/shard_map/ppermute | solution.py:521
  128.1 6.8 %collective-permute-start.63 = (f32[264,128]{1,0:T(8,128)S(1)}, f32[264,128]{1,0:T(8,128)S(1)}, u32[]{:S(2)}, u32[]{:S(2)}) collective-permute-start(f32[264,128]{1,0:T(8,128)S(1)} %collective-permute-done.62.refs_11_.refs_2_), channel_id=1, source_target_pairs={{8,0},{16,8},{24,16},{28,24},{20,28},{12,20},{4,12},{0,4},{9,1},{1... | collective-permute-start | bytes 405512 | tf_op jit(solution)/shard_map/ppermute | solution.py:521
  131.1 5.9 %collective-permute-start.49 = (f32[256,128]{1,0:T(8,128)S(1)}, f32[256,128]{1,0:T(8,128)S(1)}, u32[]{:S(2)}, u32[]{:S(2)}) collective-permute-start(f32[256,128]{1,0:T(8,128)S(1)} %collective-permute-done.48.refs_3_), channel_id=1, source_target_pairs={{8,0},{16,8},{24,16},{28,24},{20,28},{12,20},{4,12},{0,4},{9,1},{1... | collective-permute-start | bytes 393224 | tf_op jit(solution)/shard_map/ppermute | solution.py:521
  (23 other events, 115.1 us)

commit v6 on v5

--- a/solution.py
+++ b/solution.py
@@ -14,7 +14,7 @@
 TILE = 8
 LEAD = 1
 LOAD_TURN = 2
-BASE_AT = {4: 2, 6: 4}
+BASE_AT = {3: 2, 5: 4}
 CUTS = 8
 
 

time: 140 us -> 140 us (level)
    ppermute x39, starting transfers between devices: 60.2 us -> 62.1 us  [forward(): return lax.ppermute(x, 'region', ahead)]
    ppermute x29, starting transfers between devices: 17.9 us -> 16 us  [backward(): return lax.ppermute(x, 'region', behind)]
  transfers between devices with their start and end apart: 71 -> 71, of which waited for: 35 -> 33; matrix products, arithmetic and copies ran while one was open for 0% -> 0% of each run, Pallas kernels for 16% -> 16%
where the time goes in v6:
time: 140 us
  starting transfers between devices  80 us (57%)
  waiting for transfers between devices  35.5 us (25%)
  Pallas kernels  23.5 us (17%)
    ppermute x39, starting transfers between devices, forward(): return lax.ppermute(x, 'region', ahead)  62.1 us
    ppermute x39, waiting for transfers between devices, forward(): return lax.ppermute(x, 'region', ahead)  32.1 us
    pallas_call x41, Pallas kernels, call(): pl.pallas_call(body, name=name, out_shape=shapes if many else shapes[0],...  23.5 us
    ppermute x29, starting transfers between devices, backward(): return lax.ppermute(x, 'region', behind)  16 us
    ppermute x29, waiting for transfers between devices, backward(): return lax.ppermute(x, 'region', behind)  2.84 us
  transfers between devices with their start and end apart: 71, of which 33 were waited for; matrix products, arithmetic and copies ran while one was open for 0% of the time, Pallas kernels for 16%

profile of v6, /device:TPU:0, one launch (start us, length us, event | category | flops | bytes accessed | tf_op | source)
XLA Modules:
  0.0 140.0 jit_solution(333764208147623130)
XLA Ops:
  0.6 3.1 %collective-permute-start = (f32[256,256]{1,0:T(8,128)}, f32[256,256]{1,0:T(8,128)S(1)}, u32[]{:S(2)}, u32[]{:S(2)}) collective-permute-start(f32[256,256]{1,0:T(8,128)} %refs_3_.1), channel_id=1, source_target_pairs={{0,8},{8,16},{16,24},{24,28},{28,20},{20,12},{12,4},{4,0},{1,9},{9... | collective-permute-start | bytes 786440 | tf_op jit(solution)/shard_map/ppermute | solution.py:518
  3.7 4.9 %prepare.1 = (s32[32]{0:T(128)S(1)}, bf16[2048,2048]{1,0:T(8,128)(2,1)S(1)}, bf16[2048,256]{1,0:T(8,128)(2,1)S(1)}, f32[1536,256]{1,0:T(8,128)S(1)}, f32[256,256]{1,0:T(8,128)S(1)}) custom-call(s32[1]{0:T(128)} %bitcast.region_ref, s32[1,12]{1,0:T(1,128)} %target_hbm.1, bf16[2048,2048]{1,0:T(8,128)(2,1)} %refs_0_.1, bf16[2048,256]{1,0:T(8,128)(2,1)} %refs_1_.1, ...), custom_call_target="tpu_custom_call" | custom-call | bytes 12582912 | tf_op jit(solution)/shard_map/prepare/pallas_call | solution.py:63
  8.6 1.5 %collective-permute-done.refs_0_ = f32[256,256]{1,0:T(8,128)S(1)} collective-permute-done((f32[256,256]{1,0:T(8,128)}, f32[256,256]{1,0:T(8,128)S(1)}, u32[]{:S(2)}, u32[]{:S(2)}) %collective-permute-start) | collective-permute-done | bytes 262176 | tf_op jit(solution)/shard_map/ppermute | solution.py:518
  10.1 1.5 %collective-permute-done.1.refs_1_ = f32[256,256]{1,0:T(8,128)S(1)} collective-permute-done((f32[256,256]{1,0:T(8,128)}, f32[256,256]{1,0:T(8,128)S(1)}, u32[]{:S(2)}, u32[]{:S(2)}) %collective-permute-start.1) | collective-permute-done | bytes 262176 | tf_op jit(solution)/shard_map/ppermute | solution.py:521
  11.8 1.6 %collective-permute-start.4 = (f32[256,128]{1,0:T(8,128)S(1)}, f32[256,128]{1,0:T(8,128)S(1)}, u32[]{:S(2)}, u32[]{:S(2)}) collective-permute-start(f32[256,128]{1,0:T(8,128)S(1)} %get-tuple-element.77), channel_id=1, source_target_pairs={{0,8},{8,16},{16,24},{24,28},{28,20},{20,12},{12,4},{4,0},{1,9},{9... | collective-permute-start | bytes 393224 | tf_op jit(solution)/shard_map/ppermute | solution.py:518
  14.9 1.6 %collective-permute-start.22 = (f32[256,128]{1,0:T(8,128)S(1)}, f32[256,128]{1,0:T(8,128)S(1)}, u32[]{:S(2)}, u32[]{:S(2)}) collective-permute-start(f32[256,128]{1,0:T(8,128)S(1)} %get-tuple-element.94), channel_id=1, source_target_pairs={{0,8},{8,16},{16,24},{24,28},{28,20},{20,12},{12,4},{4,0},{1,9},{9... | collective-permute-start | bytes 393224 | tf_op jit(solution)/shard_map/ppermute | solution.py:518
  17.8 1.6 %collective-permute-start.5 = (f32[256,128]{1,0:T(8,128)S(1)}, f32[256,128]{1,0:T(8,128)S(1)}, u32[]{:S(2)}, u32[]{:S(2)}) collective-permute-start(f32[256,128]{1,0:T(8,128)S(1)} %collective-permute-done.4.refs_7_), channel_id=1, source_target_pairs={{0,8},{8,16},{16,24},{24,28},{28,20},{20,12},{12,4},{4,0},{1,9},{9... | collective-permute-start | bytes 393224 | tf_op jit(solution)/shard_map/ppermute | solution.py:518
  21.5 1.5 %collective-permute-start.24 = (f32[256,128]{1,0:T(8,128)S(1)}, f32[256,128]{1,0:T(8,128)S(1)}, u32[]{:S(2)}, u32[]{:S(2)}) collective-permute-start(f32[256,128]{1,0:T(8,128)S(1)} %get-tuple-element.96), channel_id=1, source_target_pairs={{0,8},{8,16},{16,24},{24,28},{28,20},{20,12},{12,4},{4,0},{1,9},{9... | collective-permute-start | bytes 393224 | tf_op jit(solution)/shard_map/ppermute | solution.py:518
  24.1 1.6 %collective-permute-start.6 = (f32[256,128]{1,0:T(8,128)S(1)}, f32[256,128]{1,0:T(8,128)S(1)}, u32[]{:S(2)}, u32[]{:S(2)}) collective-permute-start(f32[256,128]{1,0:T(8,128)S(1)} %collective-permute-done.5.refs_6_), channel_id=1, source_target_pairs={{0,8},{8,16},{16,24},{24,28},{28,20},{20,12},{12,4},{4,0},{1,9},{9... | collective-permute-start | bytes 393224 | tf_op jit(solution)/shard_map/ppermute | solution.py:518
  27.0 1.6 %collective-permute-start.25 = (f32[256,128]{1,0:T(8,128)S(1)}, f32[256,128]{1,0:T(8,128)S(1)}, u32[]{:S(2)}, u32[]{:S(2)}) collective-permute-start(f32[256,128]{1,0:T(8,128)S(1)} %collective-permute-done.24.refs_6_), channel_id=1, source_target_pairs={{0,8},{8,16},{16,24},{24,28},{28,20},{20,12},{12,4},{4,0},{1,9},{9... | collective-permute-start | bytes 393224 | tf_op jit(solution)/shard_map/ppermute | solution.py:518
  29.7 2.3 %first_solve.2 = (f32[1536,128]{1,0:T(8,128)S(1)}, f32[264,128]{1,0:T(8,128)S(1)}, f32[264,128]{1,0:T(8,128)S(1)}, f32[264,128]{1,0:T(8,128)S(1)}, f32[264,128]{...) custom-call(s32[32]{0:T(128)S(1)} %get-tuple-element.71.refs_0_, ...), custom_call_target="tpu_custom_call" | custom-call | flops 603979776 | bytes 8388608 | tf_op jit(solution)/shard_map/first_solve/pallas_call | solution.py:63
  33.3 2.3 %first_solve.3 = (f32[1536,128]{1,0:T(8,128)S(1)}, f32[256,128]{1,0:T(8,128)S(1)}, f32[256,128]{1,0:T(8,128)S(1)}, f32[256,128]{1,0:T(8,128)S(1)}, f32[256,128]{...) custom-call(s32[32]{0:T(128)S(1)} %get-tuple-element.71.refs_0_, ...), custom_call_target="tpu_custom_call" | custom-call | flops 603979776 | bytes 8388608 | tf_op jit(solution)/shard_map/first_solve/pallas_call | solution.py:63
  35.6 1.6 %collective-permute-start.26 = (f32[256,128]{1,0:T(8,128)S(1)}, f32[256,128]{1,0:T(8,128)S(1)}, u32[]{:S(2)}, u32[]{:S(2)}) collective-permute-start(f32[256,128]{1,0:T(8,128)S(1)} %get-tuple-element.98), channel_id=1, source_target_pairs={{0,8},{8,16},{16,24},{24,28},{28,20},{20,12},{12,4},{4,0},{1,9},{9... | collective-permute-start | bytes 393224 | tf_op jit(solution)/shard_map/ppermute | solution.py:518
  38.2 1.6 %collective-permute-start.8 = (f32[264,128]{1,0:T(8,128)S(1)}, f32[264,128]{1,0:T(8,128)S(1)}, u32[]{:S(2)}, u32[]{:S(2)}) collective-permute-start(f32[264,128]{1,0:T(8,128)S(1)} %add_pairs.20), channel_id=1, source_target_pairs={{0,8},{8,16},{16,24},{24,28},{28,20},{20,12},{12,4},{4,0},{1,9},{9... | collective-permute-start | bytes 405512 | tf_op jit(solution)/shard_map/ppermute | solution.py:518
  41.6 1.7 %collective-permute-start.27 = (f32[256,128]{1,0:T(8,128)S(1)}, f32[256,128]{1,0:T(8,128)S(1)}, u32[]{:S(2)}, u32[]{:S(2)}) collective-permute-start(f32[256,128]{1,0:T(8,128)S(1)} %add_pairs.25), channel_id=1, source_target_pairs={{0,8},{8,16},{16,24},{24,28},{28,20},{20,12},{12,4},{4,0},{1,9},{9... | collective-permute-start | bytes 393224 | tf_op jit(solution)/shard_map/ppermute | solution.py:518
  44.7 1.6 %collective-permute-start.9 = (f32[264,128]{1,0:T(8,128)S(1)}, f32[264,128]{1,0:T(8,128)S(1)}, u32[]{:S(2)}, u32[]{:S(2)}) collective-permute-start(f32[264,128]{1,0:T(8,128)S(1)} %add_pairs.21), channel_id=1, source_target_pairs={{0,8},{8,16},{16,24},{24,28},{28,20},{20,12},{12,4},{4,0},{1,9},{9... | collective-permute-start | bytes 405512 | tf_op jit(solution)/shard_map/ppermute | solution.py:518
  47.5 1.6 %collective-permute-start.28 = (f32[256,128]{1,0:T(8,128)S(1)}, f32[256,128]{1,0:T(8,128)S(1)}, u32[]{:S(2)}, u32[]{:S(2)}) collective-permute-start(f32[256,128]{1,0:T(8,128)S(1)} %add_pairs.26), channel_id=1, source_target_pairs={{0,8},{8,16},{16,24},{24,28},{28,20},{20,12},{12,4},{4,0},{1,9},{9... | collective-permute-start | bytes 393224 | tf_op jit(solution)/shard_map/ppermute | solution.py:518
  49.7 1.4 %collective-permute-done.9.refs_0_ = f32[264,128]{1,0:T(8,128)S(1)} collective-permute-done((f32[264,128]{1,0:T(8,128)S(1)}, f32[264,128]{1,0:T(8,128)S(1)}, u32[]{:S(2)}, u32[]{:S(2)}) %collective-permute-start.9) | collective-permute-done | bytes 135200 | tf_op jit(solution)/shard_map/ppermute | solution.py:518
  51.1 1.7 %collective-permute-start.10 = (f32[264,128]{1,0:T(8,128)S(1)}, f32[264,128]{1,0:T(8,128)S(1)}, u32[]{:S(2)}, u32[]{:S(2)}) collective-permute-start(f32[264,128]{1,0:T(8,128)S(1)} %add_pairs.22), channel_id=1, source_target_pairs={{0,8},{8,16},{16,24},{24,28},{28,20},{20,12},{12,4},{4,0},{1,9},{9... | collective-permute-start | bytes 405512 | tf_op jit(solution)/shard_map/ppermute | solution.py:518
  54.0 1.6 %collective-permute-start.29 = (f32[256,128]{1,0:T(8,128)S(1)}, f32[256,128]{1,0:T(8,128)S(1)}, u32[]{:S(2)}, u32[]{:S(2)}) collective-permute-start(f32[256,128]{1,0:T(8,128)S(1)} %add_pairs.27), channel_id=1, source_target_pairs={{0,8},{8,16},{16,24},{24,28},{28,20},{20,12},{12,4},{4,0},{1,9},{9... | collective-permute-start | bytes 393224 | tf_op jit(solution)/shard_map/ppermute | solution.py:518
  55.7 1.7 %collective-permute-done.10.refs_1_ = f32[264,128]{1,0:T(8,128)S(1)} collective-permute-done((f32[264,128]{1,0:T(8,128)S(1)}, f32[264,128]{1,0:T(8,128)S(1)}, u32[]{:S(2)}, u32[]{:S(2)}) %collective-permute-start.10) | collective-permute-done | bytes 135200 | tf_op jit(solution)/shard_map/ppermute | solution.py:518
  57.4 1.9 %collective-permute-start.17 = (f32[256,128]{1,0:T(8,128)S(1)}, f32[256,128]{1,0:T(8,128)S(1)}, u32[]{:S(2)}, u32[]{:S(2)}) collective-permute-start(f32[256,128]{1,0:T(8,128)S(1)} %get-tuple-element.88.refs_1_.refs_3_), channel_id=1, source_target_pairs={{0,8},{8,16},{16,24},{24,28},{28,20},{20,12},{12,4},{4,0},{1,9},{9... | collective-permute-start | bytes 393224 | tf_op jit(solution)/shard_map/ppermute | solution.py:518
  60.4 1.7 %collective-permute-start.36 = (f32[256,128]{1,0:T(8,128)S(1)}, f32[256,128]{1,0:T(8,128)S(1)}, u32[]{:S(2)}, u32[]{:S(2)}) collective-permute-start(f32[256,128]{1,0:T(8,128)S(1)} %get-tuple-element.106.refs_1_.refs_3_), channel_id=1, source_target_pairs={{0,8},{8,16},{16,24},{24,28},{28,20},{20,12},{12,4},{4,0},{1,9},{9... | collective-permute-start | bytes 393224 | tf_op jit(solution)/shard_map/ppermute | solution.py:518
  63.2 1.8 %collective-permute-start.18 = (f32[256,128]{1,0:T(8,128)S(1)}, f32[256,128]{1,0:T(8,128)S(1)}, u32[]{:S(2)}, u32[]{:S(2)}) collective-permute-start(f32[256,128]{1,0:T(8,128)S(1)} %collective-permute-done.17.refs_8_), channel_id=1, source_target_pairs={{0,8},{8,16},{16,24},{24,28},{28,20},{20,12},{12,4},{4,0},{1,9},{9... | collective-permute-start | bytes 393224 | tf_op jit(solution)/shard_map/ppermute | solution.py:518
  65.2 1.6 %collective-permute-done.36.refs_8_ = f32[256,128]{1,0:T(8,128)S(1)} collective-permute-done((f32[256,128]{1,0:T(8,128)S(1)}, f32[256,128]{1,0:T(8,128)S(1)}, u32[]{:S(2)}, u32[]{:S(2)}) %collective-permute-start.36) | collective-permute-done | bytes 131104 | tf_op jit(solution)/shard_map/ppermute | solution.py:518
  66.8 1.8 %collective-permute-start.37 = (f32[256,128]{1,0:T(8,128)S(1)}, f32[256,128]{1,0:T(8,128)S(1)}, u32[]{:S(2)}, u32[]{:S(2)}) collective-permute-start(f32[256,128]{1,0:T(8,128)S(1)} %collective-permute-done.36.refs_8_), channel_id=1, source_target_pairs={{0,8},{8,16},{16,24},{24,28},{28,20},{20,12},{12,4},{4,0},{1,9},{9... | collective-permute-start | bytes 393224 | tf_op jit(solution)/shard_map/ppermute | solution.py:518
  69.6 1.8 %collective-permute-start.19 = (f32[256,128]{1,0:T(8,128)S(1)}, f32[256,128]{1,0:T(8,128)S(1)}, u32[]{:S(2)}, u32[]{:S(2)}) collective-permute-start(f32[256,128]{1,0:T(8,128)S(1)} %collective-permute-done.18.refs_7_), channel_id=1, source_target_pairs={{0,8},{8,16},{16,24},{24,28},{28,20},{20,12},{12,4},{4,0},{1,9},{9... | collective-permute-start | bytes 393224 | tf_op jit(solution)/shard_map/ppermute | solution.py:518
  72.6 1.6 %collective-permute-start.38 = (f32[256,128]{1,0:T(8,128)S(1)}, f32[256,128]{1,0:T(8,128)S(1)}, u32[]{:S(2)}, u32[]{:S(2)}) collective-permute-start(f32[256,128]{1,0:T(8,128)S(1)} %collective-permute-done.37.refs_7_), channel_id=1, source_target_pairs={{0,8},{8,16},{16,24},{24,28},{28,20},{20,12},{12,4},{4,0},{1,9},{9... | collective-permute-start | bytes 393224 | tf_op jit(solution)/shard_map/ppermute | solution.py:518
  74.7 1.7 %collective-permute-start.20 = (f32[256,128]{1,0:T(8,128)S(1)}, f32[256,128]{1,0:T(8,128)S(1)}, u32[]{:S(2)}, u32[]{:S(2)}) collective-permute-start(f32[256,128]{1,0:T(8,128)S(1)} %collective-permute-done.19.refs_6_), channel_id=1, source_target_pairs={{0,8},{8,16},{16,24},{24,28},{28,20},{20,12},{12,4},{4,0},{1,9},{9... | collective-permute-start | bytes 393224 | tf_op jit(solution)/shard_map/ppermute | solution.py:518
  78.0 1.6 %collective-permute-start.39 = (f32[256,128]{1,0:T(8,128)S(1)}, f32[256,128]{1,0:T(8,128)S(1)}, u32[]{:S(2)}, u32[]{:S(2)}) collective-permute-start(f32[256,128]{1,0:T(8,128)S(1)} %collective-permute-done.38.refs_6_), channel_id=1, source_target_pairs={{0,8},{8,16},{16,24},{24,28},{28,20},{20,12},{12,4},{4,0},{1,9},{9... | collective-permute-start | bytes 393224 | tf_op jit(solution)/shard_map/ppermute | solution.py:518
  80.0 2.7 %second_solve.2 = (f32[1536,128]{1,0:T(8,128)S(1)}, bf16[1664,128]{1,0:T(8,128)(2,1)S(1)}, f32[1664,128]{1,0:T(8,128)S(1)}, f32[16,128]{1,0:T(8,128)S(1)}, f32[2...) custom-call(s32[32]{0:T(128)S(1)} %get-tuple-element.71.refs_0_, ...), custom_call_target="tpu_custom_call" | custom-call | flops 603979776 | bytes 8388608 | tf_op jit(solution)/shard_map/second_solve/pallas_call | solution.py:63
  82.7 2.1 %collective-permute-start.40 = (f32[256,128]{1,0:T(8,128)S(1)}, f32[256,128]{1,0:T(8,128)S(1)}, u32[]{:S(2)}, u32[]{:S(2)}) collective-permute-start(f32[256,128]{1,0:T(8,128)S(1)} %get-tuple-element.112), channel_id=1, source_target_pairs={{0,8},{8,16},{16,24},{24,28},{28,20},{20,12},{12,4},{4,0},{1,9},{9... | collective-permute-start | bytes 393224 | tf_op jit(solution)/shard_map/ppermute | solution.py:518
  84.8 2.7 %second_solve.3 = (f32[1536,128]{1,0:T(8,128)S(1)}, bf16[1664,128]{1,0:T(8,128)(2,1)S(1)}, f32[1664,128]{1,0:T(8,128)S(1)}, f32[16,128]{1,0:T(8,128)S(1)}, f32[2...) custom-call(s32[32]{0:T(128)S(1)} %get-tuple-element.71.refs_0_, ...), custom_call_target="tpu_custom_call" | custom-call | flops 603979776 | bytes 8388608 | tf_op jit(solution)/shard_map/second_solve/pallas_call | solution.py:63
  87.5 1.6 %collective-permute-start.54 = (f32[256,128]{1,0:T(8,128)S(1)}, f32[256,128]{1,0:T(8,128)S(1)}, u32[]{:S(2)}, u32[]{:S(2)}) collective-permute-start(f32[256,128]{1,0:T(8,128)S(1)} %get-tuple-element.121), channel_id=1, source_target_pairs={{0,8},{8,16},{16,24},{24,28},{28,20},{20,12},{12,4},{4,0},{1,9},{9... | collective-permute-start | bytes 393224 | tf_op jit(solution)/shard_map/ppermute | solution.py:518
  92.9 1.4 collective-permute-start.55
  96.7 1.5 %collective-permute-start.42 = (f32[256,128]{1,0:T(8,128)S(1)}, f32[256,128]{1,0:T(8,128)S(1)}, u32[]{:S(2)}, u32[]{:S(2)}) collective-permute-start(f32[256,128]{1,0:T(8,128)S(1)} %add_pairs.31), channel_id=1, source_target_pairs={{0,8},{8,16},{16,24},{24,28},{28,20},{20,12},{12,4},{4,0},{1,9},{9... | collective-permute-start | bytes 393224 | tf_op jit(solution)/shard_map/ppermute | solution.py:518
  98.2 1.5 %collective-permute-start.56 = (f32[256,128]{1,0:T(8,128)S(1)}, f32[256,128]{1,0:T(8,128)S(1)}, u32[]{:S(2)}, u32[]{:S(2)}) collective-permute-start(f32[256,128]{1,0:T(8,128)S(1)} %add_pairs.36), channel_id=1, source_target_pairs={{0,8},{8,16},{16,24},{24,28},{28,20},{20,12},{12,4},{4,0},{1,9},{9... | collective-permute-start | bytes 393224 | tf_op jit(solution)/shard_map/ppermute | solution.py:518
  100.7 1.4 %collective-permute-start.46 = (f32[256,128]{1,0:T(8,128)S(1)}, f32[256,128]{1,0:T(8,128)S(1)}, u32[]{:S(2)}, u32[]{:S(2)}) collective-permute-start(f32[256,128]{1,0:T(8,128)S(1)} %add_pairs.34), channel_id=1, source_target_pairs={{8,0},{16,8},{24,16},{28,24},{20,28},{12,20},{4,12},{0,4},{9,1},{1... | collective-permute-start | bytes 393224 | tf_op jit(solution)/shard_map/ppermute | solution.py:521
  103.1 1.4 %collective-permute-start.43 = (f32[256,128]{1,0:T(8,128)S(1)}, f32[256,128]{1,0:T(8,128)S(1)}, u32[]{:S(2)}, u32[]{:S(2)}) collective-permute-start(f32[256,128]{1,0:T(8,128)S(1)} %add_pairs.32), channel_id=1, source_target_pairs={{0,8},{8,16},{16,24},{24,28},{28,20},{20,12},{12,4},{4,0},{1,9},{9... | collective-permute-start | bytes 393224 | tf_op jit(solution)/shard_map/ppermute | solution.py:518
  105.9 1.4 %collective-permute-start.57 = (f32[256,128]{1,0:T(8,128)S(1)}, f32[256,128]{1,0:T(8,128)S(1)}, u32[]{:S(2)}, u32[]{:S(2)}) collective-permute-start(f32[256,128]{1,0:T(8,128)S(1)} %add_pairs.37), channel_id=1, source_target_pairs={{0,8},{8,16},{16,24},{24,28},{28,20},{20,12},{12,4},{4,0},{1,9},{9... | collective-permute-start | bytes 393224 | tf_op jit(solution)/shard_map/ppermute | solution.py:518
  107.4 1.5 %collective-permute-done.43.refs_1_ = f32[256,128]{1,0:T(8,128)S(1)} collective-permute-done((f32[256,128]{1,0:T(8,128)S(1)}, f32[256,128]{1,0:T(8,128)S(1)}, u32[]{:S(2)}, u32[]{:S(2)}) %collective-permute-start.43) | collective-permute-done | bytes 131104 | tf_op jit(solution)/shard_map/ppermute | solution.py:518
  108.9 3.5 %collective-permute-done.57.refs_1_ = f32[256,128]{1,0:T(8,128)S(1)} collective-permute-done((f32[256,128]{1,0:T(8,128)S(1)}, f32[256,128]{1,0:T(8,128)S(1)}, u32[]{:S(2)}, u32[]{:S(2)}) %collective-permute-start.57) | collective-permute-done | bytes 131104 | tf_op jit(solution)/shard_map/ppermute | solution.py:518
  113.0 1.4 collective-permute-start.64
  114.3 1.5 %collective-permute-start.50 = (f32[256,128]{1,0:T(8,128)S(1)}, f32[256,128]{1,0:T(8,128)S(1)}, u32[]{:S(2)}, u32[]{:S(2)}) collective-permute-start(f32[256,128]{1,0:T(8,128)S(1)} %get-tuple-element.119.refs_1_), channel_id=1, source_target_pairs={{0,8},{8,16},{16,24},{24,28},{28,20},{20,12},{12,4},{4,0},{1,9},{9... | collective-permute-start | bytes 393224 | tf_op jit(solution)/shard_map/ppermute | solution.py:518
  116.4 3.0 %collective-permute-done.64.refs_16_.refs_7_ = f32[264,128]{1,0:T(8,128)S(1)} collective-permute-done((f32[264,128]{1,0:T(8,128)S(1)}, f32[264,128]{1,0:T(8,128)S(1)}, u32[]{:S(2)}, u32[]{:S(2)}) %collective-permute-start.64) | collective-permute-done | bytes 135200 | tf_op jit(solution)/shard_map/ppermute | solution.py:518
  132.7 1.8 %store_state.1.refs_8_ = f32[2048,256]{1,0:T(8,128)} custom-call(f32[1536,128]{1,0:T(8,128)S(1)} %get-tuple-element.90.refs_0_, f32[1536,128]{1,0:T(8,128)S(1)} %get-tuple-element.108.refs_1_, bf16[1664,128]{1,0:T(8,128)(2,1)S(1)} %get-tuple-element.109.refs_2_, bf16[1664,128]{1,0:T(8,128)(2,1)S(1)} %get-tuple-element.110.refs_3_, ...), custom_call_target="tpu_custom_call" | custom-call | flops 402653184 | bytes 4194304 | tf_op jit(solution)/shard_map/store_state/pallas_call | solution.py:63
  134.7 1.6 %collective-permute-start.69 = (f32[8,128]{1,0:T(8,128)S(1)}, f32[8,128]{1,0:T(8,128)S(1)}, u32[]{:S(2)}, u32[]{:S(2)}) collective-permute-start(f32[8,128]{1,0:T(8,128)S(1)} %sum_tails.1.refs_0_), channel_id=1, source_target_pairs={{0,2},{1,3},{2,0},{3,1},{4,6},{5,7},{6,4},{7,5},{8,10},{9,11},{10,... | collective-permute-start | bytes 12296 | tf_op jit(solution)/shard_map/ppermute | solution.py:613
  136.6 2.2 %finish.1 = (f32[1536,256]{1,0:T(8,128)}, f32[256,256]{1,0:T(8,128)}) custom-call(s32[32]{0:T(128)S(1)} %get-tuple-element.71.refs_0_, f32[256,128]{1,0:T(8,128)S(1)} %get-tuple-element.119.refs_1_, f32[256,128]{1,0:T(8,128)S(1)} %collective-permute-done.47.refs_2_, f32[256,128]{1,0:T(8,128)S(1)} %collective-permute-done.48.refs_3_, ...), custom_call_target="tpu_custom_call" | custom-call | bytes 3145728 | tf_op jit(solution)/shard_map/finish/pallas_call | solution.py:63
  (141 shorter events, 49.9 us)
Async XLA Ops:
  0.6 9.5 %collective-permute-start = (f32[256,256]{1,0:T(8,128)}, f32[256,256]{1,0:T(8,128)S(1)}, u32[]{:S(2)}, u32[]{:S(2)}) collective-permute-start(f32[256,256]{1,0:T(8,128)} %refs_3_.1), channel_id=1, source_target_pairs={{0,8},{8,16},{16,24},{24,28},{28,20},{20,12},{12,4},{4,0},{1,9},{9... | collective-permute-start | bytes 786440 | tf_op jit(solution)/shard_map/ppermute | solution.py:518
  3.7 8.0 %collective-permute-start.1 = (f32[256,256]{1,0:T(8,128)}, f32[256,256]{1,0:T(8,128)S(1)}, u32[]{:S(2)}, u32[]{:S(2)}) collective-permute-start(f32[256,256]{1,0:T(8,128)} %refs_3_.1), channel_id=1, source_target_pairs={{8,0},{16,8},{24,16},{28,24},{20,28},{12,20},{4,12},{0,4},{9,1},{1... | collective-permute-start | bytes 786440 | tf_op jit(solution)/shard_map/ppermute | solution.py:521
  11.8 6.0 %collective-permute-start.4 = (f32[256,128]{1,0:T(8,128)S(1)}, f32[256,128]{1,0:T(8,128)S(1)}, u32[]{:S(2)}, u32[]{:S(2)}) collective-permute-start(f32[256,128]{1,0:T(8,128)S(1)} %get-tuple-element.77), channel_id=1, source_target_pairs={{0,8},{8,16},{16,24},{24,28},{28,20},{20,12},{12,4},{4,0},{1,9},{9... | collective-permute-start | bytes 393224 | tf_op jit(solution)/shard_map/ppermute | solution.py:518
  14.9 6.1 %collective-permute-start.22 = (f32[256,128]{1,0:T(8,128)S(1)}, f32[256,128]{1,0:T(8,128)S(1)}, u32[]{:S(2)}, u32[]{:S(2)}) collective-permute-start(f32[256,128]{1,0:T(8,128)S(1)} %get-tuple-element.94), channel_id=1, source_target_pairs={{0,8},{8,16},{16,24},{24,28},{28,20},{20,12},{12,4},{4,0},{1,9},{9... | collective-permute-start | bytes 393224 | tf_op jit(solution)/shard_map/ppermute | solution.py:518
  17.0 6.1 %collective-permute-start.2 = (f32[256,128]{1,0:T(8,128)S(1)}, f32[256,128]{1,0:T(8,128)S(1)}, u32[]{:S(2)}, u32[]{:S(2)}) collective-permute-start(f32[256,128]{1,0:T(8,128)S(1)} %get-tuple-element.76), channel_id=1, source_target_pairs={{8,0},{16,8},{24,16},{28,24},{20,28},{12,20},{4,12},{0,4},{9,1},{1... | collective-permute-start | bytes 393224 | tf_op jit(solution)/shard_map/ppermute | solution.py:521
  17.8 6.3 %collective-permute-start.5 = (f32[256,128]{1,0:T(8,128)S(1)}, f32[256,128]{1,0:T(8,128)S(1)}, u32[]{:S(2)}, u32[]{:S(2)}) collective-permute-start(f32[256,128]{1,0:T(8,128)S(1)} %collective-permute-done.4.refs_7_), channel_id=1, source_target_pairs={{0,8},{8,16},{16,24},{24,28},{28,20},{20,12},{12,4},{4,0},{1,9},{9... | collective-permute-start | bytes 393224 | tf_op jit(solution)/shard_map/ppermute | solution.py:518
  21.5 5.5 %collective-permute-start.24 = (f32[256,128]{1,0:T(8,128)S(1)}, f32[256,128]{1,0:T(8,128)S(1)}, u32[]{:S(2)}, u32[]{:S(2)}) collective-permute-start(f32[256,128]{1,0:T(8,128)S(1)} %get-tuple-element.96), channel_id=1, source_target_pairs={{0,8},{8,16},{16,24},{24,28},{28,20},{20,12},{12,4},{4,0},{1,9},{9... | collective-permute-start | bytes 393224 | tf_op jit(solution)/shard_map/ppermute | solution.py:518
  23.1 5.5 %collective-permute-start.3 = (f32[256,128]{1,0:T(8,128)S(1)}, f32[256,128]{1,0:T(8,128)S(1)}, u32[]{:S(2)}, u32[]{:S(2)}) collective-permute-start(f32[256,128]{1,0:T(8,128)S(1)} %collective-permute-done.2.refs_3_), channel_id=1, source_target_pairs={{8,0},{16,8},{24,16},{28,24},{20,28},{12,20},{4,12},{0,4},{9,1},{1... | collective-permute-start | bytes 393224 | tf_op jit(solution)/shard_map/ppermute | solution.py:521
  24.1 5.7 %collective-permute-start.6 = (f32[256,128]{1,0:T(8,128)S(1)}, f32[256,128]{1,0:T(8,128)S(1)}, u32[]{:S(2)}, u32[]{:S(2)}) collective-permute-start(f32[256,128]{1,0:T(8,128)S(1)} %collective-permute-done.5.refs_6_), channel_id=1, source_target_pairs={{0,8},{8,16},{16,24},{24,28},{28,20},{20,12},{12,4},{4,0},{1,9},{9... | collective-permute-start | bytes 393224 | tf_op jit(solution)/shard_map/ppermute | solution.py:518
  25.7 7.6 %collective-permute-start.23 = (f32[256,128]{1,0:T(8,128)S(1)}, f32[256,128]{1,0:T(8,128)S(1)}, u32[]{:S(2)}, u32[]{:S(2)}) collective-permute-start(f32[256,128]{1,0:T(8,128)S(1)} %get-tuple-element.95), channel_id=1, source_target_pairs={{8,0},{16,8},{24,16},{28,24},{20,28},{12,20},{4,12},{0,4},{9,1},{1... | collective-permute-start | bytes 393224 | tf_op jit(solution)/shard_map/ppermute | solution.py:521
  27.0 6.3 %collective-permute-start.25 = (f32[256,128]{1,0:T(8,128)S(1)}, f32[256,128]{1,0:T(8,128)S(1)}, u32[]{:S(2)}, u32[]{:S(2)}) collective-permute-start(f32[256,128]{1,0:T(8,128)S(1)} %collective-permute-done.24.refs_6_), channel_id=1, source_target_pairs={{0,8},{8,16},{16,24},{24,28},{28,20},{20,12},{12,4},{4,0},{1,9},{9... | collective-permute-start | bytes 393224 | tf_op jit(solution)/shard_map/ppermute | solution.py:518
  32.0 6.2 %collective-permute-start.7 = (f32[264,128]{1,0:T(8,128)S(1)}, f32[264,128]{1,0:T(8,128)S(1)}, u32[]{:S(2)}, u32[]{:S(2)}) collective-permute-start(f32[264,128]{1,0:T(8,128)S(1)} %get-tuple-element.81), channel_id=1, source_target_pairs={{0,8},{8,16},{16,24},{24,28},{28,20},{20,12},{12,4},{4,0},{1,9},{9... | collective-permute-start | bytes 405512 | tf_op jit(solution)/shard_map/ppermute | solution.py:518
  35.6 6.0 %collective-permute-start.26 = (f32[256,128]{1,0:T(8,128)S(1)}, f32[256,128]{1,0:T(8,128)S(1)}, u32[]{:S(2)}, u32[]{:S(2)}) collective-permute-start(f32[256,128]{1,0:T(8,128)S(1)} %get-tuple-element.98), channel_id=1, source_target_pairs={{0,8},{8,16},{16,24},{24,28},{28,20},{20,12},{12,4},{4,0},{1,9},{9... | collective-permute-start | bytes 393224 | tf_op jit(solution)/shard_map/ppermute | solution.py:518
  37.2 6.1 %collective-permute-start.11 = (f32[264,128]{1,0:T(8,128)S(1)}, f32[264,128]{1,0:T(8,128)S(1)}, u32[]{:S(2)}, u32[]{:S(2)}) collective-permute-start(f32[264,128]{1,0:T(8,128)S(1)} %get-tuple-element.85), channel_id=1, source_target_pairs={{8,0},{16,8},{24,16},{28,24},{20,28},{12,20},{4,12},{0,4},{9,1},{1... | collective-permute-start | bytes 405512 | tf_op jit(solution)/shard_map/ppermute | solution.py:521
  38.2 6.5 %collective-permute-start.8 = (f32[264,128]{1,0:T(8,128)S(1)}, f32[264,128]{1,0:T(8,128)S(1)}, u32[]{:S(2)}, u32[]{:S(2)}) collective-permute-start(f32[264,128]{1,0:T(8,128)S(1)} %add_pairs.20), channel_id=1, source_target_pairs={{0,8},{8,16},{16,24},{24,28},{28,20},{20,12},{12,4},{4,0},{1,9},{9... | collective-permute-start | bytes 405512 | tf_op jit(solution)/shard_map/ppermute | solution.py:518
  39.8 6.5 %collective-permute-start.30 = (f32[256,128]{1,0:T(8,128)S(1)}, f32[256,128]{1,0:T(8,128)S(1)}, u32[]{:S(2)}, u32[]{:S(2)}) collective-permute-start(f32[256,128]{1,0:T(8,128)S(1)} %get-tuple-element.102), channel_id=1, source_target_pairs={{8,0},{16,8},{24,16},{28,24},{20,28},{12,20},{4,12},{0,4},{9,1},{1... | collective-permute-start | bytes 393224 | tf_op jit(solution)/shard_map/ppermute | solution.py:521
  41.6 5.9 %collective-permute-start.27 = (f32[256,128]{1,0:T(8,128)S(1)}, f32[256,128]{1,0:T(8,128)S(1)}, u32[]{:S(2)}, u32[]{:S(2)}) collective-permute-start(f32[256,128]{1,0:T(8,128)S(1)} %add_pairs.25), channel_id=1, source_target_pairs={{0,8},{8,16},{16,24},{24,28},{28,20},{20,12},{12,4},{4,0},{1,9},{9... | collective-permute-start | bytes 393224 | tf_op jit(solution)/shard_map/ppermute | solution.py:518
  43.4 5.8 %collective-permute-start.12 = (f32[264,128]{1,0:T(8,128)S(1)}, f32[264,128]{1,0:T(8,128)S(1)}, u32[]{:S(2)}, u32[]{:S(2)}) collective-permute-start(f32[264,128]{1,0:T(8,128)S(1)} %add_pairs.23), channel_id=1, source_target_pairs={{8,0},{16,8},{24,16},{28,24},{20,28},{12,20},{4,12},{0,4},{9,1},{1... | collective-permute-start | bytes 405512 | tf_op jit(solution)/shard_map/ppermute | solution.py:521
  44.7 6.4 %collective-permute-start.9 = (f32[264,128]{1,0:T(8,128)S(1)}, f32[264,128]{1,0:T(8,128)S(1)}, u32[]{:S(2)}, u32[]{:S(2)}) collective-permute-start(f32[264,128]{1,0:T(8,128)S(1)} %add_pairs.21), channel_id=1, source_target_pairs={{0,8},{8,16},{16,24},{24,28},{28,20},{20,12},{12,4},{4,0},{1,9},{9... | collective-permute-start | bytes 405512 | tf_op jit(solution)/shard_map/ppermute | solution.py:518
  46.4 6.5 %collective-permute-start.31 = (f32[256,128]{1,0:T(8,128)S(1)}, f32[256,128]{1,0:T(8,128)S(1)}, u32[]{:S(2)}, u32[]{:S(2)}) collective-permute-start(f32[256,128]{1,0:T(8,128)S(1)} %add_pairs.28), channel_id=1, source_target_pairs={{8,0},{16,8},{24,16},{28,24},{20,28},{12,20},{4,12},{0,4},{9,1},{1... | collective-permute-start | bytes 393224 | tf_op jit(solution)/shard_map/ppermute | solution.py:521
  47.5 6.5 %collective-permute-start.28 = (f32[256,128]{1,0:T(8,128)S(1)}, f32[256,128]{1,0:T(8,128)S(1)}, u32[]{:S(2)}, u32[]{:S(2)}) collective-permute-start(f32[256,128]{1,0:T(8,128)S(1)} %add_pairs.26), channel_id=1, source_target_pairs={{0,8},{8,16},{16,24},{24,28},{28,20},{20,12},{12,4},{4,0},{1,9},{9... | collective-permute-start | bytes 393224 | tf_op jit(solution)/shard_map/ppermute | solution.py:518
  49.2 6.5 %collective-permute-start.13 = (f32[264,128]{1,0:T(8,128)S(1)}, f32[264,128]{1,0:T(8,128)S(1)}, u32[]{:S(2)}, u32[]{:S(2)}) collective-permute-start(f32[264,128]{1,0:T(8,128)S(1)} %add_pairs.24), channel_id=1, source_target_pairs={{8,0},{16,8},{24,16},{28,24},{20,28},{12,20},{4,12},{0,4},{9,1},{1... | collective-permute-start | bytes 405512 | tf_op jit(solution)/shard_map/ppermute | solution.py:521
  51.1 6.2 %collective-permute-start.10 = (f32[264,128]{1,0:T(8,128)S(1)}, f32[264,128]{1,0:T(8,128)S(1)}, u32[]{:S(2)}, u32[]{:S(2)}) collective-permute-start(f32[264,128]{1,0:T(8,128)S(1)} %add_pairs.22), channel_id=1, source_target_pairs={{0,8},{8,16},{16,24},{24,28},{28,20},{20,12},{12,4},{4,0},{1,9},{9... | collective-permute-start | bytes 405512 | tf_op jit(solution)/shard_map/ppermute | solution.py:518
  52.9 6.4 %collective-permute-start.32 = (f32[256,128]{1,0:T(8,128)S(1)}, f32[256,128]{1,0:T(8,128)S(1)}, u32[]{:S(2)}, u32[]{:S(2)}) collective-permute-start(f32[256,128]{1,0:T(8,128)S(1)} %add_pairs.29), channel_id=1, source_target_pairs={{8,0},{16,8},{24,16},{28,24},{20,28},{12,20},{4,12},{0,4},{9,1},{1... | collective-permute-start | bytes 393224 | tf_op jit(solution)/shard_map/ppermute | solution.py:521
  54.0 6.3 %collective-permute-start.29 = (f32[256,128]{1,0:T(8,128)S(1)}, f32[256,128]{1,0:T(8,128)S(1)}, u32[]{:S(2)}, u32[]{:S(2)}) collective-permute-start(f32[256,128]{1,0:T(8,128)S(1)} %add_pairs.27), channel_id=1, source_target_pairs={{0,8},{8,16},{16,24},{24,28},{28,20},{20,12},{12,4},{4,0},{1,9},{9... | collective-permute-start | bytes 393224 | tf_op jit(solution)/shard_map/ppermute | solution.py:518
  57.4 5.8 %collective-permute-start.17 = (f32[256,128]{1,0:T(8,128)S(1)}, f32[256,128]{1,0:T(8,128)S(1)}, u32[]{:S(2)}, u32[]{:S(2)}) collective-permute-start(f32[256,128]{1,0:T(8,128)S(1)} %get-tuple-element.88.refs_1_.refs_3_), channel_id=1, source_target_pairs={{0,8},{8,16},{16,24},{24,28},{28,20},{20,12},{12,4},{4,0},{1,9},{9... | collective-permute-start | bytes 393224 | tf_op jit(solution)/shard_map/ppermute | solution.py:518
  60.4 6.4 %collective-permute-start.36 = (f32[256,128]{1,0:T(8,128)S(1)}, f32[256,128]{1,0:T(8,128)S(1)}, u32[]{:S(2)}, u32[]{:S(2)}) collective-permute-start(f32[256,128]{1,0:T(8,128)S(1)} %get-tuple-element.106.refs_1_.refs_3_), channel_id=1, source_target_pairs={{0,8},{8,16},{16,24},{24,28},{28,20},{20,12},{12,4},{4,0},{1,9},{9... | collective-permute-start | bytes 393224 | tf_op jit(solution)/shard_map/ppermute | solution.py:518
  62.1 6.4 %collective-permute-start.14 = (f32[256,128]{1,0:T(8,128)S(1)}, f32[256,128]{1,0:T(8,128)S(1)}, u32[]{:S(2)}, u32[]{:S(2)}) collective-permute-start(f32[256,128]{1,0:T(8,128)S(1)} %get-tuple-element.88.refs_1_.refs_3_), channel_id=1, source_target_pairs={{8,0},{16,8},{24,16},{28,24},{20,28},{12,20},{4,12},{0,4},{9,1},{1... | collective-permute-start | bytes 393224 | tf_op jit(solution)/shard_map/ppermute | solution.py:521
  63.2 6.4 %collective-permute-start.18 = (f32[256,128]{1,0:T(8,128)S(1)}, f32[256,128]{1,0:T(8,128)S(1)}, u32[]{:S(2)}, u32[]{:S(2)}) collective-permute-start(f32[256,128]{1,0:T(8,128)S(1)} %collective-permute-done.17.refs_8_), channel_id=1, source_target_pairs={{0,8},{8,16},{16,24},{24,28},{28,20},{20,12},{12,4},{4,0},{1,9},{9... | collective-permute-start | bytes 393224 | tf_op jit(solution)/shard_map/ppermute | solution.py:518
  64.9 6.4 %collective-permute-start.33 = (f32[256,128]{1,0:T(8,128)S(1)}, f32[256,128]{1,0:T(8,128)S(1)}, u32[]{:S(2)}, u32[]{:S(2)}) collective-permute-start(f32[256,128]{1,0:T(8,128)S(1)} %get-tuple-element.106.refs_1_.refs_3_), channel_id=1, source_target_pairs={{8,0},{16,8},{24,16},{28,24},{20,28},{12,20},{4,12},{0,4},{9,1},{1... | collective-permute-start | bytes 393224 | tf_op jit(solution)/shard_map/ppermute | solution.py:521
  66.8 5.9 %collective-permute-start.37 = (f32[256,128]{1,0:T(8,128)S(1)}, f32[256,128]{1,0:T(8,128)S(1)}, u32[]{:S(2)}, u32[]{:S(2)}) collective-permute-start(f32[256,128]{1,0:T(8,128)S(1)} %collective-permute-done.36.refs_8_), channel_id=1, source_target_pairs={{0,8},{8,16},{16,24},{24,28},{28,20},{20,12},{12,4},{4,0},{1,9},{9... | collective-permute-start | bytes 393224 | tf_op jit(solution)/shard_map/ppermute | solution.py:518
  68.6 5.6 %collective-permute-start.15 = (f32[256,128]{1,0:T(8,128)S(1)}, f32[256,128]{1,0:T(8,128)S(1)}, u32[]{:S(2)}, u32[]{:S(2)}) collective-permute-start(f32[256,128]{1,0:T(8,128)S(1)} %collective-permute-done.14.refs_2_), channel_id=1, source_target_pairs={{8,0},{16,8},{24,16},{28,24},{20,28},{12,20},{4,12},{0,4},{9,1},{1... | collective-permute-start | bytes 393224 | tf_op jit(solution)/shard_map/ppermute | solution.py:521
  76.3 8.5 %collective-permute-start.35 = (f32[256,128]{1,0:T(8,128)S(1)}, f32[256,128]{1,0:T(8,128)S(1)}, u32[]{:S(2)}, u32[]{:S(2)}) collective-permute-start(f32[256,128]{1,0:T(8,128)S(1)} %collective-permute-done.34.refs_3_), channel_id=1, source_target_pairs={{8,0},{16,8},{24,16},{28,24},{20,28},{12,20},{4,12},{0,4},{9,1},{1... | collective-permute-start | bytes 393224 | tf_op jit(solution)/shard_map/ppermute | solution.py:521
  78.0 6.8 %collective-permute-start.39 = (f32[256,128]{1,0:T(8,128)S(1)}, f32[256,128]{1,0:T(8,128)S(1)}, u32[]{:S(2)}, u32[]{:S(2)}) collective-permute-start(f32[256,128]{1,0:T(8,128)S(1)} %collective-permute-done.38.refs_6_), channel_id=1, source_target_pairs={{0,8},{8,16},{16,24},{24,28},{28,20},{20,12},{12,4},{4,0},{1,9},{9... | collective-permute-start | bytes 393224 | tf_op jit(solution)/shard_map/ppermute | solution.py:518
  82.7 7.6 %collective-permute-start.40 = (f32[256,128]{1,0:T(8,128)S(1)}, f32[256,128]{1,0:T(8,128)S(1)}, u32[]{:S(2)}, u32[]{:S(2)}) collective-permute-start(f32[256,128]{1,0:T(8,128)S(1)} %get-tuple-element.112), channel_id=1, source_target_pairs={{0,8},{8,16},{16,24},{24,28},{28,20},{20,12},{12,4},{4,0},{1,9},{9... | collective-permute-start | bytes 393224 | tf_op jit(solution)/shard_map/ppermute | solution.py:518
  89.5 5.9 %collective-permute-start.44 = (f32[256,128]{1,0:T(8,128)S(1)}, f32[256,128]{1,0:T(8,128)S(1)}, u32[]{:S(2)}, u32[]{:S(2)}) collective-permute-start(f32[256,128]{1,0:T(8,128)S(1)} %get-tuple-element.116), channel_id=1, source_target_pairs={{8,0},{16,8},{24,16},{28,24},{20,28},{12,20},{4,12},{0,4},{9,1},{1... | collective-permute-start | bytes 393224 | tf_op jit(solution)/shard_map/ppermute | solution.py:521
  90.3 6.3 %collective-permute-start.41 = (f32[256,128]{1,0:T(8,128)S(1)}, f32[256,128]{1,0:T(8,128)S(1)}, u32[]{:S(2)}, u32[]{:S(2)}) collective-permute-start(f32[256,128]{1,0:T(8,128)S(1)} %add_pairs.30), channel_id=1, source_target_pairs={{0,8},{8,16},{16,24},{24,28},{28,20},{20,12},{12,4},{4,0},{1,9},{9... | collective-permute-start | bytes 393224 | tf_op jit(solution)/shard_map/ppermute | solution.py:518
  96.7 6.4 %collective-permute-start.42 = (f32[256,128]{1,0:T(8,128)S(1)}, f32[256,128]{1,0:T(8,128)S(1)}, u32[]{:S(2)}, u32[]{:S(2)}) collective-permute-start(f32[256,128]{1,0:T(8,128)S(1)} %add_pairs.31), channel_id=1, source_target_pairs={{0,8},{8,16},{16,24},{24,28},{28,20},{20,12},{12,4},{4,0},{1,9},{9... | collective-permute-start | bytes 393224 | tf_op jit(solution)/shard_map/ppermute | solution.py:518
  98.2 7.7 %collective-permute-start.56 = (f32[256,128]{1,0:T(8,128)S(1)}, f32[256,128]{1,0:T(8,128)S(1)}, u32[]{:S(2)}, u32[]{:S(2)}) collective-permute-start(f32[256,128]{1,0:T(8,128)S(1)} %add_pairs.36), channel_id=1, source_target_pairs={{0,8},{8,16},{16,24},{24,28},{28,20},{20,12},{12,4},{4,0},{1,9},{9... | collective-permute-start | bytes 393224 | tf_op jit(solution)/shard_map/ppermute | solution.py:518
  99.7 9.2 %collective-permute-start.60 = (f32[256,128]{1,0:T(8,128)S(1)}, f32[256,128]{1,0:T(8,128)S(1)}, u32[]{:S(2)}, u32[]{:S(2)}) collective-permute-start(f32[256,128]{1,0:T(8,128)S(1)} %add_pairs.39), channel_id=1, source_target_pairs={{8,0},{16,8},{24,16},{28,24},{20,28},{12,20},{4,12},{0,4},{9,1},{1... | collective-permute-start | bytes 393224 | tf_op jit(solution)/shard_map/ppermute | solution.py:521
  100.7 6.7 %collective-permute-start.46 = (f32[256,128]{1,0:T(8,128)S(1)}, f32[256,128]{1,0:T(8,128)S(1)}, u32[]{:S(2)}, u32[]{:S(2)}) collective-permute-start(f32[256,128]{1,0:T(8,128)S(1)} %add_pairs.34), channel_id=1, source_target_pairs={{8,0},{16,8},{24,16},{28,24},{20,28},{12,20},{4,12},{0,4},{9,1},{1... | collective-permute-start | bytes 393224 | tf_op jit(solution)/shard_map/ppermute | solution.py:521
  103.1 5.7 %collective-permute-start.43 = (f32[256,128]{1,0:T(8,128)S(1)}, f32[256,128]{1,0:T(8,128)S(1)}, u32[]{:S(2)}, u32[]{:S(2)}) collective-permute-start(f32[256,128]{1,0:T(8,128)S(1)} %add_pairs.32), channel_id=1, source_target_pairs={{0,8},{8,16},{16,24},{24,28},{28,20},{20,12},{12,4},{4,0},{1,9},{9... | collective-permute-start | bytes 393224 | tf_op jit(solution)/shard_map/ppermute | solution.py:518
  105.9 6.4 %collective-permute-start.57 = (f32[256,128]{1,0:T(8,128)S(1)}, f32[256,128]{1,0:T(8,128)S(1)}, u32[]{:S(2)}, u32[]{:S(2)}) collective-permute-start(f32[256,128]{1,0:T(8,128)S(1)} %add_pairs.37), channel_id=1, source_target_pairs={{0,8},{8,16},{16,24},{24,28},{28,20},{20,12},{12,4},{4,0},{1,9},{9... | collective-permute-start | bytes 393224 | tf_op jit(solution)/shard_map/ppermute | solution.py:518
  113.0 6.4 %collective-permute-start.64 = (f32[264,128]{1,0:T(8,128)S(1)}, f32[264,128]{1,0:T(8,128)S(1)}, u32[]{:S(2)}, u32[]{:S(2)}) collective-permute-start(f32[264,128]{1,0:T(8,128)S(1)} %get-tuple-element.133.refs_9_.refs_0_), channel_id=1, source_target_pairs={{0,8},{8,16},{16,24},{24,28},{28,20},{20,12},{12,4},{4,0},{1,9},{9... | collective-permute-start | bytes 405512 | tf_op jit(solution)/shard_map/ppermute | solution.py:518
  114.3 7.1 %collective-permute-start.50 = (f32[256,128]{1,0:T(8,128)S(1)}, f32[256,128]{1,0:T(8,128)S(1)}, u32[]{:S(2)}, u32[]{:S(2)}) collective-permute-start(f32[256,128]{1,0:T(8,128)S(1)} %get-tuple-element.119.refs_1_), channel_id=1, source_target_pairs={{0,8},{8,16},{16,24},{24,28},{28,20},{20,12},{12,4},{4,0},{1,9},{9... | collective-permute-start | bytes 393224 | tf_op jit(solution)/shard_map/ppermute | solution.py:518
  115.8 6.9 %collective-permute-start.61 = (f32[264,128]{1,0:T(8,128)S(1)}, f32[264,128]{1,0:T(8,128)S(1)}, u32[]{:S(2)}, u32[]{:S(2)}) collective-permute-start(f32[264,128]{1,0:T(8,128)S(1)} %get-tuple-element.133.refs_9_.refs_0_), channel_id=1, source_target_pairs={{8,0},{16,8},{24,16},{28,24},{20,28},{12,20},{4,12},{0,4},{9,1},{1... | collective-permute-start | bytes 405512 | tf_op jit(solution)/shard_map/ppermute | solution.py:521
  127.7 6.8 %collective-permute-start.63 = (f32[264,128]{1,0:T(8,128)S(1)}, f32[264,128]{1,0:T(8,128)S(1)}, u32[]{:S(2)}, u32[]{:S(2)}) collective-permute-start(f32[264,128]{1,0:T(8,128)S(1)} %collective-permute-done.62.refs_11_.refs_2_), channel_id=1, source_target_pairs={{8,0},{16,8},{24,16},{28,24},{20,28},{12,20},{4,12},{0,4},{9,1},{1... | collective-permute-start | bytes 405512 | tf_op jit(solution)/shard_map/ppermute | solution.py:521
  130.7 5.9 %collective-permute-start.49 = (f32[256,128]{1,0:T(8,128)S(1)}, f32[256,128]{1,0:T(8,128)S(1)}, u32[]{:S(2)}, u32[]{:S(2)}) collective-permute-start(f32[256,128]{1,0:T(8,128)S(1)} %collective-permute-done.48.refs_3_), channel_id=1, source_target_pairs={{8,0},{16,8},{24,16},{28,24},{20,28},{12,20},{4,12},{0,4},{9,1},{1... | collective-permute-start | bytes 393224 | tf_op jit(solution)/shard_map/ppermute | solution.py:521
  (23 other events, 114.4 us)
